TPU v7x, 32 devices: a whole 2x2x4 slice. The times are simulated.
32 devices in a mesh: row: 8 (over z, x), col: 4 (over y, core).
Axes of the slice: x: 2, y: 2, z: 4, core: 2. Of those that a mesh axis runs over, the one named last changes fastest.
Arguments:
- tokens: bfloat16 [8192, 2048], P('row', 'col'), may hold values from -6 to 6
- cotangent: bfloat16 [8192, 2048], P('row', 'col'), may hold values from -6 to 6
- segment_ids: int32 [8192], P('row'), may hold values from 0 to 128, as said below
- gain_attn: float32 [2048], replicated, may hold values from 0.1 to 1.9
- gain_ffn: float32 [2048], replicated, may hold values from 0.1 to 1.9
- gain_query: float32 [128], replicated, may hold values from 0.1 to 1.9
- gain_key: float32 [128], replicated, may hold values from 0.1 to 1.9
- w_query: bfloat16 [2048, 2048], P('row', 'col'), may hold values from -0.125 to 0.125
- w_gate: bfloat16 [2048, 2048], P('row', 'col'), may hold values from -0.125 to 0.125
- w_key: bfloat16 [2048, 1024], P('row', 'col'), may hold values from -0.125 to 0.125
- w_value: bfloat16 [2048, 1024], P('row', 'col'), may hold values from -0.125 to 0.125
- w_out: bfloat16 [2048, 2048], P('row', 'col'), may hold values from -0.75 to 0.75
- w_ffgate: bfloat16 [2048, 6144], P('row', 'col'), may hold values from -0.125 to 0.125
- w_up: bfloat16 [2048, 6144], P('row', 'col'), may hold values from -0.125 to 0.125
- w_down: bfloat16 [2048, 6144], P('row', 'col'), may hold values from -0.109375 to 0.109375
Outputs:
- output: bfloat16 [8192, 2048], P('row', 'col')
- grad_tokens: float32 [8192, 2048], P('row', 'col')
- grad_gain_attn: float32 [2048], replicated
- grad_gain_ffn: float32 [2048], replicated
- grad_gain_query: float32 [128], replicated
- grad_gain_key: float32 [128], replicated
- grad_w_query: float32 [2048, 2048], P('row', 'col')
- grad_w_gate: float32 [2048, 2048], P('row', 'col')
- grad_w_key: float32 [2048, 1024], P('row', 'col')
- grad_w_value: float32 [2048, 1024], P('row', 'col')
- grad_w_out: float32 [2048, 2048], P('row', 'col')
- grad_w_ffgate: float32 [2048, 6144], P('row', 'col')
- grad_w_up: float32 [2048, 6144], P('row', 'col')
- grad_w_down: float32 [2048, 6144], P('row', 'col')
Inputs may be any that keep to these rules, and one draw needn't show every extreme that they name: `segment_ids`: each block of 1024 tokens is one packed sequence: its numbers start at 1, never fall and rise by at most one from token to token, up to a tail of padding (0) of one or more tokens; some sequence reaches 128 documents.
All inputs are finite; a program needn't handle non-finite values.
Results may differ from a plain program's by a relative error of at most 0.023.
Values may be sent and summed in bfloat16 or wider, within the bound.
No kernel may reach another device: no remote copies, remote signals or barrier semaphores. Data moves between devices by JAX's collectives and lax.ppermute only.
A program may use at most 256 MiB of HBM per device.

v0:
```python
from functools import partial

import jax
import jax.numpy as jnp
from jax import lax
from jax.sharding import PartitionSpec as P

eps_norm = 1e-06
rope_base = 1000000.0


def norm_rows(values, gain):
    inverse = lax.rsqrt(jnp.mean(values * values, axis=-1, keepdims=True) + eps_norm)
    return (values * inverse * gain, inverse)


def rope_tables(segments, head_dim):
    count = segments.shape[0]
    index = jnp.arange(count, dtype=jnp.int32)
    previous = jnp.concatenate([jnp.full((1,), -1, jnp.int32), segments[:-1]])
    starts = lax.cummax(jnp.where(segments != previous, index, 0), axis=0)
    position = (index - starts).astype(jnp.float32)
    half = head_dim // 2
    freqs = jnp.power(rope_base, -(jnp.arange(half, dtype=jnp.float32) * 2.0 / head_dim))
    angle = position[:, None] * freqs[None, :]
    angle = jnp.concatenate([angle, angle], axis=1)
    return (jnp.cos(angle), jnp.sin(angle))


def attend_mask(segments):
    count = segments.shape[0]
    index = jnp.arange(count, dtype=jnp.int32)
    earlier = index[None, :] < index[:, None]
    same = (segments[None, :] == segments[:, None]) & (segments[None, :] > 0)
    return (index[None, :] == index[:, None]) | earlier & same


def head_prepare(raw, gain, cosine, sine):
    count = raw.shape[0]
    head_dim = gain.shape[0]
    heads = raw.reshape(count, -1, head_dim)
    inverse = lax.rsqrt(jnp.mean(heads * heads, axis=-1, keepdims=True) + eps_norm)
    normed = heads * inverse * gain
    half = head_dim // 2
    turned = jnp.concatenate([-normed[..., half:], normed[..., :half]], axis=-1)
    return (normed * cosine[:, None, :] + turned * sine[:, None, :]).reshape(count, -1)


def feature_gather(values):
    return lax.all_gather(values, "col", axis=1, tiled=True)


def feature_sum(values):
    return lax.psum_scatter(
        values.astype(jnp.bfloat16), "col", scatter_dimension=1, tiled=True
    ).astype(jnp.float32)


def rows_in(operand, weight):
    return jnp.dot(
        operand,
        lax.all_gather(weight, "row", axis=0, tiled=True),
        preferred_element_type=jnp.float32,
    )


def rows_out(operand, weight):
    return lax.dot_general(
        operand,
        lax.all_gather(weight, "row", axis=0, tiled=True),
        (((1,), (1,)), ((), ())),
        preferred_element_type=jnp.float32,
    )


def weight_grads(firsts, seconds):
    blocks = []
    for first, second in zip(firsts, seconds):
        blocks.append(
            lax.dot_general(
                first, second, (((0,), (0,)), ((), ())), preferred_element_type=jnp.float32
            )
        )
    return lax.psum_scatter(
        jnp.concatenate(blocks, axis=1).astype(jnp.bfloat16), "row", scatter_dimension=0, tiled=True
    ).astype(jnp.float32)


def norm_back(partial_grad, unit, inverse, gain, local):
    offset = lax.axis_index("col") * local
    width = unit.shape[1]
    unit_own = lax.dynamic_slice_in_dim(unit, offset, local, 1)
    grad_own = feature_sum(partial_grad)
    gain_own = lax.dynamic_slice_in_dim(gain, offset, local, 0)
    scaled = grad_own * gain_own
    dots = lax.psum(jnp.sum(scaled * unit_own, axis=1), "col")[:, None] / width
    grad_input = inverse * (scaled - unit_own * dots)
    gain_grad = lax.dynamic_update_slice_in_dim(
        jnp.zeros((width,), jnp.float32), jnp.sum(grad_own * unit_own, axis=0), offset, 0
    )
    return (grad_input, gain_grad)


def attend_scores(query, keys, allowed, kv_heads, head_dim):
    count = query.shape[0]
    grouped = query.reshape(count, kv_heads, -1, head_dim)
    keyed = keys.reshape(count, kv_heads, head_dim)
    scores = jnp.einsum(
        "qgrd,kgd->grqk", grouped, keyed, preferred_element_type=jnp.float32
    ) * head_dim ** (-0.5)
    return (jnp.where(allowed, scores, -1e30), grouped, keyed)


def attend_forward(query, keys, values, allowed, kv_heads, head_dim):
    count = query.shape[0]
    scores, grouped, keyed = attend_scores(query, keys, allowed, kv_heads, head_dim)
    peak = jnp.max(scores, axis=-1, keepdims=True)
    weights = jnp.exp(scores - peak)
    total = jnp.sum(weights, axis=-1, keepdims=True)
    probs = (weights / total).astype(jnp.bfloat16)
    valued = values.reshape(count, kv_heads, head_dim)
    attended = jnp.einsum("grqk,kgd->qgrd", probs, valued, preferred_element_type=jnp.float32)
    return (attended.reshape(count, -1), peak + jnp.log(total))


def attend_backward(query, keys, values, allowed, logsum, grad_attended, kv_heads, head_dim):
    count = query.shape[0]
    scores, grouped, keyed = attend_scores(query, keys, allowed, kv_heads, head_dim)
    probs_exact = jnp.exp(scores - logsum)
    probs = probs_exact.astype(jnp.bfloat16)
    valued = values.reshape(count, kv_heads, head_dim)
    grad_grouped = grad_attended.reshape(count, kv_heads, -1, head_dim)
    grad_values = jnp.einsum(
        "grqk,qgrd->kgd", probs, grad_grouped, preferred_element_type=jnp.float32
    )
    grad_probs = jnp.einsum(
        "qgrd,kgd->grqk", grad_grouped, valued, preferred_element_type=jnp.float32
    )
    delta = jnp.sum(probs_exact * grad_probs, axis=-1, keepdims=True)
    grad_scores = (probs_exact * (grad_probs - delta)).astype(jnp.bfloat16)
    grad_query = jnp.einsum(
        "grqk,kgd->qgrd", grad_scores, keyed, preferred_element_type=jnp.float32
    ) * head_dim ** (-0.5)
    grad_keys = jnp.einsum(
        "grqk,qgrd->kgd", grad_scores, grouped, preferred_element_type=jnp.float32
    ) * head_dim ** (-0.5)
    return (
        grad_query.reshape(count, -1),
        grad_keys.reshape(count, -1),
        grad_values.reshape(count, -1).astype(jnp.bfloat16),
    )


def body(
    tokens,
    cotangent,
    segment_ids,
    gain_attn,
    gain_ffn,
    gain_query,
    gain_key,
    w_query,
    w_gate,
    w_key,
    w_value,
    w_out,
    w_ffgate,
    w_up,
    w_down,
):
    local = tokens.shape[1]
    head_dim = gain_query.shape[0]
    query_width = w_query.shape[1]
    key_width = w_key.shape[1]
    kv_heads = key_width // head_dim
    hidden_width = w_ffgate.shape[1]
    live = (segment_ids > 0).astype(jnp.float32)[:, None]
    cosine, sine = rope_tables(segment_ids, head_dim)
    allowed = attend_mask(segment_ids)
    attn_weight = jnp.concatenate([w_query, w_gate, w_key, w_value], axis=1)
    ffn_weight = jnp.concatenate([w_ffgate, w_up], axis=1)
    blocks = (attn_weight, ffn_weight, w_out, w_down)

    def apply_in(operand, which_block):
        return rows_in(operand, blocks[which_block])

    def apply_out(operand, which_block):
        return rows_out(operand, blocks[which_block])

    inputs = feature_gather(tokens).astype(jnp.float32)
    normed1, inverse1 = norm_rows(inputs, gain_attn)
    hidden1 = normed1.astype(jnp.bfloat16)
    joint = apply_in(hidden1, 0)
    query_raw = joint[:, :query_width]
    gate_raw = joint[:, query_width : 2 * query_width]
    key_raw = joint[:, 2 * query_width : 2 * query_width + key_width]
    values = joint[:, 2 * query_width + key_width :].astype(jnp.bfloat16)
    prepare = partial(head_prepare, cosine=cosine, sine=sine)
    query = prepare(query_raw, gain_query).astype(jnp.bfloat16)
    keys = prepare(key_raw, gain_key).astype(jnp.bfloat16)
    attended, logsum = attend_forward(query, keys, values, allowed, kv_heads, head_dim)
    gate_sig = jax.nn.sigmoid(gate_raw)
    mixed = (attended * gate_sig).astype(jnp.bfloat16)
    resid = tokens.astype(jnp.float32) + feature_sum(apply_out(mixed, 2))
    resid_full = feature_gather(resid.astype(jnp.bfloat16)).astype(jnp.float32)
    normed2, inverse2 = norm_rows(resid_full, gain_ffn)
    hidden2 = normed2.astype(jnp.bfloat16)
    ffn_joint = apply_in(hidden2, 1)
    ff_gate = ffn_joint[:, :hidden_width]
    ff_up = ffn_joint[:, hidden_width:]
    sig_gate = jax.nn.sigmoid(ff_gate)
    activated = (jax.nn.silu(ff_gate) * ff_up).astype(jnp.bfloat16)
    ffn_out = feature_sum(apply_out(activated, 3))
    output = (live * (resid + ffn_out)).astype(jnp.bfloat16)
    grad_out = live * cotangent.astype(jnp.float32)
    grad_ffn_full = feature_gather(grad_out.astype(jnp.bfloat16))
    grad_act = apply_in(grad_ffn_full, 3)
    grad_ffup = (grad_act * (ff_gate * sig_gate)).astype(jnp.bfloat16)
    grad_ffgate = (grad_act * ff_up * sig_gate * (1.0 + ff_gate * (1.0 - sig_gate))).astype(
        jnp.bfloat16
    )
    grad_pair = jnp.concatenate([grad_ffgate, grad_ffup], axis=1)
    ffn_grads = weight_grads((hidden2, grad_ffn_full), (grad_pair, activated))
    grad_input2, gain_ffn_grad = norm_back(
        apply_out(grad_pair, 1), resid_full * inverse2, inverse2, gain_ffn, local
    )
    grad_resid = grad_out + grad_input2
    grad_branch_full = feature_gather(grad_resid.astype(jnp.bfloat16))
    grad_mixed = apply_in(grad_branch_full, 2)
    grad_attended = (grad_mixed * gate_sig).astype(jnp.bfloat16)
    grad_gate_raw = (grad_mixed * attended * gate_sig * (1.0 - gate_sig)).astype(jnp.bfloat16)
    grad_query, grad_keys, grad_values = attend_backward(
        query, keys, values, allowed, logsum, grad_attended, kv_heads, head_dim
    )
    unused_query, query_back = jax.vjp(prepare, query_raw, gain_query)
    grad_query_raw, grad_gain_query = query_back(grad_query)
    unused_key, key_back = jax.vjp(prepare, key_raw, gain_key)
    grad_key_raw, grad_gain_key = key_back(grad_keys)
    grad_joint = jnp.concatenate(
        [
            grad_query_raw.astype(jnp.bfloat16),
            grad_gate_raw,
            grad_key_raw.astype(jnp.bfloat16),
            grad_values,
        ],
        axis=1,
    )
    attn_grads = weight_grads((hidden1, grad_branch_full), (grad_joint, mixed))
    grad_input1, gain_attn_grad = norm_back(
        apply_out(grad_joint, 0), inputs * inverse1, inverse1, gain_attn, local
    )
    grad_tokens = grad_resid + grad_input1
    gains = lax.psum(
        (gain_attn_grad, gain_ffn_grad, grad_gain_query, grad_gain_key), ("row", "col")
    )
    second_cut = 2 * query_width
    third_cut = 2 * query_width + key_width
    fourth_cut = 2 * query_width + 2 * key_width
    return (
        output,
        grad_tokens,
        gains[0],
        gains[1],
        gains[2],
        gains[3],
        attn_grads[:, :query_width],
        attn_grads[:, query_width:second_cut],
        attn_grads[:, second_cut:third_cut],
        attn_grads[:, third_cut:fourth_cut],
        attn_grads[:, fourth_cut:],
        ffn_grads[:, :hidden_width],
        ffn_grads[:, hidden_width : 2 * hidden_width],
        ffn_grads[:, 2 * hidden_width :],
    )


def solution(mesh):
    in_specs = (
        P("row", "col"),
        P("row", "col"),
        P("row"),
        P(),
        P(),
        P(),
        P(),
        P("row", "col"),
        P("row", "col"),
        P("row", "col"),
        P("row", "col"),
        P("row", "col"),
        P("row", "col"),
        P("row", "col"),
        P("row", "col"),
    )
    out_specs = (
        P("row", "col"),
        P("row", "col"),
        P(),
        P(),
        P(),
        P(),
        P("row", "col"),
        P("row", "col"),
        P("row", "col"),
        P("row", "col"),
        P("row", "col"),
        P("row", "col"),
        P("row", "col"),
        P("row", "col"),
    )
    return jax.shard_map(body, mesh=mesh, in_specs=in_specs, out_specs=out_specs, check_vma=False)
```

profile of v0, /device:TPU:0, one launch (start us, length us, event | category | flops | bytes accessed | tf_op | source)
XLA Modules:
  0.0 1402.9 jit_solution(407615306940650517)
XLA Ops:
  8.0 2.1 pad_maximum_fusion.9
  13.1 2.7 broadcast_multiply_fusion.3
  17.1 2.8 fusion.12
  19.8 27.0 %all-gather.9.cloned.1.call-done = bf16[1024,2048]{1,0:T(8,128)(2,1)} async-done(((bf16[1024,512]{1,0:T(8,128)(2,1)}), bf16[1024,2048]{1,0:T(8,128)(2,1)}) %all-gather.9.cloned.1.call-update) | async-done | bytes 4194320 | tf_op jit(solution)/shard_map/all_gather | solution.py:50
  46.8 3.1 fusion.5
  49.9 98.7 %all-gather.11.cloned.1.call-done = bf16[2048,1536]{1,0:T(8,128)(2,1)} async-done(((bf16[256,1536]{1,0:T(8,128)(2,1)}), bf16[2048,1536]{1,0:T(8,128)(2,1)}) %all-gather.11.cloned.1.call-update) | async-done | bytes 6291472 | tf_op jit(solution)/shard_map/all_gather | solution.py:62
  148.6 10.1 fusion.36
  158.8 2.6 copy-done.10
  162.6 2.0 multiply_reduce_fusion.5
  164.5 3.1 slice.91
  175.1 2.1 reshape.243
  178.8 2.8 multiply_multiply_fusion
  185.7 2.7 fusion.29
  189.0 9.0 fusion.66
  199.4 8.0 fusion.3
  207.4 8.8 fusion.10
  216.2 1.9 copy.259
  218.1 3.9 multiply_convert_fusion.8
  222.0 6.3 convolution_convert_fusion.5
  228.4 42.7 %reduce-scatter.7.cloned.1.call-done = bf16[1024,512]{1,0:T(8,128)(2,1)} async-done(((bf16[1024,2048]{1,0:T(8,128)(2,1)}), bf16[1024,512]{1,0:T(8,128)(2,1)}) %reduce-scatter.7.cloned.1.call-update) | async-done | bytes 1048592 | tf_op jit(solution)/shard_map/reduce_scatter | solution.py:54
  271.0 2.5 fusion.35
  273.6 2.5 pad_maximum_fusion.8
  278.3 29.9 %all-gather.15.cloned.1.call-done = bf16[1024,2048]{1,0:T(8,128)(2,1)} async-done(((bf16[1024,512]{1,0:T(8,128)(2,1)}), bf16[1024,2048]{1,0:T(8,128)(2,1)}) %all-gather.15.cloned.1.call-update) | async-done | bytes 4194320 | tf_op jit(solution)/shard_map/all_gather | solution.py:50
  308.2 3.1 fusion.6
  311.3 176.2 %all-gather.17.cloned.1.call-done = bf16[2048,3072]{1,0:T(8,128)(2,1)} async-done(((bf16[256,3072]{1,0:T(8,128)(2,1)}), bf16[2048,3072]{1,0:T(8,128)(2,1)}) %all-gather.17.cloned.1.call-update) | async-done | bytes 12582928 | tf_op jit(solution)/shard_map/all_gather | solution.py:62
  487.5 19.3 %fusion.37 = f32[1024,3072]{1,0:T(8,128)} fusion(bf16[2048,3072]{1,0:T(8,128)(2,1)} %all-gather.17.cloned.1.call-done, f32[2048]{0:T(1024)S(1)} %copy-done.57, bf16[1024,2048]{1,0:T(8,128)(2,1)} %all-gather.15.cloned.1.call-done, f32[1024]{0:T(1024)S(1)} %add_rsqrt_fusion), kind=kOutput, calls=%fused_computation.89 | convolution fusion | flops 12893290496 | bytes 29372416 | tf_op jit(solution)/shard_map/dot_general | solution.py:60
  506.8 15.6 %all-gather.21.cloned.1.call-done = bf16[1024,2048]{1,0:T(8,128)(2,1)} async-done(((bf16[1024,512]{1,0:T(8,128)(2,1)}), bf16[1024,2048]{1,0:T(8,128)(2,1)}) %all-gather.21.cloned.1.call-update) | async-done | bytes 4194320 | tf_op jit(solution)/shard_map/all_gather | solution.py:50
  522.4 101.5 %all-gather.19.cloned.1.call-done = bf16[2048,1536]{1,0:T(8,128)(2,1)} async-done(((bf16[256,1536]{1,0:T(8,128)(2,1)}), bf16[2048,1536]{1,0:T(8,128)(2,1)}) %all-gather.19.cloned.1.call-update) | async-done | bytes 6291472 | tf_op jit(solution)/shard_map/all_gather | solution.py:70
  623.9 16.4 %multiply_convert_fusion.3 = (bf16[1024,1536]{1,0:T(8,128)(2,1)S(1)}, bf16[1024,1536]{1,0:T(8,128)(2,1)}, bf16[1024,1536]{1,0:T(8,128)(2,1)}) fusion(f32[1024,3072]{1,0:T(8,128)} %fusion.37, bf16[1024,2048]{1,0:T(8,128)(2,1)} %all-gather.21.cloned.1.call-done, bf16[2048,1536]{1,0:T(8,128)(2,1)} %all-gather.19.cloned.1.call-done), kind=kOutput, calls=%fused_computation.29 | convolution fusion | flops 6466043904 | bytes 32505856 | tf_op jit(solution)/shard_map/dot_general | solution.py:60
  640.3 1.7 copy-done.64
  641.9 18.5 %fusion.15 = bf16[1024,2048]{1,0:T(8,128)(2,1)} fusion(bf16[2048,3072]{1,0:T(8,128)(2,1)} %all-gather.17.cloned.1.call-done, bf16[1024,1536]{1,0:T(8,128)(2,1)} %get-tuple-element.115, bf16[1024,1536]{1,0:T(8,128)(2,1)S(1)} %get-tuple-element.114), kind=kOutput, calls=%fused_computation.40 | convolution fusion | flops 12899581952 | bytes 23068672 | tf_op jit(solution)/shard_map/dot_general | solution.py:68
  661.0 6.8 convert_multiply_fusion
  667.7 35.6 %reduce-scatter.11.cloned.1.call-done = bf16[1024,512]{1,0:T(8,128)(2,1)} async-done(((bf16[1024,2048]{1,0:T(8,128)(2,1)}), bf16[1024,512]{1,0:T(8,128)(2,1)}) %reduce-scatter.11.cloned.1.call-update) | async-done | bytes 1048592 | tf_op jit(solution)/shard_map/reduce_scatter | solution.py:54
  703.3 3.1 fusion.26
  706.4 5.7 psum.42
  712.1 3.5 fusion.59
  715.7 35.6 %all-gather.23.cloned.1.call-done = bf16[1024,2048]{1,0:T(8,128)(2,1)} async-done(((bf16[1024,512]{1,0:T(8,128)(2,1)}), bf16[1024,2048]{1,0:T(8,128)(2,1)}) %all-gather.23.cloned.1.call-update) | async-done | bytes 4194320 | tf_op jit(solution)/shard_map/all_gather | solution.py:50
  751.3 7.8 multiply_convert_fusion.5
  759.7 8.7 fusion.41
  768.4 10.7 fusion
  780.1 12.1 fusion.2
  792.2 2.6 convolution_multiply_fusion
  794.9 2.9 broadcast_multiply_fusion.1
  799.8 2.2 copy.222
  806.3 5.2 multiply_reduce_fusion
  811.9 5.3 fusion.28
  818.4 11.2 convolution_convert_fusion.3
  829.7 1.8 copy-done.62
  831.5 11.0 convolution_convert_fusion.4
  843.7 4.7 convolution_convert_fusion.6
  848.5 10.3 convolution_convert_fusion.2
  858.8 7.6 pad_maximum_fusion.1
  866.5 1.8 copy-done.63
  868.3 11.4 convolution_convert_fusion.1
  879.7 19.3 %convolution_convert_fusion = bf16[2048,3072]{1,0:T(8,128)(2,1)} fusion(bf16[1024,1536]{1,0:T(8,128)(2,1)} %get-tuple-element.115, bf16[1024,1536]{1,0:T(8,128)(2,1)} %copy-done.64, f32[2048]{0:T(1024)S(1)} %copy-done.57, bf16[1024,2048]{1,0:T(8,128)(2,1)S(1)} %copy-done.5, f32[1024]{0:T(1024)S(1)} %add_rsqrt_fusion), kind=kOutput, calls=%fused_computation.12 | convolution fusion | flops 12912164864 | bytes 23080960 | tf_op jit(solution)/shard_map/dot_general | solution.py:80
  899.0 16.3 %pad_maximum_fusion = bf16[2048,4608]{1,0:T(8,128)(2,1)} fusion(bf16[2048,1536]{1,0:T(8,128)(2,1)} %convolution_convert_fusion.1, bf16[2048,3072]{1,0:T(8,128)(2,1)} %convolution_convert_fusion), kind=kLoop, calls=%fused_computation | loop fusion | flops 37748736 | bytes 37748736 | tf_op jit(solution)/shard_map/concatenate | solution.py:85
  915.5 6.4 convert_multiply_fusion.2
  922.0 2.5 fusion.27
  924.8 42.5 %all-reduce.4 = (f32[2048]{0:T(1024)}, f32[2048]{0:T(1024)}, f32[128]{0:T(128)}, f32[128]{0:T(128)}) all-reduce(f32[2048]{0:T(1024)S(1)} %dynamic_update_slice.6, f32[2048]{0:T(1024)S(1)} %dynamic_update_slice.7, f32[128]{0:T(128)S(1)} %get-tuple-element.102, ...), channel_id=1, replica_groups=mesh['row'=8,'col'=4] {'row','col'}, use_global_device_ids=true, to_apply=%region_20.21 | all-reduce | flops 4352 | bytes 34816 | tf_op jit(solution)/shard_map/psum | solution.py:253
  967.4 6.7 psum.43
  974.2 5.1 fusion.22
  979.3 96.1 %reduce-scatter.15.cloned.1.call-done = bf16[256,2048]{0,1:T(8,128)(2,1)} async-done(((bf16[2048,2048]{0,1:T(8,128)(2,1)}), bf16[256,2048]{0,1:T(8,128)(2,1)}) %reduce-scatter.15.cloned.1.call-update) | async-done | bytes 1048592 | tf_op jit(solution)/shard_map/reduce_scatter | solution.py:84
  1081.4 310.5 %reduce-scatter.17.cloned.1.call-done = bf16[256,4608]{1,0:T(8,128)(2,1)} async-done(((bf16[2048,4608]{1,0:T(8,128)(2,1)}), bf16[256,4608]{1,0:T(8,128)(2,1)}) %reduce-scatter.17.cloned.1.call-update) | async-done | bytes 2359312 | tf_op jit(solution)/shard_map/reduce_scatter | solution.py:84
  1392.0 4.0 fusion.61
  (228 shorter events, 41.4 us)
Async XLA Ops:
  7.2 8.8 copy-start.55
  7.2 9.9 copy-start.52
  7.2 9.9 copy-start.41
  7.2 39.6 %all-gather.9.cloned.1.call-start = ((), (), s32[]{:S(2)}) async-start(), calls=%async_computation.6 | async-start | bytes 5242880 | tf_op jit(solution)/shard_map/all_gather | solution.py:50
  8.0 140.7 %all-gather.11.cloned.1.call-start = ((), (), s32[]{:S(2)}) async-start(), calls=%async_computation.7 | async-start | bytes 7077888 | tf_op jit(solution)/shard_map/all_gather | solution.py:62
  10.1 211.9 %all-gather.13.cloned.1.call-start = ((), (), s32[]{:S(2)}) async-start(), calls=%async_computation.8 | async-start | bytes 2359296 | tf_op jit(solution)/shard_map/all_gather | solution.py:70
  10.9 260.2 %reduce-scatter.7.cloned.1.call-start = ((), (), s32[]{:S(2)}) async-start(), calls=%async_computation.9 | async-start | bytes 5242880 | tf_op jit(solution)/shard_map/reduce_scatter | solution.py:54
  11.6 700.5 %copy-start.44 = (f32[1024]{0:T(1024)}, f32[1024]{0:T(1024)S(1)}, u32[]{:S(2)}) copy-start(f32[1024]{0:T(1024)S(1)} %get-tuple-element.112) | copy-start | bytes 12292
  15.8 132.8 %copy-start.58 = (f32[2048]{0:T(1024)S(1)}, f32[2048]{0:T(1024)}, u32[]{:S(2)}) copy-start(f32[2048]{0:T(1024)} %param.18) | copy-start | bytes 24580
  16.0 168.1 %copy-start.16 = (f32[1024,128]{1,0:T(8,128)}, f32[1024,128]{1,0:T(8,128)S(1)}, u32[]{:S(2)}) copy-start(f32[1024,128]{1,0:T(8,128)S(1)} %copy.205) | copy-start | bytes 1572868
  49.9 108.8 %copy-start.46 = (f32[1024]{0:T(1024)}, f32[1024]{0:T(1024)S(1)}, u32[]{:S(2)}) copy-start(f32[1024]{0:T(1024)S(1)} %add_rsqrt_fusion.1) | copy-start | bytes 12292
  158.8 2.6 copy-start.10
  162.6 6.1 copy-start.6
  164.5 3.1 copy-start.25
  177.2 4.4 copy-start
  178.5 4.3 copy-start.39
  178.8 5.7 copy-start.8
  185.7 3.3 copy-start.27
  189.0 9.0 copy-start.22
  218.1 3.9 copy-start.18
  228.3 42.8 %copy-start.11 = (bf16[1024,512]{1,0:T(8,128)(2,1)S(1)}, bf16[1024,512]{1,0:T(8,128)(2,1)}, u32[]{:S(2)}) copy-start(bf16[1024,512]{1,0:T(8,128)(2,1)} %param.15) | copy-start | bytes 3145732
  228.3 45.3 %copy-start.32 = (bf16[256,1536]{1,0:T(8,128)(2,1)S(1)}, bf16[256,1536]{1,0:T(8,128)(2,1)}, u32[]{:S(2)}) copy-start(bf16[256,1536]{1,0:T(8,128)(2,1)} %param.28) | copy-start | bytes 2359300
  228.3 47.9 %copy-start.13 = (bf16[1024,512]{1,0:T(8,128)(2,1)S(1)}, bf16[1024,512]{1,0:T(8,128)(2,1)}, u32[]{:S(2)}) copy-start(bf16[1024,512]{1,0:T(8,128)(2,1)} %param.16) | copy-start | bytes 3145732
  228.3 79.9 %all-gather.15.cloned.1.call-start = ((), (), s32[]{:S(2)}) async-start(), calls=%async_computation.10 | async-start | bytes 5242880 | tf_op jit(solution)/shard_map/all_gather | solution.py:50
  273.5 214.0 %all-gather.17.cloned.1.call-start = ((), (), s32[]{:S(2)}) async-start(), calls=%async_computation.11 | async-start | bytes 14155776 | tf_op jit(solution)/shard_map/all_gather | solution.py:62
  276.1 211.4 %copy-start.57 = (f32[2048]{0:T(1024)S(1)}, f32[2048]{0:T(1024)}, u32[]{:S(2)}) copy-start(f32[2048]{0:T(1024)} %param.19) | copy-start | bytes 24580
  276.1 246.3 %all-gather.21.cloned.1.call-start = ((), (), s32[]{:S(2)}) async-start(), calls=%async_computation.14 | async-start | bytes 5242880 | tf_op jit(solution)/shard_map/all_gather | solution.py:50
  277.5 346.4 %all-gather.19.cloned.1.call-start = ((), (), s32[]{:S(2)}) async-start(), calls=%async_computation.12 | async-start | bytes 7077888 | tf_op jit(solution)/shard_map/all_gather | solution.py:70
  278.2 425.1 %reduce-scatter.11.cloned.1.call-start = ((), (), s32[]{:S(2)}) async-start(), calls=%async_computation.15 | async-start | bytes 5242880 | tf_op jit(solution)/shard_map/reduce_scatter | solution.py:54
  660.5 90.9 %all-gather.23.cloned.1.call-start = ((), (), s32[]{:S(2)}) async-start(), calls=%async_computation.16 | async-start | bytes 5242880 | tf_op jit(solution)/shard_map/all_gather | solution.py:50
  661.0 51.1 %copy-start.50 = (f32[512]{0:T(512)}, f32[512]{0:T(512)S(1)}, u32[]{:S(2)}) copy-start(f32[512]{0:T(512)S(1)} %dynamic_slice.12) | copy-start | bytes 6148
  712.1 47.0 %copy-start.48 = (f32[1024]{0:T(1024)}, f32[1024]{0:T(1024)S(1)}, u32[]{:S(2)}) copy-start(f32[1024]{0:T(1024)S(1)} %broadcast_multiply_fusion.6) | copy-start | bytes 12292
  715.6 206.4 %reduce-scatter.13.cloned.1.call-start = ((), (), s32[]{:S(2)}) async-start(), calls=%async_computation.17 | async-start | bytes 5242880 | tf_op jit(solution)/shard_map/reduce_scatter | solution.py:54
  780.1 12.1 copy-start.28
  792.2 2.7 copy-start.19
  792.2 2.7 copy-start.23
  794.8 3.0 copy-start.7
  794.8 3.0 copy-start.26
  794.8 3.0 copy-start.38
  794.8 3.0 copy-start.56
  798.2 5.0 copy-start.21
  806.3 5.3 copy-start.40
  811.9 6.5 copy-start.33
  811.9 6.5 copy-start.35
  811.9 6.5 copy-start.60
  829.6 144.5 %reduce-scatter.9.cloned.1.call-start = ((), (), s32[]{:S(2)}) async-start(), calls=%async_computation.13 | async-start | bytes 5242880 | tf_op jit(solution)/shard_map/reduce_scatter | solution.py:54
  842.5 6.0 copy-start.47
  842.5 5.9 copy-start.59
  842.5 232.9 %reduce-scatter.15.cloned.1.call-start = ((), (), s32[]{:S(2)}) async-start(), calls=%async_computation.18 | async-start | bytes 9437184 | tf_op jit(solution)/shard_map/reduce_scatter | solution.py:84
  843.7 4.8 copy-start.4
  843.7 4.8 copy-start.31
  843.7 4.8 copy-start.34
  843.7 4.8 copy-start.36
  843.7 4.8 copy-start.61
  866.4 525.5 %reduce-scatter.17.cloned.1.call-start = ((), (), s32[]{:S(2)}) async-start(), calls=%async_computation.19 | async-start | bytes 21233664 | tf_op jit(solution)/shard_map/reduce_scatter | solution.py:84
  868.3 11.4 copy-start.5
  915.5 6.4 copy-start.54
  915.5 58.7 %copy-start.12 = (bf16[1024,512]{1,0:T(8,128)(2,1)S(1)}, bf16[1024,512]{1,0:T(8,128)(2,1)}, u32[]{:S(2)}) copy-start(bf16[1024,512]{1,0:T(8,128)(2,1)} %param.15) | copy-start | bytes 3145732
  915.5 58.7 %copy-start.14 = (bf16[1024,512]{1,0:T(8,128)(2,1)S(1)}, bf16[1024,512]{1,0:T(8,128)(2,1)}, u32[]{:S(2)}) copy-start(bf16[1024,512]{1,0:T(8,128)(2,1)} %param.16) | copy-start | bytes 3145732
  915.5 58.7 %copy-start.15 = (bf16[1024,512]{1,0:T(8,128)(2,1)S(1)}, bf16[1024,512]{1,0:T(8,128)(2,1)}, u32[]{:S(2)}) copy-start(bf16[1024,512]{1,0:T(8,128)(2,1)} %reduce-scatter.11.cloned.1.call-done) | copy-start | bytes 3145732
  915.5 58.7 %copy-start.45 = (f32[1024]{0:T(1024)S(1)}, f32[1024]{0:T(1024)}, u32[]{:S(2)}) copy-start(f32[1024]{0:T(1024)} %copy-done.44) | copy-start | bytes 12292
  915.5 58.7 %copy-start.49 = (f32[1024]{0:T(1024)S(1)}, f32[1024]{0:T(1024)}, u32[]{:S(2)}) copy-start(f32[1024]{0:T(1024)} %copy-done.48) | copy-start | bytes 12292
  915.5 58.7 %copy-start.51 = (f32[512]{0:T(512)S(1)}, f32[512]{0:T(512)}, u32[]{:S(2)}) copy-start(f32[512]{0:T(512)} %copy-done.50) | copy-start | bytes 6148
  1075.4 3.3 copy-start.24
  (15 other events, 23.2 us)
Sparse Core Ops, SparseCore 0:
  9.6 37.1 all-gather.8
  49.6 99.0 all-gather.10
  150.8 47.4 all-gather.12
  228.4 42.5 reduce-scatter.6
  273.7 34.4 all-gather.14
  311.0 176.4 all-gather.16
  489.7 32.6 all-gather.20
  524.8 99.0 all-gather.18
  660.6 42.6 reduce-scatter.10
  715.8 35.5 all-gather.22
  829.7 44.5 reduce-scatter.12
  876.8 44.5 reduce-scatter.8
  925.0 150.3 reduce-scatter.14
  1079.6 312.2 reduce-scatter.16
where the time goes:
time: 1410 us; the launch traced here: 1400 us
  waiting for transfers between devices  972 us (69%)
  matrix products  189 us (13%)
  other arithmetic  123 us (9%)
  blocking collectives  55 us (4%)
  local copies, waits for them, and re-layouts  47.6 us (3%)
  between operations  15.3 us (1%)
    reduce_scatter x2, waiting for transfers between devices, weight_grads(): lax.psum_scatter(jnp.concatenate(blocks, axis=1).astype(jnp.bfloat16), 'r...  407 us
    all_gather x2, waiting for transfers between devices, rows_in(): lax.all_gather(weight, 'row', axis=0, tiled=True)  275 us
    all_gather x4, waiting for transfers between devices, feature_gather(): return lax.all_gather(values, 'col', axis=1, tiled=True)  108 us
    all_gather x2, waiting for transfers between devices, rows_out(): lax.all_gather(weight, 'row', axis=0, tiled=True)  101 us
    reduce_scatter x4, waiting for transfers between devices, feature_sum(): lax.psum_scatter(values.astype(jnp.bfloat16), 'col', scatter_dimension=1,...  78.2 us
    dot_general x4, matrix products, rows_in(): jnp.dot(operand, lax.all_gather(weight, 'row', axis=0, tiled=True), prefe...  53.6 us
    dot_general x4, matrix products, rows_out(): lax.dot_general(operand, lax.all_gather(weight, 'row', axis=0, tiled=True...  46.9 us
    dot_general x4, matrix products, weight_grads(): lax.dot_general(first, second, (((0,), (0,)), ((), ())), preferred_elemen...  45.7 us
  transfers between devices with their start and end apart: 14, of which 11 were waited for; matrix products, arithmetic and copies ran while one was open for 16% of the time, Pallas kernels for 0%

commit v1 on v0

--- a/solution.py
+++ b/solution.py
@@ -3,6 +3,9 @@
 import jax
 import jax.numpy as jnp
 from jax import lax
+from jax.experimental import pallas as pl
+from jax.experimental.pallas import tpu as pltpu
+from jax.sharding import Mesh
 from jax.sharding import PartitionSpec as P
 
 eps_norm = 1e-06
@@ -274,38 +277,376 @@
     )
 
 
+def plain(mesh):
+    in_specs = (
+        P("row", "col"),
+        P("row", "col"),
+        P("row"),
+        P(),
+        P(),
+        P(),
+        P(),
+        P("row", "col"),
+        P("row", "col"),
+        P("row", "col"),
+        P("row", "col"),
+        P("row", "col"),
+        P("row", "col"),
+        P("row", "col"),
+        P("row", "col"),
+    )
+    out_specs = (
+        P("row", "col"),
+        P("row", "col"),
+        P(),
+        P(),
+        P(),
+        P(),
+        P("row", "col"),
+        P("row", "col"),
+        P("row", "col"),
+        P("row", "col"),
+        P("row", "col"),
+        P("row", "col"),
+        P("row", "col"),
+        P("row", "col"),
+    )
+    return jax.shard_map(body, mesh=mesh, in_specs=in_specs, out_specs=out_specs, check_vma=False)
+
+
+def flip(values, axis):
+    return lax.ppermute(values, axis, [(0, 1), (1, 0)])
+
+
+def spread(own):
+    half = own.shape[0] // 2
+    via_y = flip(own, "y")
+    via_x = flip(own, "x")
+    first = flip(via_y[:half], "x")
+    second = flip(via_x[half:], "y")
+    held = ((own, via_y), (via_x, jnp.concatenate([first, second], axis=0)))
+    return tuple(
+        tuple(block for values in pair for block in (values, flip(values, "core")))
+        for pair in held
+    )
+
+
+def pack_kernel(place_ref, gain_ref, *refs):
+    blocks, out_ref = refs[:4], refs[4]
+    width = blocks[0].shape[1]
+    place = place_ref[0]
+    if len(refs) == 6:
+        values = [block[...].astype(jnp.float32) for block in blocks]
+        squares = sum(jnp.sum(v * v, axis=1, keepdims=True) for v in values)
+        inverse = lax.rsqrt(squares / (4 * width) + eps_norm)
+        refs[5][...] = inverse
+    for index in range(4):
+        columns = pl.ds(pl.multiple_of((place ^ index) * width, width), width)
+        if len(refs) == 6:
+            result = values[index] * inverse * gain_ref[:, columns]
+            out_ref[:, columns] = result.astype(out_ref.dtype)
+        else:
+            out_ref[:, columns] = blocks[index][...]
+
+
+def pack(blocks, place, gain, normed):
+    count, width = blocks[0].shape
+    tile = 256
+    out_shape = [jax.ShapeDtypeStruct((count, 4 * width), jnp.bfloat16)]
+    out_specs = [pl.BlockSpec((tile, 4 * width), lambda i: (i, 0))]
+    if normed:
+        out_shape.append(jax.ShapeDtypeStruct((count, 1), jnp.float32))
+        out_specs.append(pl.BlockSpec((tile, 1), lambda i: (i, 0)))
+    return pl.pallas_call(
+        pack_kernel,
+        grid=(count // tile,),
+        in_specs=[
+            pl.BlockSpec(memory_space=pltpu.SMEM),
+            pl.BlockSpec((1, 4 * width), lambda i: (0, 0)),
+        ]
+        + [pl.BlockSpec((tile, width), lambda i: (i, 0))] * 4,
+        out_specs=out_specs,
+        out_shape=out_shape,
+        cost_estimate=pl.CostEstimate(
+            flops=0, bytes_accessed=count * width * 16, transcendentals=0
+        ),
+    )(place.reshape(1), gain.reshape(1, -1), *blocks)
+
+
+def gather_normed(own, place, gain):
+    first, second = spread(own)
+    normed_own, inverse = pack(first, place, gain, True)
+    normed_other, unused = pack(second, place, gain, True)
+    return (jnp.concatenate([normed_own, normed_other], axis=0), inverse)
+
+
+def gather_plain(own, place, gain):
+    first, second = spread(own)
+    return jnp.concatenate(
+        [pack(first, place, gain, False)[0], pack(second, place, gain, False)[0]], axis=0
+    )
+
+
+def halves(weights, across):
+    keep, give = [], []
+    for weight in weights:
+        width = weight.shape[1] // 2
+        keep.append(lax.dynamic_slice_in_dim(weight, across * width, width, 1))
+        give.append(lax.dynamic_slice_in_dim(weight, (1 - across) * width, width, 1))
+    return (keep, give)
+
+
+def weight_gather(keep, give, across):
+    keep = jnp.concatenate(keep, axis=1)
+    got = flip(jnp.concatenate(give, axis=1), "x")
+    top = jnp.where(across == 0, keep, got)
+    bottom = jnp.where(across == 0, got, keep)
+    return lax.all_gather(jnp.concatenate([top, bottom], axis=0), "z", axis=0, tiled=True)
+
+
+def grad_scatter(grads, across):
+    summed = lax.psum_scatter(grads, "z", scatter_dimension=0, tiled=True)
+    rows = summed.shape[0] // 2
+    keep = lax.dynamic_slice_in_dim(summed, across * rows, rows, 0)
+    got = flip(lax.dynamic_slice_in_dim(summed, (1 - across) * rows, rows, 0), "x")
+    return (jnp.where(across == 0, keep, got), jnp.where(across == 0, got, keep))
+
+
+def feature_fold(pairs, place):
+    def product(index):
+        total = None
+        for operand, weight in pairs:
+            rows = weight.shape[0] // 4
+            block = lax.dynamic_slice_in_dim(weight, (place ^ index) * rows, rows, 0)
+            term = lax.dot_general(
+                operand, block, (((1,), (1,)), ((), ())), preferred_element_type=jnp.float32
+            )
+            total = term if total is None else total + term
+        return total
+
+    low = jnp.bfloat16
+    sent = [flip(product(index).astype(low), "core") for index in (1, 3)]
+    held = [product(index) + got for index, got in zip((0, 2), sent)]
+    count = held[0].shape[0] // 2
+    half = count // 2
+    near, far = [v.astype(low) for v in held]
+    upper = flip(jnp.stack([near[count : count + half], far[count : count + half]]), "x")
+    lower = flip(jnp.stack([far[half:count], far[count + half :]]), "y")
+    upper_near = near[:half].astype(jnp.float32) + upper[0]
+    upper_far = (far[:half].astype(jnp.float32) + upper[1]).astype(low)
+    lower_own = near[half:count].astype(jnp.float32) + lower[0]
+    lower_other = (near[count + half :].astype(jnp.float32) + lower[1]).astype(low)
+    upper_final = upper_near + flip(upper_far, "y")
+    lower_final = lower_own + flip(lower_other, "x")
+    return jnp.concatenate([upper_final, lower_final], axis=0)
+
+
+def norm_back_own(grad_own, values_own, inverse, gain_own, width):
+    unit = values_own * inverse
+    scaled = grad_own * gain_own
+    dots = jnp.sum(scaled * unit, axis=1, keepdims=True)
+    dots = dots + flip(dots, "core")
+    dots = dots + flip(dots, "y")
+    grad_input = inverse * (scaled - unit * (dots / width))
+    return (grad_input, jnp.sum(grad_own * unit, axis=0))
+
+
+def dot_in(operand, weight):
+    return jnp.dot(operand, weight, preferred_element_type=jnp.float32)
+
+
+def dot_grad(first, second):
+    return lax.dot_general(
+        first, second, (((0,), (0,)), ((), ())), preferred_element_type=jnp.float32
+    ).astype(jnp.bfloat16)
+
+
+def fast_body(
+    tokens,
+    cotangent,
+    segment_ids,
+    gain_attn,
+    gain_ffn,
+    gain_query,
+    gain_key,
+    w_query,
+    w_gate,
+    w_key,
+    w_value,
+    w_out,
+    w_ffgate,
+    w_up,
+    w_down,
+):
+    across = lax.axis_index("x")
+    place = lax.axis_index("y") * 2 + lax.axis_index("core")
+    count, local = tokens.shape
+    width = gain_attn.shape[0]
+    head_dim = gain_query.shape[0]
+    low = jnp.bfloat16
+    query_width = w_query.shape[1] // 2
+    key_width = w_key.shape[1] // 2
+    kv_heads = key_width // head_dim
+    hidden_width = w_ffgate.shape[1] // 2
+    chunk = hidden_width // 2
+    live = (segment_ids > 0).astype(jnp.float32)[:, None]
+    offset = place * local
+    gain_attn_own = lax.dynamic_slice_in_dim(gain_attn, offset, local, 0)
+    gain_ffn_own = lax.dynamic_slice_in_dim(gain_ffn, offset, local, 0)
+
+    keep, give = halves([w_query, w_gate, w_key, w_value], across)
+    attn_weight = weight_gather(keep, give, across)
+    hidden1, inverse1 = gather_normed(tokens, place, gain_attn)
+    keep, give = halves([w_out], across)
+    out_weight = weight_gather(keep, give, across)
+    keep, give = halves([w_down], across)
+    down_weight = weight_gather(keep, give, across)
+    keep, give = halves([w_ffgate, w_up], across)
+    pair_weights = []
+    for part in range(2):
+        cut = slice(part * chunk, (part + 1) * chunk)
+        pair_weights.append(
+            weight_gather([v[:, cut] for v in keep], [v[:, cut] for v in give], across)
+        )
+
+    segments = jnp.stack([segment_ids, flip(segment_ids, "x")])
+    cosine, sine = jax.vmap(partial(rope_tables, head_dim=head_dim))(segments)
+    cosine = cosine.reshape(2 * count, head_dim)
+    sine = sine.reshape(2 * count, head_dim)
+    allowed = jax.vmap(attend_mask)(segments)
+
+    joint = dot_in(hidden1, attn_weight)
+    query_raw = joint[:, :query_width]
+    gate_raw = joint[:, query_width : 2 * query_width]
+    key_raw = joint[:, 2 * query_width : 2 * query_width + key_width]
+    values = joint[:, 2 * query_width + key_width :].astype(low)
+    prepare = partial(head_prepare, cosine=cosine, sine=sine)
+    query = prepare(query_raw, gain_query).astype(low)
+    keys = prepare(key_raw, gain_key).astype(low)
+    split = lambda v: v.reshape(2, count, -1)
+    attended, logsum = jax.vmap(
+        partial(attend_forward, kv_heads=kv_heads, head_dim=head_dim)
+    )(split(query), split(keys), split(values), allowed)
+    attended = attended.reshape(2 * count, -1)
+    gate_sig = jax.nn.sigmoid(gate_raw)
+    mixed = (attended * gate_sig).astype(low)
+    resid = tokens.astype(jnp.float32) + feature_fold([(mixed, out_weight)], place)
+    resid_low = resid.astype(low)
+    hidden2, inverse2 = gather_normed(resid_low, place, gain_ffn)
+
+    grad_out = live * cotangent.astype(jnp.float32)
+    grad_out_full = gather_plain(grad_out.astype(low), place, gain_ffn)
+    grad_act = dot_in(grad_out_full, down_weight)
+
+    activated, grad_pairs = [], []
+    for part in range(2):
+        ffn_joint = dot_in(hidden2, pair_weights[part])
+        ff_gate = ffn_joint[:, :chunk]
+        ff_up = ffn_joint[:, chunk:]
+        sig_gate = jax.nn.sigmoid(ff_gate)
+        activated.append((ff_gate * sig_gate * ff_up).astype(low))
+        grad_part = grad_act[:, part * chunk : (part + 1) * chunk]
+        grad_ffup = (grad_part * (ff_gate * sig_gate)).astype(low)
+        grad_ffgate = (grad_part * ff_up * sig_gate * (1.0 + ff_gate * (1.0 - sig_gate))).astype(
+            low
+        )
+        grad_pairs.append(jnp.concatenate([grad_ffgate, grad_ffup], axis=1))
+    activated = jnp.concatenate(activated, axis=1)
+    pair_grads = [dot_grad(hidden2, grad_pair) for grad_pair in grad_pairs]
+    down_grad = dot_grad(grad_out_full, activated)
+    pair_sums = [grad_scatter(grads, across) for grads in pair_grads]
+    down_sum = grad_scatter(down_grad, across)
+
+    grad_hidden2 = feature_fold(list(zip(grad_pairs, pair_weights)), place)
+    grad_input2, gain_ffn_grad = norm_back_own(
+        grad_hidden2, resid_low.astype(jnp.float32), inverse2, gain_ffn_own, width
+    )
+    grad_resid = grad_out + grad_input2
+    ffn_out = feature_fold([(activated, down_weight)], place)
+    output = (live * (resid + ffn_out)).astype(low)
+    grad_branch_full = gather_plain(grad_resid.astype(low), place, gain_ffn)
+    grad_mixed = dot_in(grad_branch_full, out_weight)
+    out_sum = grad_scatter(dot_grad(grad_branch_full, mixed), across)
+    grad_attended = (grad_mixed * gate_sig).astype(low)
+    grad_gate_raw = (grad_mixed * attended * gate_sig * (1.0 - gate_sig)).astype(low)
+    grad_query, grad_keys, grad_values = jax.vmap(
+        partial(attend_backward, kv_heads=kv_heads, head_dim=head_dim)
+    )(split(query), split(keys), split(values), allowed, logsum, split(grad_attended))
+    flat = lambda v: v.reshape(2 * count, -1)
+    unused_query, query_back = jax.vjp(prepare, query_raw, gain_query)
+    grad_query_raw, grad_gain_query = query_back(flat(grad_query))
+    unused_key, key_back = jax.vjp(prepare, key_raw, gain_key)
+    grad_key_raw, grad_gain_key = key_back(flat(grad_keys))
+    grad_joint = jnp.concatenate(
+        [grad_query_raw.astype(low), grad_gate_raw, grad_key_raw.astype(low), flat(grad_values)],
+        axis=1,
+    )
+    attn_sum = grad_scatter(dot_grad(hidden1, grad_joint), across)
+    grad_hidden1 = feature_fold([(grad_joint, attn_weight)], place)
+    grad_input1, gain_attn_grad = norm_back_own(
+        grad_hidden1, tokens.astype(jnp.float32), inverse1, gain_attn_own, width
+    )
+    grad_tokens = grad_resid + grad_input1
+
+    spot = lambda v: lax.dynamic_update_slice_in_dim(jnp.zeros((width,), jnp.float32), v, offset, 0)
+    gains = lax.psum(
+        jnp.concatenate(
+            [spot(gain_attn_grad), spot(gain_ffn_grad), grad_gain_query, grad_gain_key]
+        ),
+        ("z", "x", "y", "core"),
+    )
+
+    def join(sums, low_cut, high_cut):
+        return jnp.concatenate(
+            [s[:, low_cut:high_cut] for s in sums], axis=1
+        ).astype(jnp.float32)
+
+    def join_parts(low_cut, high_cut):
+        return jnp.concatenate(
+            [pair_sums[part][side][:, low_cut:high_cut] for side in range(2) for part in range(2)],
+            axis=1,
+        ).astype(jnp.float32)
+
+    cuts = (
+        0,
+        query_width,
+        2 * query_width,
+        2 * query_width + key_width,
+        2 * query_width + 2 * key_width,
+    )
+    return (
+        output,
+        grad_tokens,
+        gains[:width],
+        gains[width : 2 * width],
+        gains[2 * width : 2 * width + head_dim],
+        gains[2 * width + head_dim :],
+        join(attn_sum, cuts[0], cuts[1]),
+        join(attn_sum, cuts[1], cuts[2]),
+        join(attn_sum, cuts[2], cuts[3]),
+        join(attn_sum, cuts[3], cuts[4]),
+        join(out_sum, 0, query_width),
+        join_parts(0, chunk),
+        join_parts(chunk, 2 * chunk),
+        join(down_sum, 0, hidden_width),
+    )
+
+
 def solution(mesh):
-    in_specs = (
-        P("row", "col"),
-        P("row", "col"),
-        P("row"),
-        P(),
-        P(),
-        P(),
-        P(),
-        P("row", "col"),
-        P("row", "col"),
-        P("row", "col"),
-        P("row", "col"),
-        P("row", "col"),
-        P("row", "col"),
-        P("row", "col"),
-        P("row", "col"),
-    )
-    out_specs = (
-        P("row", "col"),
-        P("row", "col"),
-        P(),
-        P(),
-        P(),
-        P(),
-        P("row", "col"),
-        P("row", "col"),
-        P("row", "col"),
-        P("row", "col"),
-        P("row", "col"),
-        P("row", "col"),
-        P("row", "col"),
-        P("row", "col"),
-    )
-    return jax.shard_map(body, mesh=mesh, in_specs=in_specs, out_specs=out_specs, check_vma=False)
+    rows, columns = mesh.devices.shape
+    split = rows % 2 == 0 and columns == 4
+
+    def run(*args):
+        if not split:
+            return plain(mesh)(*args)
+        names = ("z", "x", "y", "core")
+        inner = Mesh(mesh.devices.reshape(rows // 2, 2, 2, 2), names)
+        block = P(("z", "x"), ("y", "core"))
+        whole = P()
+        in_specs = (block, block, P(("z", "x"))) + (whole,) * 4 + (block,) * 8
+        out_specs = (block, block) + (whole,) * 4 + (block,) * 8
+        return jax.shard_map(
+            fast_body, mesh=inner, in_specs=in_specs, out_specs=out_specs, check_vma=False
+        )(*args)
+
+    return run

time: 1410 us -> 876 us (0.62)
  waiting for transfers between devices: 972 us -> 282 us
  starting transfers between devices: 0.98 us -> 59.2 us
  local copies, waits for them, and re-layouts: 47.6 us -> 90.1 us
  Pallas kernels: 0 us -> 42 us
  matrix products: 189 us -> 208 us
  blocking collectives: 55 us -> 38.6 us
    reduce_scatter x6 -> x5, waiting for transfers between devices: 485 us -> 0.02 us  [grad_scatter(): summed = lax.psum_scatter(grads, 'z', scatter_dimension=0, tiled=True)]
    all_gather x8 -> x5, waiting for transfers between devices: 485 us -> 2.27 us  [weight_gather(): lax.all_gather(jnp.concatenate([top, bottom], axis=0), 'z', axis=0, tiled...]
    ppermute x0 -> x71, waiting for transfers between devices: none -> 279 us  [flip(): return lax.ppermute(values, axis, [(0, 1), (1, 0)])]
    ppermute x0 -> x71, starting transfers between devices: none -> 58.4 us  [flip(): return lax.ppermute(values, axis, [(0, 1), (1, 0)])]
    pallas_call x0 -> x8, Pallas kernels: none -> 42 us  [pack(): pl.pallas_call(pack_kernel, grid=(count // tile,), in_specs=[pl.BlockSpec...]
    concatenate x4 -> x11, other arithmetic: 28.5 us -> 6.33 us  [the longest x5 4.52 us: weight_gather(): jnp.concatenate([top, bottom], axis=0)]
    psum x3 -> x1, blocking collectives: 55 us -> 38.6 us  [fast_body(): lax.psum(jnp.concatenate([spot(gain_attn_grad), spot(gain_ffn_grad), grad...]
    another operation x2 -> x12, other arithmetic: 0.31 us -> 16.3 us  [the longest x3 11.7 us: run(): jax.shard_map(fast_body, mesh=inner, in_specs=in_specs, out_specs=out_spe...]
  transfers between devices with their start and end apart: 14 -> 81, of which waited for: 11 -> 34; matrix products, arithmetic and copies ran while one was open for 16% -> 44% of each run, Pallas kernels for 0% -> 5%
where the time goes in v1:
time: 876 us; the launch traced here: 864 us
  waiting for transfers between devices  282 us (32%)
  matrix products  208 us (24%)
  other arithmetic  127 us (14%)
  local copies, waits for them, and re-layouts  90.1 us (10%)
  starting transfers between devices  59.2 us (7%)
  Pallas kernels  42 us (5%)
  blocking collectives  38.6 us (4%)
  between operations  16.5 us (2%)
    ppermute x71, waiting for transfers between devices, flip(): return lax.ppermute(values, axis, [(0, 1), (1, 0)])  279 us
    dot_general x20, matrix products, product(): lax.dot_general(operand, block, (((1,), (1,)), ((), ())), preferred_eleme...  60.8 us
    ppermute x71, starting transfers between devices, flip(): return lax.ppermute(values, axis, [(0, 1), (1, 0)])  58.4 us
    dot_general x5, matrix products, dot_in(): return jnp.dot(operand, weight, preferred_element_type=jnp.float32)  55.3 us
    dot_general x5, matrix products, dot_grad(): lax.dot_general(first, second, (((0,), (0,)), ((), ())), preferred_elemen...  42.9 us
    pallas_call x8, Pallas kernels, pack(): pl.pallas_call(pack_kernel, grid=(count // tile,), in_specs=[pl.BlockSpec...  42 us
    psum x1, blocking collectives, fast_body(): lax.psum(jnp.concatenate([spot(gain_attn_grad), spot(gain_ffn_grad), grad...  38.6 us
    unnamed x248, local copies, waits for them, and re-layouts  24.1 us
  transfers between devices with their start and end apart: 81, of which 34 were waited for; matrix products, arithmetic and copies ran while one was open for 44% of the time, Pallas kernels for 5%

profile of v1, /device:TPU:0, one launch (start us, length us, event | category | flops | bytes accessed | tf_op | source)
XLA Modules:
  0.0 863.6 jit_solution(3562209099001994084)
XLA Ops:
  13.1 9.1 %collective-permute-done.8 = bf16[256,768]{1,0:T(8,128)(2,1)S(1)} collective-permute-done((bf16[256,768]{1,0:T(8,128)(2,1)S(1)}, bf16[256,768]{1,0:T(8,128)(2,1)S(1)}, u32[]{:S(2)}, u32[]{:S(2)}) %collective-permute-start.8) | collective-permute-done | bytes 393248 | tf_op jit(solution)/shard_map/ppermute | solution.py:318
  37.1 15.2 %collective-permute-done.9 = s32[1024]{0:T(1024)S(1)} collective-permute-done((s32[1024]{0:T(1024)S(1)}, s32[1024]{0:T(1024)S(1)}, u32[]{:S(2)}, u32[]{:S(2)}) %collective-permute-start.9) | collective-permute-done | bytes 4128 | tf_op jit(solution)/shard_map/ppermute | solution.py:318
  63.2 4.3 and_or_fusion
  68.6 14.3 %collective-permute-done.5 = bf16[512,512]{1,0:T(8,128)(2,1)} collective-permute-done((bf16[512,512]{1,0:T(8,128)(2,1)}, bf16[512,512]{1,0:T(8,128)(2,1)}, u32[]{:S(2)}, u32[]{:S(2)}) %collective-permute-start.5) | collective-permute-done | bytes 524320 | tf_op jit(solution)/shard_map/ppermute | solution.py:318
  90.9 5.7 shard_map.254
  96.6 4.9 constant_dynamic-update-slice_fusion.3
  101.5 5.7 shard_map.255
  107.2 4.8 constant_dynamic-update-slice_fusion.2
  112.0 10.4 %fusion.177 = f32[2048,768]{0,1:T(8,128)S(1)} fusion(bf16[2048,2048]{1,0:T(8,128)(2,1)} %constant_dynamic-update-slice_fusion.2, bf16[2048,768]{1,0:T(8,128)(2,1)} %all-gather.6.cloned.1.call-done), kind=kOutput, calls=%fused_computation.389 | convolution fusion | flops 6442450944 | bytes 17825792 | tf_op jit(solution)/shard_map/dot_general | solution.py:455
  128.9 7.2 fusion.56
  151.1 9.7 %fusion.176 = (f32[2,2,1024]{2,1,0:T(2,128)S(1)}, f32[2,1,2,1024,1024]{3,4,2,0,1:T(8,128)}) fusion(bf16[2,1024,2,128]{1,0,3,2:T(2,128)(2,1)S(1)} %reshape.495, bf16[2,1024,128,1]{1,0,2,3:T(2,128)(2,1)} %bitcast.300, pred[2,1024,1024]{1,2,0:T(8,128)(4,1)} %and_or_fusion), kind=kOutput, calls=%fused_computation.388 | convolution fusion | flops 1086320640 | bytes 20463616 | tf_op jit(solution)/shard_map/vmap(qgrd,kgd->grqk)/dot_general | solution.py:111
  160.9 8.1 fusion.3
  169.0 7.5 fusion.37
  200.8 22.3 %collective-permute-done.13 = bf16[2,512,512]{2,1,0:T(8,128)(2,1)} collective-permute-done((bf16[2,512,512]{2,1,0:T(8,128)(2,1)}, bf16[2,512,512]{2,1,0:T(8,128)(2,1)}, u32[]{:S(2)}, u32[]{:S(2)}) %collective-permute-start.13) | collective-permute-done | bytes 1048608 | tf_op jit(solution)/shard_map/ppermute | solution.py:318
  225.1 12.3 %collective-permute-done.14 = bf16[512,512]{1,0:T(8,128)(2,1)S(1)} collective-permute-done((bf16[512,512]{1,0:T(8,128)(2,1)S(1)}, bf16[512,512]{1,0:T(8,128)(2,1)S(1)}, u32[]{:S(2)}, u32[]{:S(2)}) %collective-permute-start.14) | collective-permute-done | bytes 524320 | tf_op jit(solution)/shard_map/ppermute | solution.py:318
  241.7 12.1 %collective-permute-done.16 = bf16[512,512]{1,0:T(8,128)(2,1)S(1)} collective-permute-done((bf16[512,512]{1,0:T(8,128)(2,1)S(1)}, bf16[512,512]{1,0:T(8,128)(2,1)S(1)}, u32[]{:S(2)}, u32[]{:S(2)}) %collective-permute-start.16) | collective-permute-done | bytes 524320 | tf_op jit(solution)/shard_map/ppermute | solution.py:318
  254.8 12.1 %collective-permute-done.35.refs_2_ = bf16[1024,512]{1,0:T(8,128)(2,1)} collective-permute-done((bf16[1024,512]{1,0:T(8,128)(2,1)S(1)}, bf16[1024,512]{1,0:T(8,128)(2,1)}, u32[]{:S(2)}, u32[]{:S(2)}) %collective-permute-start.35) | collective-permute-done | bytes 1048608 | tf_op jit(solution)/shard_map/ppermute | solution.py:318
  268.7 7.7 collective-permute-done.37.refs_0_
  279.6 7.9 collective-permute-done.39
  289.7 8.0 collective-permute-done.40
  298.5 17.3 %collective-permute-done.25 = bf16[256,768]{1,0:T(8,128)(2,1)S(1)} collective-permute-done((bf16[256,768]{1,0:T(8,128)(2,1)S(1)}, bf16[256,768]{1,0:T(8,128)(2,1)S(1)}, u32[]{:S(2)}, u32[]{:S(2)}) %collective-permute-start.25) | collective-permute-done | bytes 393248 | tf_op jit(solution)/shard_map/ppermute | solution.py:318
  321.6 4.9 shard_map.258
  326.6 4.9 shard_map.259
  336.2 13.8 %fusion.15 = f32[2048,768]{0,1:T(8,128)} fusion(bf16[2048,768]{1,0:T(8,128)(2,1)} %all-gather.14.cloned.1.call-done, bf16[1024,2048]{1,0:T(8,128)(2,1)} %shard_map.259, bf16[1024,2048]{1,0:T(8,128)(2,1)} %shard_map.258), kind=kOutput, calls=%fused_computation.23 | convolution fusion | flops 6459228160 | bytes 17825792 | tf_op jit(solution)/shard_map/dot_general | solution.py:455
  350.0 5.7 shard_map.256
  355.7 4.8 constant_dynamic-update-slice_fusion.7
  360.5 5.7 shard_map.257
  366.2 4.8 constant_dynamic-update-slice_fusion.6
  371.0 11.9 %fusion.179 = f32[2048,768]{0,1:T(8,128)} fusion(bf16[2048,2048]{1,0:T(8,128)(2,1)} %constant_dynamic-update-slice_fusion.6, bf16[2048,768]{1,0:T(8,128)(2,1)} %all-gather.12.cloned.1.call-done), kind=kOutput, calls=%fused_computation.391 | convolution fusion | flops 6442450944 | bytes 17825792 | tf_op jit(solution)/shard_map/dot_general | solution.py:455
  385.2 10.5 %fusion.178 = f32[2048,768]{0,1:T(8,128)S(1)} fusion(bf16[2048,2048]{1,0:T(8,128)(2,1)} %constant_dynamic-update-slice_fusion.6, bf16[2048,768]{1,0:T(8,128)(2,1)} %all-gather.10.cloned.1.call-done), kind=kOutput, calls=%fused_computation.390 | convolution fusion | flops 6442450944 | bytes 17825792 | tf_op jit(solution)/shard_map/dot_general | solution.py:455
  395.8 7.5 multiply_convert_fusion.1
  405.0 8.6 convolution_convert_fusion.1
  413.7 10.5 %fusion.16 = bf16[2048,768]{1,0:T(8,128)(2,1)} fusion(bf16[1024,2048]{1,0:T(8,128)(2,1)} %shard_map.259, bf16[1024,2048]{1,0:T(8,128)(2,1)} %shard_map.258, bf16[2048,384]{0,1:T(8,128)(2,1)S(1)} %get-tuple-element.44, bf16[2048,384]{0,1:T(8,128)(2,1)S(1)} %get-tuple-element.47), kind=kOutput, calls=%fused_computation.36 | convolution fusion | flops 6467092480 | bytes 14680064 | tf_op jit(solution)/shard_map/dot_general | solution.py:459
  424.5 4.2 fusion.103
  454.3 8.3 convolution_convert_fusion
  466.3 12.3 %collective-permute-done.44 = bf16[2,512,512]{2,1,0:T(8,128)(2,1)} collective-permute-done((bf16[2,512,512]{2,1,0:T(8,128)(2,1)}, bf16[2,512,512]{2,1,0:T(8,128)(2,1)}, u32[]{:S(2)}, u32[]{:S(2)}) %collective-permute-start.44) | collective-permute-done | bytes 1048608 | tf_op jit(solution)/shard_map/ppermute | solution.py:318
  481.4 3.7 add_convert_fusion.6
  485.1 3.8 add_convert_fusion.7
  490.8 10.5 %collective-permute-done.45 = bf16[512,512]{1,0:T(8,128)(2,1)S(1)} collective-permute-done((bf16[512,512]{1,0:T(8,128)(2,1)S(1)}, bf16[512,512]{1,0:T(8,128)(2,1)S(1)}, u32[]{:S(2)}, u32[]{:S(2)}) %collective-permute-start.45) | collective-permute-done | bytes 524320 | tf_op jit(solution)/shard_map/ppermute | solution.py:318
  505.2 12.5 %collective-permute-done.47 = bf16[512,512]{1,0:T(8,128)(2,1)S(1)} collective-permute-done((bf16[512,512]{1,0:T(8,128)(2,1)S(1)}, bf16[512,512]{1,0:T(8,128)(2,1)S(1)}, u32[]{:S(2)}, u32[]{:S(2)}) %collective-permute-start.47) | collective-permute-done | bytes 524320 | tf_op jit(solution)/shard_map/ppermute | solution.py:318
  530.2 9.9 %collective-permute-done.30 = bf16[2,512,512]{2,1,0:T(8,128)(2,1)S(1)} collective-permute-done((bf16[2,512,512]{2,1,0:T(8,128)(2,1)S(1)}, bf16[2,512,512]{2,1,0:T(8,128)(2,1)S(1)}, u32[]{:S(2)}, u32[]{:S(2)}) %collective-permute-start.30) | collective-permute-done | bytes 1048608 | tf_op jit(solution)/shard_map/ppermute | solution.py:318
  547.3 13.8 %collective-permute-done.53.refs_0_ = bf16[1024,512]{1,0:T(8,128)(2,1)S(1)} collective-permute-done((bf16[1024,512]{1,0:T(8,128)(2,1)S(1)}, bf16[1024,512]{1,0:T(8,128)(2,1)S(1)}, u32[]{:S(2)}, u32[]{:S(2)}) %collective-permute-start.53) | collective-permute-done | bytes 1048608 | tf_op jit(solution)/shard_map/ppermute | solution.py:318
  564.3 11.5 %collective-permute-done.32 = bf16[2,512,512]{2,1,0:T(8,128)(2,1)} collective-permute-done((bf16[2,512,512]{2,1,0:T(8,128)(2,1)}, bf16[2,512,512]{2,1,0:T(8,128)(2,1)}, u32[]{:S(2)}, u32[]{:S(2)}) %collective-permute-start.32) | collective-permute-done | bytes 1048608 | tf_op jit(solution)/shard_map/ppermute | solution.py:318
  575.8 11.2 %collective-permute-done.31 = bf16[512,512]{1,0:T(8,128)(2,1)} collective-permute-done((bf16[512,512]{1,0:T(8,128)(2,1)}, bf16[512,512]{1,0:T(8,128)(2,1)}, u32[]{:S(2)}, u32[]{:S(2)}) %collective-permute-start.31) | collective-permute-done | bytes 524320 | tf_op jit(solution)/shard_map/ppermute | solution.py:318
  612.4 4.7 shard_map.260
  624.7 4.8 shard_map.261
  629.5 7.2 fusion.22
  636.7 8.6 multiply_convert_fusion.6
  647.4 8.9 %fusion.48 = bf16[2,1024,1,128]{1,3,0,2:T(8,128)(2,1)S(1)} fusion(f32[2,1,2,1024,1024]{3,4,2,0,1:T(8,128)} %get-tuple-element.142, f32[2,2,1024]{2,1,0:T(2,128)S(1)} %log_add_fusion, bf16[2,1024,2,128]{1,0,3,2:T(2,128)(2,1)S(1)} %reshape.499), kind=kOutput, calls=%fused_computation.112 | convolution fusion | flops 1082392576 | bytes 18366464 | tf_op jit(solution)/shard_map/vmap(grqk,qgrd->kgd)/dot_general | solution.py:136
  656.3 13.1 %fusion = (f32[2,2,1024]{2,1,0:T(2,128)S(1)}, f32[2,1024,1024,2]{2,1,3,0:T(8,128)}) fusion(f32[2,1,2,1024,1024]{3,4,2,0,1:T(8,128)} %get-tuple-element.142, f32[2,2,1024]{2,1,0:T(2,128)S(1)} %log_add_fusion, bf16[2,1024,128,1]{2,1,3,0:T(8,128)(2,1)S(1)} %copy-done.39, bf16[2,1024,2,128]{1,0,3,2:T(2,128)(2,1)S(1)} %reshape.499), kind=kOutput, calls=%fused_computation.3 | convolution fusion | flops 1086320640 | bytes 35160064 | tf_op jit(solution)/shard_map/vmap(qgrd,kgd->grqk)/dot_general | solution.py:139
  669.5 10.9 %fusion.8 = bf16[2,2,1024,1024]{2,3,1,0:T(8,128)(2,1)} fusion(f32[2,1024,1024,2]{2,1,3,0:T(8,128)} %get-tuple-element.144, f32[2,1,2,1024,1024]{3,4,2,0,1:T(8,128)S(1)} %bitcast.285, f32[2,2,1024]{2,1,0:T(2,128)S(1)} %get-tuple-element.143, f32[2,2,1024]{2,1,0:T(2,128)S(1)} %log_add_fusion), kind=kLoop, calls=%fused_computation.13 | loop fusion | flops 16777216 | bytes 41975808 | tf_op jit(solution)/shard_map/reshape.19 | solution.py:648
  680.4 7.4 fusion.44
  695.8 3.5 fusion.62
  699.4 6.1 fusion.79
  713.5 5.0 convolution_convert_fusion.5
  718.5 4.4 convolution_convert_fusion.6
  723.2 8.3 convolution_convert_fusion.2
  731.6 4.1 add_convert_fusion
  735.9 3.9 add_convert_fusion.1
  746.9 18.5 %collective-permute-done.60 = bf16[2,512,512]{2,1,0:T(8,128)(2,1)S(1)} collective-permute-done((bf16[2,512,512]{2,1,0:T(8,128)(2,1)S(1)}, bf16[2,512,512]{2,1,0:T(8,128)(2,1)S(1)}, u32[]{:S(2)}, u32[]{:S(2)}) %collective-permute-start.60) | collective-permute-done | bytes 1048608 | tf_op jit(solution)/shard_map/ppermute | solution.py:318
  771.7 10.5 %collective-permute-done.61 = bf16[512,512]{1,0:T(8,128)(2,1)} collective-permute-done((bf16[512,512]{1,0:T(8,128)(2,1)}, bf16[512,512]{1,0:T(8,128)(2,1)}, u32[]{:S(2)}, u32[]{:S(2)}) %collective-permute-start.61) | collective-permute-done | bytes 524320 | tf_op jit(solution)/shard_map/ppermute | solution.py:318
  787.3 9.9 %collective-permute-done.63 = bf16[512,512]{1,0:T(8,128)(2,1)S(1)} collective-permute-done((bf16[512,512]{1,0:T(8,128)(2,1)S(1)}, bf16[512,512]{1,0:T(8,128)(2,1)S(1)}, u32[]{:S(2)}, u32[]{:S(2)}) %collective-permute-start.63) | collective-permute-done | bytes 524320 | tf_op jit(solution)/shard_map/ppermute | solution.py:318
  799.7 38.6 %psum.7 = f32[4352]{0:T(1024)S(1)} all-reduce(f32[4352]{0:T(1024)S(1)} %pad_maximum_fusion.37), channel_id=1, replica_groups=mesh['z'=4,'x'=2,'y'=2,'core'=2] {'z','x','y','core'}, use_global_device_ids=true, to_apply=%region_15.16 | all-reduce | flops 4352 | bytes 34816 | tf_op jit(solution)/shard_map/psum | solution.py:592
  846.0 5.3 fusion.26
  (566 shorter events, 261.5 us)
Async XLA Ops:
  7.2 104.8 %all-gather.6.cloned.1.call-start = ((), (), s32[]{:S(2)}) async-start(), calls=%async_computation.5 | async-start | bytes 3932160 | tf_op jit(solution)/shard_map/all_gather | solution.py:404
  24.3 158.2 %all-gather.8.cloned.1.call-start = ((), (), s32[]{:S(2)}) async-start(), calls=%async_computation.6 | async-start | bytes 1310720 | tf_op jit(solution)/shard_map/all_gather | solution.py:404
  24.4 33.9 %collective-permute-start.1 = (bf16[1024,512]{1,0:T(8,128)(2,1)S(1)}, bf16[1024,512]{1,0:T(8,128)(2,1)}, u32[]{:S(2)}, u32[]{:S(2)}) collective-permute-start(bf16[1024,512]{1,0:T(8,128)(2,1)S(1)} %copy-done.8), channel_id=1, source_target_pairs={{0,2},{2,0},{1,3},{3,1},{4,6},{6,4},{5,7},{7,5},{8,10},{10,8},{9,1... | collective-permute-start | bytes 3145736 | tf_op jit(solution)/shard_map/ppermute | solution.py:318
  26.2 64.7 %collective-permute-start = (bf16[1024,512]{1,0:T(8,128)(2,1)S(1)}, bf16[1024,512]{1,0:T(8,128)(2,1)}, u32[]{:S(2)}, u32[]{:S(2)}) collective-permute-start(bf16[1024,512]{1,0:T(8,128)(2,1)S(1)} %copy-done.8), channel_id=1, source_target_pairs={{0,1},{1,0},{2,3},{3,2},{4,5},{5,4},{6,7},{7,6},{8,9},{9,8},{10,11... | collective-permute-start | bytes 3145736 | tf_op jit(solution)/shard_map/ppermute | solution.py:318
  26.2 34.6 %collective-permute-start.3 = (bf16[1024,512]{1,0:T(8,128)(2,1)S(1)}, bf16[1024,512]{1,0:T(8,128)(2,1)}, u32[]{:S(2)}, u32[]{:S(2)}) collective-permute-start(bf16[1024,512]{1,0:T(8,128)(2,1)S(1)} %copy-done.8), channel_id=1, source_target_pairs={{0,4},{4,0},{1,5},{5,1},{2,6},{6,2},{3,7},{7,3},{8,12},{12,8},{9,1... | collective-permute-start | bytes 3145736 | tf_op jit(solution)/shard_map/ppermute | solution.py:318
  27.7 24.6 %collective-permute-start.9 = (s32[1024]{0:T(1024)S(1)}, s32[1024]{0:T(1024)S(1)}, u32[]{:S(2)}, u32[]{:S(2)}) collective-permute-start(s32[1024]{0:T(1024)S(1)} %copy-done.89), channel_id=1, source_target_pairs={{0,4},{4,0},{1,5},{5,1},{2,6},{6,2},{3,7},{7,3},{8,12},{12,8},{9,1... | collective-permute-start | bytes 12296 | tf_op jit(solution)/shard_map/ppermute | solution.py:318
  29.8 25.3 %collective-permute-start.10 = (bf16[256,256]{1,0:T(8,128)(2,1)}, bf16[256,256]{1,0:T(8,128)(2,1)}, u32[]{:S(2)}, u32[]{:S(2)}) collective-permute-start(bf16[256,256]{1,0:T(8,128)(2,1)} %constant_dynamic-slice_fusion.14), channel_id=1, source_target_pairs={{0,4},{4,0},{1,5},{5,1},{2,6},{6,2},{3,7},{7,3},{8,12},{12,8},{9,1... | collective-permute-start | bytes 393224 | tf_op jit(solution)/shard_map/ppermute | solution.py:318
  52.3 33.4 %collective-permute-start.27 = (bf16[256,768]{1,0:T(8,128)(2,1)}, bf16[256,768]{1,0:T(8,128)(2,1)}, u32[]{:S(2)}, u32[]{:S(2)}) collective-permute-start(bf16[256,768]{1,0:T(8,128)(2,1)} %constant_dynamic-slice_fusion.9), channel_id=1, source_target_pairs={{0,4},{4,0},{1,5},{5,1},{2,6},{6,2},{3,7},{7,3},{8,12},{12,8},{9,1... | collective-permute-start | bytes 1179656 | tf_op jit(solution)/shard_map/ppermute | solution.py:318
  55.1 32.3 %collective-permute-start.26 = (bf16[256,768]{1,0:T(8,128)(2,1)S(1)}, bf16[256,768]{1,0:T(8,128)(2,1)}, u32[]{:S(2)}, u32[]{:S(2)}) collective-permute-start(bf16[256,768]{1,0:T(8,128)(2,1)S(1)} %pad_maximum_fusion.35), channel_id=1, source_target_pairs={{0,4},{4,0},{1,5},{5,1},{2,6},{6,2},{3,7},{7,3},{8,12},{12,8},{9,1... | collective-permute-start | bytes 1179656 | tf_op jit(solution)/shard_map/ppermute | solution.py:318
  58.2 278.0 %all-gather.14.cloned.1.call-start = ((), (), s32[]{:S(2)}) async-start(), calls=%async_computation.9 | async-start | bytes 3932160 | tf_op jit(solution)/shard_map/all_gather | solution.py:404
  60.1 22.8 %collective-permute-start.5 = (bf16[512,512]{1,0:T(8,128)(2,1)}, bf16[512,512]{1,0:T(8,128)(2,1)}, u32[]{:S(2)}, u32[]{:S(2)}) collective-permute-start(bf16[512,512]{1,0:T(8,128)(2,1)} %slice.405), channel_id=1, source_target_pairs={{0,4},{4,0},{1,5},{5,1},{2,6},{6,2},{3,7},{7,3},{8,12},{12,8},{9,1... | collective-permute-start | bytes 1572872 | tf_op jit(solution)/shard_map/ppermute | solution.py:318
  62.7 21.3 %collective-permute-start.6 = (bf16[512,512]{1,0:T(8,128)(2,1)}, bf16[512,512]{1,0:T(8,128)(2,1)}, u32[]{:S(2)}, u32[]{:S(2)}) collective-permute-start(bf16[512,512]{1,0:T(8,128)(2,1)} %slice.406), channel_id=1, source_target_pairs={{0,2},{2,0},{1,3},{3,1},{4,6},{6,4},{5,7},{7,5},{8,10},{10,8},{9,1... | collective-permute-start | bytes 1572872 | tf_op jit(solution)/shard_map/ppermute | solution.py:318
  84.0 17.5 %collective-permute-start.4 = (bf16[1024,512]{1,0:T(8,128)(2,1)}, bf16[1024,512]{1,0:T(8,128)(2,1)}, u32[]{:S(2)}, u32[]{:S(2)}) collective-permute-start(bf16[1024,512]{1,0:T(8,128)(2,1)} %collective-permute-done.3.refs_0_), channel_id=1, source_target_pairs={{0,1},{1,0},{2,3},{3,2},{4,5},{5,4},{6,7},{7,6},{8,9},{9,8},{10,11... | collective-permute-start | bytes 3145736 | tf_op jit(solution)/shard_map/ppermute | solution.py:318
  85.7 15.8 %collective-permute-start.7 = (bf16[1024,512]{1,0:T(8,128)(2,1)S(1)}, bf16[1024,512]{1,0:T(8,128)(2,1)}, u32[]{:S(2)}, u32[]{:S(2)}) collective-permute-start(bf16[1024,512]{1,0:T(8,128)(2,1)S(1)} %constant_dynamic-update-slice_fusion.refs_2_), channel_id=1, source_target_pairs={{0,1},{1,0},{2,3},{3,2},{4,5},{5,4},{6,7},{7,6},{8,9},{9,8},{10,11... | collective-permute-start | bytes 3145736 | tf_op jit(solution)/shard_map/ppermute | solution.py:318
  90.7 280.3 %all-gather.12.cloned.1.call-start = ((), (), s32[]{:S(2)}) async-start(), calls=%async_computation.8 | async-start | bytes 3932160 | tf_op jit(solution)/shard_map/all_gather | solution.py:404
  197.5 25.5 %collective-permute-start.13 = (bf16[2,512,512]{2,1,0:T(8,128)(2,1)}, bf16[2,512,512]{2,1,0:T(8,128)(2,1)}, u32[]{:S(2)}, u32[]{:S(2)}) collective-permute-start(bf16[2,512,512]{2,1,0:T(8,128)(2,1)} %pad_maximum_fusion.17), channel_id=1, source_target_pairs={{0,4},{4,0},{1,5},{5,1},{2,6},{6,2},{3,7},{7,3},{8,12},{12,8},{9,1... | collective-permute-start | bytes 3145736 | tf_op jit(solution)/shard_map/ppermute | solution.py:318
  199.9 185.3 %all-gather.10.cloned.1.call-start = ((), (), s32[]{:S(2)}) async-start(), calls=%async_computation.7 | async-start | bytes 3932160 | tf_op jit(solution)/shard_map/all_gather | solution.py:404
  200.1 25.0 %collective-permute-start.15 = (bf16[2,512,512]{2,1,0:T(8,128)(2,1)S(1)}, bf16[2,512,512]{2,1,0:T(8,128)(2,1)S(1)}, u32[]{:S(2)}, u32[]{:S(2)}) collective-permute-start(bf16[2,512,512]{2,1,0:T(8,128)(2,1)S(1)} %pad_maximum_fusion.18), channel_id=1, source_target_pairs={{0,2},{2,0},{1,3},{3,1},{4,6},{6,4},{5,7},{7,5},{8,10},{10,8},{9,1... | collective-permute-start | bytes 3145736 | tf_op jit(solution)/shard_map/ppermute | solution.py:318
  238.8 14.9 %collective-permute-start.16 = (bf16[512,512]{1,0:T(8,128)(2,1)S(1)}, bf16[512,512]{1,0:T(8,128)(2,1)S(1)}, u32[]{:S(2)}, u32[]{:S(2)}) collective-permute-start(bf16[512,512]{1,0:T(8,128)(2,1)S(1)} %get-tuple-element.66), channel_id=1, source_target_pairs={{0,4},{4,0},{1,5},{5,1},{2,6},{6,2},{3,7},{7,3},{8,12},{12,8},{9,1... | collective-permute-start | bytes 1572872 | tf_op jit(solution)/shard_map/ppermute | solution.py:318
  240.6 26.3 %collective-permute-start.35 = (bf16[1024,512]{1,0:T(8,128)(2,1)S(1)}, bf16[1024,512]{1,0:T(8,128)(2,1)}, u32[]{:S(2)}, u32[]{:S(2)}) collective-permute-start(bf16[1024,512]{1,0:T(8,128)(2,1)S(1)} %fusion.36.refs_0_), channel_id=1, source_target_pairs={{0,2},{2,0},{1,3},{3,1},{4,6},{6,4},{5,7},{7,5},{8,10},{10,8},{9,1... | collective-permute-start | bytes 3145736 | tf_op jit(solution)/shard_map/ppermute | solution.py:318
  241.3 35.0 %collective-permute-start.37 = (bf16[1024,512]{1,0:T(8,128)(2,1)S(1)}, bf16[1024,512]{1,0:T(8,128)(2,1)}, u32[]{:S(2)}, u32[]{:S(2)}) collective-permute-start(bf16[1024,512]{1,0:T(8,128)(2,1)S(1)} %fusion.36.refs_0_), channel_id=1, source_target_pairs={{0,4},{4,0},{1,5},{5,1},{2,6},{6,2},{3,7},{7,3},{8,12},{12,8},{9,1... | collective-permute-start | bytes 3145736 | tf_op jit(solution)/shard_map/ppermute | solution.py:318
  254.4 61.4 %collective-permute-start.18 = (bf16[1024,512]{1,0:T(8,128)(2,1)S(1)}, bf16[1024,512]{1,0:T(8,128)(2,1)S(1)}, u32[]{:S(2)}, u32[]{:S(2)}) collective-permute-start(bf16[1024,512]{1,0:T(8,128)(2,1)S(1)} %fusion.51.refs_0_), channel_id=1, source_target_pairs={{0,2},{2,0},{1,3},{3,1},{4,6},{6,4},{5,7},{7,5},{8,10},{10,8},{9,1... | collective-permute-start | bytes 3145736 | tf_op jit(solution)/shard_map/ppermute | solution.py:318
  268.0 19.5 %collective-permute-start.39 = (bf16[512,512]{1,0:T(8,128)(2,1)S(1)}, bf16[512,512]{1,0:T(8,128)(2,1)S(1)}, u32[]{:S(2)}, u32[]{:S(2)}) collective-permute-start(bf16[512,512]{1,0:T(8,128)(2,1)S(1)} %slice.448), channel_id=1, source_target_pairs={{0,4},{4,0},{1,5},{5,1},{2,6},{6,2},{3,7},{7,3},{8,12},{12,8},{9,1... | collective-permute-start | bytes 1572872 | tf_op jit(solution)/shard_map/ppermute | solution.py:318
  277.4 20.2 %collective-permute-start.40 = (bf16[512,512]{1,0:T(8,128)(2,1)S(1)}, bf16[512,512]{1,0:T(8,128)(2,1)S(1)}, u32[]{:S(2)}, u32[]{:S(2)}) collective-permute-start(bf16[512,512]{1,0:T(8,128)(2,1)S(1)} %slice.449), channel_id=1, source_target_pairs={{0,2},{2,0},{1,3},{3,1},{4,6},{6,4},{5,7},{7,5},{8,10},{10,8},{9,1... | collective-permute-start | bytes 1572872 | tf_op jit(solution)/shard_map/ppermute | solution.py:318
  277.9 39.3 %collective-permute-start.20 = (bf16[1024,512]{1,0:T(8,128)(2,1)S(1)}, bf16[1024,512]{1,0:T(8,128)(2,1)S(1)}, u32[]{:S(2)}, u32[]{:S(2)}) collective-permute-start(bf16[1024,512]{1,0:T(8,128)(2,1)S(1)} %fusion.51.refs_0_), channel_id=1, source_target_pairs={{0,4},{4,0},{1,5},{5,1},{2,6},{6,2},{3,7},{7,3},{8,12},{12,8},{9,1... | collective-permute-start | bytes 3145736 | tf_op jit(solution)/shard_map/ppermute | solution.py:318
  279.5 39.9 %collective-permute-start.34 = (bf16[1024,512]{1,0:T(8,128)(2,1)S(1)}, bf16[1024,512]{1,0:T(8,128)(2,1)S(1)}, u32[]{:S(2)}, u32[]{:S(2)}) collective-permute-start(bf16[1024,512]{1,0:T(8,128)(2,1)S(1)} %fusion.36.refs_0_), channel_id=1, source_target_pairs={{0,1},{1,0},{2,3},{3,2},{4,5},{5,4},{6,7},{7,6},{8,9},{9,8},{10,11... | collective-permute-start | bytes 3145736 | tf_op jit(solution)/shard_map/ppermute | solution.py:318
  287.5 28.3 %collective-permute-start.25 = (bf16[256,768]{1,0:T(8,128)(2,1)S(1)}, bf16[256,768]{1,0:T(8,128)(2,1)S(1)}, u32[]{:S(2)}, u32[]{:S(2)}) collective-permute-start(bf16[256,768]{1,0:T(8,128)(2,1)S(1)} %pad_maximum_fusion.33), channel_id=1, source_target_pairs={{0,4},{4,0},{1,5},{5,1},{2,6},{6,2},{3,7},{7,3},{8,12},{12,8},{9,1... | collective-permute-start | bytes 1179656 | tf_op jit(solution)/shard_map/ppermute | solution.py:318
  297.7 24.0 %collective-permute-start.36 = (bf16[1024,512]{1,0:T(8,128)(2,1)}, bf16[1024,512]{1,0:T(8,128)(2,1)}, u32[]{:S(2)}, u32[]{:S(2)}) collective-permute-start(bf16[1024,512]{1,0:T(8,128)(2,1)} %collective-permute-done.35.refs_2_), channel_id=1, source_target_pairs={{0,1},{1,0},{2,3},{3,2},{4,5},{5,4},{6,7},{7,6},{8,9},{9,8},{10,11... | collective-permute-start | bytes 3145736 | tf_op jit(solution)/shard_map/ppermute | solution.py:318
  317.2 14.9 %collective-permute-start.22 = (bf16[512,512]{1,0:T(8,128)(2,1)}, bf16[512,512]{1,0:T(8,128)(2,1)}, u32[]{:S(2)}, u32[]{:S(2)}) collective-permute-start(bf16[512,512]{1,0:T(8,128)(2,1)} %slice.430), channel_id=1, source_target_pairs={{0,4},{4,0},{1,5},{5,1},{2,6},{6,2},{3,7},{7,3},{8,12},{12,8},{9,1... | collective-permute-start | bytes 1572872 | tf_op jit(solution)/shard_map/ppermute | solution.py:318
  319.4 14.5 %collective-permute-start.23 = (bf16[512,512]{1,0:T(8,128)(2,1)}, bf16[512,512]{1,0:T(8,128)(2,1)}, u32[]{:S(2)}, u32[]{:S(2)}) collective-permute-start(bf16[512,512]{1,0:T(8,128)(2,1)} %slice.431), channel_id=1, source_target_pairs={{0,2},{2,0},{1,3},{3,1},{4,6},{6,4},{5,7},{7,5},{8,10},{10,8},{9,1... | collective-permute-start | bytes 1572872 | tf_op jit(solution)/shard_map/ppermute | solution.py:318
  321.6 275.5 %reduce-scatter.10.cloned.1.call-start = ((), (), s32[]{:S(2)}) async-start(), calls=%async_computation.12 | async-start | bytes 3932160 | tf_op jit(solution)/shard_map/reduce_scatter | solution.py:408
  331.5 18.6 %collective-permute-start.17 = (bf16[1024,512]{1,0:T(8,128)(2,1)S(1)}, bf16[1024,512]{1,0:T(8,128)(2,1)}, u32[]{:S(2)}, u32[]{:S(2)}) collective-permute-start(bf16[1024,512]{1,0:T(8,128)(2,1)S(1)} %fusion.51.refs_0_), channel_id=1, source_target_pairs={{0,1},{1,0},{2,3},{3,2},{4,5},{5,4},{6,7},{7,6},{8,9},{9,8},{10,11... | collective-permute-start | bytes 3145736 | tf_op jit(solution)/shard_map/ppermute | solution.py:318
  331.5 29.0 %collective-permute-start.21 = (bf16[1024,512]{1,0:T(8,128)(2,1)S(1)}, bf16[1024,512]{1,0:T(8,128)(2,1)}, u32[]{:S(2)}, u32[]{:S(2)}) collective-permute-start(bf16[1024,512]{1,0:T(8,128)(2,1)S(1)} %copy-done.36), channel_id=1, source_target_pairs={{0,1},{1,0},{2,3},{3,2},{4,5},{5,4},{6,7},{7,6},{8,9},{9,8},{10,11... | collective-permute-start | bytes 3145736 | tf_op jit(solution)/shard_map/ppermute | solution.py:318
  332.0 18.0 %collective-permute-start.19 = (bf16[1024,512]{1,0:T(8,128)(2,1)S(1)}, bf16[1024,512]{1,0:T(8,128)(2,1)}, u32[]{:S(2)}, u32[]{:S(2)}) collective-permute-start(bf16[1024,512]{1,0:T(8,128)(2,1)S(1)} %collective-permute-done.18.refs_2_), channel_id=1, source_target_pairs={{0,1},{1,0},{2,3},{3,2},{4,5},{5,4},{6,7},{7,6},{8,9},{9,8},{10,11... | collective-permute-start | bytes 3145736 | tf_op jit(solution)/shard_map/ppermute | solution.py:318
  335.8 24.7 %collective-permute-start.24 = (bf16[1024,512]{1,0:T(8,128)(2,1)}, bf16[1024,512]{1,0:T(8,128)(2,1)}, u32[]{:S(2)}, u32[]{:S(2)}) collective-permute-start(bf16[1024,512]{1,0:T(8,128)(2,1)} %constant_dynamic-update-slice_fusion.4.refs_2_), channel_id=1, source_target_pairs={{0,1},{1,0},{2,3},{3,2},{4,5},{5,4},{6,7},{7,6},{8,9},{9,8},{10,11... | collective-permute-start | bytes 3145736 | tf_op jit(solution)/shard_map/ppermute | solution.py:318
  413.6 193.1 %reduce-scatter.14.cloned.1.call-start = ((), (), s32[]{:S(2)}) async-start(), calls=%async_computation.14 | async-start | bytes 3932160 | tf_op jit(solution)/shard_map/reduce_scatter | solution.py:408
  424.2 184.3 %reduce-scatter.12.cloned.1.call-start = ((), (), s32[]{:S(2)}) async-start(), calls=%async_computation.13 | async-start | bytes 3932160 | tf_op jit(solution)/shard_map/reduce_scatter | solution.py:408
  430.8 16.2 %collective-permute-start.42 = (bf16[2048,512]{1,0:T(8,128)(2,1)S(1)}, bf16[2048,512]{1,0:T(8,128)(2,1)S(1)}, u32[]{:S(2)}, u32[]{:S(2)}) collective-permute-start(bf16[2048,512]{1,0:T(8,128)(2,1)S(1)} %add_convert_fusion.5), channel_id=1, source_target_pairs={{0,1},{1,0},{2,3},{3,2},{4,5},{5,4},{6,7},{7,6},{8,9},{9,8},{10,11... | collective-permute-start | bytes 6291464 | tf_op jit(solution)/shard_map/ppermute | solution.py:318
  438.9 42.5 %collective-permute-start.29 = (bf16[2048,512]{1,0:T(8,128)(2,1)}, bf16[2048,512]{1,0:T(8,128)(2,1)}, u32[]{:S(2)}, u32[]{:S(2)}) collective-permute-start(bf16[2048,512]{1,0:T(8,128)(2,1)} %convolution_convert_fusion.7), channel_id=1, source_target_pairs={{0,1},{1,0},{2,3},{3,2},{4,5},{5,4},{6,7},{7,6},{8,9},{9,8},{10,11... | collective-permute-start | bytes 6291464 | tf_op jit(solution)/shard_map/ppermute | solution.py:318
  442.7 42.4 %collective-permute-start.28 = (bf16[2048,512]{1,0:T(8,128)(2,1)}, bf16[2048,512]{1,0:T(8,128)(2,1)}, u32[]{:S(2)}, u32[]{:S(2)}) collective-permute-start(bf16[2048,512]{1,0:T(8,128)(2,1)} %convolution_convert_fusion.8), channel_id=1, source_target_pairs={{0,1},{1,0},{2,3},{3,2},{4,5},{5,4},{6,7},{7,6},{8,9},{9,8},{10,11... | collective-permute-start | bytes 6291464 | tf_op jit(solution)/shard_map/ppermute | solution.py:318
  452.8 25.9 %collective-permute-start.44 = (bf16[2,512,512]{2,1,0:T(8,128)(2,1)}, bf16[2,512,512]{2,1,0:T(8,128)(2,1)}, u32[]{:S(2)}, u32[]{:S(2)}) collective-permute-start(bf16[2,512,512]{2,1,0:T(8,128)(2,1)} %pad_maximum_fusion.21), channel_id=1, source_target_pairs={{0,4},{4,0},{1,5},{5,1},{2,6},{6,2},{3,7},{7,3},{8,12},{12,8},{9,1... | collective-permute-start | bytes 3145736 | tf_op jit(solution)/shard_map/ppermute | solution.py:318
  462.5 306.7 %reduce-scatter.8.cloned.1.call-start = ((), (), s32[]{:S(2)}) async-start(), calls=%async_computation.11 | async-start | bytes 1310720 | tf_op jit(solution)/shard_map/reduce_scatter | solution.py:408
  464.8 26.1 %collective-permute-start.46 = (bf16[2,512,512]{2,1,0:T(8,128)(2,1)S(1)}, bf16[2,512,512]{2,1,0:T(8,128)(2,1)S(1)}, u32[]{:S(2)}, u32[]{:S(2)}) collective-permute-start(bf16[2,512,512]{2,1,0:T(8,128)(2,1)S(1)} %pad_maximum_fusion.22), channel_id=1, source_target_pairs={{0,2},{2,0},{1,3},{3,1},{4,6},{6,4},{5,7},{7,5},{8,10},{10,8},{9,1... | collective-permute-start | bytes 3145736 | tf_op jit(solution)/shard_map/ppermute | solution.py:318
  479.8 21.5 %collective-permute-start.45 = (bf16[512,512]{1,0:T(8,128)(2,1)S(1)}, bf16[512,512]{1,0:T(8,128)(2,1)S(1)}, u32[]{:S(2)}, u32[]{:S(2)}) collective-permute-start(bf16[512,512]{1,0:T(8,128)(2,1)S(1)} %fusion.69), channel_id=1, source_target_pairs={{0,2},{2,0},{1,3},{3,1},{4,6},{6,4},{5,7},{7,5},{8,10},{10,8},{9,1... | collective-permute-start | bytes 1572872 | tf_op jit(solution)/shard_map/ppermute | solution.py:318
  502.7 14.9 %collective-permute-start.47 = (bf16[512,512]{1,0:T(8,128)(2,1)S(1)}, bf16[512,512]{1,0:T(8,128)(2,1)S(1)}, u32[]{:S(2)}, u32[]{:S(2)}) collective-permute-start(bf16[512,512]{1,0:T(8,128)(2,1)S(1)} %get-tuple-element.56), channel_id=1, source_target_pairs={{0,4},{4,0},{1,5},{5,1},{2,6},{6,2},{3,7},{7,3},{8,12},{12,8},{9,1... | collective-permute-start | bytes 1572872 | tf_op jit(solution)/shard_map/ppermute | solution.py:318
  503.6 36.5 %collective-permute-start.30 = (bf16[2,512,512]{2,1,0:T(8,128)(2,1)S(1)}, bf16[2,512,512]{2,1,0:T(8,128)(2,1)S(1)}, u32[]{:S(2)}, u32[]{:S(2)}) collective-permute-start(bf16[2,512,512]{2,1,0:T(8,128)(2,1)S(1)} %pad_maximum_fusion.19), channel_id=1, source_target_pairs={{0,4},{4,0},{1,5},{5,1},{2,6},{6,2},{3,7},{7,3},{8,12},{12,8},{9,1... | collective-permute-start | bytes 3145736 | tf_op jit(solution)/shard_map/ppermute | solution.py:318
  526.6 34.5 %collective-permute-start.53 = (bf16[1024,512]{1,0:T(8,128)(2,1)S(1)}, bf16[1024,512]{1,0:T(8,128)(2,1)S(1)}, u32[]{:S(2)}, u32[]{:S(2)}) collective-permute-start(bf16[1024,512]{1,0:T(8,128)(2,1)S(1)} %get-tuple-element.36.refs_0_), channel_id=1, source_target_pairs={{0,4},{4,0},{1,5},{5,1},{2,6},{6,2},{3,7},{7,3},{8,12},{12,8},{9,1... | collective-permute-start | bytes 3145736 | tf_op jit(solution)/shard_map/ppermute | solution.py:318
  527.1 35.5 %collective-permute-start.51 = (bf16[1024,512]{1,0:T(8,128)(2,1)S(1)}, bf16[1024,512]{1,0:T(8,128)(2,1)}, u32[]{:S(2)}, u32[]{:S(2)}) collective-permute-start(bf16[1024,512]{1,0:T(8,128)(2,1)S(1)} %get-tuple-element.36.refs_0_), channel_id=1, source_target_pairs={{0,2},{2,0},{1,3},{3,1},{4,6},{6,4},{5,7},{7,5},{8,10},{10,8},{9,1... | collective-permute-start | bytes 3145736 | tf_op jit(solution)/shard_map/ppermute | solution.py:318
  529.7 46.1 %collective-permute-start.32 = (bf16[2,512,512]{2,1,0:T(8,128)(2,1)}, bf16[2,512,512]{2,1,0:T(8,128)(2,1)}, u32[]{:S(2)}, u32[]{:S(2)}) collective-permute-start(bf16[2,512,512]{2,1,0:T(8,128)(2,1)} %pad_maximum_fusion.20), channel_id=1, source_target_pairs={{0,2},{2,0},{1,3},{3,1},{4,6},{6,4},{5,7},{7,5},{8,10},{10,8},{9,1... | collective-permute-start | bytes 3145736 | tf_op jit(solution)/shard_map/ppermute | solution.py:318
  541.3 45.8 %collective-permute-start.31 = (bf16[512,512]{1,0:T(8,128)(2,1)}, bf16[512,512]{1,0:T(8,128)(2,1)}, u32[]{:S(2)}, u32[]{:S(2)}) collective-permute-start(bf16[512,512]{1,0:T(8,128)(2,1)} %fusion.73), channel_id=1, source_target_pairs={{0,2},{2,0},{1,3},{3,1},{4,6},{6,4},{5,7},{7,5},{8,10},{10,8},{9,1... | collective-permute-start | bytes 1572872 | tf_op jit(solution)/shard_map/ppermute | solution.py:318
  561.1 35.2 %collective-permute-start.56 = (bf16[512,512]{1,0:T(8,128)(2,1)S(1)}, bf16[512,512]{1,0:T(8,128)(2,1)S(1)}, u32[]{:S(2)}, u32[]{:S(2)}) collective-permute-start(bf16[512,512]{1,0:T(8,128)(2,1)S(1)} %slice.465), channel_id=1, source_target_pairs={{0,2},{2,0},{1,3},{3,1},{4,6},{6,4},{5,7},{7,5},{8,10},{10,8},{9,1... | collective-permute-start | bytes 1572872 | tf_op jit(solution)/shard_map/ppermute | solution.py:318
  563.7 28.5 %collective-permute-start.55 = (bf16[512,512]{1,0:T(8,128)(2,1)S(1)}, bf16[512,512]{1,0:T(8,128)(2,1)S(1)}, u32[]{:S(2)}, u32[]{:S(2)}) collective-permute-start(bf16[512,512]{1,0:T(8,128)(2,1)S(1)} %slice.464), channel_id=1, source_target_pairs={{0,4},{4,0},{1,5},{5,1},{2,6},{6,2},{3,7},{7,3},{8,12},{12,8},{9,1... | collective-permute-start | bytes 1572872 | tf_op jit(solution)/shard_map/ppermute | solution.py:318
  591.7 18.6 %collective-permute-start.50 = (bf16[1024,512]{1,0:T(8,128)(2,1)S(1)}, bf16[1024,512]{1,0:T(8,128)(2,1)S(1)}, u32[]{:S(2)}, u32[]{:S(2)}) collective-permute-start(bf16[1024,512]{1,0:T(8,128)(2,1)S(1)} %get-tuple-element.36.refs_0_), channel_id=1, source_target_pairs={{0,1},{1,0},{2,3},{3,2},{4,5},{5,4},{6,7},{7,6},{8,9},{9,8},{10,11... | collective-permute-start | bytes 3145736 | tf_op jit(solution)/shard_map/ppermute | solution.py:318
  591.7 19.2 %collective-permute-start.52 = (bf16[1024,512]{1,0:T(8,128)(2,1)}, bf16[1024,512]{1,0:T(8,128)(2,1)}, u32[]{:S(2)}, u32[]{:S(2)}) collective-permute-start(bf16[1024,512]{1,0:T(8,128)(2,1)} %collective-permute-done.51.refs_2_), channel_id=1, source_target_pairs={{0,1},{1,0},{2,3},{3,2},{4,5},{5,4},{6,7},{7,6},{8,9},{9,8},{10,11... | collective-permute-start | bytes 3145736 | tf_op jit(solution)/shard_map/ppermute | solution.py:318
  592.3 32.5 %collective-permute-start.54 = (bf16[1024,512]{1,0:T(8,128)(2,1)S(1)}, bf16[1024,512]{1,0:T(8,128)(2,1)}, u32[]{:S(2)}, u32[]{:S(2)}) collective-permute-start(bf16[1024,512]{1,0:T(8,128)(2,1)S(1)} %collective-permute-done.53.refs_0_), channel_id=1, source_target_pairs={{0,1},{1,0},{2,3},{3,2},{4,5},{5,4},{6,7},{7,6},{8,9},{9,8},{10,11... | collective-permute-start | bytes 3145736 | tf_op jit(solution)/shard_map/ppermute | solution.py:318
  597.1 27.6 %collective-permute-start.57 = (bf16[1024,512]{1,0:T(8,128)(2,1)}, bf16[1024,512]{1,0:T(8,128)(2,1)}, u32[]{:S(2)}, u32[]{:S(2)}) collective-permute-start(bf16[1024,512]{1,0:T(8,128)(2,1)} %constant_dynamic-update-slice_fusion.10.refs_2_), channel_id=1, source_target_pairs={{0,1},{1,0},{2,3},{3,2},{4,5},{5,4},{6,7},{7,6},{8,9},{9,8},{10,11... | collective-permute-start | bytes 3145736 | tf_op jit(solution)/shard_map/ppermute | solution.py:318
  600.7 16.4 %collective-permute-start.68 = (bf16[256,768]{1,0:T(8,128)(2,1)S(1)}, bf16[256,768]{1,0:T(8,128)(2,1)}, u32[]{:S(2)}, u32[]{:S(2)}) collective-permute-start(bf16[256,768]{1,0:T(8,128)(2,1)S(1)} %constant_dynamic-slice_fusion.6), channel_id=1, source_target_pairs={{0,4},{4,0},{1,5},{5,1},{2,6},{6,2},{3,7},{7,3},{8,12},{12,8},{9,1... | collective-permute-start | bytes 1179656 | tf_op jit(solution)/shard_map/ppermute | solution.py:318
  610.9 130.2 %collective-permute-start.69 = (bf16[256,768]{1,0:T(8,128)(2,1)}, bf16[256,768]{1,0:T(8,128)(2,1)}, u32[]{:S(2)}, u32[]{:S(2)}) collective-permute-start(bf16[256,768]{1,0:T(8,128)(2,1)} %constant_dynamic-slice_fusion.5), channel_id=1, source_target_pairs={{0,4},{4,0},{1,5},{5,1},{2,6},{6,2},{3,7},{7,3},{8,12},{12,8},{9,1... | collective-permute-start | bytes 1179656 | tf_op jit(solution)/shard_map/ppermute | solution.py:318
  690.6 152.3 %reduce-scatter.6.cloned.1.call-start = ((), (), s32[]{:S(2)}) async-start(), calls=%async_computation.10 | async-start | bytes 3932160 | tf_op jit(solution)/shard_map/reduce_scatter | solution.py:408
  740.0 25.3 %collective-permute-start.60 = (bf16[2,512,512]{2,1,0:T(8,128)(2,1)S(1)}, bf16[2,512,512]{2,1,0:T(8,128)(2,1)S(1)}, u32[]{:S(2)}, u32[]{:S(2)}) collective-permute-start(bf16[2,512,512]{2,1,0:T(8,128)(2,1)S(1)} %pad_maximum_fusion.24), channel_id=1, source_target_pairs={{0,4},{4,0},{1,5},{5,1},{2,6},{6,2},{3,7},{7,3},{8,12},{12,8},{9,1... | collective-permute-start | bytes 3145736 | tf_op jit(solution)/shard_map/ppermute | solution.py:318
  745.4 26.3 %collective-permute-start.62 = (bf16[2,512,512]{2,1,0:T(8,128)(2,1)}, bf16[2,512,512]{2,1,0:T(8,128)(2,1)}, u32[]{:S(2)}, u32[]{:S(2)}) collective-permute-start(bf16[2,512,512]{2,1,0:T(8,128)(2,1)} %pad_maximum_fusion.25), channel_id=1, source_target_pairs={{0,2},{2,0},{1,3},{3,1},{4,6},{6,4},{5,7},{7,5},{8,10},{10,8},{9,1... | collective-permute-start | bytes 3145736 | tf_op jit(solution)/shard_map/ppermute | solution.py:318
  766.4 15.8 %collective-permute-start.61 = (bf16[512,512]{1,0:T(8,128)(2,1)}, bf16[512,512]{1,0:T(8,128)(2,1)}, u32[]{:S(2)}, u32[]{:S(2)}) collective-permute-start(bf16[512,512]{1,0:T(8,128)(2,1)} %fusion.65), channel_id=1, source_target_pairs={{0,2},{2,0},{1,3},{3,1},{4,6},{6,4},{5,7},{7,5},{8,10},{10,8},{9,1... | collective-permute-start | bytes 1572872 | tf_op jit(solution)/shard_map/ppermute | solution.py:318
  770.1 16.2 %collective-permute-start.67 = (bf16[256,256]{1,0:T(8,128)(2,1)S(1)}, bf16[256,256]{1,0:T(8,128)(2,1)S(1)}, u32[]{:S(2)}, u32[]{:S(2)}) collective-permute-start(bf16[256,256]{1,0:T(8,128)(2,1)S(1)} %constant_dynamic-slice_fusion.7), channel_id=1, source_target_pairs={{0,4},{4,0},{1,5},{5,1},{2,6},{6,2},{3,7},{7,3},{8,12},{12,8},{9,1... | collective-permute-start | bytes 393224 | tf_op jit(solution)/shard_map/ppermute | solution.py:318
  799.4 39.6 %collective-permute-start.64 = (f32[1024,1]{0,1:T(1,128)S(1)}, f32[1024,1]{0,1:T(1,128)S(1)}, u32[]{:S(2)}, u32[]{:S(2)}) collective-permute-start(f32[1024,1]{0,1:T(1,128)S(1)} %bitcast.327), channel_id=1, source_target_pairs={{0,1},{1,0},{2,3},{3,2},{4,5},{5,4},{6,7},{7,6},{8,9},{9,8},{10,11... | collective-permute-start | bytes 12296 | tf_op jit(solution)/shard_map/ppermute | solution.py:318
  (136 other events, 1828.3 us)
Sparse Core Ops, SparseCore 0:
  24.5 64.9 all-gather.5
  91.6 26.5 all-gather.7
  119.8 62.9 all-gather.13
  200.0 62.9 all-gather.11
  321.7 63.4 all-gather.9
  413.8 58.8 reduce-scatter.9
  475.0 60.2 reduce-scatter.13
  537.6 60.2 reduce-scatter.11
  690.7 24.6 reduce-scatter.7
  731.7 57.8 reduce-scatter.5

commit v2 on v1

--- a/solution.py
+++ b/solution.py
@@ -314,16 +314,23 @@
     return jax.shard_map(body, mesh=mesh, in_specs=in_specs, out_specs=out_specs, check_vma=False)
 
 
+def tie(*values):
+    return lax.optimization_barrier(values)
+
+
 def flip(values, axis):
     return lax.ppermute(values, axis, [(0, 1), (1, 0)])
 
 
+def flip_both(first, first_axis, second, second_axis):
+    first, second = tie(first, second)
+    return tie(flip(first, first_axis), flip(second, second_axis))
+
+
 def spread(own):
     half = own.shape[0] // 2
-    via_y = flip(own, "y")
-    via_x = flip(own, "x")
-    first = flip(via_y[:half], "x")
-    second = flip(via_x[half:], "y")
+    via_y, via_x = flip_both(own, "y", own, "x")
+    first, second = flip_both(via_y[:half], "x", via_x[half:], "y")
     held = ((own, via_y), (via_x, jnp.concatenate([first, second], axis=0)))
     return tuple(
         tuple(block for values in pair for block in (values, flip(values, "core")))
@@ -331,60 +338,67 @@
     )
 
 
-def pack_kernel(place_ref, gain_ref, *refs):
-    blocks, out_ref = refs[:4], refs[4]
+def pack_kernel(normed, place_ref, gain_ref, *refs):
+    blocks, out_ref = refs[:4], refs[5]
     width = blocks[0].shape[1]
     place = place_ref[0]
-    if len(refs) == 6:
+    if normed:
         values = [block[...].astype(jnp.float32) for block in blocks]
         squares = sum(jnp.sum(v * v, axis=1, keepdims=True) for v in values)
         inverse = lax.rsqrt(squares / (4 * width) + eps_norm)
-        refs[5][...] = inverse
+        refs[6][...] = inverse
     for index in range(4):
         columns = pl.ds(pl.multiple_of((place ^ index) * width, width), width)
-        if len(refs) == 6:
+        if normed:
             result = values[index] * inverse * gain_ref[:, columns]
             out_ref[:, columns] = result.astype(out_ref.dtype)
         else:
             out_ref[:, columns] = blocks[index][...]
 
 
-def pack(blocks, place, gain, normed):
+def pack(blocks, place, gain, normed, step, target):
     count, width = blocks[0].shape
     tile = 256
-    out_shape = [jax.ShapeDtypeStruct((count, 4 * width), jnp.bfloat16)]
-    out_specs = [pl.BlockSpec((tile, 4 * width), lambda i: (i, 0))]
+    tiles = count // tile
+    out_shape = [jax.ShapeDtypeStruct((2 * count, 4 * width), jnp.bfloat16)]
+    out_specs = [pl.BlockSpec((tile, 4 * width), lambda i: (i + step * tiles, 0))]
     if normed:
         out_shape.append(jax.ShapeDtypeStruct((count, 1), jnp.float32))
         out_specs.append(pl.BlockSpec((tile, 1), lambda i: (i, 0)))
+    aliases = {}
+    if target is None:
+        target = place.reshape(1)
+    else:
+        aliases = {6: 0}
     return pl.pallas_call(
-        pack_kernel,
-        grid=(count // tile,),
+        partial(pack_kernel, normed),
+        grid=(tiles,),
         in_specs=[
             pl.BlockSpec(memory_space=pltpu.SMEM),
             pl.BlockSpec((1, 4 * width), lambda i: (0, 0)),
         ]
-        + [pl.BlockSpec((tile, width), lambda i: (i, 0))] * 4,
+        + [pl.BlockSpec((tile, width), lambda i: (i, 0))] * 4
+        + [pl.BlockSpec(memory_space=pl.ANY if aliases else pltpu.SMEM)],
         out_specs=out_specs,
         out_shape=out_shape,
+        input_output_aliases=aliases,
         cost_estimate=pl.CostEstimate(
             flops=0, bytes_accessed=count * width * 16, transcendentals=0
         ),
-    )(place.reshape(1), gain.reshape(1, -1), *blocks)
+    )(place.reshape(1), gain.reshape(1, -1), *blocks, target)
 
 
 def gather_normed(own, place, gain):
     first, second = spread(own)
-    normed_own, inverse = pack(first, place, gain, True)
-    normed_other, unused = pack(second, place, gain, True)
-    return (jnp.concatenate([normed_own, normed_other], axis=0), inverse)
+    target, inverse = pack(first, place, gain, True, 0, None)
+    normed, unused = pack(second, place, gain, True, 1, target)
+    return (normed, inverse)
 
 
 def gather_plain(own, place, gain):
     first, second = spread(own)
-    return jnp.concatenate(
-        [pack(first, place, gain, False)[0], pack(second, place, gain, False)[0]], axis=0
-    )
+    target = pack(first, place, gain, False, 0, None)[0]
+    return pack(second, place, gain, False, 1, target)[0]
 
 
 def halves(weights, across):
@@ -425,20 +439,23 @@
         return total
 
     low = jnp.bfloat16
-    sent = [flip(product(index).astype(low), "core") for index in (1, 3)]
-    held = [product(index) + got for index, got in zip((0, 2), sent)]
-    count = held[0].shape[0] // 2
+    sent = [flip(product(index).astype(low), "core") for index in (3, 1)]
+    far = (product(2) + sent[0]).astype(low)
+    near = (product(0) + sent[1]).astype(low)
+    count = far.shape[0] // 2
     half = count // 2
-    near, far = [v.astype(low) for v in held]
-    upper = flip(jnp.stack([near[count : count + half], far[count : count + half]]), "x")
-    lower = flip(jnp.stack([far[half:count], far[count + half :]]), "y")
+    upper, lower = flip_both(
+        jnp.stack([near[count : count + half], far[count : count + half]]),
+        "x",
+        jnp.stack([far[half:count], far[count + half :]]),
+        "y",
+    )
     upper_near = near[:half].astype(jnp.float32) + upper[0]
     upper_far = (far[:half].astype(jnp.float32) + upper[1]).astype(low)
     lower_own = near[half:count].astype(jnp.float32) + lower[0]
     lower_other = (near[count + half :].astype(jnp.float32) + lower[1]).astype(low)
-    upper_final = upper_near + flip(upper_far, "y")
-    lower_final = lower_own + flip(lower_other, "x")
-    return jnp.concatenate([upper_final, lower_final], axis=0)
+    upper_got, lower_got = flip_both(upper_far, "y", lower_other, "x")
+    return jnp.concatenate([upper_near + upper_got, lower_own + lower_got], axis=0)
 
 
 def norm_back_own(grad_own, values_own, inverse, gain_own, width):
@@ -459,6 +476,264 @@
     return lax.dot_general(
         first, second, (((0,), (0,)), ((), ())), preferred_element_type=jnp.float32
     ).astype(jnp.bfloat16)
+
+
+def row_tables(segments, head_dim):
+    count = segments.shape[0]
+    index = jnp.arange(count, dtype=jnp.int32)
+    previous = jnp.concatenate([jnp.full((1,), -1, jnp.int32), segments[:-1]])
+    starts = lax.cummax(jnp.where(segments != previous, index, 0), axis=0)
+    position = (index - starts).astype(jnp.float32)
+    half = head_dim // 2
+    freqs = jnp.power(rope_base, -(jnp.arange(half, dtype=jnp.float32) * 2.0 / head_dim))
+    angle = position[:, None] * freqs[None, :]
+    cosine, sine = jnp.cos(angle), jnp.sin(angle)
+    return (
+        jnp.concatenate([cosine, cosine], axis=1),
+        jnp.concatenate([-sine, sine], axis=1),
+        jnp.where(segments > 0, starts, index)[None, :],
+    )
+
+
+def product_nt(first, second):
+    return lax.dot_general(
+        first, second, (((1,), (1,)), ((), ())), preferred_element_type=jnp.float32
+    )
+
+
+def product_tn(first, second):
+    return lax.dot_general(
+        first, second, (((0,), (0,)), ((), ())), preferred_element_type=jnp.float32
+    )
+
+
+def product_nn(first, second):
+    return lax.dot_general(
+        first, second, (((1,), (0,)), ((), ())), preferred_element_type=jnp.float32
+    )
+
+
+def prepare_tile(raw, gain, cosine, sine):
+    inverse = lax.rsqrt(jnp.mean(raw * raw, axis=1, keepdims=True) + eps_norm)
+    normed = raw * inverse * gain
+    turned = pltpu.roll(normed, raw.shape[1] // 2, 1)
+    return (normed * cosine + turned * sine).astype(jnp.bfloat16)
+
+
+def prepare_back(raw, gain, cosine, sine, grad):
+    inverse = lax.rsqrt(jnp.mean(raw * raw, axis=1, keepdims=True) + eps_norm)
+    unit = raw * inverse
+    grad_normed = grad * cosine + pltpu.roll(grad * sine, raw.shape[1] // 2, 1)
+    scaled = grad_normed * gain
+    grad_raw = inverse * (scaled - unit * jnp.mean(scaled * unit, axis=1, keepdims=True))
+    return (grad_raw.astype(jnp.bfloat16), jnp.sum(grad_normed * unit, axis=0, keepdims=True))
+
+
+def allowed_tile(first_ref, start, tile, reach):
+    rows = lax.broadcasted_iota(jnp.int32, (reach, tile), 0)
+    columns = lax.broadcasted_iota(jnp.int32, (reach, tile), 1) + start
+    return (rows >= first_ref[0, :, pl.ds(start, tile)]) & (rows <= columns)
+
+
+def attend_kernel(
+    heads, tile, joint_ref, cos_ref, sin_ref, first_ref, gain_query_ref, gain_key_ref,
+    mixed_ref, attended_ref, query_ref, key_ref, logsum_ref,
+):
+    count, head_dim = cos_ref.shape
+    scale = head_dim ** (-0.5)
+    low = jnp.bfloat16
+    key_at = 2 * heads * head_dim
+    tiles = count // tile
+    for part in range(tiles):
+        rows = pl.ds(part * tile, tile)
+        key_ref[rows, :] = prepare_tile(
+            joint_ref[rows, key_at : key_at + head_dim],
+            gain_key_ref[...],
+            cos_ref[rows, :],
+            sin_ref[rows, :],
+        )
+    for head in range(heads):
+        columns = slice(head * head_dim, (head + 1) * head_dim)
+        gates = slice((heads + head) * head_dim, (heads + head + 1) * head_dim)
+        for part in range(tiles):
+            rows = pl.ds(part * tile, tile)
+            reach = (part + 1) * tile
+            query = prepare_tile(
+                joint_ref[rows, columns], gain_query_ref[...], cos_ref[rows, :], sin_ref[rows, :]
+            )
+            query_ref[rows, columns] = query
+            scores = product_nt(key_ref[:reach, :], query) * scale
+            scores = jnp.where(allowed_tile(first_ref, part * tile, tile, reach), scores, -1e30)
+            peak = jnp.max(scores, axis=0, keepdims=True)
+            weights = jnp.exp(scores - peak)
+            total = jnp.sum(weights, axis=0, keepdims=True)
+            probs = (weights * (1.0 / total)).astype(low)
+            logsum_ref[0, head : head + 1, rows] = peak + jnp.log(total)
+            values = joint_ref[:reach, key_at + head_dim : key_at + 2 * head_dim].astype(low)
+            attended = product_tn(values, probs).T
+            attended_ref[rows, columns] = attended
+            gate = joint_ref[rows, gates]
+            mixed_ref[rows, columns] = (attended * jax.nn.sigmoid(gate)).astype(low)
+
+
+def attend_back_kernel(
+    heads, tile, joint_ref, cos_ref, sin_ref, first_ref, gain_query_ref, gain_key_ref,
+    attended_ref, query_ref, key_ref, logsum_ref, grad_mixed_ref,
+    grad_joint_ref, grad_gain_ref, grad_key_acc, grad_value_acc,
+):
+    count, head_dim = cos_ref.shape
+    scale = head_dim ** (-0.5)
+    low = jnp.bfloat16
+    key_at = 2 * heads * head_dim
+    value_at = key_at + head_dim
+    tiles = count // tile
+    gain_query = jnp.zeros((1, head_dim), jnp.float32)
+    gain_key = jnp.zeros((1, head_dim), jnp.float32)
+    for head in range(heads):
+        columns = slice(head * head_dim, (head + 1) * head_dim)
+        gates = slice((heads + head) * head_dim, (heads + head + 1) * head_dim)
+        for part in reversed(range(tiles)):
+            rows = pl.ds(part * tile, tile)
+            reach = (part + 1) * tile
+            fresh = head == 0 and part == tiles - 1
+            gate = jax.nn.sigmoid(joint_ref[rows, gates])
+            grad_mixed = grad_mixed_ref[rows, columns]
+            gated = grad_mixed * gate
+            grad_attended = gated.astype(low)
+            grad_joint_ref[rows, gates] = (gated * attended_ref[rows, columns] * (1.0 - gate)).astype(
+                low
+            )
+            query = query_ref[rows, columns]
+            keys = key_ref[:reach, :]
+            values = joint_ref[:reach, value_at : value_at + head_dim].astype(low)
+            scores = product_nt(keys, query) * scale
+            logsum = logsum_ref[0, head : head + 1, rows]
+            probs = jnp.where(
+                allowed_tile(first_ref, part * tile, tile, reach), jnp.exp(scores - logsum), 0.0
+            )
+            grad_value = product_nn(probs.astype(low), grad_attended)
+            grad_probs = product_nt(values, grad_attended)
+            delta = jnp.sum(probs * grad_probs, axis=0, keepdims=True)
+            grad_scores = (probs * (grad_probs - delta)).astype(low)
+            grad_key = product_nn(grad_scores, query)
+            if fresh:
+                grad_value_acc[...] = grad_value
+                grad_key_acc[...] = grad_key
+            else:
+                grad_value_acc[:reach, :] += grad_value
+                grad_key_acc[:reach, :] += grad_key
+            grad_query = product_tn(keys, grad_scores).T * scale
+            grad_raw, gain_part = prepare_back(
+                joint_ref[rows, columns],
+                gain_query_ref[...],
+                cos_ref[rows, :],
+                sin_ref[rows, :],
+                grad_query,
+            )
+            grad_joint_ref[rows, columns] = grad_raw
+            gain_query = gain_query + gain_part
+    for part in range(tiles):
+        rows = pl.ds(part * tile, tile)
+        grad_raw, gain_part = prepare_back(
+            joint_ref[rows, key_at:value_at],
+            gain_key_ref[...],
+            cos_ref[rows, :],
+            sin_ref[rows, :],
+            grad_key_acc[rows, :] * scale,
+        )
+        grad_joint_ref[rows, key_at:value_at] = grad_raw
+        gain_key = gain_key + gain_part
+        grad_joint_ref[rows, value_at : value_at + head_dim] = grad_value_acc[rows, :].astype(low)
+    both = jnp.concatenate([gain_query, gain_key], axis=0)
+
+    @pl.when(pl.program_id(0) == 0)
+    def begin():
+        grad_gain_ref[...] = both
+
+    @pl.when(pl.program_id(0) > 0)
+    def add():
+        grad_gain_ref[...] += both
+
+
+def attend_specs(count, head_dim, heads, joint_width):
+    wide = lambda width: pl.BlockSpec((count, width), lambda s: (s, 0))
+    row = pl.BlockSpec((1, head_dim), lambda s: (0, 0))
+    lead = [
+        wide(joint_width),
+        wide(head_dim),
+        wide(head_dim),
+        pl.BlockSpec((1, 1, count), lambda s: (s, 0, 0)),
+        row,
+        row,
+    ]
+    kept = [
+        wide(heads * head_dim),
+        wide(heads * head_dim),
+        wide(head_dim),
+        pl.BlockSpec((1, heads, count), lambda s: (s, 0, 0)),
+    ]
+    return (lead, kept, wide)
+
+
+def attend_fwd(joint, cosine, sine, first, gain_query, gain_key, heads, count):
+    head_dim = cosine.shape[1]
+    lead, kept, wide = attend_specs(count, head_dim, heads, joint.shape[1])
+    total = joint.shape[0]
+    shape = jax.ShapeDtypeStruct
+    return pl.pallas_call(
+        partial(attend_kernel, heads, 256),
+        grid=(total // count,),
+        in_specs=lead,
+        out_specs=[wide(heads * head_dim)] + kept,
+        out_shape=[
+            shape((total, heads * head_dim), jnp.bfloat16),
+            shape((total, heads * head_dim), jnp.float32),
+            shape((total, heads * head_dim), jnp.bfloat16),
+            shape((total, head_dim), jnp.bfloat16),
+            shape((total // count, heads, count), jnp.float32),
+        ],
+        compiler_params=pltpu.CompilerParams(vmem_limit_bytes=40 * 1024 * 1024),
+        cost_estimate=pl.CostEstimate(
+            flops=4 * total * count * heads * head_dim,
+            bytes_accessed=total * head_dim * 60,
+            transcendentals=total * count * heads,
+        ),
+    )(joint, cosine, sine, first, gain_query.reshape(1, -1), gain_key.reshape(1, -1))
+
+
+def attend_bwd(joint, cosine, sine, first, gain_query, gain_key, kept_values, grad_mixed, count):
+    head_dim = cosine.shape[1]
+    heads = grad_mixed.shape[1] // head_dim
+    lead, kept, wide = attend_specs(count, head_dim, heads, joint.shape[1])
+    total = joint.shape[0]
+    shape = jax.ShapeDtypeStruct
+    return pl.pallas_call(
+        partial(attend_back_kernel, heads, 256),
+        grid=(total // count,),
+        in_specs=lead + kept + [wide(heads * head_dim)],
+        out_specs=[wide(joint.shape[1]), pl.BlockSpec((2, head_dim), lambda s: (0, 0))],
+        out_shape=[shape(joint.shape, jnp.bfloat16), shape((2, head_dim), jnp.float32)],
+        scratch_shapes=[
+            pltpu.VMEM((count, head_dim), jnp.float32),
+            pltpu.VMEM((count, head_dim), jnp.float32),
+        ],
+        compiler_params=pltpu.CompilerParams(vmem_limit_bytes=48 * 1024 * 1024),
+        cost_estimate=pl.CostEstimate(
+            flops=10 * total * count * heads * head_dim,
+            bytes_accessed=total * head_dim * 80,
+            transcendentals=total * count * heads,
+        ),
+    )(
+        joint, cosine, sine, first, gain_query.reshape(1, -1), gain_key.reshape(1, -1),
+        *kept_values, grad_mixed,
+    )
+
+
+def sum_all(values):
+    values = values + flip(values, "x")
+    for step in (1, 2):
+        values = values + lax.ppermute(values, "z", [(i, i ^ step) for i in range(4)])
+    return values
 
 
 def fast_body(
@@ -486,7 +761,7 @@
     low = jnp.bfloat16
     query_width = w_query.shape[1] // 2
     key_width = w_key.shape[1] // 2
-    kv_heads = key_width // head_dim
+    heads = query_width // head_dim
     hidden_width = w_ffgate.shape[1] // 2
     chunk = hidden_width // 2
     live = (segment_ids > 0).astype(jnp.float32)[:, None]
@@ -510,33 +785,21 @@
         )
 
     segments = jnp.stack([segment_ids, flip(segment_ids, "x")])
-    cosine, sine = jax.vmap(partial(rope_tables, head_dim=head_dim))(segments)
+    cosine, sine, first = jax.vmap(partial(row_tables, head_dim=head_dim))(segments)
     cosine = cosine.reshape(2 * count, head_dim)
     sine = sine.reshape(2 * count, head_dim)
-    allowed = jax.vmap(attend_mask)(segments)
+
+    grad_out = live * cotangent.astype(jnp.float32)
+    grad_out_low, hidden1 = tie(grad_out.astype(low), hidden1)
+    grad_out_full = gather_plain(grad_out_low, place, gain_ffn)
 
     joint = dot_in(hidden1, attn_weight)
-    query_raw = joint[:, :query_width]
-    gate_raw = joint[:, query_width : 2 * query_width]
-    key_raw = joint[:, 2 * query_width : 2 * query_width + key_width]
-    values = joint[:, 2 * query_width + key_width :].astype(low)
-    prepare = partial(head_prepare, cosine=cosine, sine=sine)
-    query = prepare(query_raw, gain_query).astype(low)
-    keys = prepare(key_raw, gain_key).astype(low)
-    split = lambda v: v.reshape(2, count, -1)
-    attended, logsum = jax.vmap(
-        partial(attend_forward, kv_heads=kv_heads, head_dim=head_dim)
-    )(split(query), split(keys), split(values), allowed)
-    attended = attended.reshape(2 * count, -1)
-    gate_sig = jax.nn.sigmoid(gate_raw)
-    mixed = (attended * gate_sig).astype(low)
+    mixed, *kept = attend_fwd(joint, cosine, sine, first, gain_query, gain_key, heads, count)
+    mixed, grad_out_full = tie(mixed, grad_out_full)
     resid = tokens.astype(jnp.float32) + feature_fold([(mixed, out_weight)], place)
-    resid_low = resid.astype(low)
+    grad_act = dot_in(grad_out_full, down_weight)
+    resid_low, grad_act = tie(resid.astype(low), grad_act)
     hidden2, inverse2 = gather_normed(resid_low, place, gain_ffn)
-
-    grad_out = live * cotangent.astype(jnp.float32)
-    grad_out_full = gather_plain(grad_out.astype(low), place, gain_ffn)
-    grad_act = dot_in(grad_out_full, down_weight)
 
     activated, grad_pairs = [], []
     for part in range(2):
@@ -562,24 +825,14 @@
         grad_hidden2, resid_low.astype(jnp.float32), inverse2, gain_ffn_own, width
     )
     grad_resid = grad_out + grad_input2
+    grad_branch_full = gather_plain(grad_resid.astype(low), place, gain_ffn)
+    grad_branch_full, activated = tie(grad_branch_full, activated)
     ffn_out = feature_fold([(activated, down_weight)], place)
     output = (live * (resid + ffn_out)).astype(low)
-    grad_branch_full = gather_plain(grad_resid.astype(low), place, gain_ffn)
     grad_mixed = dot_in(grad_branch_full, out_weight)
     out_sum = grad_scatter(dot_grad(grad_branch_full, mixed), across)
-    grad_attended = (grad_mixed * gate_sig).astype(low)
-    grad_gate_raw = (grad_mixed * attended * gate_sig * (1.0 - gate_sig)).astype(low)
-    grad_query, grad_keys, grad_values = jax.vmap(
-        partial(attend_backward, kv_heads=kv_heads, head_dim=head_dim)
-    )(split(query), split(keys), split(values), allowed, logsum, split(grad_attended))
-    flat = lambda v: v.reshape(2 * count, -1)
-    unused_query, query_back = jax.vjp(prepare, query_raw, gain_query)
-    grad_query_raw, grad_gain_query = query_back(flat(grad_query))
-    unused_key, key_back = jax.vjp(prepare, key_raw, gain_key)
-    grad_key_raw, grad_gain_key = key_back(flat(grad_keys))
-    grad_joint = jnp.concatenate(
-        [grad_query_raw.astype(low), grad_gate_raw, grad_key_raw.astype(low), flat(grad_values)],
-        axis=1,
+    grad_joint, grad_head_gains = attend_bwd(
+        joint, cosine, sine, first, gain_query, gain_key, kept, grad_mixed, count
     )
     attn_sum = grad_scatter(dot_grad(hidden1, grad_joint), across)
     grad_hidden1 = feature_fold([(grad_joint, attn_weight)], place)
@@ -588,18 +841,18 @@
     )
     grad_tokens = grad_resid + grad_input1
 
-    spot = lambda v: lax.dynamic_update_slice_in_dim(jnp.zeros((width,), jnp.float32), v, offset, 0)
-    gains = lax.psum(
-        jnp.concatenate(
-            [spot(gain_attn_grad), spot(gain_ffn_grad), grad_gain_query, grad_gain_key]
-        ),
-        ("z", "x", "y", "core"),
-    )
+    own_gains = sum_all(jnp.stack([gain_attn_grad, gain_ffn_grad]))
+    head_gains = sum_all(grad_head_gains)
+    for axis in ("core", "y"):
+        head_gains = head_gains + flip(head_gains, axis)
+    spot = lax.dynamic_update_slice_in_dim(
+        jnp.zeros((2, width), jnp.float32), own_gains, offset, 1
+    )
+    for axis in ("core", "y"):
+        spot = spot + flip(spot, axis)
 
     def join(sums, low_cut, high_cut):
-        return jnp.concatenate(
-            [s[:, low_cut:high_cut] for s in sums], axis=1
-        ).astype(jnp.float32)
+        return jnp.concatenate([s[:, low_cut:high_cut] for s in sums], axis=1).astype(jnp.float32)
 
     def join_parts(low_cut, high_cut):
         return jnp.concatenate(
@@ -617,10 +870,10 @@
     return (
         output,
         grad_tokens,
-        gains[:width],
-        gains[width : 2 * width],
-        gains[2 * width : 2 * width + head_dim],
-        gains[2 * width + head_dim :],
+        spot[0],
+        spot[1],
+        head_gains[0],
+        head_gains[1],
         join(attn_sum, cuts[0], cuts[1]),
         join(attn_sum, cuts[1], cuts[2]),
         join(attn_sum, cuts[2], cuts[3]),
@@ -634,13 +887,15 @@
 
 def solution(mesh):
     rows, columns = mesh.devices.shape
-    split = rows % 2 == 0 and columns == 4
 
     def run(*args):
-        if not split:
+        head_dim = args[5].shape[0]
+        query_width, key_width = args[7].shape[1], args[9].shape[1]
+        one_key_head = key_width == 2 * columns * head_dim and query_width % key_width == 0
+        if not (rows == 8 and columns == 4 and one_key_head):
             return plain(mesh)(*args)
         names = ("z", "x", "y", "core")
-        inner = Mesh(mesh.devices.reshape(rows // 2, 2, 2, 2), names)
+        inner = Mesh(mesh.devices.reshape(4, 2, 2, 2), names)
         block = P(("z", "x"), ("y", "core"))
         whole = P()
         in_specs = (block, block, P(("z", "x"))) + (whole,) * 4 + (block,) * 8

time: 876 us -> 754 us (0.86)
  other arithmetic: 127 us -> 78.1 us
  matrix products: 208 us -> 160 us
  local copies, waits for them, and re-layouts: 90.1 us -> 48.8 us
  blocking collectives: 38.6 us -> 0 us
  Pallas kernels: 42 us -> 68.6 us
  waiting for transfers between devices: 282 us -> 299 us
  starting transfers between devices: 59.2 us -> 74.8 us
    dot_general x6 -> x0, matrix products: 49.3 us -> none  [the longest x1 13.1 us: attend_backward(): jnp.einsum('qgrd,kgd->grqk', grad_grouped, valued, preferred_element_type...]
    psum x1 -> x0, blocking collectives: 38.6 us -> none  [fast_body(): lax.psum(jnp.concatenate([spot(gain_attn_grad), spot(gain_ffn_grad), grad...]
    pallas_call x8 -> x10, Pallas kernels: 42 us -> 68.6 us  [the longest x8 41.6 us: pack(): pl.pallas_call(partial(pack_kernel, normed), grid=(tiles,), in_specs=[pl....]
    ppermute x71 -> x77, waiting for transfers between devices: 279 us -> 256 us  [flip(): return lax.ppermute(values, axis, [(0, 1), (1, 0)])]
    reduce_scatter x5, waiting for transfers between devices: 0.02 us -> 20 us  [grad_scatter(): summed = lax.psum_scatter(grads, 'z', scatter_dimension=0, tiled=True)]
    all_gather x5, waiting for transfers between devices: 2.27 us -> 20.9 us  [weight_gather(): lax.all_gather(jnp.concatenate([top, bottom], axis=0), 'z', axis=0, tiled...]
    reduce_sum x5 -> x0, other arithmetic: 16.8 us -> none  [the longest x2 8.44 us: head_prepare(): normed = heads * inverse * gain]
    all_gather x5, starting transfers between devices: 0.38 us -> 12.1 us  [weight_gather(): lax.all_gather(jnp.concatenate([top, bottom], axis=0), 'z', axis=0, tiled...]
  transfers between devices with their start and end apart: 81 -> 91, of which waited for: 34 -> 42; matrix products, arithmetic and copies ran while one was open for 44% -> 33% of each run, Pallas kernels for 5% -> 9%
where the time goes in v2:
time: 754 us; the launch traced here: 745 us
  waiting for transfers between devices  299 us (40%)
  matrix products  160 us (21%)
  other arithmetic  78.1 us (10%)
  starting transfers between devices  74.8 us (10%)
  Pallas kernels  68.6 us (9%)
  local copies, waits for them, and re-layouts  48.8 us (6%)
  between operations  15.8 us (2%)
    ppermute x77, waiting for transfers between devices, flip(): return lax.ppermute(values, axis, [(0, 1), (1, 0)])  256 us
    dot_general x20, matrix products, product(): lax.dot_general(operand, block, (((1,), (1,)), ((), ())), preferred_eleme...  60.9 us
    ppermute x77, starting transfers between devices, flip(): return lax.ppermute(values, axis, [(0, 1), (1, 0)])  56.9 us
    dot_general x5, matrix products, dot_in(): return jnp.dot(operand, weight, preferred_element_type=jnp.float32)  51.2 us
    dot_general x5, matrix products, dot_grad(): lax.dot_general(first, second, (((0,), (0,)), ((), ())), preferred_elemen...  48.1 us
    pallas_call x8, Pallas kernels, pack(): pl.pallas_call(partial(pack_kernel, normed), grid=(tiles,), in_specs=[pl....  41.6 us
    all_gather x5, waiting for transfers between devices, weight_gather(): lax.all_gather(jnp.concatenate([top, bottom], axis=0), 'z', axis=0, tiled...  20.9 us
    reduce_scatter x5, waiting for transfers between devices, grad_scatter(): summed = lax.psum_scatter(grads, 'z', scatter_dimension=0, tiled=True)  20 us
  transfers between devices with their start and end apart: 91, of which 42 were waited for; matrix products, arithmetic and copies ran while one was open for 33% of the time, Pallas kernels for 9%

profile of v2, /device:TPU:0, one launch (start us, length us, event | category | flops | bytes accessed | tf_op | source)
XLA Modules:
  0.0 745.3 jit_solution(1066480578580364059)
XLA Ops:
  9.5 3.0 collective-permute-start.8
  12.5 9.1 %collective-permute-done.8 = bf16[256,768]{1,0:T(8,128)(2,1)S(1)} collective-permute-done((bf16[256,768]{1,0:T(8,128)(2,1)S(1)}, bf16[256,768]{1,0:T(8,128)(2,1)S(1)}, u32[]{:S(2)}, u32[]{:S(2)}) %collective-permute-start.8) | collective-permute-done | bytes 393248 | tf_op jit(solution)/shard_map/ppermute | solution.py:322
  26.1 21.2 %collective-permute-done.refs_2_ = bf16[1024,512]{1,0:T(8,128)(2,1)} collective-permute-done((bf16[1024,512]{1,0:T(8,128)(2,1)S(1)}, bf16[1024,512]{1,0:T(8,128)(2,1)}, u32[]{:S(2)}, u32[]{:S(2)}) %collective-permute-start) | collective-permute-done | bytes 1048608 | tf_op jit(solution)/shard_map/ppermute | solution.py:322
  56.6 6.8 collective-permute-done.3
  72.3 5.6 shard_map.254
  78.0 5.7 shard_map.255
  86.4 3.7 fusion.56
  90.2 18.7 %collective-permute-done.10.refs_2_ = bf16[1024,512]{1,0:T(8,128)(2,1)} collective-permute-done((bf16[1024,512]{1,0:T(8,128)(2,1)S(1)}, bf16[1024,512]{1,0:T(8,128)(2,1)}, u32[]{:S(2)}, u32[]{:S(2)}) %collective-permute-start.10) | collective-permute-done | bytes 1048608 | tf_op jit(solution)/shard_map/ppermute | solution.py:322
  117.9 9.2 %collective-permute-done.13 = bf16[512,512]{1,0:T(8,128)(2,1)} collective-permute-done((bf16[512,512]{1,0:T(8,128)(2,1)}, bf16[512,512]{1,0:T(8,128)(2,1)}, u32[]{:S(2)}, u32[]{:S(2)}) %collective-permute-start.13) | collective-permute-done | bytes 524320 | tf_op jit(solution)/shard_map/ppermute | solution.py:322
  131.4 4.7 shard_map.257.refs_4_
  136.2 10.0 %fusion.96.joint_ref = f32[2048,768]{1,0:T(8,128)S(1)} fusion(bf16[2048,2048]{1,0:T(8,128)(2,1)} %get-tuple-element.109, bf16[2048,768]{1,0:T(8,128)(2,1)} %all-gather.6.cloned.1.call-done), kind=kOutput, calls=%fused_computation.268 | convolution fusion | flops 6442450944 | bytes 17825792 | tf_op jit(solution)/shard_map/dot_general | solution.py:472
  146.3 10.3 %shard_map.256 = (bf16[2048,256]{1,0:T(8,128)(2,1)S(1)}, f32[2048,256]{1,0:T(8,128)S(1)}, bf16[2048,256]{1,0:T(8,128)(2,1)S(1)}, bf16[2048,128]{1,0:T(8,128)(2,1)S(1)}, f32[2,2,1024]{2,1,0:T(2,128)S(1)}) custom-call(f32[2048,768]{1,0:T(8,128)S(1)} %fusion.96.joint_ref, f32[2048,128]{1,0:T(8,128)S(1)} %get-tuple-element.289.cos_ref, ...), custom_call_target="tpu_custom_call" | custom-call | flops 2147483648 | bytes 15728640 | tf_op jit(solution)/shard_map/pallas_call | solution.py:683
  159.7 4.7 shard_map.258
  164.5 3.0 convolution_convert_fusion.4
  167.9 3.0 convolution_convert_fusion.5
  178.6 9.4 %collective-permute-done.35 = bf16[256,768]{1,0:T(8,128)(2,1)} collective-permute-done((bf16[256,768]{1,0:T(8,128)(2,1)}, bf16[256,768]{1,0:T(8,128)(2,1)}, u32[]{:S(2)}, u32[]{:S(2)}) %collective-permute-start.35) | collective-permute-done | bytes 393248 | tf_op jit(solution)/shard_map/ppermute | solution.py:322
  188.1 8.0 %collective-permute-done.34 = bf16[256,768]{1,0:T(8,128)(2,1)} collective-permute-done((bf16[256,768]{1,0:T(8,128)(2,1)}, bf16[256,768]{1,0:T(8,128)(2,1)}, u32[]{:S(2)}, u32[]{:S(2)}) %collective-permute-start.34) | collective-permute-done | bytes 393248 | tf_op jit(solution)/shard_map/ppermute | solution.py:322
  196.0 2.5 broadcast_select_fusion.9
  198.5 2.3 add_convert_fusion.8
  202.5 2.3 add_convert_fusion.9
  210.9 11.7 %all-gather.12.cloned.1.call-start = ((), (), s32[]{:S(2)}) async-start(), calls=%async_computation.8 | async-start | bytes 3932160 | tf_op jit(solution)/shard_map/all_gather | solution.py:418
  222.6 9.8 %collective-permute-done.21 = bf16[2,512,512]{2,1,0:T(8,128)(2,1)} collective-permute-done((bf16[2,512,512]{2,1,0:T(8,128)(2,1)}, bf16[2,512,512]{2,1,0:T(8,128)(2,1)}, u32[]{:S(2)}, u32[]{:S(2)}) %collective-permute-start.21) | collective-permute-done | bytes 1048608 | tf_op jit(solution)/shard_map/ppermute | solution.py:322
  239.6 11.9 %fusion.97 = f32[2048,768]{1,0:T(8,128)} fusion(bf16[2048,2048]{1,0:T(8,128)(2,1)} %shard_map.258, bf16[2048,768]{1,0:T(8,128)(2,1)} %all-gather.10.cloned.1.call-done), kind=kOutput, calls=%fused_computation.269 | convolution fusion | flops 6442450944 | bytes 17825792 | tf_op jit(solution)/shard_map/dot_general | solution.py:472
  257.9 20.2 %collective-permute-done.27.refs_2_ = bf16[1024,512]{1,0:T(8,128)(2,1)} collective-permute-done((bf16[1024,512]{1,0:T(8,128)(2,1)}, bf16[1024,512]{1,0:T(8,128)(2,1)}, u32[]{:S(2)}, u32[]{:S(2)}) %collective-permute-start.27) | collective-permute-done | bytes 1048608 | tf_op jit(solution)/shard_map/ppermute | solution.py:322
  284.1 7.4 collective-permute-done.31
  294.1 5.8 shard_map.259
  299.9 5.7 shard_map.260
  305.6 11.7 %fusion.99 = f32[2048,768]{1,0:T(8,128)} fusion(bf16[2048,2048]{1,0:T(8,128)(2,1)} %get-tuple-element.142, bf16[2048,768]{1,0:T(8,128)(2,1)} %all-gather.14.cloned.1.call-done), kind=kOutput, calls=%fused_computation.271 | convolution fusion | flops 6442450944 | bytes 17825792 | tf_op jit(solution)/shard_map/dot_general | solution.py:472
  317.3 20.8 %all-gather.12.cloned.1.call-done = bf16[2048,768]{1,0:T(8,128)(2,1)} async-done(((bf16[512,768]{1,0:T(8,128)(2,1)}), bf16[2048,768]{1,0:T(8,128)(2,1)}) %all-gather.12.cloned.1.call-update) | async-done | bytes 3145744 | tf_op jit(solution)/shard_map/all_gather | solution.py:418
  338.1 10.1 %fusion.98 = f32[2048,768]{1,0:T(8,128)S(1)} fusion(bf16[2048,2048]{1,0:T(8,128)(2,1)} %get-tuple-element.142, bf16[2048,768]{1,0:T(8,128)(2,1)} %all-gather.12.cloned.1.call-done), kind=kOutput, calls=%fused_computation.270 | convolution fusion | flops 6442450944 | bytes 17825792 | tf_op jit(solution)/shard_map/dot_general | solution.py:472
  348.3 7.0 multiply_convert_fusion.5
  356.9 10.4 %convolution_convert_fusion = bf16[2048,768]{1,0:T(8,128)(2,1)} fusion(bf16[2048,2048]{1,0:T(8,128)(2,1)} %shard_map.258, bf16[2048,384]{1,0:T(8,128)(2,1)S(1)} %get-tuple-element.201, bf16[2048,384]{1,0:T(8,128)(2,1)S(1)} %get-tuple-element.198), kind=kOutput, calls=%fused_computation.10 | convolution fusion | flops 6450315264 | bytes 14680064 | tf_op jit(solution)/shard_map/dot_general | solution.py:476
  367.4 11.8 %convolution_convert_fusion.1 = bf16[2048,768]{1,0:T(8,128)(2,1)} fusion(bf16[2048,2048]{1,0:T(8,128)(2,1)} %get-tuple-element.142, bf16[2048,384]{1,0:T(8,128)(2,1)} %get-tuple-element.199, bf16[2048,384]{1,0:T(8,128)(2,1)} %get-tuple-element.200), kind=kOutput, calls=%fused_computation.11 | convolution fusion | flops 6450315264 | bytes 14680064 | tf_op jit(solution)/shard_map/dot_general | solution.py:476
  379.3 4.1 fusion.51
  383.5 3.2 add_convert_fusion.7
  386.8 3.1 fusion.45
  389.9 3.3 add_convert_fusion.5
  393.7 8.7 %convolution_convert_fusion.2 = bf16[2048,768]{1,0:T(8,128)(2,1)} fusion(bf16[2048,2048]{1,0:T(8,128)(2,1)S(1)} %bitcast.152, bf16[2048,384]{1,0:T(8,128)(2,1)S(1)} %copy-done.40, bf16[2048,384]{1,0:T(8,128)(2,1)S(1)} %copy-done.38), kind=kOutput, calls=%fused_computation.12 | convolution fusion | flops 6450315264 | bytes 14680064 | tf_op jit(solution)/shard_map/dot_general | solution.py:476
  402.5 4.2 fusion.48
  406.7 3.2 fusion.54
  410.0 3.7 add_convert_fusion.6
  413.8 4.4 add_convert_fusion.4
  421.6 22.1 %collective-permute-done.38 = bf16[2,512,512]{2,1,0:T(8,128)(2,1)S(1)} collective-permute-done((bf16[2,512,512]{2,1,0:T(8,128)(2,1)S(1)}, bf16[2,512,512]{2,1,0:T(8,128)(2,1)S(1)}, u32[]{:S(2)}, u32[]{:S(2)}) %collective-permute-start.38) | collective-permute-done | bytes 1048608 | tf_op jit(solution)/shard_map/ppermute | solution.py:322
  451.0 8.9 %collective-permute-done.40 = bf16[512,512]{1,0:T(8,128)(2,1)} collective-permute-done((bf16[512,512]{1,0:T(8,128)(2,1)}, bf16[512,512]{1,0:T(8,128)(2,1)}, u32[]{:S(2)}, u32[]{:S(2)}) %collective-permute-start.40) | collective-permute-done | bytes 524320 | tf_op jit(solution)/shard_map/ppermute | solution.py:322
  467.2 3.0 collective-permute-done.43
  470.2 3.9 fusion.86
  475.3 23.7 %collective-permute-done.44.refs_2_ = bf16[1024,512]{1,0:T(8,128)(2,1)} collective-permute-done((bf16[1024,512]{1,0:T(8,128)(2,1)}, bf16[1024,512]{1,0:T(8,128)(2,1)}, u32[]{:S(2)}, u32[]{:S(2)}) %collective-permute-start.44) | collective-permute-done | bytes 1048608 | tf_op jit(solution)/shard_map/ppermute | solution.py:322
  504.1 9.6 %collective-permute-done.47 = bf16[512,512]{1,0:T(8,128)(2,1)S(1)} collective-permute-done((bf16[512,512]{1,0:T(8,128)(2,1)S(1)}, bf16[512,512]{1,0:T(8,128)(2,1)S(1)}, u32[]{:S(2)}, u32[]{:S(2)}) %collective-permute-start.47) | collective-permute-done | bytes 524320 | tf_op jit(solution)/shard_map/ppermute | solution.py:322
  517.6 3.8 pad_maximum_fusion.2
  521.4 4.7 shard_map.261.refs_4_
  531.6 20.0 %reduce-scatter.10.cloned.1.call-done = bf16[512,768]{1,0:T(8,128)(2,1)} async-done(((bf16[2048,768]{1,0:T(8,128)(2,1)}), bf16[512,768]{1,0:T(8,128)(2,1)}) %reduce-scatter.10.cloned.1.call-update) | async-done | bytes 786448 | tf_op jit(solution)/shard_map/reduce_scatter | solution.py:422
  554.9 4.7 shard_map.262
  559.6 6.9 convolution_convert_fusion.10
  566.6 7.4 fusion.100.grad_mixed_ref
  574.1 16.6 %shard_map.263 = (bf16[2048,768]{1,0:T(8,128)(2,1)}, f32[2,128]{1,0:T(2,128)S(1)}) custom-call(f32[2048,768]{1,0:T(8,128)} %copy-done, f32[2048,128]{1,0:T(8,128)S(1)} %get-tuple-element.289.cos_ref, f32[2048,128]{1,0:T(8,128)S(1)} %get-tuple-element.290.sin_ref, s32[2,1,1024]{2,1,0:T(1,128)S(1)} %compare_select_fusion.first_ref, f32[1,128]{1,0:T(1,128)S(1)} %bitcast.146, ...), custom_call_target="tpu_custom_call" | custom-call | flops 5368709120 | bytes 20971520 | tf_op jit(solution)/shard_map/pallas_call | solution.py:710
  591.2 10.3 %convolution_convert_fusion.3 = bf16[2048,768]{1,0:T(8,128)(2,1)} fusion(bf16[2048,2048]{1,0:T(8,128)(2,1)S(1)} %bitcast.150, bf16[2048,768]{1,0:T(8,128)(2,1)} %get-tuple-element.174), kind=kOutput, calls=%fused_computation.13 | convolution fusion | flops 6444023808 | bytes 14680064 | tf_op jit(solution)/shard_map/dot_general | solution.py:476
  602.6 5.2 convolution_convert_fusion.8
  609.7 4.0 convolution_convert_fusion.6
  648.6 8.5 %collective-permute-done.54 = bf16[2,512,512]{2,1,0:T(8,128)(2,1)S(1)} collective-permute-done((bf16[2,512,512]{2,1,0:T(8,128)(2,1)}, bf16[2,512,512]{2,1,0:T(8,128)(2,1)S(1)}, u32[]{:S(2)}, u32[]{:S(2)}) %collective-permute-start.54) | collective-permute-done | bytes 1048608 | tf_op jit(solution)/shard_map/ppermute | solution.py:322
  658.8 21.0 %collective-permute-done.60 = bf16[2,512,512]{2,1,0:T(8,128)(2,1)} collective-permute-done((bf16[2,512,512]{2,1,0:T(8,128)(2,1)}, bf16[2,512,512]{2,1,0:T(8,128)(2,1)}, u32[]{:S(2)}, u32[]{:S(2)}) %collective-permute-start.60) | collective-permute-done | bytes 1048608 | tf_op jit(solution)/shard_map/ppermute | solution.py:322
  689.8 8.3 %collective-permute-done.62 = bf16[512,512]{1,0:T(8,128)(2,1)S(1)} collective-permute-done((bf16[512,512]{1,0:T(8,128)(2,1)S(1)}, bf16[512,512]{1,0:T(8,128)(2,1)S(1)}, u32[]{:S(2)}, u32[]{:S(2)}) %collective-permute-start.62) | collective-permute-done | bytes 524320 | tf_op jit(solution)/shard_map/ppermute | solution.py:322
  702.8 6.1 collective-permute-done.66
  719.8 2.8 fusion.8
  725.4 8.5 %collective-permute-done.76 = bf16[256,768]{1,0:T(8,128)(2,1)S(1)} collective-permute-done((bf16[256,768]{1,0:T(8,128)(2,1)S(1)}, bf16[256,768]{1,0:T(8,128)(2,1)S(1)}, u32[]{:S(2)}, u32[]{:S(2)}) %collective-permute-start.76) | collective-permute-done | bytes 393248 | tf_op jit(solution)/shard_map/ppermute | solution.py:322
  (437 shorter events, 193.8 us)
Async XLA Ops:
  7.2 129.0 %all-gather.6.cloned.1.call-start = ((), (), s32[]{:S(2)}) async-start(), calls=%async_computation.5 | async-start | bytes 3932160 | tf_op jit(solution)/shard_map/all_gather | solution.py:418
  9.5 12.1 %collective-permute-start.8 = (bf16[256,768]{1,0:T(8,128)(2,1)S(1)}, bf16[256,768]{1,0:T(8,128)(2,1)S(1)}, u32[]{:S(2)}, u32[]{:S(2)}) collective-permute-start(bf16[256,768]{1,0:T(8,128)(2,1)S(1)} %pad_maximum_fusion.20), channel_id=1, source_target_pairs={{0,4},{4,0},{1,5},{5,1},{2,6},{6,2},{3,7},{7,3},{8,12},{12,8},{9,1... | collective-permute-start | bytes 1179656 | tf_op jit(solution)/shard_map/ppermute | solution.py:322
  22.7 141.7 %all-gather.8.cloned.1.call-start = ((), (), s32[]{:S(2)}) async-start(), calls=%async_computation.6 | async-start | bytes 1310720 | tf_op jit(solution)/shard_map/all_gather | solution.py:418
  22.8 24.5 %collective-permute-start = (bf16[1024,512]{1,0:T(8,128)(2,1)S(1)}, bf16[1024,512]{1,0:T(8,128)(2,1)}, u32[]{:S(2)}, u32[]{:S(2)}) collective-permute-start(bf16[1024,512]{1,0:T(8,128)(2,1)S(1)} %copy-done.9), channel_id=1, source_target_pairs={{0,2},{2,0},{1,3},{3,1},{4,6},{6,4},{5,7},{7,5},{8,10},{10,8},{9,1... | collective-permute-start | bytes 3145736 | tf_op jit(solution)/shard_map/ppermute | solution.py:322
  24.6 23.9 %collective-permute-start.1 = (bf16[1024,512]{1,0:T(8,128)(2,1)S(1)}, bf16[1024,512]{1,0:T(8,128)(2,1)}, u32[]{:S(2)}, u32[]{:S(2)}) collective-permute-start(bf16[1024,512]{1,0:T(8,128)(2,1)S(1)} %copy-done.9), channel_id=1, source_target_pairs={{0,4},{4,0},{1,5},{5,1},{2,6},{6,2},{3,7},{7,3},{8,12},{12,8},{9,1... | collective-permute-start | bytes 3145736 | tf_op jit(solution)/shard_map/ppermute | solution.py:322
  53.4 17.9 %collective-permute-start.6 = (bf16[1024,512]{1,0:T(8,128)(2,1)S(1)}, bf16[1024,512]{1,0:T(8,128)(2,1)}, u32[]{:S(2)}, u32[]{:S(2)}) collective-permute-start(bf16[1024,512]{1,0:T(8,128)(2,1)S(1)} %copy-done.9), channel_id=1, source_target_pairs={{0,1},{1,0},{2,3},{3,2},{4,5},{5,4},{6,7},{7,6},{8,9},{9,8},{10,11... | collective-permute-start | bytes 3145736 | tf_op jit(solution)/shard_map/ppermute | solution.py:322
  53.5 15.7 %collective-permute-start.9 = (s32[1024]{0:T(1024)S(1)}, s32[1024]{0:T(1024)S(1)}, u32[]{:S(2)}, u32[]{:S(2)}) collective-permute-start(s32[1024]{0:T(1024)S(1)} %copy-done.57), channel_id=1, source_target_pairs={{0,4},{4,0},{1,5},{5,1},{2,6},{6,2},{3,7},{7,3},{8,12},{12,8},{9,1... | collective-permute-start | bytes 12296 | tf_op jit(solution)/shard_map/ppermute | solution.py:322
  56.4 21.6 %collective-permute-start.2 = (bf16[1024,512]{1,0:T(8,128)(2,1)}, bf16[1024,512]{1,0:T(8,128)(2,1)}, u32[]{:S(2)}, u32[]{:S(2)}) collective-permute-start(bf16[1024,512]{1,0:T(8,128)(2,1)} %collective-permute-done.1.refs_0_), channel_id=1, source_target_pairs={{0,1},{1,0},{2,3},{3,2},{4,5},{5,4},{6,7},{7,6},{8,9},{9,8},{10,11... | collective-permute-start | bytes 3145736 | tf_op jit(solution)/shard_map/ppermute | solution.py:322
  69.1 16.3 %collective-permute-start.18 = (bf16[256,256]{1,0:T(8,128)(2,1)}, bf16[256,256]{1,0:T(8,128)(2,1)S(1)}, u32[]{:S(2)}, u32[]{:S(2)}) collective-permute-start(bf16[256,256]{1,0:T(8,128)(2,1)} %constant_dynamic-slice_fusion.15), channel_id=1, source_target_pairs={{0,4},{4,0},{1,5},{5,1},{2,6},{6,2},{3,7},{7,3},{8,12},{12,8},{9,1... | collective-permute-start | bytes 393224 | tf_op jit(solution)/shard_map/ppermute | solution.py:322
  71.3 44.1 %collective-permute-start.25 = (bf16[256,768]{1,0:T(8,128)(2,1)S(1)}, bf16[256,768]{1,0:T(8,128)(2,1)}, u32[]{:S(2)}, u32[]{:S(2)}) collective-permute-start(bf16[256,768]{1,0:T(8,128)(2,1)S(1)} %copy-done.52), channel_id=1, source_target_pairs={{0,4},{4,0},{1,5},{5,1},{2,6},{6,2},{3,7},{7,3},{8,12},{12,8},{9,1... | collective-permute-start | bytes 1179656 | tf_op jit(solution)/shard_map/ppermute | solution.py:322
  83.8 25.1 %collective-permute-start.10 = (bf16[1024,512]{1,0:T(8,128)(2,1)S(1)}, bf16[1024,512]{1,0:T(8,128)(2,1)}, u32[]{:S(2)}, u32[]{:S(2)}) collective-permute-start(bf16[1024,512]{1,0:T(8,128)(2,1)S(1)} %fusion.12.refs_0_), channel_id=1, source_target_pairs={{0,2},{2,0},{1,3},{3,1},{4,6},{6,4},{5,7},{7,5},{8,10},{10,8},{9,1... | collective-permute-start | bytes 3145736 | tf_op jit(solution)/shard_map/ppermute | solution.py:322
  84.4 24.7 %collective-permute-start.11 = (bf16[1024,512]{1,0:T(8,128)(2,1)S(1)}, bf16[1024,512]{1,0:T(8,128)(2,1)S(1)}, u32[]{:S(2)}, u32[]{:S(2)}) collective-permute-start(bf16[1024,512]{1,0:T(8,128)(2,1)S(1)} %fusion.12.refs_0_), channel_id=1, source_target_pairs={{0,4},{4,0},{1,5},{5,1},{2,6},{6,2},{3,7},{7,3},{8,12},{12,8},{9,1... | collective-permute-start | bytes 3145736 | tf_op jit(solution)/shard_map/ppermute | solution.py:322
  86.2 153.3 %all-gather.10.cloned.1.call-start = ((), (), s32[]{:S(2)}) async-start(), calls=%async_computation.7 | async-start | bytes 3932160 | tf_op jit(solution)/shard_map/all_gather | solution.py:418
  90.1 41.3 %collective-permute-start.16 = (bf16[1024,512]{1,0:T(8,128)(2,1)S(1)}, bf16[1024,512]{1,0:T(8,128)(2,1)}, u32[]{:S(2)}, u32[]{:S(2)}) collective-permute-start(bf16[1024,512]{1,0:T(8,128)(2,1)S(1)} %fusion.12.refs_0_), channel_id=1, source_target_pairs={{0,1},{1,0},{2,3},{3,2},{4,5},{5,4},{6,7},{7,6},{8,9},{9,8},{10,11... | collective-permute-start | bytes 3145736 | tf_op jit(solution)/shard_map/ppermute | solution.py:322
  109.1 22.3 %collective-permute-start.17 = (bf16[1024,512]{1,0:T(8,128)(2,1)}, bf16[1024,512]{1,0:T(8,128)(2,1)}, u32[]{:S(2)}, u32[]{:S(2)}) collective-permute-start(bf16[1024,512]{1,0:T(8,128)(2,1)} %collective-permute-done.10.refs_2_), channel_id=1, source_target_pairs={{0,1},{1,0},{2,3},{3,2},{4,5},{5,4},{6,7},{7,6},{8,9},{9,8},{10,11... | collective-permute-start | bytes 3145736 | tf_op jit(solution)/shard_map/ppermute | solution.py:322
  113.4 13.7 %collective-permute-start.13 = (bf16[512,512]{1,0:T(8,128)(2,1)}, bf16[512,512]{1,0:T(8,128)(2,1)}, u32[]{:S(2)}, u32[]{:S(2)}) collective-permute-start(bf16[512,512]{1,0:T(8,128)(2,1)} %slice.284), channel_id=1, source_target_pairs={{0,4},{4,0},{1,5},{5,1},{2,6},{6,2},{3,7},{7,3},{8,12},{12,8},{9,1... | collective-permute-start | bytes 1572872 | tf_op jit(solution)/shard_map/ppermute | solution.py:322
  114.2 13.4 %collective-permute-start.14 = (bf16[512,512]{1,0:T(8,128)(2,1)}, bf16[512,512]{1,0:T(8,128)(2,1)}, u32[]{:S(2)}, u32[]{:S(2)}) collective-permute-start(bf16[512,512]{1,0:T(8,128)(2,1)} %slice.285), channel_id=1, source_target_pairs={{0,2},{2,0},{1,3},{3,1},{4,6},{6,4},{5,7},{7,5},{8,10},{10,8},{9,1... | collective-permute-start | bytes 1572872 | tf_op jit(solution)/shard_map/ppermute | solution.py:322
  117.5 188.1 %all-gather.14.cloned.1.call-start = ((), (), s32[]{:S(2)}) async-start(), calls=%async_computation.9 | async-start | bytes 3932160 | tf_op jit(solution)/shard_map/all_gather | solution.py:418
  117.8 41.9 %collective-permute-start.12 = (bf16[1024,512]{1,0:T(8,128)(2,1)}, bf16[1024,512]{1,0:T(8,128)(2,1)}, u32[]{:S(2)}, u32[]{:S(2)}) collective-permute-start(bf16[1024,512]{1,0:T(8,128)(2,1)} %copy-done.27), channel_id=1, source_target_pairs={{0,1},{1,0},{2,3},{3,2},{4,5},{5,4},{6,7},{7,6},{8,9},{9,8},{10,11... | collective-permute-start | bytes 3145736 | tf_op jit(solution)/shard_map/ppermute | solution.py:322
  131.4 28.4 %collective-permute-start.15 = (bf16[1024,512]{1,0:T(8,128)(2,1)}, bf16[1024,512]{1,0:T(8,128)(2,1)}, u32[]{:S(2)}, u32[]{:S(2)}) collective-permute-start(bf16[1024,512]{1,0:T(8,128)(2,1)} %constant_dynamic-update-slice_fusion.2.refs_2_), channel_id=1, source_target_pairs={{0,1},{1,0},{2,3},{3,2},{4,5},{5,4},{6,7},{7,6},{8,9},{9,8},{10,11... | collective-permute-start | bytes 3145736 | tf_op jit(solution)/shard_map/ppermute | solution.py:322
  167.5 31.1 %collective-permute-start.20 = (bf16[2048,512]{1,0:T(8,128)(2,1)}, bf16[2048,512]{1,0:T(8,128)(2,1)}, u32[]{:S(2)}, u32[]{:S(2)}) collective-permute-start(bf16[2048,512]{1,0:T(8,128)(2,1)} %convolution_convert_fusion.4), channel_id=1, source_target_pairs={{0,1},{1,0},{2,3},{3,2},{4,5},{5,4},{6,7},{7,6},{8,9},{9,8},{10,11... | collective-permute-start | bytes 6291464 | tf_op jit(solution)/shard_map/ppermute | solution.py:322
  171.0 31.6 %collective-permute-start.19 = (bf16[2048,512]{1,0:T(8,128)(2,1)}, bf16[2048,512]{1,0:T(8,128)(2,1)}, u32[]{:S(2)}, u32[]{:S(2)}) collective-permute-start(bf16[2048,512]{1,0:T(8,128)(2,1)} %convolution_convert_fusion.5), channel_id=1, source_target_pairs={{0,1},{1,0},{2,3},{3,2},{4,5},{5,4},{6,7},{7,6},{8,9},{9,8},{10,11... | collective-permute-start | bytes 6291464 | tf_op jit(solution)/shard_map/ppermute | solution.py:322
  175.8 12.2 %collective-permute-start.35 = (bf16[256,768]{1,0:T(8,128)(2,1)}, bf16[256,768]{1,0:T(8,128)(2,1)}, u32[]{:S(2)}, u32[]{:S(2)}) collective-permute-start(bf16[256,768]{1,0:T(8,128)(2,1)} %pad_maximum_fusion.24), channel_id=1, source_target_pairs={{0,4},{4,0},{1,5},{5,1},{2,6},{6,2},{3,7},{7,3},{8,12},{12,8},{9,1... | collective-permute-start | bytes 1179656 | tf_op jit(solution)/shard_map/ppermute | solution.py:322
  177.8 18.2 %collective-permute-start.34 = (bf16[256,768]{1,0:T(8,128)(2,1)}, bf16[256,768]{1,0:T(8,128)(2,1)}, u32[]{:S(2)}, u32[]{:S(2)}) collective-permute-start(bf16[256,768]{1,0:T(8,128)(2,1)} %pad_maximum_fusion.22), channel_id=1, source_target_pairs={{0,4},{4,0},{1,5},{5,1},{2,6},{6,2},{3,7},{7,3},{8,12},{12,8},{9,1... | collective-permute-start | bytes 1179656 | tf_op jit(solution)/shard_map/ppermute | solution.py:322
  207.3 25.1 %collective-permute-start.21 = (bf16[2,512,512]{2,1,0:T(8,128)(2,1)}, bf16[2,512,512]{2,1,0:T(8,128)(2,1)}, u32[]{:S(2)}, u32[]{:S(2)}) collective-permute-start(bf16[2,512,512]{2,1,0:T(8,128)(2,1)} %pad_maximum_fusion.7), channel_id=1, source_target_pairs={{0,4},{4,0},{1,5},{5,1},{2,6},{6,2},{3,7},{7,3},{8,12},{12,8},{9,1... | collective-permute-start | bytes 3145736 | tf_op jit(solution)/shard_map/ppermute | solution.py:322
  208.5 24.8 %collective-permute-start.22 = (bf16[2,512,512]{2,1,0:T(8,128)(2,1)}, bf16[2,512,512]{2,1,0:T(8,128)(2,1)}, u32[]{:S(2)}, u32[]{:S(2)}) collective-permute-start(bf16[2,512,512]{2,1,0:T(8,128)(2,1)} %pad_maximum_fusion.8), channel_id=1, source_target_pairs={{0,2},{2,0},{1,3},{3,1},{4,6},{6,4},{5,7},{7,5},{8,10},{10,8},{9,1... | collective-permute-start | bytes 3145736 | tf_op jit(solution)/shard_map/ppermute | solution.py:322
  210.9 127.2 %all-gather.12.cloned.1.call-start = ((), (), s32[]{:S(2)}) async-start(), calls=%async_computation.8 | async-start | bytes 3932160 | tf_op jit(solution)/shard_map/all_gather | solution.py:418
  237.6 13.9 %collective-permute-start.23 = (bf16[512,512]{1,0:T(8,128)(2,1)}, bf16[512,512]{1,0:T(8,128)(2,1)}, u32[]{:S(2)}, u32[]{:S(2)}) collective-permute-start(bf16[512,512]{1,0:T(8,128)(2,1)} %fusion.28), channel_id=1, source_target_pairs={{0,2},{2,0},{1,3},{3,1},{4,6},{6,4},{5,7},{7,5},{8,10},{10,8},{9,1... | collective-permute-start | bytes 1572872 | tf_op jit(solution)/shard_map/ppermute | solution.py:322
  239.0 12.4 %collective-permute-start.24 = (bf16[512,512]{1,0:T(8,128)(2,1)}, bf16[512,512]{1,0:T(8,128)(2,1)}, u32[]{:S(2)}, u32[]{:S(2)}) collective-permute-start(bf16[512,512]{1,0:T(8,128)(2,1)} %fusion.27), channel_id=1, source_target_pairs={{0,4},{4,0},{1,5},{5,1},{2,6},{6,2},{3,7},{7,3},{8,12},{12,8},{9,1... | collective-permute-start | bytes 1572872 | tf_op jit(solution)/shard_map/ppermute | solution.py:322
  254.8 23.3 %collective-permute-start.27 = (bf16[1024,512]{1,0:T(8,128)(2,1)}, bf16[1024,512]{1,0:T(8,128)(2,1)}, u32[]{:S(2)}, u32[]{:S(2)}) collective-permute-start(bf16[1024,512]{1,0:T(8,128)(2,1)} %fusion.13.refs_0_), channel_id=1, source_target_pairs={{0,2},{2,0},{1,3},{3,1},{4,6},{6,4},{5,7},{7,5},{8,10},{10,8},{9,1... | collective-permute-start | bytes 3145736 | tf_op jit(solution)/shard_map/ppermute | solution.py:322
  255.7 23.0 %collective-permute-start.28 = (bf16[1024,512]{1,0:T(8,128)(2,1)}, bf16[1024,512]{1,0:T(8,128)(2,1)}, u32[]{:S(2)}, u32[]{:S(2)}) collective-permute-start(bf16[1024,512]{1,0:T(8,128)(2,1)} %fusion.13.refs_0_), channel_id=1, source_target_pairs={{0,4},{4,0},{1,5},{5,1},{2,6},{6,2},{3,7},{7,3},{8,12},{12,8},{9,1... | collective-permute-start | bytes 3145736 | tf_op jit(solution)/shard_map/ppermute | solution.py:322
  257.8 268.2 %reduce-scatter.14.cloned.1.call-start = ((), (), s32[]{:S(2)}) async-start(), calls=%async_computation.14 | async-start | bytes 3932160 | tf_op jit(solution)/shard_map/reduce_scatter | solution.py:422
  284.1 15.8 %collective-permute-start.30 = (bf16[1024,512]{1,0:T(8,128)(2,1)}, bf16[1024,512]{1,0:T(8,128)(2,1)}, u32[]{:S(2)}, u32[]{:S(2)}) collective-permute-start(bf16[1024,512]{1,0:T(8,128)(2,1)} %collective-permute-done.28.refs_0_), channel_id=1, source_target_pairs={{0,1},{1,0},{2,3},{3,2},{4,5},{5,4},{6,7},{7,6},{8,9},{9,8},{10,11... | collective-permute-start | bytes 3145736 | tf_op jit(solution)/shard_map/ppermute | solution.py:322
  367.4 161.9 %reduce-scatter.12.cloned.1.call-start = ((), (), s32[]{:S(2)}) async-start(), calls=%async_computation.13 | async-start | bytes 3932160 | tf_op jit(solution)/shard_map/reduce_scatter | solution.py:422
  379.2 172.4 %reduce-scatter.10.cloned.1.call-start = ((), (), s32[]{:S(2)}) async-start(), calls=%async_computation.12 | async-start | bytes 3932160 | tf_op jit(solution)/shard_map/reduce_scatter | solution.py:422
  386.7 23.2 %collective-permute-start.36 = (bf16[2048,512]{1,0:T(8,128)(2,1)}, bf16[2048,512]{1,0:T(8,128)(2,1)}, u32[]{:S(2)}, u32[]{:S(2)}) collective-permute-start(bf16[2048,512]{1,0:T(8,128)(2,1)} %add_convert_fusion.7), channel_id=1, source_target_pairs={{0,1},{1,0},{2,3},{3,2},{4,5},{5,4},{6,7},{7,6},{8,9},{9,8},{10,11... | collective-permute-start | bytes 6291464 | tf_op jit(solution)/shard_map/ppermute | solution.py:322
  393.2 20.5 %collective-permute-start.37 = (bf16[2048,512]{1,0:T(8,128)(2,1)}, bf16[2048,512]{1,0:T(8,128)(2,1)}, u32[]{:S(2)}, u32[]{:S(2)}) collective-permute-start(bf16[2048,512]{1,0:T(8,128)(2,1)} %add_convert_fusion.5), channel_id=1, source_target_pairs={{0,1},{1,0},{2,3},{3,2},{4,5},{5,4},{6,7},{7,6},{8,9},{9,8},{10,11... | collective-permute-start | bytes 6291464 | tf_op jit(solution)/shard_map/ppermute | solution.py:322
  402.4 243.7 %reduce-scatter.8.cloned.1.call-start = ((), (), s32[]{:S(2)}) async-start(), calls=%async_computation.11 | async-start | bytes 1310720 | tf_op jit(solution)/shard_map/reduce_scatter | solution.py:422
  418.5 25.2 %collective-permute-start.38 = (bf16[2,512,512]{2,1,0:T(8,128)(2,1)S(1)}, bf16[2,512,512]{2,1,0:T(8,128)(2,1)S(1)}, u32[]{:S(2)}, u32[]{:S(2)}) collective-permute-start(bf16[2,512,512]{2,1,0:T(8,128)(2,1)S(1)} %pad_maximum_fusion.9), channel_id=1, source_target_pairs={{0,4},{4,0},{1,5},{5,1},{2,6},{6,2},{3,7},{7,3},{8,12},{12,8},{9,1... | collective-permute-start | bytes 3145736 | tf_op jit(solution)/shard_map/ppermute | solution.py:322
  420.1 24.8 %collective-permute-start.39 = (bf16[2,512,512]{2,1,0:T(8,128)(2,1)S(1)}, bf16[2,512,512]{2,1,0:T(8,128)(2,1)S(1)}, u32[]{:S(2)}, u32[]{:S(2)}) collective-permute-start(bf16[2,512,512]{2,1,0:T(8,128)(2,1)S(1)} %pad_maximum_fusion.10), channel_id=1, source_target_pairs={{0,2},{2,0},{1,3},{3,1},{4,6},{6,4},{5,7},{7,5},{8,10},{10,8},{9,1... | collective-permute-start | bytes 3145736 | tf_op jit(solution)/shard_map/ppermute | solution.py:322
  446.9 13.1 %collective-permute-start.40 = (bf16[512,512]{1,0:T(8,128)(2,1)}, bf16[512,512]{1,0:T(8,128)(2,1)}, u32[]{:S(2)}, u32[]{:S(2)}) collective-permute-start(bf16[512,512]{1,0:T(8,128)(2,1)} %fusion.24), channel_id=1, source_target_pairs={{0,2},{2,0},{1,3},{3,1},{4,6},{6,4},{5,7},{7,5},{8,10},{10,8},{9,1... | collective-permute-start | bytes 1572872 | tf_op jit(solution)/shard_map/ppermute | solution.py:322
  448.4 12.8 %collective-permute-start.41 = (bf16[512,512]{1,0:T(8,128)(2,1)}, bf16[512,512]{1,0:T(8,128)(2,1)}, u32[]{:S(2)}, u32[]{:S(2)}) collective-permute-start(bf16[512,512]{1,0:T(8,128)(2,1)} %fusion.23), channel_id=1, source_target_pairs={{0,4},{4,0},{1,5},{5,1},{2,6},{6,2},{3,7},{7,3},{8,12},{12,8},{9,1... | collective-permute-start | bytes 1572872 | tf_op jit(solution)/shard_map/ppermute | solution.py:322
  474.1 24.8 %collective-permute-start.44 = (bf16[1024,512]{1,0:T(8,128)(2,1)}, bf16[1024,512]{1,0:T(8,128)(2,1)}, u32[]{:S(2)}, u32[]{:S(2)}) collective-permute-start(bf16[1024,512]{1,0:T(8,128)(2,1)} %get-tuple-element.152.refs_0_), channel_id=1, source_target_pairs={{0,2},{2,0},{1,3},{3,1},{4,6},{6,4},{5,7},{7,5},{8,10},{10,8},{9,1... | collective-permute-start | bytes 3145736 | tf_op jit(solution)/shard_map/ppermute | solution.py:322
  474.7 24.5 %collective-permute-start.45 = (bf16[1024,512]{1,0:T(8,128)(2,1)}, bf16[1024,512]{1,0:T(8,128)(2,1)}, u32[]{:S(2)}, u32[]{:S(2)}) collective-permute-start(bf16[1024,512]{1,0:T(8,128)(2,1)} %get-tuple-element.152.refs_0_), channel_id=1, source_target_pairs={{0,4},{4,0},{1,5},{5,1},{2,6},{6,2},{3,7},{7,3},{8,12},{12,8},{9,1... | collective-permute-start | bytes 3145736 | tf_op jit(solution)/shard_map/ppermute | solution.py:322
  501.4 12.2 %collective-permute-start.47 = (bf16[512,512]{1,0:T(8,128)(2,1)S(1)}, bf16[512,512]{1,0:T(8,128)(2,1)S(1)}, u32[]{:S(2)}, u32[]{:S(2)}) collective-permute-start(bf16[512,512]{1,0:T(8,128)(2,1)S(1)} %slice.326), channel_id=1, source_target_pairs={{0,4},{4,0},{1,5},{5,1},{2,6},{6,2},{3,7},{7,3},{8,12},{12,8},{9,1... | collective-permute-start | bytes 1572872 | tf_op jit(solution)/shard_map/ppermute | solution.py:322
  503.6 17.9 %collective-permute-start.50 = (bf16[1024,512]{1,0:T(8,128)(2,1)}, bf16[1024,512]{1,0:T(8,128)(2,1)}, u32[]{:S(2)}, u32[]{:S(2)}) collective-permute-start(bf16[1024,512]{1,0:T(8,128)(2,1)} %get-tuple-element.152.refs_0_), channel_id=1, source_target_pairs={{0,1},{1,0},{2,3},{3,2},{4,5},{5,4},{6,7},{7,6},{8,9},{9,8},{10,11... | collective-permute-start | bytes 3145736 | tf_op jit(solution)/shard_map/ppermute | solution.py:322
  503.6 17.9 %collective-permute-start.51 = (bf16[1024,512]{1,0:T(8,128)(2,1)}, bf16[1024,512]{1,0:T(8,128)(2,1)}, u32[]{:S(2)}, u32[]{:S(2)}) collective-permute-start(bf16[1024,512]{1,0:T(8,128)(2,1)} %collective-permute-done.44.refs_2_), channel_id=1, source_target_pairs={{0,1},{1,0},{2,3},{3,2},{4,5},{5,4},{6,7},{7,6},{8,9},{9,8},{10,11... | collective-permute-start | bytes 3145736 | tf_op jit(solution)/shard_map/ppermute | solution.py:322
  504.1 50.8 %collective-permute-start.46 = (bf16[1024,512]{1,0:T(8,128)(2,1)}, bf16[1024,512]{1,0:T(8,128)(2,1)}, u32[]{:S(2)}, u32[]{:S(2)}) collective-permute-start(bf16[1024,512]{1,0:T(8,128)(2,1)} %collective-permute-done.45.refs_0_), channel_id=1, source_target_pairs={{0,1},{1,0},{2,3},{3,2},{4,5},{5,4},{6,7},{7,6},{8,9},{9,8},{10,11... | collective-permute-start | bytes 3145736 | tf_op jit(solution)/shard_map/ppermute | solution.py:322
  515.6 39.3 %collective-permute-start.49 = (bf16[1024,512]{1,0:T(8,128)(2,1)}, bf16[1024,512]{1,0:T(8,128)(2,1)}, u32[]{:S(2)}, u32[]{:S(2)}) collective-permute-start(bf16[1024,512]{1,0:T(8,128)(2,1)} %constant_dynamic-update-slice_fusion.6.refs_2_), channel_id=1, source_target_pairs={{0,1},{1,0},{2,3},{3,2},{4,5},{5,4},{6,7},{7,6},{8,9},{9,8},{10,11... | collective-permute-start | bytes 3145736 | tf_op jit(solution)/shard_map/ppermute | solution.py:322
  527.8 94.2 %collective-permute-start.80 = (bf16[256,768]{1,0:T(8,128)(2,1)}, bf16[256,768]{1,0:T(8,128)(2,1)}, u32[]{:S(2)}, u32[]{:S(2)}) collective-permute-start(bf16[256,768]{1,0:T(8,128)(2,1)} %constant_dynamic-slice_fusion.4), channel_id=1, source_target_pairs={{0,4},{4,0},{1,5},{5,1},{2,6},{6,2},{3,7},{7,3},{8,12},{12,8},{9,1... | collective-permute-start | bytes 1179656 | tf_op jit(solution)/shard_map/ppermute | solution.py:322
  531.0 89.3 %collective-permute-start.79 = (bf16[256,768]{1,0:T(8,128)(2,1)}, bf16[256,768]{1,0:T(8,128)(2,1)}, u32[]{:S(2)}, u32[]{:S(2)}) collective-permute-start(bf16[256,768]{1,0:T(8,128)(2,1)} %constant_dynamic-slice_fusion.5), channel_id=1, source_target_pairs={{0,4},{4,0},{1,5},{5,1},{2,6},{6,2},{3,7},{7,3},{8,12},{12,8},{9,1... | collective-permute-start | bytes 1179656 | tf_op jit(solution)/shard_map/ppermute | solution.py:322
  553.4 69.9 %collective-permute-start.78 = (bf16[256,768]{1,0:T(8,128)(2,1)}, bf16[256,768]{1,0:T(8,128)(2,1)}, u32[]{:S(2)}, u32[]{:S(2)}) collective-permute-start(bf16[256,768]{1,0:T(8,128)(2,1)} %constant_dynamic-slice_fusion.6), channel_id=1, source_target_pairs={{0,4},{4,0},{1,5},{5,1},{2,6},{6,2},{3,7},{7,3},{8,12},{12,8},{9,1... | collective-permute-start | bytes 1179656 | tf_op jit(solution)/shard_map/ppermute | solution.py:322
  566.5 156.5 %reduce-scatter.6.cloned.1.call-start = ((), (), s32[]{:S(2)}) async-start(), calls=%async_computation.10 | async-start | bytes 3932160 | tf_op jit(solution)/shard_map/reduce_scatter | solution.py:422
  607.9 16.7 %collective-permute-start.53 = (bf16[2048,512]{1,0:T(8,128)(2,1)}, bf16[2048,512]{1,0:T(8,128)(2,1)S(1)}, u32[]{:S(2)}, u32[]{:S(2)}) collective-permute-start(bf16[2048,512]{1,0:T(8,128)(2,1)} %convolution_convert_fusion.8), channel_id=1, source_target_pairs={{0,1},{1,0},{2,3},{3,2},{4,5},{5,4},{6,7},{7,6},{8,9},{9,8},{10,11... | collective-permute-start | bytes 6291464 | tf_op jit(solution)/shard_map/ppermute | solution.py:322
  620.3 17.5 %collective-permute-start.58 = (bf16[2048,512]{1,0:T(8,128)(2,1)S(1)}, bf16[2048,512]{1,0:T(8,128)(2,1)S(1)}, u32[]{:S(2)}, u32[]{:S(2)}) collective-permute-start(bf16[2048,512]{1,0:T(8,128)(2,1)S(1)} %convolution_convert_fusion.7), channel_id=1, source_target_pairs={{0,1},{1,0},{2,3},{3,2},{4,5},{5,4},{6,7},{7,6},{8,9},{9,8},{10,11... | collective-permute-start | bytes 6291464 | tf_op jit(solution)/shard_map/ppermute | solution.py:322
  631.0 26.2 %collective-permute-start.54 = (bf16[2,512,512]{2,1,0:T(8,128)(2,1)}, bf16[2,512,512]{2,1,0:T(8,128)(2,1)S(1)}, u32[]{:S(2)}, u32[]{:S(2)}) collective-permute-start(bf16[2,512,512]{2,1,0:T(8,128)(2,1)} %pad_maximum_fusion.11), channel_id=1, source_target_pairs={{0,4},{4,0},{1,5},{5,1},{2,6},{6,2},{3,7},{7,3},{8,12},{12,8},{9,1... | collective-permute-start | bytes 3145736 | tf_op jit(solution)/shard_map/ppermute | solution.py:322
  632.5 26.3 %collective-permute-start.55 = (bf16[2,512,512]{2,1,0:T(8,128)(2,1)}, bf16[2,512,512]{2,1,0:T(8,128)(2,1)}, u32[]{:S(2)}, u32[]{:S(2)}) collective-permute-start(bf16[2,512,512]{2,1,0:T(8,128)(2,1)} %pad_maximum_fusion.12), channel_id=1, source_target_pairs={{0,2},{2,0},{1,3},{3,1},{4,6},{6,4},{5,7},{7,5},{8,10},{10,8},{9,1... | collective-permute-start | bytes 3145736 | tf_op jit(solution)/shard_map/ppermute | solution.py:322
  641.0 38.7 %collective-permute-start.60 = (bf16[2,512,512]{2,1,0:T(8,128)(2,1)}, bf16[2,512,512]{2,1,0:T(8,128)(2,1)}, u32[]{:S(2)}, u32[]{:S(2)}) collective-permute-start(bf16[2,512,512]{2,1,0:T(8,128)(2,1)} %pad_maximum_fusion.13), channel_id=1, source_target_pairs={{0,4},{4,0},{1,5},{5,1},{2,6},{6,2},{3,7},{7,3},{8,12},{12,8},{9,1... | collective-permute-start | bytes 3145736 | tf_op jit(solution)/shard_map/ppermute | solution.py:322
  641.6 38.9 %collective-permute-start.61 = (bf16[2,512,512]{2,1,0:T(8,128)(2,1)}, bf16[2,512,512]{2,1,0:T(8,128)(2,1)}, u32[]{:S(2)}, u32[]{:S(2)}) collective-permute-start(bf16[2,512,512]{2,1,0:T(8,128)(2,1)} %pad_maximum_fusion.14), channel_id=1, source_target_pairs={{0,2},{2,0},{1,3},{3,1},{4,6},{6,4},{5,7},{7,5},{8,10},{10,8},{9,1... | collective-permute-start | bytes 3145736 | tf_op jit(solution)/shard_map/ppermute | solution.py:322
  647.1 55.7 %collective-permute-start.77 = (bf16[256,256]{1,0:T(8,128)(2,1)S(1)}, bf16[256,256]{1,0:T(8,128)(2,1)S(1)}, u32[]{:S(2)}, u32[]{:S(2)}) collective-permute-start(bf16[256,256]{1,0:T(8,128)(2,1)S(1)} %constant_dynamic-slice_fusion.7), channel_id=1, source_target_pairs={{0,4},{4,0},{1,5},{5,1},{2,6},{6,2},{3,7},{7,3},{8,12},{12,8},{9,1... | collective-permute-start | bytes 393224 | tf_op jit(solution)/shard_map/ppermute | solution.py:322
  683.2 14.9 %collective-permute-start.62 = (bf16[512,512]{1,0:T(8,128)(2,1)S(1)}, bf16[512,512]{1,0:T(8,128)(2,1)S(1)}, u32[]{:S(2)}, u32[]{:S(2)}) collective-permute-start(bf16[512,512]{1,0:T(8,128)(2,1)S(1)} %fusion.16), channel_id=1, source_target_pairs={{0,2},{2,0},{1,3},{3,1},{4,6},{6,4},{5,7},{7,5},{8,10},{10,8},{9,1... | collective-permute-start | bytes 1572872 | tf_op jit(solution)/shard_map/ppermute | solution.py:322
  684.7 14.9 %collective-permute-start.63 = (bf16[512,512]{1,0:T(8,128)(2,1)S(1)}, bf16[512,512]{1,0:T(8,128)(2,1)S(1)}, u32[]{:S(2)}, u32[]{:S(2)}) collective-permute-start(bf16[512,512]{1,0:T(8,128)(2,1)S(1)} %fusion.15), channel_id=1, source_target_pairs={{0,4},{4,0},{1,5},{5,1},{2,6},{6,2},{3,7},{7,3},{8,12},{12,8},{9,1... | collective-permute-start | bytes 1572872 | tf_op jit(solution)/shard_map/ppermute | solution.py:322
  687.9 23.4 %collective-permute-start.56 = (bf16[512,512]{1,0:T(8,128)(2,1)S(1)}, bf16[512,512]{1,0:T(8,128)(2,1)S(1)}, u32[]{:S(2)}, u32[]{:S(2)}) collective-permute-start(bf16[512,512]{1,0:T(8,128)(2,1)S(1)} %fusion.20), channel_id=1, source_target_pairs={{0,2},{2,0},{1,3},{3,1},{4,6},{6,4},{5,7},{7,5},{8,10},{10,8},{9,1... | collective-permute-start | bytes 1572872 | tf_op jit(solution)/shard_map/ppermute | solution.py:322
  688.5 22.8 %collective-permute-start.57 = (bf16[512,512]{1,0:T(8,128)(2,1)S(1)}, bf16[512,512]{1,0:T(8,128)(2,1)S(1)}, u32[]{:S(2)}, u32[]{:S(2)}) collective-permute-start(bf16[512,512]{1,0:T(8,128)(2,1)S(1)} %fusion.19), channel_id=1, source_target_pairs={{0,4},{4,0},{1,5},{5,1},{2,6},{6,2},{3,7},{7,3},{8,12},{12,8},{9,1... | collective-permute-start | bytes 1572872 | tf_op jit(solution)/shard_map/ppermute | solution.py:322
  (95 other events, 852.7 us)
Sparse Core Ops, SparseCore 0:
  22.9 64.9 all-gather.5
  90.0 26.5 all-gather.7
  118.2 63.1 all-gather.9
  211.0 62.8 all-gather.13
  276.0 62.1 all-gather.11
  367.5 58.8 reduce-scatter.13
  428.7 60.2 reduce-scatter.11
  491.3 60.2 reduce-scatter.9
  566.6 26.2 reduce-scatter.7
  608.0 60.9 reduce-scatter.5

commit v3 on v2

--- a/solution.py
+++ b/solution.py
@@ -322,20 +322,22 @@
     return lax.ppermute(values, axis, [(0, 1), (1, 0)])
 
 
-def flip_both(first, first_axis, second, second_axis):
-    first, second = tie(first, second)
-    return tie(flip(first, first_axis), flip(second, second_axis))
-
-
-def spread(own):
-    half = own.shape[0] // 2
-    via_y, via_x = flip_both(own, "y", own, "x")
-    first, second = flip_both(via_y[:half], "x", via_x[half:], "y")
-    held = ((own, via_y), (via_x, jnp.concatenate([first, second], axis=0)))
-    return tuple(
-        tuple(block for values in pair for block in (values, flip(values, "core")))
-        for pair in held
-    )
+light = pl.CostEstimate(flops=0, bytes_accessed=0, transcendentals=0)
+
+
+class Line:
+    def __init__(self):
+        self.token = jnp.zeros((8, 128), jnp.float32)
+
+    def enter(self, *values):
+        *values, self.token = lax.optimization_barrier((*values, self.token))
+        return values
+
+    def run(self, work, *values):
+        result = work(*self.enter(*values))
+        if isinstance(result, (tuple, list)):
+            return self.enter(*result)
+        return self.enter(result)[0]
 
 
 def pack_kernel(normed, place_ref, gain_ref, *refs):
@@ -382,100 +384,212 @@
         out_specs=out_specs,
         out_shape=out_shape,
         input_output_aliases=aliases,
-        cost_estimate=pl.CostEstimate(
-            flops=0, bytes_accessed=count * width * 16, transcendentals=0
-        ),
+        cost_estimate=light,
     )(place.reshape(1), gain.reshape(1, -1), *blocks, target)
 
 
-def gather_normed(own, place, gain):
-    first, second = spread(own)
-    target, inverse = pack(first, place, gain, True, 0, None)
-    normed, unused = pack(second, place, gain, True, 1, target)
-    return (normed, inverse)
-
-
-def gather_plain(own, place, gain):
-    first, second = spread(own)
-    target = pack(first, place, gain, False, 0, None)[0]
-    return pack(second, place, gain, False, 1, target)[0]
+def direct(own):
+    return (flip(own, "y"), flip(own, "x"), flip(own, "core"))
+
+
+def relay(own, via_y, via_x, own_core, place, gain, normed):
+    half = own.shape[0] // 2
+    upper = flip(via_y[:half], "x")
+    lower = flip(via_x[half:], "y")
+    x_core = flip(via_x, "core")
+    near = pack((own, own_core, via_y, flip(via_y, "core")), place, gain, normed, 0, None)
+    return (via_x, x_core, upper, lower, *near)
+
+
+def diagonal(via_x, x_core, upper, lower, target, place, gain, normed):
+    crossed = jnp.concatenate([upper, lower], axis=0)
+    far = (via_x, x_core, crossed, flip(crossed, "core"))
+    return pack(far, place, gain, normed, 1, target)[0]
+
+
+def halves_kernel(count, across_ref, *refs):
+    across = across_ref[0]
+    keep_ref, give_ref = refs[count:]
+    at = 0
+    for weight_ref in refs[:count]:
+        width = weight_ref.shape[1] // 2
+        for target, side in ((keep_ref, across), (give_ref, 1 - across)):
+            target[:, at : at + width] = weight_ref[:, pl.ds(pl.multiple_of(side * width, width), width)]
+        at += width
 
 
 def halves(weights, across):
-    keep, give = [], []
-    for weight in weights:
-        width = weight.shape[1] // 2
-        keep.append(lax.dynamic_slice_in_dim(weight, across * width, width, 1))
-        give.append(lax.dynamic_slice_in_dim(weight, (1 - across) * width, width, 1))
-    return (keep, give)
-
-
-def weight_gather(keep, give, across):
-    keep = jnp.concatenate(keep, axis=1)
-    got = flip(jnp.concatenate(give, axis=1), "x")
+    rows = weights[0].shape[0]
+    width = sum(weight.shape[1] for weight in weights) // 2
+    shape = jax.ShapeDtypeStruct((rows, width), jnp.bfloat16)
+    whole = pl.BlockSpec(memory_space=pltpu.VMEM)
+    return pl.pallas_call(
+        partial(halves_kernel, len(weights)),
+        in_specs=[pl.BlockSpec(memory_space=pltpu.SMEM)] + [whole] * len(weights),
+        out_specs=[whole, whole],
+        out_shape=[shape, shape],
+        cost_estimate=light,
+    )(across.reshape(1), *weights)
+
+
+def weight_rows(keep, got, across):
     top = jnp.where(across == 0, keep, got)
     bottom = jnp.where(across == 0, got, keep)
-    return lax.all_gather(jnp.concatenate([top, bottom], axis=0), "z", axis=0, tiled=True)
-
-
-def grad_scatter(grads, across):
-    summed = lax.psum_scatter(grads, "z", scatter_dimension=0, tiled=True)
+    return jnp.concatenate([top, bottom], axis=0)
+
+
+def weight_gather(rows):
+    return lax.all_gather(rows, "z", axis=0, tiled=True)
+
+
+def grad_scatter(grads):
+    return lax.psum_scatter(grads, "z", scatter_dimension=0, tiled=True)
+
+
+def keep_rows(summed, across):
     rows = summed.shape[0] // 2
-    keep = lax.dynamic_slice_in_dim(summed, across * rows, rows, 0)
-    got = flip(lax.dynamic_slice_in_dim(summed, (1 - across) * rows, rows, 0), "x")
-    return (jnp.where(across == 0, keep, got), jnp.where(across == 0, got, keep))
-
-
-def feature_fold(pairs, place):
-    def product(index):
-        total = None
-        for operand, weight in pairs:
-            rows = weight.shape[0] // 4
-            block = lax.dynamic_slice_in_dim(weight, (place ^ index) * rows, rows, 0)
-            term = lax.dot_general(
-                operand, block, (((1,), (1,)), ((), ())), preferred_element_type=jnp.float32
-            )
-            total = term if total is None else total + term
-        return total
-
+    return lax.dynamic_slice_in_dim(summed, across * rows, rows, 0)
+
+
+def give_rows(summed, across):
+    return keep_rows(summed, 1 - across)
+
+
+def z_flip(values, step):
+    return lax.ppermute(values, "z", [(i, i ^ step) for i in range(4)])
+
+
+vmem = pltpu.CompilerParams(vmem_limit_bytes=56 * 1024 * 1024)
+
+
+def fold_dot(operand, weight, place, index, column):
+    rows, width = weight.shape[0] // 4, operand.shape[1]
+    block = lax.dynamic_slice(
+        weight, ((place ^ index) * rows, jnp.int32(column * width)), (rows, width)
+    )
+    return product_nt(operand, block)
+
+
+def fold_sent(operand, weight, place, column=0):
+    return tuple(
+        flip(fold_dot(operand, weight, place, index, column).astype(jnp.bfloat16), "core")
+        for index in (3, 1)
+    )
+
+
+def fold_held(operand, weight, place, far_got, near_got, column=0):
     low = jnp.bfloat16
-    sent = [flip(product(index).astype(low), "core") for index in (3, 1)]
-    far = (product(2) + sent[0]).astype(low)
-    near = (product(0) + sent[1]).astype(low)
+    far = (fold_dot(operand, weight, place, 2, column) + far_got).astype(low)
+    near = (fold_dot(operand, weight, place, 0, column) + near_got).astype(low)
     count = far.shape[0] // 2
     half = count // 2
-    upper, lower = flip_both(
-        jnp.stack([near[count : count + half], far[count : count + half]]),
-        "x",
-        jnp.stack([far[half:count], far[count + half :]]),
-        "y",
-    )
-    upper_near = near[:half].astype(jnp.float32) + upper[0]
-    upper_far = (far[:half].astype(jnp.float32) + upper[1]).astype(low)
-    lower_own = near[half:count].astype(jnp.float32) + lower[0]
-    lower_other = (near[count + half :].astype(jnp.float32) + lower[1]).astype(low)
-    upper_got, lower_got = flip_both(upper_far, "y", lower_other, "x")
+    upper = jnp.stack([near[count : count + half], far[count : count + half]])
+    lower = jnp.stack([far[half:count], far[count + half :]])
+    return (near, far, upper, lower)
+
+
+def fold_begin(operand, weight, place, column=0):
+    return fold_held(operand, weight, place, *fold_sent(operand, weight, place, column), column)
+
+
+def fold_cross(near, far, upper, lower):
+    return (near, far, flip(upper, "x"), flip(lower, "y"))
+
+
+def fold_close(near, far, upper, lower):
+    low, wide = jnp.bfloat16, jnp.float32
+    count = far.shape[0] // 2
+    half = count // 2
+    upper_near = near[:half].astype(wide) + upper[0]
+    upper_far = (far[:half].astype(wide) + upper[1]).astype(low)
+    lower_own = near[half:count].astype(wide) + lower[0]
+    lower_other = (near[count + half :].astype(wide) + lower[1]).astype(low)
+    return (upper_near, flip(upper_far, "y"), lower_own, flip(lower_other, "x"))
+
+
+def fold_end(upper_near, upper_got, lower_own, lower_got):
     return jnp.concatenate([upper_near + upper_got, lower_own + lower_got], axis=0)
 
 
-def norm_back_own(grad_own, values_own, inverse, gain_own, width):
-    unit = values_own * inverse
-    scaled = grad_own * gain_own
-    dots = jnp.sum(scaled * unit, axis=1, keepdims=True)
-    dots = dots + flip(dots, "core")
-    dots = dots + flip(dots, "y")
-    grad_input = inverse * (scaled - unit * (dots / width))
-    return (grad_input, jnp.sum(grad_own * unit, axis=0))
-
-
-def dot_in(operand, weight):
-    return jnp.dot(operand, weight, preferred_element_type=jnp.float32)
-
-
-def dot_grad(first, second):
-    return lax.dot_general(
-        first, second, (((0,), (0,)), ((), ())), preferred_element_type=jnp.float32
-    ).astype(jnp.bfloat16)
+def matmul_kernel(form, operand_ref, weight_ref, out_ref):
+    out_ref[...] = form(operand_ref[...], weight_ref[...]).astype(out_ref.dtype)
+
+
+def dot_in(operand, weight, width, column=0):
+    count, depth = operand.shape
+    tile = 512
+    return pl.pallas_call(
+        partial(matmul_kernel, product_nn),
+        grid=(count // tile,),
+        in_specs=[
+            pl.BlockSpec((tile, depth), lambda i: (i, 0)),
+            pl.BlockSpec((depth, width), lambda i: (0, column)),
+        ],
+        out_specs=pl.BlockSpec((tile, width), lambda i: (i, 0)),
+        out_shape=jax.ShapeDtypeStruct((count, width), jnp.float32),
+        compiler_params=vmem,
+        cost_estimate=light,
+    )(operand, weight)
+
+
+def dot_grad(first, second, width=None, column=0):
+    count, rows = first.shape
+    width = second.shape[1] if width is None else width
+    tile = 512
+    return pl.pallas_call(
+        partial(matmul_kernel, product_tn),
+        grid=(rows // tile,),
+        in_specs=[
+            pl.BlockSpec((count, tile), lambda i: (0, i)),
+            pl.BlockSpec((count, width), lambda i: (0, column)),
+        ],
+        out_specs=pl.BlockSpec((tile, width), lambda i: (i, 0)),
+        out_shape=jax.ShapeDtypeStruct((rows, width), jnp.bfloat16),
+        compiler_params=vmem,
+        cost_estimate=light,
+    )(first, second)
+
+
+def ffn_kernel(hidden_ref, weight_ref, grad_ref, activated_ref, pair_ref):
+    width = activated_ref.shape[1]
+    low = jnp.bfloat16
+    step = 256
+    for at in range(0, width, step):
+        ff_gate = product_nn(hidden_ref[...], weight_ref[:, at : at + step])
+        ff_up = product_nn(hidden_ref[...], weight_ref[:, width + at : width + at + step])
+        grad = grad_ref[:, at : at + step]
+        sig_gate = jax.nn.sigmoid(ff_gate)
+        passed = ff_gate * sig_gate
+        activated_ref[:, at : at + step] = (passed * ff_up).astype(low)
+        pair_ref[:, width + at : width + at + step] = (grad * passed).astype(low)
+        pair_ref[:, at : at + step] = (
+            grad * ff_up * sig_gate * (1.0 + ff_gate * (1.0 - sig_gate))
+        ).astype(low)
+
+
+def ffn(hidden, weight, grad):
+    count, depth = hidden.shape
+    width = weight.shape[1] // 2
+    tile = 256
+    return pl.pallas_call(
+        ffn_kernel,
+        grid=(count // tile,),
+        in_specs=[
+            pl.BlockSpec((tile, depth), lambda i: (i, 0)),
+            pl.BlockSpec((depth, 2 * width), lambda i: (0, 0)),
+            pl.BlockSpec((tile, width), lambda i: (i, 0)),
+        ],
+        out_specs=[
+            pl.BlockSpec((tile, width), lambda i: (i, 0)),
+            pl.BlockSpec((tile, 2 * width), lambda i: (i, 0)),
+        ],
+        out_shape=[
+            jax.ShapeDtypeStruct((count, width), jnp.bfloat16),
+            jax.ShapeDtypeStruct((count, 2 * width), jnp.bfloat16),
+        ],
+        compiler_params=vmem,
+        cost_estimate=light,
+    )(hidden, weight, grad)
 
 
 def row_tables(segments, head_dim):
@@ -693,11 +807,7 @@
             shape((total // count, heads, count), jnp.float32),
         ],
         compiler_params=pltpu.CompilerParams(vmem_limit_bytes=40 * 1024 * 1024),
-        cost_estimate=pl.CostEstimate(
-            flops=4 * total * count * heads * head_dim,
-            bytes_accessed=total * head_dim * 60,
-            transcendentals=total * count * heads,
-        ),
+        cost_estimate=light,
     )(joint, cosine, sine, first, gain_query.reshape(1, -1), gain_key.reshape(1, -1))
 
 
@@ -718,22 +828,11 @@
             pltpu.VMEM((count, head_dim), jnp.float32),
         ],
         compiler_params=pltpu.CompilerParams(vmem_limit_bytes=48 * 1024 * 1024),
-        cost_estimate=pl.CostEstimate(
-            flops=10 * total * count * heads * head_dim,
-            bytes_accessed=total * head_dim * 80,
-            transcendentals=total * count * heads,
-        ),
+        cost_estimate=light,
     )(
         joint, cosine, sine, first, gain_query.reshape(1, -1), gain_key.reshape(1, -1),
         *kept_values, grad_mixed,
     )
-
-
-def sum_all(values):
-    values = values + flip(values, "x")
-    for step in (1, 2):
-        values = values + lax.ppermute(values, "z", [(i, i ^ step) for i in range(4)])
-    return values
 
 
 def fast_body(
@@ -763,103 +862,258 @@
     key_width = w_key.shape[1] // 2
     heads = query_width // head_dim
     hidden_width = w_ffgate.shape[1] // 2
-    chunk = hidden_width // 2
     live = (segment_ids > 0).astype(jnp.float32)[:, None]
     offset = place * local
     gain_attn_own = lax.dynamic_slice_in_dim(gain_attn, offset, local, 0)
     gain_ffn_own = lax.dynamic_slice_in_dim(gain_ffn, offset, local, 0)
 
-    keep, give = halves([w_query, w_gate, w_key, w_value], across)
-    attn_weight = weight_gather(keep, give, across)
-    hidden1, inverse1 = gather_normed(tokens, place, gain_attn)
-    keep, give = halves([w_out], across)
-    out_weight = weight_gather(keep, give, across)
-    keep, give = halves([w_down], across)
-    down_weight = weight_gather(keep, give, across)
-    keep, give = halves([w_ffgate, w_up], across)
-    pair_weights = []
-    for part in range(2):
-        cut = slice(part * chunk, (part + 1) * chunk)
-        pair_weights.append(
-            weight_gather([v[:, cut] for v in keep], [v[:, cut] for v in give], across)
+    line = Line()
+    half = count // 2
+    joint_width = 2 * query_width + 2 * key_width
+    rows_of = partial(weight_rows, across=across)
+
+    first_columns = [w_query, w_gate, w_key, w_value, w_out]
+
+    def open_first(tokens, *weights):
+        upper_y = flip(tokens[:half], "y")
+        keep, give = halves(weights, across)
+        got = flip(give, "x")
+        return (rows_of(keep, got), upper_y)
+
+    first_rows, upper_y = line.run(open_first, tokens, *first_columns)
+    first_weight = weight_gather(first_rows)
+    grad_out = live * cotangent.astype(jnp.float32)
+    grad_out_low = grad_out.astype(low)
+
+    def open_second(tokens, segment_ids, upper_y, w_ffgate, w_up, w_down):
+        lower_y = flip(tokens[half:], "y")
+        via_x = flip(tokens, "x")
+        own_core = flip(tokens, "core")
+        other = flip(segment_ids, "x")
+        via_y = jnp.concatenate([upper_y, lower_y], axis=0)
+        return (via_y, via_x, own_core, other, *halves([w_ffgate, w_up], across), *halves([w_down], across))
+
+    via_y, via_x, own_core, segment_other, keep_pair, give_pair, keep_down, give_down = line.run(
+        open_second, tokens, segment_ids, upper_y, w_ffgate, w_up, w_down
+    )
+
+    def open_third(tokens, via_y, via_x, own_core, keep_down, give_down):
+        steps = relay(tokens, via_y, via_x, own_core, place, gain_attn, True)
+        return (rows_of(keep_down, flip(give_down, "x")), *steps)
+
+    down_rows, *steps, target, inverse1 = line.run(
+        open_third, tokens, via_y, via_x, own_core, keep_down, give_down
+    )
+    down_weight = weight_gather(down_rows)
+
+    def open_fourth(keep_pair, give_pair, segment_ids, segment_other, *steps):
+        hidden1 = diagonal(*steps, place, gain_attn, True)
+        pair_rows = rows_of(keep_pair, flip(give_pair, "x"))
+        segments = jnp.stack([segment_ids, segment_other])
+        cosine, sine, first = jax.vmap(partial(row_tables, head_dim=head_dim))(segments)
+        cosine = cosine.reshape(2 * count, head_dim)
+        sine = sine.reshape(2 * count, head_dim)
+        return (hidden1, pair_rows, cosine, sine, first)
+
+    hidden1, pair_rows, cosine, sine, first = line.run(
+        open_fourth, keep_pair, give_pair, segment_ids, segment_other, *steps, target
+    )
+    pair_weight = weight_gather(pair_rows)
+    out_column = joint_width // query_width
+
+    def attend(hidden1, first_weight, grad_out_low):
+        via_out = direct(grad_out_low)
+        joint = dot_in(hidden1, first_weight, joint_width)
+        mixed, *kept = attend_fwd(
+            joint, cosine, sine, first, gain_query, gain_key, heads, count
         )
-
-    segments = jnp.stack([segment_ids, flip(segment_ids, "x")])
-    cosine, sine, first = jax.vmap(partial(row_tables, head_dim=head_dim))(segments)
-    cosine = cosine.reshape(2 * count, head_dim)
-    sine = sine.reshape(2 * count, head_dim)
-
-    grad_out = live * cotangent.astype(jnp.float32)
-    grad_out_low, hidden1 = tie(grad_out.astype(low), hidden1)
-    grad_out_full = gather_plain(grad_out_low, place, gain_ffn)
-
-    joint = dot_in(hidden1, attn_weight)
-    mixed, *kept = attend_fwd(joint, cosine, sine, first, gain_query, gain_key, heads, count)
-    mixed, grad_out_full = tie(mixed, grad_out_full)
-    resid = tokens.astype(jnp.float32) + feature_fold([(mixed, out_weight)], place)
-    grad_act = dot_in(grad_out_full, down_weight)
-    resid_low, grad_act = tie(resid.astype(low), grad_act)
-    hidden2, inverse2 = gather_normed(resid_low, place, gain_ffn)
-
-    activated, grad_pairs = [], []
-    for part in range(2):
-        ffn_joint = dot_in(hidden2, pair_weights[part])
-        ff_gate = ffn_joint[:, :chunk]
-        ff_up = ffn_joint[:, chunk:]
-        sig_gate = jax.nn.sigmoid(ff_gate)
-        activated.append((ff_gate * sig_gate * ff_up).astype(low))
-        grad_part = grad_act[:, part * chunk : (part + 1) * chunk]
-        grad_ffup = (grad_part * (ff_gate * sig_gate)).astype(low)
-        grad_ffgate = (grad_part * ff_up * sig_gate * (1.0 + ff_gate * (1.0 - sig_gate))).astype(
-            low
+        return (joint, mixed, *kept, *via_out)
+
+    joint, mixed, *rest = line.run(attend, hidden1, first_weight, grad_out_low)
+    kept, via_out = rest[:4], rest[4:]
+
+    def begin_out(mixed, first_weight, grad_out_low, *via_out):
+        steps = relay(grad_out_low, *via_out, place, gain_ffn, False)
+        return (*fold_begin(mixed, first_weight, place, out_column), *steps)
+
+    sums = line.run(begin_out, mixed, first_weight, grad_out_low, *via_out)
+    sums, steps = sums[:4], sums[4:]
+
+    def cross_out(*values):
+        return (*fold_cross(*values[:4]), diagonal(*values[4:], place, gain_ffn, False))
+
+    *sums, grad_out_full = line.run(cross_out, *sums, *steps)
+    ends = line.run(fold_close, *sums)
+
+    def residual(values, *ends):
+        total = values.astype(jnp.float32) + fold_end(*ends)
+        return (total, total.astype(low))
+
+    resid, resid_low = line.run(residual, tokens, *ends)
+
+    def start_resid(resid_low, grad_out_full, down_weight):
+        return (*direct(resid_low), dot_in(grad_out_full, down_weight, hidden_width))
+
+    *via_resid, grad_act = line.run(start_resid, resid_low, grad_out_full, down_weight)
+    *steps, target, inverse2 = line.run(
+        lambda *v: relay(*v, place, gain_ffn, True), resid_low, *via_resid
+    )
+    hidden2 = line.run(lambda *v: diagonal(*v, place, gain_ffn, True), *steps, target)
+    activated, grad_pair = line.run(ffn, hidden2, pair_weight, grad_act)
+    gate_grad = line.run(lambda h, g: dot_grad(h, g, hidden_width), hidden2, grad_pair)
+    gate_sum = grad_scatter(gate_grad)
+    sums = line.run(lambda g, w: fold_begin(g, w, place), grad_pair, pair_weight)
+    sums = line.run(fold_cross, *sums)
+
+    def close_pair(hidden2, grad_pair, *sums):
+        return (*fold_close(*sums), dot_grad(hidden2, grad_pair, hidden_width, 1))
+
+    *ends, up_grad = line.run(close_pair, hidden2, grad_pair, *sums)
+    gate_sum, = line.enter(gate_sum)
+    up_sum = grad_scatter(up_grad)
+    grad_hidden2 = line.run(fold_end, *ends)
+
+    def partial_dots(grad_own, values, inverse, gain_own):
+        dots = jnp.sum(grad_own * gain_own * values.astype(jnp.float32) * inverse, axis=1)
+        dots = dots.reshape(-1, 128)
+        dots = dots + flip(dots, "core")
+        return dots + flip(dots, "y")
+
+    def norm_back(grad_own, values, inverse, gain_own, dots, extra):
+        unit = values.astype(jnp.float32) * inverse
+        dots = dots.reshape(-1, 1) / width
+        grad_input = inverse * (grad_own * gain_own - unit * dots) + extra
+        return (grad_input, grad_input.astype(low))
+
+    def gain_part(grad_own, values, inverse):
+        return jnp.sum(grad_own * (values.astype(jnp.float32) * inverse), axis=0).reshape(-1, 128)
+
+    def back_dots(grad_own, values, inverse, gain_own):
+        return (
+            partial_dots(grad_own, values, inverse, gain_own),
+            gain_part(grad_own, values, inverse),
         )
-        grad_pairs.append(jnp.concatenate([grad_ffgate, grad_ffup], axis=1))
-    activated = jnp.concatenate(activated, axis=1)
-    pair_grads = [dot_grad(hidden2, grad_pair) for grad_pair in grad_pairs]
-    down_grad = dot_grad(grad_out_full, activated)
-    pair_sums = [grad_scatter(grads, across) for grads in pair_grads]
-    down_sum = grad_scatter(down_grad, across)
-
-    grad_hidden2 = feature_fold(list(zip(grad_pairs, pair_weights)), place)
-    grad_input2, gain_ffn_grad = norm_back_own(
-        grad_hidden2, resid_low.astype(jnp.float32), inverse2, gain_ffn_own, width
-    )
-    grad_resid = grad_out + grad_input2
-    grad_branch_full = gather_plain(grad_resid.astype(low), place, gain_ffn)
-    grad_branch_full, activated = tie(grad_branch_full, activated)
-    ffn_out = feature_fold([(activated, down_weight)], place)
-    output = (live * (resid + ffn_out)).astype(low)
-    grad_mixed = dot_in(grad_branch_full, out_weight)
-    out_sum = grad_scatter(dot_grad(grad_branch_full, mixed), across)
-    grad_joint, grad_head_gains = attend_bwd(
-        joint, cosine, sine, first, gain_query, gain_key, kept, grad_mixed, count
-    )
-    attn_sum = grad_scatter(dot_grad(hidden1, grad_joint), across)
-    grad_hidden1 = feature_fold([(grad_joint, attn_weight)], place)
-    grad_input1, gain_attn_grad = norm_back_own(
-        grad_hidden1, tokens.astype(jnp.float32), inverse1, gain_attn_own, width
-    )
-    grad_tokens = grad_resid + grad_input1
-
-    own_gains = sum_all(jnp.stack([gain_attn_grad, gain_ffn_grad]))
-    head_gains = sum_all(grad_head_gains)
-    for axis in ("core", "y"):
-        head_gains = head_gains + flip(head_gains, axis)
-    spot = lax.dynamic_update_slice_in_dim(
-        jnp.zeros((2, width), jnp.float32), own_gains, offset, 1
-    )
-    for axis in ("core", "y"):
-        spot = spot + flip(spot, axis)
-
-    def join(sums, low_cut, high_cut):
-        return jnp.concatenate([s[:, low_cut:high_cut] for s in sums], axis=1).astype(jnp.float32)
-
-    def join_parts(low_cut, high_cut):
-        return jnp.concatenate(
-            [pair_sums[part][side][:, low_cut:high_cut] for side in range(2) for part in range(2)],
-            axis=1,
-        ).astype(jnp.float32)
-
+
+    dots, gain_ffn_grad = line.run(back_dots, grad_hidden2, resid_low, inverse2, gain_ffn_own)
+    grad_resid, grad_branch = line.run(
+        norm_back, grad_hidden2, resid_low, inverse2, gain_ffn_own, dots, grad_out
+    )
+
+    def start_branch(grad_branch, grad_out_full, activated):
+        return (*direct(grad_branch), dot_grad(grad_out_full, activated))
+
+    *via_branch, down_grad = line.run(start_branch, grad_branch, grad_out_full, activated)
+    down_sum = grad_scatter(down_grad)
+
+    def relay_branch(grad_branch, gate_sum, activated, down_weight, *via_branch):
+        steps = relay(grad_branch, *via_branch, place, gain_ffn, False)
+        got = fold_sent(activated, down_weight, place)
+        return (flip(give_rows(gate_sum, across), "x"), *got, *steps)
+
+    got_gate, far_got, near_got, *steps = line.run(
+        relay_branch, grad_branch, gate_sum, activated, down_weight, *via_branch
+    )
+    grad_branch_full = line.run(lambda *v: diagonal(*v, place, gain_ffn, False), *steps)
+
+    def mix_back(grad_branch_full, first_weight, mixed):
+        return (
+            dot_in(grad_branch_full, first_weight, query_width, out_column),
+            dot_grad(grad_branch_full, mixed),
+        )
+
+    grad_mixed, out_grad = line.run(mix_back, grad_branch_full, first_weight, mixed)
+    out_sum = grad_scatter(out_grad)
+    sums_ffn = line.run(
+        lambda *v: fold_held(v[0], v[1], place, *v[2:]), activated, down_weight, far_got, near_got
+    )
+
+    def attend_back(joint, grad_mixed, up_sum, *sums):
+        grad_joint, head_gains = attend_bwd(
+            joint, cosine, sine, first, gain_query, gain_key, kept, grad_mixed, count
+        )
+        return (
+            grad_joint,
+            head_gains,
+            *fold_cross(*sums),
+            flip(give_rows(up_sum, across), "x"),
+        )
+
+    grad_joint, head_gains, *sums_ffn, got_up = line.run(
+        attend_back, joint, grad_mixed, up_sum, *sums_ffn
+    )
+
+    def close_ffn(hidden1, grad_joint, gain_ffn_grad, head_gains, *sums):
+        early = jnp.concatenate([gain_ffn_grad, head_gains], axis=0)
+        early = early + flip(early, "x")
+        return (*fold_close(*sums), dot_grad(hidden1, grad_joint), early)
+
+    *ends_ffn, attn_grads, early = line.run(
+        close_ffn, hidden1, grad_joint, gain_ffn_grad, head_gains, *sums_ffn
+    )
+    attn_sum = grad_scatter(attn_grads)
+
+    def fold_attn(grad_joint, first_weight, early, down_sum):
+        early = early + z_flip(early, 1)
+        early = early + z_flip(early, 2)
+        got_down = flip(give_rows(down_sum, across), "x")
+        return (early, got_down, *fold_begin(grad_joint, first_weight, place))
+
+    early, got_down, *sums = line.run(fold_attn, grad_joint, first_weight, early, down_sum)
+
+    def join(rows, got, low_cut, high_cut):
+        keep = keep_rows(rows, across)[:, low_cut:high_cut]
+        got = got[:, low_cut:high_cut]
+        first, second = jnp.where(across == 0, keep, got), jnp.where(across == 0, got, keep)
+        return jnp.concatenate([first, second], axis=1).astype(jnp.float32)
+
+    def join_all(rows, got):
+        return join(rows, got, 0, rows.shape[1])
+
+    def cross_attn(resid, gate_sum, got_gate, up_sum, got_up, out_sum, *values):
+        output = (live * (resid + fold_end(*values[4:]))).astype(low)
+        return (
+            output,
+            join_all(gate_sum, got_gate),
+            join_all(up_sum, got_up),
+            flip(give_rows(out_sum, across), "x"),
+            *fold_cross(*values[:4]),
+        )
+
+    output, ffgate_grad, up_grad, got_out, *sums = line.run(
+        cross_attn, resid, gate_sum, got_gate, up_sum, got_up, out_sum, *sums, *ends_ffn
+    )
+
+    def close_attn(down_sum, got_down, out_sum, got_out, *sums):
+        return (join_all(down_sum, got_down), join_all(out_sum, got_out), *fold_close(*sums))
+
+    down_part, out_part, *ends = line.run(
+        close_attn, down_sum, got_down, out_sum, got_out, *sums
+    )
+
+    def last_dots(tokens, inverse1, *ends):
+        grad_own = fold_end(*ends)
+        late = gain_part(grad_own, tokens, inverse1)
+        return (
+            grad_own,
+            partial_dots(grad_own, tokens, inverse1, gain_attn_own),
+            late + flip(late, "x"),
+        )
+
+    grad_hidden1, dots, late = line.run(last_dots, tokens, inverse1, *ends)
+
+    def last_norm(grad_hidden1, tokens, inverse1, dots, grad_resid, late):
+        grad_tokens, unused = norm_back(
+            grad_hidden1, tokens, inverse1, gain_attn_own, dots, grad_resid
+        )
+        late = late + z_flip(late, 1)
+        return (grad_tokens, late)
+
+    grad_tokens, late = line.run(
+        last_norm, grad_hidden1, tokens, inverse1, dots, grad_resid, late
+    )
+    late, got_attn = line.run(
+        lambda v, s: (v + z_flip(v, 2), flip(give_rows(s, across), "x")), late, attn_sum
+    )
     cuts = (
         0,
         query_width,
@@ -867,21 +1121,32 @@
         2 * query_width + key_width,
         2 * query_width + 2 * key_width,
     )
+    blocks = local // 128
+
+    def last_parts(attn_sum, got_attn, late, early):
+        own = jnp.stack([late, early[:blocks]])
+        spot = lax.dynamic_update_slice_in_dim(
+            jnp.zeros((2, width // 128, 128), jnp.float32), own, offset // 128, 1
+        ).reshape(-1, 128)
+        spot = jnp.concatenate([spot, early[blocks:]], axis=0)
+        spot = spot + flip(spot, "core")
+        spot = spot + flip(spot, "y")
+        return (spot, *[join(attn_sum, got_attn, cuts[i], cuts[i + 1]) for i in range(4)])
+
+    spot, *attn_parts = line.run(last_parts, attn_sum, got_attn, late, early)
+    lines = width // 128
     return (
         output,
         grad_tokens,
-        spot[0],
-        spot[1],
-        head_gains[0],
-        head_gains[1],
-        join(attn_sum, cuts[0], cuts[1]),
-        join(attn_sum, cuts[1], cuts[2]),
-        join(attn_sum, cuts[2], cuts[3]),
-        join(attn_sum, cuts[3], cuts[4]),
-        join(out_sum, 0, query_width),
-        join_parts(0, chunk),
-        join_parts(chunk, 2 * chunk),
-        join(down_sum, 0, hidden_width),
+        spot[:lines].reshape(width),
+        spot[lines : 2 * lines].reshape(width),
+        spot[2 * lines],
+        spot[2 * lines + 1],
+        *attn_parts,
+        out_part,
+        ffgate_grad,
+        up_grad,
+        down_part,
     )
 
 

time: 754 us -> 678 us (0.90)
  Pallas kernels: 68.6 us -> 177 us
  matrix products: 160 us -> 77.7 us
  waiting for transfers between devices: 299 us -> 226 us
  starting transfers between devices: 74.8 us -> 61.7 us
  other arithmetic: 78.1 us -> 68.7 us
    pallas_call x0 -> x12, Pallas kernels: none -> 108 us  [the longest x5 50.8 us: dot_grad(): pl.pallas_call(partial(matmul_kernel, product_tn), grid=(rows // tile,),...]
    dot_general x30 -> x16, matrix products: 160 us -> 77.7 us  [product_nt(): lax.dot_general(first, second, (((1,), (1,)), ((), ())), preferred_elemen...]
    ppermute x77 -> x74, waiting for transfers between devices: 256 us -> 194 us  [flip(): return lax.ppermute(values, axis, [(0, 1), (1, 0)])]
    reduce_scatter x5, waiting for transfers between devices: 20 us -> 0.04 us  [grad_scatter(): return lax.psum_scatter(grads, 'z', scatter_dimension=0, tiled=True)]
    all_gather x5 -> x3, starting transfers between devices: 12.1 us -> 0.29 us  [weight_gather(): return lax.all_gather(rows, 'z', axis=0, tiled=True)]
    convert_element_type x20 -> x15, other arithmetic: 31.9 us -> 23.3 us  [the longest x8 7.98 us: join(): return jnp.concatenate([first, second], axis=1).astype(jnp.float32)]
    unnamed x142 -> x118, local copies, waits for them, and re-layouts: 14 us -> 22.3 us
    dynamic_slice x9 -> x5, local copies, waits for them, and re-layouts: 11.8 us -> 4.02 us  [keep_rows(): return lax.dynamic_slice_in_dim(summed, across * rows, rows, 0)]
  transfers between devices with their start and end apart: 91 -> 86, of which waited for: 42 -> 43; matrix products, arithmetic and copies ran while one was open for 33% -> 24% of each run, Pallas kernels for 9% -> 21%
where the time goes in v3:
time: 678 us; the launch traced here: 672 us
  waiting for transfers between devices  226 us (33%)
  Pallas kernels  177 us (26%)
  matrix products  77.7 us (11%)
  other arithmetic  68.7 us (10%)
  starting transfers between devices  61.7 us (9%)
  local copies, waits for them, and re-layouts  46.1 us (7%)
  between operations  15.4 us (2%)
    ppermute x74, waiting for transfers between devices, flip(): return lax.ppermute(values, axis, [(0, 1), (1, 0)])  194 us
    dot_general x16, matrix products, product_nt(): lax.dot_general(first, second, (((1,), (1,)), ((), ())), preferred_elemen...  77.7 us
    ppermute x74, starting transfers between devices, flip(): return lax.ppermute(values, axis, [(0, 1), (1, 0)])  58.6 us
    pallas_call x5, Pallas kernels, dot_grad(): pl.pallas_call(partial(matmul_kernel, product_tn), grid=(rows // tile,),...  50.8 us
    pallas_call x8, Pallas kernels, pack(): pl.pallas_call(partial(pack_kernel, normed), grid=(tiles,), in_specs=[pl....  42.3 us
    pallas_call x3, Pallas kernels, dot_in(): pl.pallas_call(partial(matmul_kernel, product_nn), grid=(count // tile,),...  29.6 us
    all_gather x3, waiting for transfers between devices, weight_gather(): return lax.all_gather(rows, 'z', axis=0, tiled=True)  23.6 us
    unnamed x118, local copies, waits for them, and re-layouts  22.3 us
  transfers between devices with their start and end apart: 86, of which 43 were waited for; matrix products, arithmetic and copies ran while one was open for 24% of the time, Pallas kernels for 21%

profile of v3, /device:TPU:0, one launch (start us, length us, event | category | flops | bytes accessed | tf_op | source)
XLA Modules:
  0.0 672.2 jit_solution(788146272860563068)
XLA Ops:
  9.6 2.9 collective-permute-start
  15.2 9.5 %collective-permute-done = bf16[256,1024]{1,0:T(8,128)(2,1)S(1)} collective-permute-done((bf16[256,1024]{1,0:T(8,128)(2,1)}, bf16[256,1024]{1,0:T(8,128)(2,1)S(1)}, u32[]{:S(2)}, u32[]{:S(2)}) %collective-permute-start) | collective-permute-done | bytes 524320 | tf_op jit(solution)/shard_map/ppermute | solution.py:322
  36.0 7.7 %collective-permute-done.2 = bf16[512,512]{1,0:T(8,128)(2,1)} collective-permute-done((bf16[512,512]{1,0:T(8,128)(2,1)S(1)}, bf16[512,512]{1,0:T(8,128)(2,1)}, u32[]{:S(2)}, u32[]{:S(2)}) %collective-permute-start.2) | collective-permute-done | bytes 524320 | tf_op jit(solution)/shard_map/ppermute | solution.py:322
  45.0 6.8 %collective-permute-done.5 = s32[1024]{0:T(1024)S(1)} collective-permute-done((s32[1024]{0:T(1024)S(1)}, s32[1024]{0:T(1024)S(1)}, u32[]{:S(2)}, u32[]{:S(2)}) %collective-permute-start.5) | collective-permute-done | bytes 4128 | tf_op jit(solution)/shard_map/ppermute | solution.py:322
  53.8 3.2 convert_multiply_fusion.4
  61.3 3.4 collective-permute-done.6
  67.7 5.6 shard_map.257
  80.2 3.7 fusion.42
  84.7 13.2 %collective-permute-done.12 = bf16[256,1536]{1,0:T(8,128)(2,1)} collective-permute-done((bf16[256,1536]{1,0:T(8,128)(2,1)}, bf16[256,1536]{1,0:T(8,128)(2,1)}, u32[]{:S(2)}, u32[]{:S(2)}) %collective-permute-start.12) | collective-permute-done | bytes 786464 | tf_op jit(solution)/shard_map/ppermute | solution.py:322
  100.3 5.8 shard_map.258
  106.1 3.2 all-gather.4.cloned.1.call-done.weight_ref
  112.3 11.4 %shard_map.259.joint_ref = f32[2048,768]{1,0:T(8,128)} custom-call(bf16[2048,2048]{1,0:T(8,128)(2,1)} %get-tuple-element.696.operand_ref, bf16[2048,1024]{1,0:T(8,128)(2,1)} %all-gather.4.cloned.1.call-done.weight_ref), custom_call_target="tpu_custom_call" | custom-call | tf_op jit(solution)/shard_map/pallas_call | solution.py:521
  123.7 2.8 copy-done
  126.5 10.5 %shard_map.260 = (bf16[2048,256]{1,0:T(8,128)(2,1)S(1)}, f32[2048,256]{1,0:T(8,128)S(1)}, bf16[2048,256]{1,0:T(8,128)(2,1)S(1)}, bf16[2048,128]{1,0:T(8,128)(2,1)S(1)}, f32[2,2,1024]{2,1,0:T(2,128)S(1)}) custom-call(f32[2048,768]{1,0:T(8,128)S(1)} %copy-done, f32[2048,128]{1,0:T(8,128)S(1)} %pad_maximum_fusion.5.cos_ref, ...), custom_call_target="tpu_custom_call" | custom-call | tf_op jit(solution)/shard_map/pallas_call | solution.py:797
  140.1 3.2 convolution_convert_fusion
  143.9 3.0 convolution_convert_fusion.1
  153.6 4.7 shard_map.261.refs_4_
  160.9 3.0 add_convert_fusion.7
  172.2 4.7 shard_map.262.operand_ref
  176.9 18.4 %collective-permute-done.22 = bf16[2,512,512]{2,1,0:T(8,128)(2,1)} collective-permute-done((bf16[2,512,512]{2,1,0:T(8,128)(2,1)}, bf16[2,512,512]{2,1,0:T(8,128)(2,1)}, u32[]{:S(2)}, u32[]{:S(2)}) %collective-permute-start.22) | collective-permute-done | bytes 1048608 | tf_op jit(solution)/shard_map/ppermute | solution.py:322
  195.7 2.8 fusion.26
  200.6 11.1 %collective-permute-done.25 = bf16[512,512]{1,0:T(8,128)(2,1)S(1)} collective-permute-done((bf16[512,512]{1,0:T(8,128)(2,1)S(1)}, bf16[512,512]{1,0:T(8,128)(2,1)S(1)}, u32[]{:S(2)}, u32[]{:S(2)}) %collective-permute-start.25) | collective-permute-done | bytes 524320 | tf_op jit(solution)/shard_map/ppermute | solution.py:322
  217.7 11.3 %shard_map.263.grad_ref = f32[2048,768]{1,0:T(8,128)} custom-call(bf16[2048,2048]{1,0:T(8,128)(2,1)} %shard_map.262.operand_ref, bf16[2048,768]{1,0:T(8,128)(2,1)} %all-gather.6.cloned.1.call-done.weight_ref), custom_call_target="tpu_custom_call" | custom-call | tf_op jit(solution)/shard_map/pallas_call | solution.py:521
  229.1 9.3 %collective-permute-done.27.refs_2_ = bf16[1024,512]{1,0:T(8,128)(2,1)S(1)} collective-permute-done((bf16[1024,512]{1,0:T(8,128)(2,1)S(1)}, bf16[1024,512]{1,0:T(8,128)(2,1)S(1)}, u32[]{:S(2)}, u32[]{:S(2)}) %collective-permute-start.27) | collective-permute-done | bytes 1048608 | tf_op jit(solution)/shard_map/ppermute | solution.py:322
  245.8 5.8 shard_map.264
  251.6 5.3 collective-permute-done.31
  260.2 2.8 collective-permute-done.34.refs_3_
  263.0 5.7 shard_map.265
  268.7 20.4 %all-gather.8.cloned.1.call-done.weight_ref = bf16[2048,1536]{1,0:T(8,128)(2,1)} async-done(((bf16[512,1536]{1,0:T(8,128)(2,1)}), bf16[2048,1536]{1,0:T(8,128)(2,1)}) %all-gather.8.cloned.1.call-update) | async-done | bytes 6291472 | tf_op jit(solution)/shard_map/all_gather | solution.py:442
  289.1 20.2 %shard_map.266 = (bf16[2048,768]{1,0:T(8,128)(2,1)}, bf16[2048,1536]{1,0:T(8,128)(2,1)}) custom-call(bf16[2048,2048]{1,0:T(8,128)(2,1)} %get-tuple-element.582.hidden_ref.operand_ref, bf16[2048,1536]{1,0:T(8,128)(2,1)} %all-gather.8.cloned.1.call-done.weight_ref, f32[2048,768]{1,0:T(8,128)} %shard_map.263.grad_ref), custom_call_target="tpu_custom_call" | custom-call | tf_op jit(solution)/shard_map/pallas_call | solution.py:574
  309.4 11.2 %shard_map.267 = bf16[2048,768]{1,0:T(8,128)(2,1)} custom-call(bf16[2048,2048]{1,0:T(8,128)(2,1)} %get-tuple-element.582.hidden_ref.operand_ref, bf16[2048,1536]{1,0:T(8,128)(2,1)} %get-tuple-element.583.weight_ref), custom_call_target="tpu_custom_call" | custom-call | tf_op jit(solution)/shard_map/pallas_call | solution.py:539
  320.6 8.0 %convolution_convert_fusion.7 = bf16[2048,512]{1,0:T(8,128)(2,1)} fusion(bf16[2048,1536]{1,0:T(8,128)(2,1)} %get-tuple-element.583.weight_ref, bf16[2048,1536]{1,0:T(8,128)(2,1)} %all-gather.8.cloned.1.call-done.weight_ref, s32[]{:T(128)S(6)} %select_n.186), kind=kOutput, calls=%fused_computation.15 | convolution fusion | flops 3222274048 | bytes 9961476 | tf_op jit(solution)/shard_map/dot_general | solution.py:613
  328.7 6.8 %convolution_convert_fusion.6 = bf16[2048,512]{1,0:T(8,128)(2,1)S(1)} fusion(bf16[2048,1536]{1,0:T(8,128)(2,1)} %get-tuple-element.583.weight_ref, bf16[2048,1536]{1,0:T(8,128)(2,1)} %all-gather.8.cloned.1.call-done.weight_ref, s32[]{:T(128)S(6)} %select_n.188), kind=kOutput, calls=%fused_computation.14 | convolution fusion | flops 3222274048 | bytes 9961476 | tf_op jit(solution)/shard_map/dot_general | solution.py:613
  336.1 7.4 %add_convert_fusion.5 = bf16[2048,512]{1,0:T(8,128)(2,1)S(1)} fusion(bf16[2048,512]{1,0:T(8,128)(2,1)} %collective-permute-done.35, bf16[2048,1536]{1,0:T(8,128)(2,1)} %get-tuple-element.583.weight_ref, bf16[2048,1536]{1,0:T(8,128)(2,1)} %all-gather.8.cloned.1.call-done.weight_ref, s32[]{:T(128)S(6)} %select_n.185), kind=kOutput, calls=%fused_computation.5 | convolution fusion | flops 3224371200 | bytes 12058628 | tf_op jit(solution)/shard_map/dot_general | solution.py:613
  343.6 5.3 add_convert_fusion.4
  352.3 22.2 %collective-permute-done.37 = bf16[2,512,512]{2,1,0:T(8,128)(2,1)S(1)} collective-permute-done((bf16[2,512,512]{2,1,0:T(8,128)(2,1)S(1)}, bf16[2,512,512]{2,1,0:T(8,128)(2,1)S(1)}, u32[]{:S(2)}, u32[]{:S(2)}) %collective-permute-start.37) | collective-permute-done | bytes 1048608 | tf_op jit(solution)/shard_map/ppermute | solution.py:322
  379.3 10.9 %shard_map.268 = bf16[2048,768]{1,0:T(8,128)(2,1)} custom-call(bf16[2048,2048]{1,0:T(8,128)(2,1)} %get-tuple-element.582.hidden_ref.operand_ref, bf16[2048,1536]{1,0:T(8,128)(2,1)} %get-tuple-element.583.weight_ref), custom_call_target="tpu_custom_call" | custom-call | tf_op jit(solution)/shard_map/pallas_call | solution.py:539
  402.3 3.0 collective-permute-done.42
  406.5 4.5 fusion.75
  412.2 10.9 %shard_map.269 = bf16[2048,768]{1,0:T(8,128)(2,1)} custom-call(bf16[2048,2048]{1,0:T(8,128)(2,1)} %shard_map.262.operand_ref, bf16[2048,768]{1,0:T(8,128)(2,1)} %get-tuple-element.658.weight_ref), custom_call_target="tpu_custom_call" | custom-call | tf_op jit(solution)/shard_map/pallas_call | solution.py:539
  423.1 12.8 %collective-permute-done.43.refs_2_ = bf16[1024,512]{1,0:T(8,128)(2,1)} collective-permute-done((bf16[1024,512]{1,0:T(8,128)(2,1)}, bf16[1024,512]{1,0:T(8,128)(2,1)}, u32[]{:S(2)}, u32[]{:S(2)}) %collective-permute-start.43) | collective-permute-done | bytes 1048608 | tf_op jit(solution)/shard_map/ppermute | solution.py:322
  436.0 5.7 convolution_convert_fusion.5
  441.8 5.2 convolution_convert_fusion.4
  452.4 7.7 %collective-permute-done.46 = bf16[256,768]{1,0:T(8,128)(2,1)S(1)} collective-permute-done((bf16[256,768]{1,0:T(8,128)(2,1)S(1)}, bf16[256,768]{1,0:T(8,128)(2,1)S(1)}, u32[]{:S(2)}, u32[]{:S(2)}) %collective-permute-start.46) | collective-permute-done | bytes 393248 | tf_op jit(solution)/shard_map/ppermute | solution.py:322
  463.0 5.1 shard_map.270.refs_4_
  468.2 6.0 collective-permute-done.50
  476.8 5.0 add_convert_fusion.3
  483.3 3.8 add_convert_fusion.2
  489.9 4.8 shard_map.271.operand_ref
  494.6 6.8 %shard_map.272.grad_mixed_ref = f32[2048,256]{1,0:T(8,128)} custom-call(bf16[2048,2048]{1,0:T(8,128)(2,1)} %shard_map.271.operand_ref, bf16[2048,1024]{1,0:T(8,128)(2,1)} %all-gather.4.cloned.1.call-done.weight_ref), custom_call_target="tpu_custom_call" | custom-call | tf_op jit(solution)/shard_map/pallas_call | solution.py:521
  501.5 6.8 %shard_map.273 = bf16[2048,256]{1,0:T(8,128)(2,1)} custom-call(bf16[2048,2048]{1,0:T(8,128)(2,1)} %shard_map.271.operand_ref, bf16[2048,256]{1,0:T(8,128)(2,1)} %copy-done.1), custom_call_target="tpu_custom_call" | custom-call | tf_op jit(solution)/shard_map/pallas_call | solution.py:539
  515.6 16.1 %shard_map.274 = (bf16[2048,768]{1,0:T(8,128)(2,1)}, f32[2,128]{1,0:T(2,128)S(1)}) custom-call(f32[2048,768]{1,0:T(8,128)} %shard_map.259.joint_ref, f32[2048,128]{1,0:T(8,128)S(1)} %pad_maximum_fusion.5.cos_ref, f32[2048,128]{1,0:T(8,128)S(1)} %pad_maximum_fusion.6.sin_ref, s32[2,1,1024]{2,1,0:T(1,128)S(1)} %compare_select_fusion.first_ref, ...), custom_call_target="tpu_custom_call" | custom-call | tf_op jit(solution)/shard_map/pallas_call | solution.py:820
  531.7 10.4 %collective-permute-done.56 = bf16[256,768]{1,0:T(8,128)(2,1)S(1)} collective-permute-done((bf16[256,768]{1,0:T(8,128)(2,1)S(1)}, bf16[256,768]{1,0:T(8,128)(2,1)S(1)}, u32[]{:S(2)}, u32[]{:S(2)}) %collective-permute-start.56) | collective-permute-done | bytes 393248 | tf_op jit(solution)/shard_map/ppermute | solution.py:322
  547.7 11.0 %shard_map.275 = bf16[2048,768]{1,0:T(8,128)(2,1)} custom-call(bf16[2048,2048]{1,0:T(8,128)(2,1)} %get-tuple-element.696.operand_ref, bf16[2048,768]{1,0:T(8,128)(2,1)} %get-tuple-element.705.weight_ref), custom_call_target="tpu_custom_call" | custom-call | tf_op jit(solution)/shard_map/pallas_call | solution.py:539
  558.8 5.5 convolution_convert_fusion.2
  564.3 4.4 convolution_convert_fusion.3
  570.0 2.8 collective-permute-done.60
  577.3 5.2 add_convert_fusion
  585.1 3.7 add_convert_fusion.1
  601.1 15.6 %collective-permute-done.66 = bf16[2,512,512]{2,1,0:T(8,128)(2,1)S(1)} collective-permute-done((bf16[2,512,512]{2,1,0:T(8,128)(2,1)S(1)}, bf16[2,512,512]{2,1,0:T(8,128)(2,1)S(1)}, u32[]{:S(2)}, u32[]{:S(2)}) %collective-permute-start.66) | collective-permute-done | bytes 1048608 | tf_op jit(solution)/shard_map/ppermute | solution.py:322
  623.5 5.8 collective-permute-done.68
  641.1 3.4 multiply_add_fusion
  648.2 3.1 collective-permute-done.74
  651.3 4.2 collective-permute-done.75
  (388 shorter events, 184.0 us)
Async XLA Ops:
  7.2 102.1 %all-gather.4.cloned.1.call-start = ((), (), s32[]{:S(2)}) async-start(), calls=%async_computation.5 | async-start | bytes 5242880 | tf_op jit(solution)/shard_map/all_gather | solution.py:442
  9.6 15.1 %collective-permute-start = (bf16[256,1024]{1,0:T(8,128)(2,1)}, bf16[256,1024]{1,0:T(8,128)(2,1)S(1)}, u32[]{:S(2)}, u32[]{:S(2)}) collective-permute-start(bf16[256,1024]{1,0:T(8,128)(2,1)} %get-tuple-element.406), channel_id=1, source_target_pairs={{0,4},{4,0},{1,5},{5,1},{2,6},{6,2},{3,7},{7,3},{8,12},{12,8},{9,1... | collective-permute-start | bytes 1572872 | tf_op jit(solution)/shard_map/ppermute | solution.py:322
  13.6 13.4 %collective-permute-start.1 = (bf16[512,512]{1,0:T(8,128)(2,1)S(1)}, bf16[512,512]{1,0:T(8,128)(2,1)S(1)}, u32[]{:S(2)}, u32[]{:S(2)}) collective-permute-start(bf16[512,512]{1,0:T(8,128)(2,1)S(1)} %slice.225), channel_id=1, source_target_pairs={{0,2},{2,0},{1,3},{3,1},{4,6},{6,4},{5,7},{7,5},{8,10},{10,8},{9,1... | collective-permute-start | bytes 1572872 | tf_op jit(solution)/shard_map/ppermute | solution.py:322
  27.1 187.9 %all-gather.6.cloned.1.call-start = ((), (), s32[]{:S(2)}) async-start(), calls=%async_computation.6 | async-start | bytes 3932160 | tf_op jit(solution)/shard_map/all_gather | solution.py:442
  27.4 24.4 %collective-permute-start.3 = (bf16[1024,512]{1,0:T(8,128)(2,1)S(1)}, bf16[1024,512]{1,0:T(8,128)(2,1)S(1)}, u32[]{:S(2)}, u32[]{:S(2)}) collective-permute-start(bf16[1024,512]{1,0:T(8,128)(2,1)S(1)} %copy-done.10), channel_id=1, source_target_pairs={{0,4},{4,0},{1,5},{5,1},{2,6},{6,2},{3,7},{7,3},{8,12},{12,8},{9,1... | collective-permute-start | bytes 3145736 | tf_op jit(solution)/shard_map/ppermute | solution.py:322
  29.1 22.7 %collective-permute-start.4 = (bf16[1024,512]{1,0:T(8,128)(2,1)S(1)}, bf16[1024,512]{1,0:T(8,128)(2,1)}, u32[]{:S(2)}, u32[]{:S(2)}) collective-permute-start(bf16[1024,512]{1,0:T(8,128)(2,1)S(1)} %copy-done.10), channel_id=1, source_target_pairs={{0,1},{1,0},{2,3},{3,2},{4,5},{5,4},{6,7},{7,6},{8,9},{9,8},{10,11... | collective-permute-start | bytes 3145736 | tf_op jit(solution)/shard_map/ppermute | solution.py:322
  29.2 14.5 %collective-permute-start.2 = (bf16[512,512]{1,0:T(8,128)(2,1)S(1)}, bf16[512,512]{1,0:T(8,128)(2,1)}, u32[]{:S(2)}, u32[]{:S(2)}) collective-permute-start(bf16[512,512]{1,0:T(8,128)(2,1)S(1)} %slice.226), channel_id=1, source_target_pairs={{0,2},{2,0},{1,3},{3,1},{4,6},{6,4},{5,7},{7,5},{8,10},{10,8},{9,1... | collective-permute-start | bytes 1572872 | tf_op jit(solution)/shard_map/ppermute | solution.py:322
  30.8 21.1 %collective-permute-start.5 = (s32[1024]{0:T(1024)S(1)}, s32[1024]{0:T(1024)S(1)}, u32[]{:S(2)}, u32[]{:S(2)}) collective-permute-start(s32[1024]{0:T(1024)S(1)} %copy-done.50), channel_id=1, source_target_pairs={{0,4},{4,0},{1,5},{5,1},{2,6},{6,2},{3,7},{7,3},{8,12},{12,8},{9,1... | collective-permute-start | bytes 12296 | tf_op jit(solution)/shard_map/ppermute | solution.py:322
  51.8 23.2 %collective-permute-start.7 = (bf16[1024,512]{1,0:T(8,128)(2,1)S(1)}, bf16[1024,512]{1,0:T(8,128)(2,1)}, u32[]{:S(2)}, u32[]{:S(2)}) collective-permute-start(bf16[1024,512]{1,0:T(8,128)(2,1)S(1)} %collective-permute-done.3.refs_0_), channel_id=1, source_target_pairs={{0,1},{1,0},{2,3},{3,2},{4,5},{5,4},{6,7},{7,6},{8,9},{9,8},{10,11... | collective-permute-start | bytes 3145736 | tf_op jit(solution)/shard_map/ppermute | solution.py:322
  51.9 14.8 %collective-permute-start.10 = (bf16[1024,512]{1,0:T(8,128)(2,1)S(1)}, bf16[1024,512]{1,0:T(8,128)(2,1)S(1)}, u32[]{:S(2)}, u32[]{:S(2)}) collective-permute-start(bf16[1024,512]{1,0:T(8,128)(2,1)S(1)} %pad_maximum_fusion.4.refs_2_), channel_id=1, source_target_pairs={{0,1},{1,0},{2,3},{3,2},{4,5},{5,4},{6,7},{7,6},{8,9},{9,8},{10,11... | collective-permute-start | bytes 3145736 | tf_op jit(solution)/shard_map/ppermute | solution.py:322
  52.4 12.3 %collective-permute-start.6 = (bf16[256,768]{1,0:T(8,128)(2,1)}, bf16[256,768]{1,0:T(8,128)(2,1)}, u32[]{:S(2)}, u32[]{:S(2)}) collective-permute-start(bf16[256,768]{1,0:T(8,128)(2,1)} %get-tuple-element.432), channel_id=1, source_target_pairs={{0,4},{4,0},{1,5},{5,1},{2,6},{6,2},{3,7},{7,3},{8,12},{12,8},{9,1... | collective-permute-start | bytes 1179656 | tf_op jit(solution)/shard_map/ppermute | solution.py:322
  58.7 16.4 %collective-permute-start.8 = (bf16[512,512]{1,0:T(8,128)(2,1)}, bf16[512,512]{1,0:T(8,128)(2,1)}, u32[]{:S(2)}, u32[]{:S(2)}) collective-permute-start(bf16[512,512]{1,0:T(8,128)(2,1)} %slice.227), channel_id=1, source_target_pairs={{0,4},{4,0},{1,5},{5,1},{2,6},{6,2},{3,7},{7,3},{8,12},{12,8},{9,1... | collective-permute-start | bytes 1572872 | tf_op jit(solution)/shard_map/ppermute | solution.py:322
  59.3 15.8 %collective-permute-start.9 = (bf16[512,512]{1,0:T(8,128)(2,1)}, bf16[512,512]{1,0:T(8,128)(2,1)}, u32[]{:S(2)}, u32[]{:S(2)}) collective-permute-start(bf16[512,512]{1,0:T(8,128)(2,1)} %slice.228), channel_id=1, source_target_pairs={{0,2},{2,0},{1,3},{3,1},{4,6},{6,4},{5,7},{7,5},{8,10},{10,8},{9,1... | collective-permute-start | bytes 1572872 | tf_op jit(solution)/shard_map/ppermute | solution.py:322
  76.2 212.9 %all-gather.8.cloned.1.call-start = ((), (), s32[]{:S(2)}) async-start(), calls=%async_computation.7 | async-start | bytes 7864320 | tf_op jit(solution)/shard_map/all_gather | solution.py:442
  77.5 22.8 %collective-permute-start.11 = (bf16[1024,512]{1,0:T(8,128)(2,1)S(1)}, bf16[1024,512]{1,0:T(8,128)(2,1)}, u32[]{:S(2)}, u32[]{:S(2)}) collective-permute-start(bf16[1024,512]{1,0:T(8,128)(2,1)S(1)} %constant_dynamic-update-slice_fusion.refs_2_), channel_id=1, source_target_pairs={{0,1},{1,0},{2,3},{3,2},{4,5},{5,4},{6,7},{7,6},{8,9},{9,8},{10,11... | collective-permute-start | bytes 3145736 | tf_op jit(solution)/shard_map/ppermute | solution.py:322
  77.6 20.3 %collective-permute-start.12 = (bf16[256,1536]{1,0:T(8,128)(2,1)}, bf16[256,1536]{1,0:T(8,128)(2,1)}, u32[]{:S(2)}, u32[]{:S(2)}) collective-permute-start(bf16[256,1536]{1,0:T(8,128)(2,1)} %get-tuple-element.453), channel_id=1, source_target_pairs={{0,4},{4,0},{1,5},{5,1},{2,6},{6,2},{3,7},{7,3},{8,12},{12,8},{9,1... | collective-permute-start | bytes 2359304 | tf_op jit(solution)/shard_map/ppermute | solution.py:322
  109.3 30.8 %collective-permute-start.13 = (bf16[1024,512]{1,0:T(8,128)(2,1)}, bf16[1024,512]{1,0:T(8,128)(2,1)}, u32[]{:S(2)}, u32[]{:S(2)}) collective-permute-start(bf16[1024,512]{1,0:T(8,128)(2,1)} %get-tuple-element.481.refs_0_), channel_id=1, source_target_pairs={{0,2},{2,0},{1,3},{3,1},{4,6},{6,4},{5,7},{7,5},{8,10},{10,8},{9,1... | collective-permute-start | bytes 3145736 | tf_op jit(solution)/shard_map/ppermute | solution.py:322
  110.8 29.3 %collective-permute-start.14 = (bf16[1024,512]{1,0:T(8,128)(2,1)}, bf16[1024,512]{1,0:T(8,128)(2,1)}, u32[]{:S(2)}, u32[]{:S(2)}) collective-permute-start(bf16[1024,512]{1,0:T(8,128)(2,1)} %get-tuple-element.481.refs_0_), channel_id=1, source_target_pairs={{0,4},{4,0},{1,5},{5,1},{2,6},{6,2},{3,7},{7,3},{8,12},{12,8},{9,1... | collective-permute-start | bytes 3145736 | tf_op jit(solution)/shard_map/ppermute | solution.py:322
  112.3 27.9 %collective-permute-start.15 = (bf16[1024,512]{1,0:T(8,128)(2,1)}, bf16[1024,512]{1,0:T(8,128)(2,1)}, u32[]{:S(2)}, u32[]{:S(2)}) collective-permute-start(bf16[1024,512]{1,0:T(8,128)(2,1)} %get-tuple-element.481.refs_0_), channel_id=1, source_target_pairs={{0,1},{1,0},{2,3},{3,2},{4,5},{5,4},{6,7},{7,6},{8,9},{9,8},{10,11... | collective-permute-start | bytes 3145736 | tf_op jit(solution)/shard_map/ppermute | solution.py:322
  143.4 14.9 %collective-permute-start.17 = (bf16[2048,512]{1,0:T(8,128)(2,1)}, bf16[2048,512]{1,0:T(8,128)(2,1)}, u32[]{:S(2)}, u32[]{:S(2)}) collective-permute-start(bf16[2048,512]{1,0:T(8,128)(2,1)} %convolution_convert_fusion), channel_id=1, source_target_pairs={{0,1},{1,0},{2,3},{3,2},{4,5},{5,4},{6,7},{7,6},{8,9},{9,8},{10,11... | collective-permute-start | bytes 6291464 | tf_op jit(solution)/shard_map/ppermute | solution.py:322
  146.9 14.0 %collective-permute-start.16 = (bf16[2048,512]{1,0:T(8,128)(2,1)}, bf16[2048,512]{1,0:T(8,128)(2,1)}, u32[]{:S(2)}, u32[]{:S(2)}) collective-permute-start(bf16[2048,512]{1,0:T(8,128)(2,1)} %convolution_convert_fusion.1), channel_id=1, source_target_pairs={{0,1},{1,0},{2,3},{3,2},{4,5},{5,4},{6,7},{7,6},{8,9},{9,8},{10,11... | collective-permute-start | bytes 6291464 | tf_op jit(solution)/shard_map/ppermute | solution.py:322
  146.9 245.7 %reduce-scatter.6.cloned.1.call-start = ((), (), s32[]{:S(2)}) async-start(), calls=%async_computation.8 | async-start | bytes 3932160 | tf_op jit(solution)/shard_map/reduce_scatter | solution.py:446
  149.4 17.8 %collective-permute-start.18 = (bf16[1024,512]{1,0:T(8,128)(2,1)}, bf16[1024,512]{1,0:T(8,128)(2,1)}, u32[]{:S(2)}, u32[]{:S(2)}) collective-permute-start(bf16[1024,512]{1,0:T(8,128)(2,1)} %collective-permute-done.14.refs_0_), channel_id=1, source_target_pairs={{0,1},{1,0},{2,3},{3,2},{4,5},{5,4},{6,7},{7,6},{8,9},{9,8},{10,11... | collective-permute-start | bytes 3145736 | tf_op jit(solution)/shard_map/ppermute | solution.py:322
  151.3 14.9 %collective-permute-start.19 = (bf16[512,512]{1,0:T(8,128)(2,1)}, bf16[512,512]{1,0:T(8,128)(2,1)}, u32[]{:S(2)}, u32[]{:S(2)}) collective-permute-start(bf16[512,512]{1,0:T(8,128)(2,1)} %slice.236), channel_id=1, source_target_pairs={{0,4},{4,0},{1,5},{5,1},{2,6},{6,2},{3,7},{7,3},{8,12},{12,8},{9,1... | collective-permute-start | bytes 1572872 | tf_op jit(solution)/shard_map/ppermute | solution.py:322
  152.9 14.3 %collective-permute-start.20 = (bf16[512,512]{1,0:T(8,128)(2,1)}, bf16[512,512]{1,0:T(8,128)(2,1)}, u32[]{:S(2)}, u32[]{:S(2)}) collective-permute-start(bf16[512,512]{1,0:T(8,128)(2,1)} %slice.237), channel_id=1, source_target_pairs={{0,2},{2,0},{1,3},{3,1},{4,6},{6,4},{5,7},{7,5},{8,10},{10,8},{9,1... | collective-permute-start | bytes 1572872 | tf_op jit(solution)/shard_map/ppermute | solution.py:322
  169.4 25.9 %collective-permute-start.22 = (bf16[2,512,512]{2,1,0:T(8,128)(2,1)}, bf16[2,512,512]{2,1,0:T(8,128)(2,1)}, u32[]{:S(2)}, u32[]{:S(2)}) collective-permute-start(bf16[2,512,512]{2,1,0:T(8,128)(2,1)} %pad_maximum_fusion.7), channel_id=1, source_target_pairs={{0,4},{4,0},{1,5},{5,1},{2,6},{6,2},{3,7},{7,3},{8,12},{12,8},{9,1... | collective-permute-start | bytes 3145736 | tf_op jit(solution)/shard_map/ppermute | solution.py:322
  170.2 25.5 %collective-permute-start.23 = (bf16[2,512,512]{2,1,0:T(8,128)(2,1)}, bf16[2,512,512]{2,1,0:T(8,128)(2,1)}, u32[]{:S(2)}, u32[]{:S(2)}) collective-permute-start(bf16[2,512,512]{2,1,0:T(8,128)(2,1)} %pad_maximum_fusion.8), channel_id=1, source_target_pairs={{0,2},{2,0},{1,3},{3,1},{4,6},{6,4},{5,7},{7,5},{8,10},{10,8},{9,1... | collective-permute-start | bytes 3145736 | tf_op jit(solution)/shard_map/ppermute | solution.py:322
  198.5 13.2 %collective-permute-start.25 = (bf16[512,512]{1,0:T(8,128)(2,1)S(1)}, bf16[512,512]{1,0:T(8,128)(2,1)S(1)}, u32[]{:S(2)}, u32[]{:S(2)}) collective-permute-start(bf16[512,512]{1,0:T(8,128)(2,1)S(1)} %get-tuple-element.839), channel_id=1, source_target_pairs={{0,2},{2,0},{1,3},{3,1},{4,6},{6,4},{5,7},{7,5},{8,10},{10,8},{9,1... | collective-permute-start | bytes 1572872 | tf_op jit(solution)/shard_map/ppermute | solution.py:322
  199.1 13.0 %collective-permute-start.26 = (bf16[512,512]{1,0:T(8,128)(2,1)S(1)}, bf16[512,512]{1,0:T(8,128)(2,1)S(1)}, u32[]{:S(2)}, u32[]{:S(2)}) collective-permute-start(bf16[512,512]{1,0:T(8,128)(2,1)S(1)} %get-tuple-element.802), channel_id=1, source_target_pairs={{0,4},{4,0},{1,5},{5,1},{2,6},{6,2},{3,7},{7,3},{8,12},{12,8},{9,1... | collective-permute-start | bytes 1572872 | tf_op jit(solution)/shard_map/ppermute | solution.py:322
  215.0 23.4 %collective-permute-start.27 = (bf16[1024,512]{1,0:T(8,128)(2,1)S(1)}, bf16[1024,512]{1,0:T(8,128)(2,1)S(1)}, u32[]{:S(2)}, u32[]{:S(2)}) collective-permute-start(bf16[1024,512]{1,0:T(8,128)(2,1)S(1)} %get-tuple-element.610.refs_0_), channel_id=1, source_target_pairs={{0,2},{2,0},{1,3},{3,1},{4,6},{6,4},{5,7},{7,5},{8,10},{10,8},{9,1... | collective-permute-start | bytes 3145736 | tf_op jit(solution)/shard_map/ppermute | solution.py:322
  216.4 23.1 %collective-permute-start.28 = (bf16[1024,512]{1,0:T(8,128)(2,1)S(1)}, bf16[1024,512]{1,0:T(8,128)(2,1)}, u32[]{:S(2)}, u32[]{:S(2)}) collective-permute-start(bf16[1024,512]{1,0:T(8,128)(2,1)S(1)} %get-tuple-element.610.refs_0_), channel_id=1, source_target_pairs={{0,4},{4,0},{1,5},{5,1},{2,6},{6,2},{3,7},{7,3},{8,12},{12,8},{9,1... | collective-permute-start | bytes 3145736 | tf_op jit(solution)/shard_map/ppermute | solution.py:322
  217.7 21.8 %collective-permute-start.29 = (bf16[1024,512]{1,0:T(8,128)(2,1)S(1)}, bf16[1024,512]{1,0:T(8,128)(2,1)S(1)}, u32[]{:S(2)}, u32[]{:S(2)}) collective-permute-start(bf16[1024,512]{1,0:T(8,128)(2,1)S(1)} %get-tuple-element.610.refs_0_), channel_id=1, source_target_pairs={{0,1},{1,0},{2,3},{3,2},{4,5},{5,4},{6,7},{7,6},{8,9},{9,8},{10,11... | collective-permute-start | bytes 3145736 | tf_op jit(solution)/shard_map/ppermute | solution.py:322
  239.5 18.5 %collective-permute-start.30 = (bf16[1024,512]{1,0:T(8,128)(2,1)}, bf16[1024,512]{1,0:T(8,128)(2,1)}, u32[]{:S(2)}, u32[]{:S(2)}) collective-permute-start(bf16[1024,512]{1,0:T(8,128)(2,1)} %collective-permute-done.28.refs_0_), channel_id=1, source_target_pairs={{0,1},{1,0},{2,3},{3,2},{4,5},{5,4},{6,7},{7,6},{8,9},{9,8},{10,11... | collective-permute-start | bytes 3145736 | tf_op jit(solution)/shard_map/ppermute | solution.py:322
  242.7 14.2 %collective-permute-start.31 = (bf16[512,512]{1,0:T(8,128)(2,1)}, bf16[512,512]{1,0:T(8,128)(2,1)}, u32[]{:S(2)}, u32[]{:S(2)}) collective-permute-start(bf16[512,512]{1,0:T(8,128)(2,1)} %slice.246), channel_id=1, source_target_pairs={{0,4},{4,0},{1,5},{5,1},{2,6},{6,2},{3,7},{7,3},{8,12},{12,8},{9,1... | collective-permute-start | bytes 1572872 | tf_op jit(solution)/shard_map/ppermute | solution.py:322
  244.1 13.9 %collective-permute-start.32 = (bf16[512,512]{1,0:T(8,128)(2,1)}, bf16[512,512]{1,0:T(8,128)(2,1)}, u32[]{:S(2)}, u32[]{:S(2)}) collective-permute-start(bf16[512,512]{1,0:T(8,128)(2,1)} %slice.247), channel_id=1, source_target_pairs={{0,2},{2,0},{1,3},{3,1},{4,6},{6,4},{5,7},{7,5},{8,10},{10,8},{9,1... | collective-permute-start | bytes 1572872 | tf_op jit(solution)/shard_map/ppermute | solution.py:322
  328.7 179.6 %reduce-scatter.8.cloned.1.call-start = ((), (), s32[]{:S(2)}) async-start(), calls=%async_computation.9 | async-start | bytes 3932160 | tf_op jit(solution)/shard_map/reduce_scatter | solution.py:446
  349.2 25.3 %collective-permute-start.37 = (bf16[2,512,512]{2,1,0:T(8,128)(2,1)S(1)}, bf16[2,512,512]{2,1,0:T(8,128)(2,1)S(1)}, u32[]{:S(2)}, u32[]{:S(2)}) collective-permute-start(bf16[2,512,512]{2,1,0:T(8,128)(2,1)S(1)} %pad_maximum_fusion.9), channel_id=1, source_target_pairs={{0,4},{4,0},{1,5},{5,1},{2,6},{6,2},{3,7},{7,3},{8,12},{12,8},{9,1... | collective-permute-start | bytes 3145736 | tf_op jit(solution)/shard_map/ppermute | solution.py:322
  350.8 24.9 %collective-permute-start.38 = (bf16[2,512,512]{2,1,0:T(8,128)(2,1)S(1)}, bf16[2,512,512]{2,1,0:T(8,128)(2,1)S(1)}, u32[]{:S(2)}, u32[]{:S(2)}) collective-permute-start(bf16[2,512,512]{2,1,0:T(8,128)(2,1)S(1)} %pad_maximum_fusion.10), channel_id=1, source_target_pairs={{0,2},{2,0},{1,3},{3,1},{4,6},{6,4},{5,7},{7,5},{8,10},{10,8},{9,1... | collective-permute-start | bytes 3145736 | tf_op jit(solution)/shard_map/ppermute | solution.py:322
  377.3 13.2 %collective-permute-start.39 = (bf16[512,512]{1,0:T(8,128)(2,1)}, bf16[512,512]{1,0:T(8,128)(2,1)}, u32[]{:S(2)}, u32[]{:S(2)}) collective-permute-start(bf16[512,512]{1,0:T(8,128)(2,1)} %get-tuple-element.840), channel_id=1, source_target_pairs={{0,2},{2,0},{1,3},{3,1},{4,6},{6,4},{5,7},{7,5},{8,10},{10,8},{9,1... | collective-permute-start | bytes 1572872 | tf_op jit(solution)/shard_map/ppermute | solution.py:322
  378.8 12.9 %collective-permute-start.40 = (bf16[512,512]{1,0:T(8,128)(2,1)}, bf16[512,512]{1,0:T(8,128)(2,1)}, u32[]{:S(2)}, u32[]{:S(2)}) collective-permute-start(bf16[512,512]{1,0:T(8,128)(2,1)} %get-tuple-element.800), channel_id=1, source_target_pairs={{0,4},{4,0},{1,5},{5,1},{2,6},{6,2},{3,7},{7,3},{8,12},{12,8},{9,1... | collective-permute-start | bytes 1572872 | tf_op jit(solution)/shard_map/ppermute | solution.py:322
  391.8 167.0 %reduce-scatter.12.cloned.1.call-start = ((), (), s32[]{:S(2)}) async-start(), calls=%async_computation.11 | async-start | bytes 3932160 | tf_op jit(solution)/shard_map/reduce_scatter | solution.py:446
  411.0 24.8 %collective-permute-start.43 = (bf16[1024,512]{1,0:T(8,128)(2,1)}, bf16[1024,512]{1,0:T(8,128)(2,1)}, u32[]{:S(2)}, u32[]{:S(2)}) collective-permute-start(bf16[1024,512]{1,0:T(8,128)(2,1)} %get-tuple-element.630.refs_0_), channel_id=1, source_target_pairs={{0,2},{2,0},{1,3},{3,1},{4,6},{6,4},{5,7},{7,5},{8,10},{10,8},{9,1... | collective-permute-start | bytes 3145736 | tf_op jit(solution)/shard_map/ppermute | solution.py:322
  411.6 24.4 %collective-permute-start.44 = (bf16[1024,512]{1,0:T(8,128)(2,1)}, bf16[1024,512]{1,0:T(8,128)(2,1)S(1)}, u32[]{:S(2)}, u32[]{:S(2)}) collective-permute-start(bf16[1024,512]{1,0:T(8,128)(2,1)} %get-tuple-element.630.refs_0_), channel_id=1, source_target_pairs={{0,4},{4,0},{1,5},{5,1},{2,6},{6,2},{3,7},{7,3},{8,12},{12,8},{9,1... | collective-permute-start | bytes 3145736 | tf_op jit(solution)/shard_map/ppermute | solution.py:322
  412.2 23.9 %collective-permute-start.45 = (bf16[1024,512]{1,0:T(8,128)(2,1)}, bf16[1024,512]{1,0:T(8,128)(2,1)}, u32[]{:S(2)}, u32[]{:S(2)}) collective-permute-start(bf16[1024,512]{1,0:T(8,128)(2,1)} %get-tuple-element.630.refs_0_), channel_id=1, source_target_pairs={{0,1},{1,0},{2,3},{3,2},{4,5},{5,4},{6,7},{7,6},{8,9},{9,8},{10,11... | collective-permute-start | bytes 3145736 | tf_op jit(solution)/shard_map/ppermute | solution.py:322
  441.7 148.9 %reduce-scatter.10.cloned.1.call-start = ((), (), s32[]{:S(2)}) async-start(), calls=%async_computation.10 | async-start | bytes 1310720 | tf_op jit(solution)/shard_map/reduce_scatter | solution.py:446
  447.0 27.5 %collective-permute-start.47 = (bf16[2048,512]{1,0:T(8,128)(2,1)}, bf16[2048,512]{1,0:T(8,128)(2,1)}, u32[]{:S(2)}, u32[]{:S(2)}) collective-permute-start(bf16[2048,512]{1,0:T(8,128)(2,1)} %convolution_convert_fusion.5), channel_id=1, source_target_pairs={{0,1},{1,0},{2,3},{3,2},{4,5},{5,4},{6,7},{7,6},{8,9},{9,8},{10,11... | collective-permute-start | bytes 6291464 | tf_op jit(solution)/shard_map/ppermute | solution.py:322
  447.0 27.5 %collective-permute-start.48 = (bf16[2048,512]{1,0:T(8,128)(2,1)}, bf16[2048,512]{1,0:T(8,128)(2,1)}, u32[]{:S(2)}, u32[]{:S(2)}) collective-permute-start(bf16[2048,512]{1,0:T(8,128)(2,1)} %convolution_convert_fusion.4), channel_id=1, source_target_pairs={{0,1},{1,0},{2,3},{3,2},{4,5},{5,4},{6,7},{7,6},{8,9},{9,8},{10,11... | collective-permute-start | bytes 6291464 | tf_op jit(solution)/shard_map/ppermute | solution.py:322
  447.5 14.0 %collective-permute-start.52 = (bf16[1024,512]{1,0:T(8,128)(2,1)}, bf16[1024,512]{1,0:T(8,128)(2,1)}, u32[]{:S(2)}, u32[]{:S(2)}) collective-permute-start(bf16[1024,512]{1,0:T(8,128)(2,1)} %collective-permute-done.43.refs_2_), channel_id=1, source_target_pairs={{0,1},{1,0},{2,3},{3,2},{4,5},{5,4},{6,7},{7,6},{8,9},{9,8},{10,11... | collective-permute-start | bytes 3145736 | tf_op jit(solution)/shard_map/ppermute | solution.py:322
  447.5 27.0 %collective-permute-start.49 = (bf16[1024,512]{1,0:T(8,128)(2,1)S(1)}, bf16[1024,512]{1,0:T(8,128)(2,1)}, u32[]{:S(2)}, u32[]{:S(2)}) collective-permute-start(bf16[1024,512]{1,0:T(8,128)(2,1)S(1)} %collective-permute-done.44.refs_0_), channel_id=1, source_target_pairs={{0,1},{1,0},{2,3},{3,2},{4,5},{5,4},{6,7},{7,6},{8,9},{9,8},{10,11... | collective-permute-start | bytes 3145736 | tf_op jit(solution)/shard_map/ppermute | solution.py:322
  460.9 13.3 %collective-permute-start.50 = (bf16[512,512]{1,0:T(8,128)(2,1)}, bf16[512,512]{1,0:T(8,128)(2,1)}, u32[]{:S(2)}, u32[]{:S(2)}) collective-permute-start(bf16[512,512]{1,0:T(8,128)(2,1)} %slice.260), channel_id=1, source_target_pairs={{0,4},{4,0},{1,5},{5,1},{2,6},{6,2},{3,7},{7,3},{8,12},{12,8},{9,1... | collective-permute-start | bytes 1572872 | tf_op jit(solution)/shard_map/ppermute | solution.py:322
  461.5 13.0 %collective-permute-start.51 = (bf16[512,512]{1,0:T(8,128)(2,1)}, bf16[512,512]{1,0:T(8,128)(2,1)}, u32[]{:S(2)}, u32[]{:S(2)}) collective-permute-start(bf16[512,512]{1,0:T(8,128)(2,1)} %slice.261), channel_id=1, source_target_pairs={{0,2},{2,0},{1,3},{3,1},{4,6},{6,4},{5,7},{7,5},{8,10},{10,8},{9,1... | collective-permute-start | bytes 1572872 | tf_op jit(solution)/shard_map/ppermute | solution.py:322
  476.7 13.2 %collective-permute-start.53 = (bf16[1024,512]{1,0:T(8,128)(2,1)S(1)}, bf16[1024,512]{1,0:T(8,128)(2,1)}, u32[]{:S(2)}, u32[]{:S(2)}) collective-permute-start(bf16[1024,512]{1,0:T(8,128)(2,1)S(1)} %constant_dynamic-update-slice_fusion.6.refs_2_), channel_id=1, source_target_pairs={{0,1},{1,0},{2,3},{3,2},{4,5},{5,4},{6,7},{7,6},{8,9},{9,8},{10,11... | collective-permute-start | bytes 3145736 | tf_op jit(solution)/shard_map/ppermute | solution.py:322
  508.3 33.8 %collective-permute-start.54 = (bf16[2,512,512]{2,1,0:T(8,128)(2,1)}, bf16[2,512,512]{2,1,0:T(8,128)(2,1)S(1)}, u32[]{:S(2)}, u32[]{:S(2)}) collective-permute-start(bf16[2,512,512]{2,1,0:T(8,128)(2,1)} %pad_maximum_fusion.11), channel_id=1, source_target_pairs={{0,4},{4,0},{1,5},{5,1},{2,6},{6,2},{3,7},{7,3},{8,12},{12,8},{9,1... | collective-permute-start | bytes 3145736 | tf_op jit(solution)/shard_map/ppermute | solution.py:322
  509.7 32.4 %collective-permute-start.55 = (bf16[2,512,512]{2,1,0:T(8,128)(2,1)}, bf16[2,512,512]{2,1,0:T(8,128)(2,1)S(1)}, u32[]{:S(2)}, u32[]{:S(2)}) collective-permute-start(bf16[2,512,512]{2,1,0:T(8,128)(2,1)} %pad_maximum_fusion.12), channel_id=1, source_target_pairs={{0,2},{2,0},{1,3},{3,1},{4,6},{6,4},{5,7},{7,5},{8,10},{10,8},{9,1... | collective-permute-start | bytes 3145736 | tf_op jit(solution)/shard_map/ppermute | solution.py:322
  512.2 29.9 %collective-permute-start.56 = (bf16[256,768]{1,0:T(8,128)(2,1)S(1)}, bf16[256,768]{1,0:T(8,128)(2,1)S(1)}, u32[]{:S(2)}, u32[]{:S(2)}) collective-permute-start(bf16[256,768]{1,0:T(8,128)(2,1)S(1)} %constant_dynamic-slice_fusion.3), channel_id=1, source_target_pairs={{0,4},{4,0},{1,5},{5,1},{2,6},{6,2},{3,7},{7,3},{8,12},{12,8},{9,1... | collective-permute-start | bytes 1179656 | tf_op jit(solution)/shard_map/ppermute | solution.py:322
  543.9 14.8 %collective-permute-start.57 = (bf16[512,512]{1,0:T(8,128)(2,1)S(1)}, bf16[512,512]{1,0:T(8,128)(2,1)}, u32[]{:S(2)}, u32[]{:S(2)}) collective-permute-start(bf16[512,512]{1,0:T(8,128)(2,1)S(1)} %get-tuple-element.841), channel_id=1, source_target_pairs={{0,2},{2,0},{1,3},{3,1},{4,6},{6,4},{5,7},{7,5},{8,10},{10,8},{9,1... | collective-permute-start | bytes 1572872 | tf_op jit(solution)/shard_map/ppermute | solution.py:322
  545.6 13.2 %collective-permute-start.58 = (bf16[512,512]{1,0:T(8,128)(2,1)S(1)}, bf16[512,512]{1,0:T(8,128)(2,1)}, u32[]{:S(2)}, u32[]{:S(2)}) collective-permute-start(bf16[512,512]{1,0:T(8,128)(2,1)S(1)} %get-tuple-element.798), channel_id=1, source_target_pairs={{0,4},{4,0},{1,5},{5,1},{2,6},{6,2},{3,7},{7,3},{8,12},{12,8},{9,1... | collective-permute-start | bytes 1572872 | tf_op jit(solution)/shard_map/ppermute | solution.py:322
  546.9 11.8 %collective-permute-start.59 = (f32[6,128]{1,0:T(8,128)S(1)}, f32[6,128]{1,0:T(8,128)S(1)}, u32[]{:S(2)}, u32[]{:S(2)}) collective-permute-start(f32[6,128]{1,0:T(8,128)S(1)} %pad_maximum_fusion.17), channel_id=1, source_target_pairs={{0,4},{4,0},{1,5},{5,1},{2,6},{6,2},{3,7},{7,3},{8,12},{12,8},{9,1... | collective-permute-start | bytes 9224 | tf_op jit(solution)/shard_map/ppermute | solution.py:322
  547.6 97.0 %reduce-scatter.14.cloned.1.call-start = ((), (), s32[]{:S(2)}) async-start(), calls=%async_computation.12 | async-start | bytes 3932160 | tf_op jit(solution)/shard_map/reduce_scatter | solution.py:446
  564.3 13.0 %collective-permute-start.64 = (bf16[2048,512]{1,0:T(8,128)(2,1)}, bf16[2048,512]{1,0:T(8,128)(2,1)}, u32[]{:S(2)}, u32[]{:S(2)}) collective-permute-start(bf16[2048,512]{1,0:T(8,128)(2,1)} %convolution_convert_fusion.2), channel_id=1, source_target_pairs={{0,1},{1,0},{2,3},{3,2},{4,5},{5,4},{6,7},{7,6},{8,9},{9,8},{10,11... | collective-permute-start | bytes 6291464 | tf_op jit(solution)/shard_map/ppermute | solution.py:322
  568.7 14.0 %collective-permute-start.63 = (bf16[2048,512]{1,0:T(8,128)(2,1)}, bf16[2048,512]{1,0:T(8,128)(2,1)}, u32[]{:S(2)}, u32[]{:S(2)}) collective-permute-start(bf16[2048,512]{1,0:T(8,128)(2,1)} %convolution_convert_fusion.3), channel_id=1, source_target_pairs={{0,1},{1,0},{2,3},{3,2},{4,5},{5,4},{6,7},{7,6},{8,9},{9,8},{10,11... | collective-permute-start | bytes 6291464 | tf_op jit(solution)/shard_map/ppermute | solution.py:322
  573.7 17.0 %collective-permute-start.62 = (bf16[256,768]{1,0:T(8,128)(2,1)S(1)}, bf16[256,768]{1,0:T(8,128)(2,1)S(1)}, u32[]{:S(2)}, u32[]{:S(2)}) collective-permute-start(bf16[256,768]{1,0:T(8,128)(2,1)S(1)} %constant_dynamic-slice_fusion.2), channel_id=1, source_target_pairs={{0,4},{4,0},{1,5},{5,1},{2,6},{6,2},{3,7},{7,3},{8,12},{12,8},{9,1... | collective-permute-start | bytes 1179656 | tf_op jit(solution)/shard_map/ppermute | solution.py:322
  592.4 24.2 %collective-permute-start.66 = (bf16[2,512,512]{2,1,0:T(8,128)(2,1)S(1)}, bf16[2,512,512]{2,1,0:T(8,128)(2,1)S(1)}, u32[]{:S(2)}, u32[]{:S(2)}) collective-permute-start(bf16[2,512,512]{2,1,0:T(8,128)(2,1)S(1)} %pad_maximum_fusion.13), channel_id=1, source_target_pairs={{0,4},{4,0},{1,5},{5,1},{2,6},{6,2},{3,7},{7,3},{8,12},{12,8},{9,1... | collective-permute-start | bytes 3145736 | tf_op jit(solution)/shard_map/ppermute | solution.py:322
  593.6 23.0 %collective-permute-start.67 = (bf16[2,512,512]{2,1,0:T(8,128)(2,1)}, bf16[2,512,512]{2,1,0:T(8,128)(2,1)S(1)}, u32[]{:S(2)}, u32[]{:S(2)}) collective-permute-start(bf16[2,512,512]{2,1,0:T(8,128)(2,1)} %pad_maximum_fusion.14), channel_id=1, source_target_pairs={{0,2},{2,0},{1,3},{3,1},{4,6},{6,4},{5,7},{7,5},{8,10},{10,8},{9,1... | collective-permute-start | bytes 3145736 | tf_op jit(solution)/shard_map/ppermute | solution.py:322
  (78 other events, 474.6 us)
Sparse Core Ops, SparseCore 0:
  27.2 82.0 all-gather.3
  110.9 62.0 all-gather.5
  175.1 113.9 all-gather.7
  328.8 58.6 reduce-scatter.5
  391.9 58.0 reduce-scatter.7
  452.1 60.2 reduce-scatter.11
  547.7 24.5 reduce-scatter.9
  574.8 58.9 reduce-scatter.13

commit v4 on v3

--- a/solution.py
+++ b/solution.py
@@ -325,6 +325,9 @@
 light = pl.CostEstimate(flops=0, bytes_accessed=0, transcendentals=0)
 
 
+heavy = light
+
+
 class Line:
     def __init__(self):
         self.token = jnp.zeros((8, 128), jnp.float32)
@@ -462,49 +465,122 @@
 vmem = pltpu.CompilerParams(vmem_limit_bytes=56 * 1024 * 1024)
 
 
-def fold_dot(operand, weight, place, index, column):
-    rows, width = weight.shape[0] // 4, operand.shape[1]
-    block = lax.dynamic_slice(
-        weight, ((place ^ index) * rows, jnp.int32(column * width)), (rows, width)
-    )
-    return product_nt(operand, block)
+def fold_turn(near_ref, far_ref, near_turned, far_turned):
+    @pl.when(pl.program_id(0) == 0)
+    def turn():
+        near_turned[...] = near_ref[...].T
+        far_turned[...] = far_ref[...].T
+
+
+def fold_sent_kernel(
+    place_ref, operand_ref, near_ref, far_ref, near_out, far_out, near_turned, far_turned
+):
+    fold_turn(near_ref, far_ref, near_turned, far_turned)
+    for weight_ref, out_ref in ((near_turned, near_out), (far_turned, far_out)):
+        out_ref[...] = product_nn(operand_ref[...], weight_ref[...]).astype(out_ref.dtype)
+
+
+def fold_held_kernel(
+    place_ref, operand_ref, near_ref, far_ref, near_got, far_got,
+    upper_send, upper_keep, lower_send, lower_keep, near_turned, far_turned,
+):
+    fold_turn(near_ref, far_ref, near_turned, far_turned)
+    low = upper_send.dtype
+    near = product_nn(operand_ref[...], near_turned[...]) + near_got[...].astype(jnp.float32)
+    far = product_nn(operand_ref[...], far_turned[...]) + far_got[...].astype(jnp.float32)
+    near, far = near.astype(low), far.astype(low)
+    step = pl.program_id(0)
+
+    @pl.when(step == 0)
+    def first():
+        upper_send[0] = near
+        upper_send[1] = far
+
+    @pl.when(step == 1)
+    def second():
+        upper_keep[0] = near
+        upper_keep[1] = far
+
+    @pl.when(step >= 2)
+    def third():
+        lower_send[...] = far
+        lower_keep[...] = near
+
+
+def fold_rows(i):
+    return (1 - i % 2) * 2 + i // 2
+
+
+def fold_specs(tile, width, rows, column, near, far):
+    return [
+        pl.BlockSpec((tile, width), lambda i, p: (fold_rows(i), 0)),
+        pl.BlockSpec((rows, width), lambda i, p: (p[0] ^ near, column)),
+        pl.BlockSpec((rows, width), lambda i, p: (p[0] ^ far, column)),
+    ]
 
 
 def fold_sent(operand, weight, place, column=0):
-    return tuple(
-        flip(fold_dot(operand, weight, place, index, column).astype(jnp.bfloat16), "core")
-        for index in (3, 1)
-    )
-
-
-def fold_held(operand, weight, place, far_got, near_got, column=0):
-    low = jnp.bfloat16
-    far = (fold_dot(operand, weight, place, 2, column) + far_got).astype(low)
-    near = (fold_dot(operand, weight, place, 0, column) + near_got).astype(low)
-    count = far.shape[0] // 2
-    half = count // 2
-    upper = jnp.stack([near[count : count + half], far[count : count + half]])
-    lower = jnp.stack([far[half:count], far[count + half :]])
-    return (near, far, upper, lower)
-
-
-def fold_begin(operand, weight, place, column=0):
-    return fold_held(operand, weight, place, *fold_sent(operand, weight, place, column), column)
-
-
-def fold_cross(near, far, upper, lower):
-    return (near, far, flip(upper, "x"), flip(lower, "y"))
-
-
-def fold_close(near, far, upper, lower):
+    count, width = operand.shape
+    rows, tile = weight.shape[0] // 4, count // 4
+    out = pl.BlockSpec((tile, rows), lambda i, p: (fold_rows(i), 0))
+    near, far = pl.pallas_call(
+        fold_sent_kernel,
+        grid_spec=pltpu.PrefetchScalarGridSpec(
+            num_scalar_prefetch=1,
+            grid=(4,),
+            in_specs=fold_specs(tile, width, rows, column, 1, 3),
+            out_specs=[out, out],
+            scratch_shapes=[pltpu.VMEM((width, rows), jnp.bfloat16)] * 2,
+        ),
+        out_shape=[jax.ShapeDtypeStruct((count, rows), jnp.bfloat16)] * 2,
+        compiler_params=vmem,
+        cost_estimate=light,
+    )(place.reshape(1), operand, weight, weight)
+    return (near, far)
+
+
+def fold_swap(operand, weight, place, column=0):
+    return tuple(flip(v, "core") for v in fold_sent(operand, weight, place, column))
+
+
+def fold_held(operand, weight, place, near_got, far_got, column=0):
+    count, width = operand.shape
+    rows, tile = weight.shape[0] // 4, count // 4
+    got = pl.BlockSpec((tile, rows), lambda i, p: (fold_rows(i), 0))
+    whole = pl.BlockSpec((2, tile, rows), lambda i, p: (0, 0, 0))
+    late = pl.BlockSpec((tile, rows), lambda i, p: (jnp.where(i < 3, 1, 0), 0))
+    shape = jax.ShapeDtypeStruct
+    return pl.pallas_call(
+        fold_held_kernel,
+        grid_spec=pltpu.PrefetchScalarGridSpec(
+            num_scalar_prefetch=1,
+            grid=(4,),
+            in_specs=fold_specs(tile, width, rows, column, 0, 2) + [got, got],
+            out_specs=[whole, whole, late, late],
+            scratch_shapes=[pltpu.VMEM((width, rows), jnp.bfloat16)] * 2,
+        ),
+        out_shape=[shape((2, tile, rows), jnp.bfloat16)] * 2
+        + [shape((2 * tile, rows), jnp.bfloat16)] * 2,
+        compiler_params=vmem,
+        cost_estimate=light,
+    )(place.reshape(1), operand, weight, weight, near_got, far_got)
+
+
+def fold_cross(upper_send, upper_keep, lower_send, lower_keep):
+    return (flip(upper_send, "x"), upper_keep, flip(lower_send, "y"), lower_keep)
+
+
+def fold_close(upper, upper_keep, lower, lower_keep):
     low, wide = jnp.bfloat16, jnp.float32
-    count = far.shape[0] // 2
-    half = count // 2
-    upper_near = near[:half].astype(wide) + upper[0]
-    upper_far = (far[:half].astype(wide) + upper[1]).astype(low)
-    lower_own = near[half:count].astype(wide) + lower[0]
-    lower_other = (near[count + half :].astype(wide) + lower[1]).astype(low)
-    return (upper_near, flip(upper_far, "y"), lower_own, flip(lower_other, "x"))
+    half = lower.shape[0] // 2
+    upper_got = flip((upper_keep[1].astype(wide) + upper[1]).astype(low), "y")
+    lower_got = flip((lower_keep[half:].astype(wide) + lower[half:]).astype(low), "x")
+    return (
+        upper_keep[0].astype(wide) + upper[0],
+        upper_got,
+        lower_keep[:half].astype(wide) + lower[:half],
+        lower_got,
+    )
 
 
 def fold_end(upper_near, upper_got, lower_own, lower_got):
@@ -532,7 +608,7 @@
     )(operand, weight)
 
 
-def dot_grad(first, second, width=None, column=0):
+def dot_grad(first, second, width=None, column=0, cost=light):
     count, rows = first.shape
     width = second.shape[1] if width is None else width
     tile = 512
@@ -546,7 +622,7 @@
         out_specs=pl.BlockSpec((tile, width), lambda i: (i, 0)),
         out_shape=jax.ShapeDtypeStruct((rows, width), jnp.bfloat16),
         compiler_params=vmem,
-        cost_estimate=light,
+        cost_estimate=cost,
     )(first, second)
 
 
@@ -906,38 +982,40 @@
     )
     down_weight = weight_gather(down_rows)
 
-    def open_fourth(keep_pair, give_pair, segment_ids, segment_other, *steps):
+    def open_fourth(grad_out_low, segment_ids, segment_other, *steps):
+        via_out = direct(grad_out_low)
         hidden1 = diagonal(*steps, place, gain_attn, True)
-        pair_rows = rows_of(keep_pair, flip(give_pair, "x"))
         segments = jnp.stack([segment_ids, segment_other])
         cosine, sine, first = jax.vmap(partial(row_tables, head_dim=head_dim))(segments)
         cosine = cosine.reshape(2 * count, head_dim)
         sine = sine.reshape(2 * count, head_dim)
-        return (hidden1, pair_rows, cosine, sine, first)
-
-    hidden1, pair_rows, cosine, sine, first = line.run(
-        open_fourth, keep_pair, give_pair, segment_ids, segment_other, *steps, target
-    )
-    pair_weight = weight_gather(pair_rows)
+        return (hidden1, cosine, sine, first, *via_out)
+
+    hidden1, cosine, sine, first, *via_out = line.run(
+        open_fourth, grad_out_low, segment_ids, segment_other, *steps, target
+    )
+    steps = line.run(
+        lambda *v: relay(*v, place, gain_ffn, False), grad_out_low, *via_out
+    )
     out_column = joint_width // query_width
 
-    def attend(hidden1, first_weight, grad_out_low):
-        via_out = direct(grad_out_low)
+    def attend(hidden1, first_weight, keep_pair, give_pair):
+        got_pair = flip(give_pair, "x")
         joint = dot_in(hidden1, first_weight, joint_width)
         mixed, *kept = attend_fwd(
             joint, cosine, sine, first, gain_query, gain_key, heads, count
         )
-        return (joint, mixed, *kept, *via_out)
-
-    joint, mixed, *rest = line.run(attend, hidden1, first_weight, grad_out_low)
-    kept, via_out = rest[:4], rest[4:]
-
-    def begin_out(mixed, first_weight, grad_out_low, *via_out):
-        steps = relay(grad_out_low, *via_out, place, gain_ffn, False)
-        return (*fold_begin(mixed, first_weight, place, out_column), *steps)
-
-    sums = line.run(begin_out, mixed, first_weight, grad_out_low, *via_out)
-    sums, steps = sums[:4], sums[4:]
+        return (rows_of(keep_pair, got_pair), joint, mixed, *kept)
+
+    pair_rows, joint, mixed, *kept = line.run(attend, hidden1, first_weight, keep_pair, give_pair)
+    pair_weight = weight_gather(pair_rows)
+    near_got, far_got = line.run(
+        lambda m, w: fold_swap(m, w, place, out_column), mixed, first_weight
+    )
+    sums = line.run(
+        lambda *v: fold_held(v[0], v[1], place, *v[2:], out_column),
+        mixed, first_weight, near_got, far_got,
+    )
 
     def cross_out(*values):
         return (*fold_cross(*values[:4]), diagonal(*values[4:], place, gain_ffn, False))
@@ -960,18 +1038,38 @@
     )
     hidden2 = line.run(lambda *v: diagonal(*v, place, gain_ffn, True), *steps, target)
     activated, grad_pair = line.run(ffn, hidden2, pair_weight, grad_act)
+
     gate_grad = line.run(lambda h, g: dot_grad(h, g, hidden_width), hidden2, grad_pair)
     gate_sum = grad_scatter(gate_grad)
-    sums = line.run(lambda g, w: fold_begin(g, w, place), grad_pair, pair_weight)
-    sums = line.run(fold_cross, *sums)
-
-    def close_pair(hidden2, grad_pair, *sums):
-        return (*fold_close(*sums), dot_grad(hidden2, grad_pair, hidden_width, 1))
-
-    *ends, up_grad = line.run(close_pair, hidden2, grad_pair, *sums)
-    gate_sum, = line.enter(gate_sum)
+
+    def sent_pair(hidden2, grad_pair, pair_weight):
+        return (
+            *fold_swap(grad_pair, pair_weight, place),
+            dot_grad(hidden2, grad_pair, hidden_width, 1),
+        )
+
+    near_got, far_got, up_grad = line.run(sent_pair, hidden2, grad_pair, pair_weight)
     up_sum = grad_scatter(up_grad)
-    grad_hidden2 = line.run(fold_end, *ends)
+    sums = line.run(
+        lambda *v: fold_held(v[0], v[1], place, *v[2:]), grad_pair, pair_weight, near_got, far_got
+    )
+
+    def cross_pair(grad_out_full, activated, down_weight, *sums):
+        return (
+            *fold_cross(*sums),
+            dot_grad(grad_out_full, activated),
+            *fold_sent(activated, down_weight, place),
+        )
+
+    *sums, down_grad, near_ffn, far_ffn = line.run(
+        cross_pair, grad_out_full, activated, down_weight, *sums
+    )
+    down_sum = grad_scatter(down_grad)
+
+    def close_pair(near_ffn, far_ffn, *sums):
+        return (*fold_close(*sums), flip(near_ffn, "core"), flip(far_ffn, "core"))
+
+    *ends, near_got, far_got = line.run(close_pair, near_ffn, far_ffn, *sums)
 
     def partial_dots(grad_own, values, inverse, gain_own):
         dots = jnp.sum(grad_own * gain_own * values.astype(jnp.float32) * inverse, axis=1)
@@ -988,77 +1086,85 @@
     def gain_part(grad_own, values, inverse):
         return jnp.sum(grad_own * (values.astype(jnp.float32) * inverse), axis=0).reshape(-1, 128)
 
-    def back_dots(grad_own, values, inverse, gain_own):
+    def back_dots(values, inverse, gain_own, *ends):
+        grad_own = fold_end(*ends)
         return (
+            grad_own,
             partial_dots(grad_own, values, inverse, gain_own),
             gain_part(grad_own, values, inverse),
         )
 
-    dots, gain_ffn_grad = line.run(back_dots, grad_hidden2, resid_low, inverse2, gain_ffn_own)
+    grad_hidden2, dots, gain_ffn_grad = line.run(
+        back_dots, resid_low, inverse2, gain_ffn_own, *ends
+    )
     grad_resid, grad_branch = line.run(
         norm_back, grad_hidden2, resid_low, inverse2, gain_ffn_own, dots, grad_out
     )
 
-    def start_branch(grad_branch, grad_out_full, activated):
-        return (*direct(grad_branch), dot_grad(grad_out_full, activated))
-
-    *via_branch, down_grad = line.run(start_branch, grad_branch, grad_out_full, activated)
-    down_sum = grad_scatter(down_grad)
-
-    def relay_branch(grad_branch, gate_sum, activated, down_weight, *via_branch):
-        steps = relay(grad_branch, *via_branch, place, gain_ffn, False)
-        got = fold_sent(activated, down_weight, place)
-        return (flip(give_rows(gate_sum, across), "x"), *got, *steps)
-
-    got_gate, far_got, near_got, *steps = line.run(
-        relay_branch, grad_branch, gate_sum, activated, down_weight, *via_branch
-    )
-    grad_branch_full = line.run(lambda *v: diagonal(*v, place, gain_ffn, False), *steps)
-
-    def mix_back(grad_branch_full, first_weight, mixed):
+    def start_branch(grad_branch, activated, down_weight, near_got, far_got):
         return (
-            dot_in(grad_branch_full, first_weight, query_width, out_column),
-            dot_grad(grad_branch_full, mixed),
-        )
-
-    grad_mixed, out_grad = line.run(mix_back, grad_branch_full, first_weight, mixed)
-    out_sum = grad_scatter(out_grad)
-    sums_ffn = line.run(
-        lambda *v: fold_held(v[0], v[1], place, *v[2:]), activated, down_weight, far_got, near_got
-    )
-
-    def attend_back(joint, grad_mixed, up_sum, *sums):
+            *direct(grad_branch),
+            *fold_held(activated, down_weight, place, near_got, far_got),
+        )
+
+    via_y, via_x, own_core, *sums_ffn = line.run(
+        start_branch, grad_branch, activated, down_weight, near_got, far_got
+    )
+    gate_sum, = line.enter(gate_sum)
+    steps = line.run(
+        lambda *v: relay(*v, place, gain_ffn, False), grad_branch, via_y, via_x, own_core
+    )
+
+    def mix_back(gate_sum, first_weight, *steps):
+        got = flip(give_rows(gate_sum, across), "x")
+        grad_branch_full = diagonal(*steps, place, gain_ffn, False)
+        grad_mixed = dot_in(grad_branch_full, first_weight, query_width, out_column)
+        return (got, grad_branch_full, grad_mixed)
+
+    got_gate, grad_branch_full, grad_mixed = line.run(mix_back, gate_sum, first_weight, *steps)
+    up_sum, = line.enter(up_sum)
+
+    def attend_back(joint, grad_mixed, grad_branch_full, mixed, *sums):
         grad_joint, head_gains = attend_bwd(
             joint, cosine, sine, first, gain_query, gain_key, kept, grad_mixed, count
         )
+        out_grad = dot_grad(grad_branch_full, mixed, None, 0, heavy)
+        return (grad_joint, head_gains, out_grad, *fold_cross(*sums))
+
+    grad_joint, head_gains, out_grad, *sums_ffn = line.run(
+        attend_back, joint, grad_mixed, grad_branch_full, mixed, *sums_ffn
+    )
+    out_sum = grad_scatter(out_grad)
+
+    down_sum, = line.enter(down_sum)
+
+    def sent_attn(hidden1, grad_joint, first_weight, up_sum, down_sum):
         return (
-            grad_joint,
-            head_gains,
-            *fold_cross(*sums),
+            *fold_swap(grad_joint, first_weight, place),
             flip(give_rows(up_sum, across), "x"),
-        )
-
-    grad_joint, head_gains, *sums_ffn, got_up = line.run(
-        attend_back, joint, grad_mixed, up_sum, *sums_ffn
-    )
-
-    def close_ffn(hidden1, grad_joint, gain_ffn_grad, head_gains, *sums):
+            flip(give_rows(down_sum, across), "x"),
+            dot_grad(hidden1, grad_joint, None, 0, heavy),
+        )
+
+    near_got, far_got, got_up, got_down, attn_grads = line.run(
+        sent_attn, hidden1, grad_joint, first_weight, up_sum, down_sum
+    )
+    attn_sum = grad_scatter(attn_grads)
+    out_sum, = line.enter(out_sum)
+
+    def held_attn(grad_joint, first_weight, near_got, far_got, gain_ffn_grad, head_gains, *sums):
         early = jnp.concatenate([gain_ffn_grad, head_gains], axis=0)
         early = early + flip(early, "x")
-        return (*fold_close(*sums), dot_grad(hidden1, grad_joint), early)
-
-    *ends_ffn, attn_grads, early = line.run(
-        close_ffn, hidden1, grad_joint, gain_ffn_grad, head_gains, *sums_ffn
-    )
-    attn_sum = grad_scatter(attn_grads)
-
-    def fold_attn(grad_joint, first_weight, early, down_sum):
-        early = early + z_flip(early, 1)
-        early = early + z_flip(early, 2)
-        got_down = flip(give_rows(down_sum, across), "x")
-        return (early, got_down, *fold_begin(grad_joint, first_weight, place))
-
-    early, got_down, *sums = line.run(fold_attn, grad_joint, first_weight, early, down_sum)
+        return (
+            early,
+            *fold_held(grad_joint, first_weight, place, near_got, far_got),
+            *fold_close(*sums),
+        )
+
+    early, *sums = line.run(
+        held_attn, grad_joint, first_weight, near_got, far_got, gain_ffn_grad, head_gains, *sums_ffn
+    )
+    sums, ends_ffn = sums[:4], sums[4:]
 
     def join(rows, got, low_cut, high_cut):
         keep = keep_rows(rows, across)[:, low_cut:high_cut]
@@ -1069,51 +1175,67 @@
     def join_all(rows, got):
         return join(rows, got, 0, rows.shape[1])
 
-    def cross_attn(resid, gate_sum, got_gate, up_sum, got_up, out_sum, *values):
+    def cross_attn(early, resid, gate_sum, got_gate, *values):
+        sums = fold_cross(*values[:4])
         output = (live * (resid + fold_end(*values[4:]))).astype(low)
-        return (
-            output,
-            join_all(gate_sum, got_gate),
-            join_all(up_sum, got_up),
-            flip(give_rows(out_sum, across), "x"),
-            *fold_cross(*values[:4]),
-        )
-
-    output, ffgate_grad, up_grad, got_out, *sums = line.run(
-        cross_attn, resid, gate_sum, got_gate, up_sum, got_up, out_sum, *sums, *ends_ffn
-    )
-
-    def close_attn(down_sum, got_down, out_sum, got_out, *sums):
-        return (join_all(down_sum, got_down), join_all(out_sum, got_out), *fold_close(*sums))
-
-    down_part, out_part, *ends = line.run(
-        close_attn, down_sum, got_down, out_sum, got_out, *sums
-    )
-
-    def last_dots(tokens, inverse1, *ends):
+        return (early + z_flip(early, 1), output, join_all(gate_sum, got_gate), *sums)
+
+    early, output, ffgate_grad, *sums = line.run(
+        cross_attn, early, resid, gate_sum, got_gate, *sums, *ends_ffn
+    )
+
+    def close_attn(early, up_sum, got_up, *sums):
+        return (early + z_flip(early, 2), join_all(up_sum, got_up), *fold_close(*sums))
+
+    early, up_grad, *ends = line.run(close_attn, early, up_sum, got_up, *sums)
+
+    def last_dots(tokens, inverse1, out_sum, *ends):
         grad_own = fold_end(*ends)
         late = gain_part(grad_own, tokens, inverse1)
         return (
+            flip(give_rows(out_sum, across), "x"),
             grad_own,
             partial_dots(grad_own, tokens, inverse1, gain_attn_own),
-            late + flip(late, "x"),
-        )
-
-    grad_hidden1, dots, late = line.run(last_dots, tokens, inverse1, *ends)
+            late,
+        )
+
+    got_out, grad_hidden1, dots, late = line.run(last_dots, tokens, inverse1, out_sum, *ends)
 
     def last_norm(grad_hidden1, tokens, inverse1, dots, grad_resid, late):
         grad_tokens, unused = norm_back(
             grad_hidden1, tokens, inverse1, gain_attn_own, dots, grad_resid
         )
-        late = late + z_flip(late, 1)
-        return (grad_tokens, late)
+        return (grad_tokens, late + flip(late, "x"))
 
     grad_tokens, late = line.run(
         last_norm, grad_hidden1, tokens, inverse1, dots, grad_resid, late
     )
-    late, got_attn = line.run(
-        lambda v, s: (v + z_flip(v, 2), flip(give_rows(s, across), "x")), late, attn_sum
-    )
+    attn_sum, = line.enter(attn_sum)
+
+    def last_out(late, attn_sum, out_sum, got_out, down_sum, got_down):
+        got_attn = flip(give_rows(attn_sum, across), "x")
+        late = late + z_flip(late, 1)
+        return (
+            got_attn,
+            late + z_flip(late, 2),
+            join_all(out_sum, got_out),
+            join_all(down_sum, got_down),
+        )
+
+    got_attn, late, out_part, down_part = line.run(
+        last_out, late, attn_sum, out_sum, got_out, down_sum, got_down
+    )
+    blocks = local // 128
+
+    def last_spot(late, early):
+        own = jnp.stack([late, early[:blocks]])
+        spot = lax.dynamic_update_slice_in_dim(
+            jnp.zeros((2, width // 128, 128), jnp.float32), own, offset // 128, 1
+        ).reshape(-1, 128)
+        spot = jnp.concatenate([spot, early[blocks:]], axis=0)
+        spot = spot + flip(spot, "core")
+        return spot + flip(spot, "y")
+
     cuts = (
         0,
         query_width,
@@ -1121,17 +1243,12 @@
         2 * query_width + key_width,
         2 * query_width + 2 * key_width,
     )
-    blocks = local // 128
 
     def last_parts(attn_sum, got_attn, late, early):
-        own = jnp.stack([late, early[:blocks]])
-        spot = lax.dynamic_update_slice_in_dim(
-            jnp.zeros((2, width // 128, 128), jnp.float32), own, offset // 128, 1
-        ).reshape(-1, 128)
-        spot = jnp.concatenate([spot, early[blocks:]], axis=0)
-        spot = spot + flip(spot, "core")
-        spot = spot + flip(spot, "y")
-        return (spot, *[join(attn_sum, got_attn, cuts[i], cuts[i + 1]) for i in range(4)])
+        return (
+            last_spot(late, early),
+            *[join(attn_sum, got_attn, cuts[i], cuts[i + 1]) for i in range(4)],
+        )
 
     spot, *attn_parts = line.run(last_parts, attn_sum, got_attn, late, early)
     lines = width // 128
@@ -1140,7 +1257,7 @@
         grad_tokens,
         spot[:lines].reshape(width),
         spot[lines : 2 * lines].reshape(width),
-        spot[2 * lines],
+        spot[2 * lines] + line.token[0],
         spot[2 * lines + 1],
         *attn_parts,
         out_part,

time: 678 us -> 655 us (0.966)
  matrix products: 77.7 us -> 0 us
  Pallas kernels: 177 us -> 245 us
  waiting for transfers between devices: 226 us -> 209 us
    dot_general x16 -> x0, matrix products: 77.7 us -> none  [product_nt(): lax.dot_general(first, second, (((1,), (1,)), ((), ())), preferred_elemen...]
    pallas_call x0 -> x8, Pallas kernels: none -> 69.4 us  [the longest x4 38.2 us: fold_held(): pl.pallas_call(fold_held_kernel, grid_spec=pltpu.PrefetchScalarGridSpec(n...]
    all_gather x3, waiting for transfers between devices: 23.6 us -> 14 us  [weight_gather(): return lax.all_gather(rows, 'z', axis=0, tiled=True)]
    convert_element_type x4 -> x8, other arithmetic: 7.81 us -> 14.4 us  [the longest x4 7.7 us: fold_close(): (lower_keep[half:].astype(wide) + lower[half:]).astype(low)]
    unnamed x118 -> x104, local copies, waits for them, and re-layouts: 22.3 us -> 22.5 us
  transfers between devices with their start and end apart: 86 -> 86, of which waited for: 43 -> 48; matrix products, arithmetic and copies ran while one was open for 24% -> 15% of each run, Pallas kernels for 21% -> 32%
where the time goes in v4:
time: 655 us; the launch traced here: 649 us
  Pallas kernels  245 us (37%)
  waiting for transfers between devices  209 us (32%)
  other arithmetic  67.3 us (10%)
  starting transfers between devices  63.2 us (10%)
  local copies, waits for them, and re-layouts  49.4 us (8%)
  between operations  15.1 us (2%)
    ppermute x74, waiting for transfers between devices, flip(): return lax.ppermute(values, axis, [(0, 1), (1, 0)])  189 us
    ppermute x74, starting transfers between devices, flip(): return lax.ppermute(values, axis, [(0, 1), (1, 0)])  59.6 us
    pallas_call x5, Pallas kernels, dot_grad(): pl.pallas_call(partial(matmul_kernel, product_tn), grid=(rows // tile,),...  50.4 us
    pallas_call x8, Pallas kernels, pack(): pl.pallas_call(partial(pack_kernel, normed), grid=(tiles,), in_specs=[pl....  41.8 us
    pallas_call x4, Pallas kernels, fold_held(): pl.pallas_call(fold_held_kernel, grid_spec=pltpu.PrefetchScalarGridSpec(n...  38.2 us
    pallas_call x4, Pallas kernels, fold_sent(): pl.pallas_call(fold_sent_kernel, grid_spec=pltpu.PrefetchScalarGridSpec(n...  31.2 us
    pallas_call x3, Pallas kernels, dot_in(): pl.pallas_call(partial(matmul_kernel, product_nn), grid=(count // tile,),...  29.6 us
    unnamed x104, local copies, waits for them, and re-layouts  22.5 us
  transfers between devices with their start and end apart: 86, of which 48 were waited for; matrix products, arithmetic and copies ran while one was open for 15% of the time, Pallas kernels for 32%

profile of v4, /device:TPU:0, one launch (start us, length us, event | category | flops | bytes accessed | tf_op | source)
XLA Modules:
  0.0 648.8 jit_solution(2253059263877560176)
XLA Ops:
  7.2 2.4 shard_map.254
  9.6 2.9 collective-permute-start
  15.2 9.5 %collective-permute-done = bf16[256,1024]{1,0:T(8,128)(2,1)S(1)} collective-permute-done((bf16[256,1024]{1,0:T(8,128)(2,1)}, bf16[256,1024]{1,0:T(8,128)(2,1)S(1)}, u32[]{:S(2)}, u32[]{:S(2)}) %collective-permute-start) | collective-permute-done | bytes 524320 | tf_op jit(solution)/shard_map/ppermute | solution.py:322
  33.6 2.7 shard_map.255
  36.3 7.6 %collective-permute-done.2 = bf16[512,512]{1,0:T(8,128)(2,1)} collective-permute-done((bf16[512,512]{1,0:T(8,128)(2,1)S(1)}, bf16[512,512]{1,0:T(8,128)(2,1)}, u32[]{:S(2)}, u32[]{:S(2)}) %collective-permute-start.2) | collective-permute-done | bytes 524320 | tf_op jit(solution)/shard_map/ppermute | solution.py:322
  45.2 6.9 %collective-permute-done.5 = s32[1024]{0:T(1024)S(1)} collective-permute-done((s32[1024]{0:T(1024)S(1)}, s32[1024]{0:T(1024)S(1)}, u32[]{:S(2)}, u32[]{:S(2)}) %collective-permute-start.5) | collective-permute-done | bytes 4128 | tf_op jit(solution)/shard_map/ppermute | solution.py:322
  60.6 4.5 collective-permute-done.6
  67.2 5.6 shard_map.257
  72.8 2.6 collective-permute-done.8
  82.6 3.7 fusion.14
  87.0 5.7 shard_map.258
  92.7 7.3 %collective-permute-done.12.refs_2_ = bf16[1024,512]{1,0:T(8,128)(2,1)} collective-permute-done((bf16[1024,512]{1,0:T(8,128)(2,1)S(1)}, bf16[1024,512]{1,0:T(8,128)(2,1)}, u32[]{:S(2)}, u32[]{:S(2)}) %collective-permute-start.12) | collective-permute-done | bytes 1048608 | tf_op jit(solution)/shard_map/ppermute | solution.py:322
  107.4 4.7 shard_map.259.refs_4_
  112.1 7.4 %collective-permute-done.16 = bf16[512,512]{1,0:T(8,128)(2,1)} collective-permute-done((bf16[512,512]{1,0:T(8,128)(2,1)}, bf16[512,512]{1,0:T(8,128)(2,1)}, u32[]{:S(2)}, u32[]{:S(2)}) %collective-permute-start.16) | collective-permute-done | bytes 524320 | tf_op jit(solution)/shard_map/ppermute | solution.py:322
  121.3 11.3 %shard_map.260.joint_ref = f32[2048,768]{1,0:T(8,128)} custom-call(bf16[2048,2048]{1,0:T(8,128)(2,1)} %get-tuple-element.820.operand_ref, bf16[2048,1024]{1,0:T(8,128)(2,1)} %all-gather.4.cloned.1.call-done.weight_ref.near_ref.far_ref), custom_call_target="tpu_custom_call" | custom-call | tf_op jit(solution)/shard_map/pallas_call | solution.py:597
  132.7 2.8 copy-done
  135.5 10.6 %shard_map.261 = (bf16[2048,256]{1,0:T(8,128)(2,1)S(1)}, f32[2048,256]{1,0:T(8,128)S(1)}, bf16[2048,256]{1,0:T(8,128)(2,1)S(1)}, bf16[2048,128]{1,0:T(8,128)(2,1)S(1)}, f32[2,2,1024]{2,1,0:T(2,128)S(1)}) custom-call(f32[2048,768]{1,0:T(8,128)S(1)} %copy-done, f32[2048,128]{1,0:T(8,128)S(1)} %get-tuple-element.554.cos_ref, ...), custom_call_target="tpu_custom_call" | custom-call | tf_op jit(solution)/shard_map/pallas_call | solution.py:873
  150.6 4.9 shard_map.262
  156.0 3.9 collective-permute-done.20.near_got
  159.9 3.0 collective-permute-done.21.far_got
  164.2 6.6 %shard_map.263 = (bf16[2,512,512]{2,1,0:T(8,128)(2,1)}, bf16[2,512,512]{2,1,0:T(8,128)(2,1)}, bf16[1024,512]{1,0:T(8,128)(2,1)}, bf16[1024,512]{1,0:T(8,128)(2,1)}) custom-call(s32[1]{0:T(128)} %bitcast.place_ref.refs_4_, bf16[2048,256]{1,0:T(8,128)(2,1)} %copy-done.1, bf16[2048,1024]{1,0:T(8,128)(2,1)} %all-gather.4.cloned.1.call-done.weight_ref.near_ref.far_ref, ...), custom_call_target="tpu_custom_call" | custom-call | tf_op jit(solution)/shard_map/pallas_call | solution.py:553
  176.7 4.8 shard_map.264.operand_ref
  181.5 18.3 %collective-permute-done.22 = bf16[2,512,512]{2,1,0:T(8,128)(2,1)} collective-permute-done((bf16[2,512,512]{2,1,0:T(8,128)(2,1)}, bf16[2,512,512]{2,1,0:T(8,128)(2,1)}, u32[]{:S(2)}, u32[]{:S(2)}) %collective-permute-start.22) | collective-permute-done | bytes 1048608 | tf_op jit(solution)/shard_map/ppermute | solution.py:322
  205.5 10.4 %collective-permute-done.26 = bf16[512,512]{1,0:T(8,128)(2,1)S(1)} collective-permute-done((bf16[512,512]{1,0:T(8,128)(2,1)S(1)}, bf16[512,512]{1,0:T(8,128)(2,1)S(1)}, u32[]{:S(2)}, u32[]{:S(2)}) %collective-permute-start.26) | collective-permute-done | bytes 524320 | tf_op jit(solution)/shard_map/ppermute | solution.py:322
  223.1 11.4 %shard_map.265.grad_ref = f32[2048,768]{1,0:T(8,128)} custom-call(bf16[2048,2048]{1,0:T(8,128)(2,1)} %shard_map.264.operand_ref, bf16[2048,768]{1,0:T(8,128)(2,1)} %all-gather.6.cloned.1.call-done.weight_ref.near_ref.far_ref), custom_call_target="tpu_custom_call" | custom-call | tf_op jit(solution)/shard_map/pallas_call | solution.py:597
  234.4 10.2 %collective-permute-done.27.refs_2_ = bf16[1024,512]{1,0:T(8,128)(2,1)S(1)} collective-permute-done((bf16[1024,512]{1,0:T(8,128)(2,1)}, bf16[1024,512]{1,0:T(8,128)(2,1)S(1)}, u32[]{:S(2)}, u32[]{:S(2)}) %collective-permute-start.27) | collective-permute-done | bytes 1048608 | tf_op jit(solution)/shard_map/ppermute | solution.py:322
  251.0 5.7 shard_map.266
  256.7 5.6 collective-permute-done.31
  266.6 2.8 collective-permute-done.34.refs_3_
  269.4 5.7 shard_map.267
  275.1 14.0 %all-gather.8.cloned.1.call-done.weight_ref.near_ref.far_ref = bf16[2048,1536]{1,0:T(8,128)(2,1)} async-done(((bf16[512,1536]{1,0:T(8,128)(2,1)}), bf16[2048,1536]{1,0:T(8,128)(2,1)}) %all-gather.8.cloned.1.call-update) | async-done | bytes 6291472 | tf_op jit(solution)/shard_map/all_gather | solution.py:445
  289.1 20.2 %shard_map.268 = (bf16[2048,768]{1,0:T(8,128)(2,1)}, bf16[2048,1536]{1,0:T(8,128)(2,1)}) custom-call(bf16[2048,2048]{1,0:T(8,128)(2,1)} %get-tuple-element.679.hidden_ref.operand_ref, bf16[2048,1536]{1,0:T(8,128)(2,1)} %all-gather.8.cloned.1.call-done.weight_ref.near_ref.far_ref, f32[2048,768]{1,0:T(8,128)} %shard_map.265.grad_ref), custom_call_target="tpu_custom_call" | custom-call | tf_op jit(solution)/shard_map/pallas_call | solution.py:650
  309.4 10.9 %shard_map.269 = bf16[2048,768]{1,0:T(8,128)(2,1)} custom-call(bf16[2048,2048]{1,0:T(8,128)(2,1)} %get-tuple-element.679.hidden_ref.operand_ref, bf16[2048,1536]{1,0:T(8,128)(2,1)} %get-tuple-element.684.weight_ref.operand_ref), custom_call_target="tpu_custom_call" | custom-call | tf_op jit(solution)/shard_map/pallas_call | solution.py:615
  320.3 11.7 %shard_map.270 = (bf16[2048,512]{1,0:T(8,128)(2,1)}, bf16[2048,512]{1,0:T(8,128)(2,1)}) custom-call(s32[1]{0:T(128)} %bitcast.place_ref.refs_4_, bf16[2048,1536]{1,0:T(8,128)(2,1)} %get-tuple-element.684.weight_ref.operand_ref, bf16[2048,1536]{1,0:T(8,128)(2,1)} %all-gather.8.cloned.1.call-done.weight_ref.near_ref.far_ref, ...), custom_call_target="tpu_custom_call" | custom-call | tf_op jit(solution)/shard_map/pallas_call | solution.py:526
  332.5 10.9 %shard_map.271 = bf16[2048,768]{1,0:T(8,128)(2,1)} custom-call(bf16[2048,2048]{1,0:T(8,128)(2,1)} %get-tuple-element.679.hidden_ref.operand_ref, bf16[2048,1536]{1,0:T(8,128)(2,1)} %get-tuple-element.684.weight_ref.operand_ref), custom_call_target="tpu_custom_call" | custom-call | tf_op jit(solution)/shard_map/pallas_call | solution.py:615
  343.5 13.2 %shard_map.272 = (bf16[2,512,512]{2,1,0:T(8,128)(2,1)}, bf16[2,512,512]{2,1,0:T(8,128)(2,1)}, bf16[1024,512]{1,0:T(8,128)(2,1)}, bf16[1024,512]{1,0:T(8,128)(2,1)}) custom-call(s32[1]{0:T(128)} %bitcast.place_ref.refs_4_, bf16[2048,1536]{1,0:T(8,128)(2,1)} %get-tuple-element.684.weight_ref.operand_ref, ...), custom_call_target="tpu_custom_call" | custom-call | tf_op jit(solution)/shard_map/pallas_call | solution.py:553
  359.6 7.3 %shard_map.274 = (bf16[2048,512]{1,0:T(8,128)(2,1)}, bf16[2048,512]{1,0:T(8,128)(2,1)}) custom-call(s32[1]{0:T(128)} %bitcast.place_ref.refs_4_, bf16[2048,768]{1,0:T(8,128)(2,1)} %get-tuple-element.750.weight_ref.operand_ref, bf16[2048,768]{1,0:T(8,128)(2,1)} %all-gather.6.cloned.1.call-done.weight_ref.near_ref.far_ref, ...), custom_call_target="tpu_custom_call" | custom-call | tf_op jit(solution)/shard_map/pallas_call | solution.py:526
  366.9 10.9 %shard_map.273 = bf16[2048,768]{1,0:T(8,128)(2,1)} custom-call(bf16[2048,2048]{1,0:T(8,128)(2,1)} %shard_map.264.operand_ref, bf16[2048,768]{1,0:T(8,128)(2,1)} %get-tuple-element.750.weight_ref.operand_ref), custom_call_target="tpu_custom_call" | custom-call | tf_op jit(solution)/shard_map/pallas_call | solution.py:615
  377.8 4.4 collective-permute-done.37
  383.9 2.9 add_convert_fusion.4
  387.4 2.6 fusion.11
  392.4 8.6 %collective-permute-done.40 = bf16[512,512]{1,0:T(8,128)(2,1)} collective-permute-done((bf16[512,512]{1,0:T(8,128)(2,1)}, bf16[512,512]{1,0:T(8,128)(2,1)}, u32[]{:S(2)}, u32[]{:S(2)}) %collective-permute-start.40) | collective-permute-done | bytes 524320 | tf_op jit(solution)/shard_map/ppermute | solution.py:322
  401.0 3.1 collective-permute-done.39
  404.1 2.5 convert_add_fusion.7
  418.0 4.5 fusion.21
  425.4 9.3 %shard_map.275 = (bf16[2,512,512]{2,1,0:T(8,128)(2,1)}, bf16[2,512,512]{2,1,0:T(8,128)(2,1)}, bf16[1024,512]{1,0:T(8,128)(2,1)}, bf16[1024,512]{1,0:T(8,128)(2,1)}) custom-call(s32[1]{0:T(128)} %bitcast.place_ref.refs_4_, bf16[2048,768]{1,0:T(8,128)(2,1)} %get-tuple-element.750.weight_ref.operand_ref, ...), custom_call_target="tpu_custom_call" | custom-call | tf_op jit(solution)/shard_map/pallas_call | solution.py:553
  434.6 12.3 %collective-permute-done.45.refs_2_ = bf16[1024,512]{1,0:T(8,128)(2,1)S(1)} collective-permute-done((bf16[1024,512]{1,0:T(8,128)(2,1)S(1)}, bf16[1024,512]{1,0:T(8,128)(2,1)S(1)}, u32[]{:S(2)}, u32[]{:S(2)}) %collective-permute-start.45) | collective-permute-done | bytes 1048608 | tf_op jit(solution)/shard_map/ppermute | solution.py:322
  456.5 4.7 shard_map.276.refs_4_
  461.3 7.2 %collective-permute-done.49 = bf16[512,512]{1,0:T(8,128)(2,1)} collective-permute-done((bf16[512,512]{1,0:T(8,128)(2,1)}, bf16[512,512]{1,0:T(8,128)(2,1)}, u32[]{:S(2)}, u32[]{:S(2)}) %collective-permute-start.49) | collective-permute-done | bytes 524320 | tf_op jit(solution)/shard_map/ppermute | solution.py:322
  476.4 4.7 shard_map.277.operand_ref
  481.2 6.8 %shard_map.278.grad_mixed_ref = f32[2048,256]{1,0:T(8,128)} custom-call(bf16[2048,2048]{1,0:T(8,128)(2,1)} %shard_map.277.operand_ref, bf16[2048,1024]{1,0:T(8,128)(2,1)} %all-gather.4.cloned.1.call-done.weight_ref.near_ref.far_ref), custom_call_target="tpu_custom_call" | custom-call | tf_op jit(solution)/shard_map/pallas_call | solution.py:597
  489.7 6.8 %shard_map.280 = bf16[2048,256]{1,0:T(8,128)(2,1)} custom-call(bf16[2048,2048]{1,0:T(8,128)(2,1)} %shard_map.277.operand_ref, bf16[2048,256]{1,0:T(8,128)(2,1)} %copy-done.1), custom_call_target="tpu_custom_call" | custom-call | tf_op jit(solution)/shard_map/pallas_call | solution.py:615
  499.1 16.0 %shard_map.279 = (bf16[2048,768]{1,0:T(8,128)(2,1)}, f32[2,128]{1,0:T(2,128)S(1)}) custom-call(f32[2048,768]{1,0:T(8,128)} %shard_map.260.joint_ref, f32[2048,128]{1,0:T(8,128)S(1)} %get-tuple-element.554.cos_ref, f32[2048,128]{1,0:T(8,128)S(1)} %get-tuple-element.555.sin_ref, s32[2,1,1024]{2,1,0:T(1,128)S(1)} %compare_select_fusion.first_ref, ...), custom_call_target="tpu_custom_call" | custom-call | tf_op jit(solution)/shard_map/pallas_call | solution.py:896
  515.1 7.3 %shard_map.281 = (bf16[2048,512]{1,0:T(8,128)(2,1)}, bf16[2048,512]{1,0:T(8,128)(2,1)}) custom-call(s32[1]{0:T(128)} %bitcast.place_ref.refs_4_, bf16[2048,768]{1,0:T(8,128)(2,1)} %get-tuple-element.835.operand_ref.weight_ref, bf16[2048,1024]{1,0:T(8,128)(2,1)} %all-gather.4.cloned.1.call-done.weight_ref.near_ref.far_ref, ...), custom_call_target="tpu_custom_call" | custom-call | tf_op jit(solution)/shard_map/pallas_call | solution.py:526
  527.6 11.1 %shard_map.282 = bf16[2048,768]{1,0:T(8,128)(2,1)} custom-call(bf16[2048,2048]{1,0:T(8,128)(2,1)} %get-tuple-element.820.operand_ref, bf16[2048,768]{1,0:T(8,128)(2,1)} %get-tuple-element.835.operand_ref.weight_ref), custom_call_target="tpu_custom_call" | custom-call | tf_op jit(solution)/shard_map/pallas_call | solution.py:615
  538.7 5.8 collective-permute-done.59
  545.3 2.6 reduce-scatter.12.cloned.1.call-done
  547.9 2.7 add_convert_fusion.2
  557.2 9.1 %shard_map.283 = (bf16[2,512,512]{2,1,0:T(8,128)(2,1)}, bf16[2,512,512]{2,1,0:T(8,128)(2,1)}, bf16[1024,512]{1,0:T(8,128)(2,1)}, bf16[1024,512]{1,0:T(8,128)(2,1)}) custom-call(s32[1]{0:T(128)} %bitcast.place_ref.refs_4_, bf16[2048,768]{1,0:T(8,128)(2,1)} %get-tuple-element.835.operand_ref.weight_ref, ...), custom_call_target="tpu_custom_call" | custom-call | tf_op jit(solution)/shard_map/pallas_call | solution.py:553
  575.1 16.5 %collective-permute-done.64 = bf16[2,512,512]{2,1,0:T(8,128)(2,1)S(1)} collective-permute-done((bf16[2,512,512]{2,1,0:T(8,128)(2,1)}, bf16[2,512,512]{2,1,0:T(8,128)(2,1)S(1)}, u32[]{:S(2)}, u32[]{:S(2)}) %collective-permute-start.64) | collective-permute-done | bytes 1048608 | tf_op jit(solution)/shard_map/ppermute | solution.py:322
  600.4 3.4 collective-permute-done.68
  613.7 3.2 collective-permute-done.69
  619.4 3.4 multiply_add_fusion
  638.1 2.5 collective-permute-done.77
  (354 shorter events, 179.2 us)
Async XLA Ops:
  7.2 113.6 %all-gather.4.cloned.1.call-start = ((), (), s32[]{:S(2)}) async-start(), calls=%async_computation.5 | async-start | bytes 5242880 | tf_op jit(solution)/shard_map/all_gather | solution.py:445
  9.6 15.1 %collective-permute-start = (bf16[256,1024]{1,0:T(8,128)(2,1)}, bf16[256,1024]{1,0:T(8,128)(2,1)S(1)}, u32[]{:S(2)}, u32[]{:S(2)}) collective-permute-start(bf16[256,1024]{1,0:T(8,128)(2,1)} %get-tuple-element.488), channel_id=1, source_target_pairs={{0,4},{4,0},{1,5},{5,1},{2,6},{6,2},{3,7},{7,3},{8,12},{12,8},{9,1... | collective-permute-start | bytes 1572872 | tf_op jit(solution)/shard_map/ppermute | solution.py:322
  13.6 13.4 %collective-permute-start.1 = (bf16[512,512]{1,0:T(8,128)(2,1)S(1)}, bf16[512,512]{1,0:T(8,128)(2,1)S(1)}, u32[]{:S(2)}, u32[]{:S(2)}) collective-permute-start(bf16[512,512]{1,0:T(8,128)(2,1)S(1)} %slice.180), channel_id=1, source_target_pairs={{0,2},{2,0},{1,3},{3,1},{4,6},{6,4},{5,7},{7,5},{8,10},{10,8},{9,1... | collective-permute-start | bytes 1572872 | tf_op jit(solution)/shard_map/ppermute | solution.py:322
  27.1 194.0 %all-gather.6.cloned.1.call-start = ((), (), s32[]{:S(2)}) async-start(), calls=%async_computation.6 | async-start | bytes 3932160 | tf_op jit(solution)/shard_map/all_gather | solution.py:445
  27.9 24.3 %collective-permute-start.3 = (bf16[1024,512]{1,0:T(8,128)(2,1)S(1)}, bf16[1024,512]{1,0:T(8,128)(2,1)}, u32[]{:S(2)}, u32[]{:S(2)}) collective-permute-start(bf16[1024,512]{1,0:T(8,128)(2,1)S(1)} %copy-done.8), channel_id=1, source_target_pairs={{0,4},{4,0},{1,5},{5,1},{2,6},{6,2},{3,7},{7,3},{8,12},{12,8},{9,1... | collective-permute-start | bytes 3145736 | tf_op jit(solution)/shard_map/ppermute | solution.py:322
  29.4 22.8 %collective-permute-start.4 = (bf16[1024,512]{1,0:T(8,128)(2,1)S(1)}, bf16[1024,512]{1,0:T(8,128)(2,1)S(1)}, u32[]{:S(2)}, u32[]{:S(2)}) collective-permute-start(bf16[1024,512]{1,0:T(8,128)(2,1)S(1)} %copy-done.8), channel_id=1, source_target_pairs={{0,1},{1,0},{2,3},{3,2},{4,5},{5,4},{6,7},{7,6},{8,9},{9,8},{10,11... | collective-permute-start | bytes 3145736 | tf_op jit(solution)/shard_map/ppermute | solution.py:322
  29.4 14.5 %collective-permute-start.2 = (bf16[512,512]{1,0:T(8,128)(2,1)S(1)}, bf16[512,512]{1,0:T(8,128)(2,1)}, u32[]{:S(2)}, u32[]{:S(2)}) collective-permute-start(bf16[512,512]{1,0:T(8,128)(2,1)S(1)} %slice.181), channel_id=1, source_target_pairs={{0,2},{2,0},{1,3},{3,1},{4,6},{6,4},{5,7},{7,5},{8,10},{10,8},{9,1... | collective-permute-start | bytes 1572872 | tf_op jit(solution)/shard_map/ppermute | solution.py:322
  33.1 19.1 %collective-permute-start.5 = (s32[1024]{0:T(1024)S(1)}, s32[1024]{0:T(1024)S(1)}, u32[]{:S(2)}, u32[]{:S(2)}) collective-permute-start(s32[1024]{0:T(1024)S(1)} %copy-done.48), channel_id=1, source_target_pairs={{0,4},{4,0},{1,5},{5,1},{2,6},{6,2},{3,7},{7,3},{8,12},{12,8},{9,1... | collective-permute-start | bytes 12296 | tf_op jit(solution)/shard_map/ppermute | solution.py:322
  52.1 15.0 %collective-permute-start.10 = (bf16[1024,512]{1,0:T(8,128)(2,1)S(1)}, bf16[1024,512]{1,0:T(8,128)(2,1)}, u32[]{:S(2)}, u32[]{:S(2)}) collective-permute-start(bf16[1024,512]{1,0:T(8,128)(2,1)S(1)} %pad_maximum_fusion.4.refs_2_), channel_id=1, source_target_pairs={{0,1},{1,0},{2,3},{3,2},{4,5},{5,4},{6,7},{7,6},{8,9},{9,8},{10,11... | collective-permute-start | bytes 3145736 | tf_op jit(solution)/shard_map/ppermute | solution.py:322
  52.2 23.2 %collective-permute-start.7 = (bf16[1024,512]{1,0:T(8,128)(2,1)}, bf16[1024,512]{1,0:T(8,128)(2,1)}, u32[]{:S(2)}, u32[]{:S(2)}) collective-permute-start(bf16[1024,512]{1,0:T(8,128)(2,1)} %collective-permute-done.3.refs_0_), channel_id=1, source_target_pairs={{0,1},{1,0},{2,3},{3,2},{4,5},{5,4},{6,7},{7,6},{8,9},{9,8},{10,11... | collective-permute-start | bytes 3145736 | tf_op jit(solution)/shard_map/ppermute | solution.py:322
  52.7 12.3 %collective-permute-start.6 = (bf16[256,768]{1,0:T(8,128)(2,1)}, bf16[256,768]{1,0:T(8,128)(2,1)}, u32[]{:S(2)}, u32[]{:S(2)}) collective-permute-start(bf16[256,768]{1,0:T(8,128)(2,1)} %get-tuple-element.512), channel_id=1, source_target_pairs={{0,4},{4,0},{1,5},{5,1},{2,6},{6,2},{3,7},{7,3},{8,12},{12,8},{9,1... | collective-permute-start | bytes 1179656 | tf_op jit(solution)/shard_map/ppermute | solution.py:322
  56.9 18.5 %collective-permute-start.8 = (bf16[512,512]{1,0:T(8,128)(2,1)}, bf16[512,512]{1,0:T(8,128)(2,1)}, u32[]{:S(2)}, u32[]{:S(2)}) collective-permute-start(bf16[512,512]{1,0:T(8,128)(2,1)} %slice.182), channel_id=1, source_target_pairs={{0,4},{4,0},{1,5},{5,1},{2,6},{6,2},{3,7},{7,3},{8,12},{12,8},{9,1... | collective-permute-start | bytes 1572872 | tf_op jit(solution)/shard_map/ppermute | solution.py:322
  57.5 17.9 %collective-permute-start.9 = (bf16[512,512]{1,0:T(8,128)(2,1)}, bf16[512,512]{1,0:T(8,128)(2,1)}, u32[]{:S(2)}, u32[]{:S(2)}) collective-permute-start(bf16[512,512]{1,0:T(8,128)(2,1)} %slice.183), channel_id=1, source_target_pairs={{0,2},{2,0},{1,3},{3,1},{4,6},{6,4},{5,7},{7,5},{8,10},{10,8},{9,1... | collective-permute-start | bytes 1572872 | tf_op jit(solution)/shard_map/ppermute | solution.py:322
  75.4 213.7 %all-gather.8.cloned.1.call-start = ((), (), s32[]{:S(2)}) async-start(), calls=%async_computation.7 | async-start | bytes 7864320 | tf_op jit(solution)/shard_map/all_gather | solution.py:445
  75.5 24.5 %collective-permute-start.12 = (bf16[1024,512]{1,0:T(8,128)(2,1)S(1)}, bf16[1024,512]{1,0:T(8,128)(2,1)}, u32[]{:S(2)}, u32[]{:S(2)}) collective-permute-start(bf16[1024,512]{1,0:T(8,128)(2,1)S(1)} %get-tuple-element.546.refs_0_), channel_id=1, source_target_pairs={{0,2},{2,0},{1,3},{3,1},{4,6},{6,4},{5,7},{7,5},{8,10},{10,8},{9,1... | collective-permute-start | bytes 3145736 | tf_op jit(solution)/shard_map/ppermute | solution.py:322
  77.0 24.1 %collective-permute-start.13 = (bf16[1024,512]{1,0:T(8,128)(2,1)S(1)}, bf16[1024,512]{1,0:T(8,128)(2,1)}, u32[]{:S(2)}, u32[]{:S(2)}) collective-permute-start(bf16[1024,512]{1,0:T(8,128)(2,1)S(1)} %get-tuple-element.546.refs_0_), channel_id=1, source_target_pairs={{0,4},{4,0},{1,5},{5,1},{2,6},{6,2},{3,7},{7,3},{8,12},{12,8},{9,1... | collective-permute-start | bytes 3145736 | tf_op jit(solution)/shard_map/ppermute | solution.py:322
  78.5 22.6 %collective-permute-start.14 = (bf16[1024,512]{1,0:T(8,128)(2,1)S(1)}, bf16[1024,512]{1,0:T(8,128)(2,1)}, u32[]{:S(2)}, u32[]{:S(2)}) collective-permute-start(bf16[1024,512]{1,0:T(8,128)(2,1)S(1)} %get-tuple-element.546.refs_0_), channel_id=1, source_target_pairs={{0,1},{1,0},{2,3},{3,2},{4,5},{5,4},{6,7},{7,6},{8,9},{9,8},{10,11... | collective-permute-start | bytes 3145736 | tf_op jit(solution)/shard_map/ppermute | solution.py:322
  101.1 19.6 %collective-permute-start.15 = (bf16[1024,512]{1,0:T(8,128)(2,1)}, bf16[1024,512]{1,0:T(8,128)(2,1)S(1)}, u32[]{:S(2)}, u32[]{:S(2)}) collective-permute-start(bf16[1024,512]{1,0:T(8,128)(2,1)} %collective-permute-done.13.refs_0_), channel_id=1, source_target_pairs={{0,1},{1,0},{2,3},{3,2},{4,5},{5,4},{6,7},{7,6},{8,9},{9,8},{10,11... | collective-permute-start | bytes 3145736 | tf_op jit(solution)/shard_map/ppermute | solution.py:322
  105.4 14.1 %collective-permute-start.16 = (bf16[512,512]{1,0:T(8,128)(2,1)}, bf16[512,512]{1,0:T(8,128)(2,1)}, u32[]{:S(2)}, u32[]{:S(2)}) collective-permute-start(bf16[512,512]{1,0:T(8,128)(2,1)} %slice.187), channel_id=1, source_target_pairs={{0,4},{4,0},{1,5},{5,1},{2,6},{6,2},{3,7},{7,3},{8,12},{12,8},{9,1... | collective-permute-start | bytes 1572872 | tf_op jit(solution)/shard_map/ppermute | solution.py:322
  106.9 13.9 %collective-permute-start.17 = (bf16[512,512]{1,0:T(8,128)(2,1)}, bf16[512,512]{1,0:T(8,128)(2,1)}, u32[]{:S(2)}, u32[]{:S(2)}) collective-permute-start(bf16[512,512]{1,0:T(8,128)(2,1)} %slice.188), channel_id=1, source_target_pairs={{0,2},{2,0},{1,3},{3,1},{4,6},{6,4},{5,7},{7,5},{8,10},{10,8},{9,1... | collective-permute-start | bytes 1572872 | tf_op jit(solution)/shard_map/ppermute | solution.py:322
  120.8 28.5 %collective-permute-start.19 = (bf16[256,1536]{1,0:T(8,128)(2,1)}, bf16[256,1536]{1,0:T(8,128)(2,1)S(1)}, u32[]{:S(2)}, u32[]{:S(2)}) collective-permute-start(bf16[256,1536]{1,0:T(8,128)(2,1)} %get-tuple-element.551), channel_id=1, source_target_pairs={{0,4},{4,0},{1,5},{5,1},{2,6},{6,2},{3,7},{7,3},{8,12},{12,8},{9,1... | collective-permute-start | bytes 2359304 | tf_op jit(solution)/shard_map/ppermute | solution.py:322
  150.6 299.5 %reduce-scatter.6.cloned.1.call-start = ((), (), s32[]{:S(2)}) async-start(), calls=%async_computation.8 | async-start | bytes 3932160 | tf_op jit(solution)/shard_map/reduce_scatter | solution.py:449
  174.0 25.8 %collective-permute-start.22 = (bf16[2,512,512]{2,1,0:T(8,128)(2,1)}, bf16[2,512,512]{2,1,0:T(8,128)(2,1)}, u32[]{:S(2)}, u32[]{:S(2)}) collective-permute-start(bf16[2,512,512]{2,1,0:T(8,128)(2,1)} %get-tuple-element.593), channel_id=1, source_target_pairs={{0,4},{4,0},{1,5},{5,1},{2,6},{6,2},{3,7},{7,3},{8,12},{12,8},{9,1... | collective-permute-start | bytes 3145736 | tf_op jit(solution)/shard_map/ppermute | solution.py:322
  175.5 25.5 %collective-permute-start.23 = (bf16[1024,512]{1,0:T(8,128)(2,1)}, bf16[1024,512]{1,0:T(8,128)(2,1)}, u32[]{:S(2)}, u32[]{:S(2)}) collective-permute-start(bf16[1024,512]{1,0:T(8,128)(2,1)} %get-tuple-element.595), channel_id=1, source_target_pairs={{0,2},{2,0},{1,3},{3,1},{4,6},{6,4},{5,7},{7,5},{8,10},{10,8},{9,1... | collective-permute-start | bytes 3145736 | tf_op jit(solution)/shard_map/ppermute | solution.py:322
  202.8 13.1 %collective-permute-start.26 = (bf16[512,512]{1,0:T(8,128)(2,1)S(1)}, bf16[512,512]{1,0:T(8,128)(2,1)S(1)}, u32[]{:S(2)}, u32[]{:S(2)}) collective-permute-start(bf16[512,512]{1,0:T(8,128)(2,1)S(1)} %get-tuple-element.974), channel_id=1, source_target_pairs={{0,4},{4,0},{1,5},{5,1},{2,6},{6,2},{3,7},{7,3},{8,12},{12,8},{9,1... | collective-permute-start | bytes 1572872 | tf_op jit(solution)/shard_map/ppermute | solution.py:322
  204.9 12.9 %collective-permute-start.25 = (bf16[512,512]{1,0:T(8,128)(2,1)S(1)}, bf16[512,512]{1,0:T(8,128)(2,1)S(1)}, u32[]{:S(2)}, u32[]{:S(2)}) collective-permute-start(bf16[512,512]{1,0:T(8,128)(2,1)S(1)} %get-tuple-element.976), channel_id=1, source_target_pairs={{0,2},{2,0},{1,3},{3,1},{4,6},{6,4},{5,7},{7,5},{8,10},{10,8},{9,1... | collective-permute-start | bytes 1572872 | tf_op jit(solution)/shard_map/ppermute | solution.py:322
  221.1 23.5 %collective-permute-start.27 = (bf16[1024,512]{1,0:T(8,128)(2,1)}, bf16[1024,512]{1,0:T(8,128)(2,1)S(1)}, u32[]{:S(2)}, u32[]{:S(2)}) collective-permute-start(bf16[1024,512]{1,0:T(8,128)(2,1)} %get-tuple-element.741.refs_0_), channel_id=1, source_target_pairs={{0,2},{2,0},{1,3},{3,1},{4,6},{6,4},{5,7},{7,5},{8,10},{10,8},{9,1... | collective-permute-start | bytes 3145736 | tf_op jit(solution)/shard_map/ppermute | solution.py:322
  221.6 23.2 %collective-permute-start.28 = (bf16[1024,512]{1,0:T(8,128)(2,1)}, bf16[1024,512]{1,0:T(8,128)(2,1)}, u32[]{:S(2)}, u32[]{:S(2)}) collective-permute-start(bf16[1024,512]{1,0:T(8,128)(2,1)} %get-tuple-element.741.refs_0_), channel_id=1, source_target_pairs={{0,4},{4,0},{1,5},{5,1},{2,6},{6,2},{3,7},{7,3},{8,12},{12,8},{9,1... | collective-permute-start | bytes 3145736 | tf_op jit(solution)/shard_map/ppermute | solution.py:322
  223.1 21.8 %collective-permute-start.29 = (bf16[1024,512]{1,0:T(8,128)(2,1)}, bf16[1024,512]{1,0:T(8,128)(2,1)S(1)}, u32[]{:S(2)}, u32[]{:S(2)}) collective-permute-start(bf16[1024,512]{1,0:T(8,128)(2,1)} %get-tuple-element.741.refs_0_), channel_id=1, source_target_pairs={{0,1},{1,0},{2,3},{3,2},{4,5},{5,4},{6,7},{7,6},{8,9},{9,8},{10,11... | collective-permute-start | bytes 3145736 | tf_op jit(solution)/shard_map/ppermute | solution.py:322
  244.9 18.6 %collective-permute-start.30 = (bf16[1024,512]{1,0:T(8,128)(2,1)}, bf16[1024,512]{1,0:T(8,128)(2,1)}, u32[]{:S(2)}, u32[]{:S(2)}) collective-permute-start(bf16[1024,512]{1,0:T(8,128)(2,1)} %collective-permute-done.28.refs_0_), channel_id=1, source_target_pairs={{0,1},{1,0},{2,3},{3,2},{4,5},{5,4},{6,7},{7,6},{8,9},{9,8},{10,11... | collective-permute-start | bytes 3145736 | tf_op jit(solution)/shard_map/ppermute | solution.py:322
  248.3 14.1 %collective-permute-start.31 = (bf16[512,512]{1,0:T(8,128)(2,1)}, bf16[512,512]{1,0:T(8,128)(2,1)}, u32[]{:S(2)}, u32[]{:S(2)}) collective-permute-start(bf16[512,512]{1,0:T(8,128)(2,1)} %slice.197), channel_id=1, source_target_pairs={{0,4},{4,0},{1,5},{5,1},{2,6},{6,2},{3,7},{7,3},{8,12},{12,8},{9,1... | collective-permute-start | bytes 1572872 | tf_op jit(solution)/shard_map/ppermute | solution.py:322
  249.6 13.8 %collective-permute-start.32 = (bf16[512,512]{1,0:T(8,128)(2,1)}, bf16[512,512]{1,0:T(8,128)(2,1)}, u32[]{:S(2)}, u32[]{:S(2)}) collective-permute-start(bf16[512,512]{1,0:T(8,128)(2,1)} %slice.198), channel_id=1, source_target_pairs={{0,2},{2,0},{1,3},{3,1},{4,6},{6,4},{5,7},{7,5},{8,10},{10,8},{9,1... | collective-permute-start | bytes 1572872 | tf_op jit(solution)/shard_map/ppermute | solution.py:322
  320.2 167.8 %reduce-scatter.8.cloned.1.call-start = ((), (), s32[]{:S(2)}) async-start(), calls=%async_computation.9 | async-start | bytes 3932160 | tf_op jit(solution)/shard_map/reduce_scatter | solution.py:449
  332.0 11.4 %collective-permute-start.35 = (bf16[2048,512]{1,0:T(8,128)(2,1)}, bf16[2048,512]{1,0:T(8,128)(2,1)}, u32[]{:S(2)}, u32[]{:S(2)}) collective-permute-start(bf16[2048,512]{1,0:T(8,128)(2,1)} %get-tuple-element.677), channel_id=1, source_target_pairs={{0,1},{1,0},{2,3},{3,2},{4,5},{5,4},{6,7},{7,6},{8,9},{9,8},{10,11... | collective-permute-start | bytes 6291464 | tf_op jit(solution)/shard_map/ppermute | solution.py:322
  332.1 11.3 %collective-permute-start.36 = (bf16[2048,512]{1,0:T(8,128)(2,1)}, bf16[2048,512]{1,0:T(8,128)(2,1)}, u32[]{:S(2)}, u32[]{:S(2)}) collective-permute-start(bf16[2048,512]{1,0:T(8,128)(2,1)} %get-tuple-element.678), channel_id=1, source_target_pairs={{0,1},{1,0},{2,3},{3,2},{4,5},{5,4},{6,7},{7,6},{8,9},{9,8},{10,11... | collective-permute-start | bytes 6291464 | tf_op jit(solution)/shard_map/ppermute | solution.py:322
  343.4 171.7 %reduce-scatter.10.cloned.1.call-start = ((), (), s32[]{:S(2)}) async-start(), calls=%async_computation.10 | async-start | bytes 3932160 | tf_op jit(solution)/shard_map/reduce_scatter | solution.py:449
  356.7 25.5 %collective-permute-start.37 = (bf16[2,512,512]{2,1,0:T(8,128)(2,1)}, bf16[2,512,512]{2,1,0:T(8,128)(2,1)}, u32[]{:S(2)}, u32[]{:S(2)}) collective-permute-start(bf16[2,512,512]{2,1,0:T(8,128)(2,1)} %get-tuple-element.698), channel_id=1, source_target_pairs={{0,4},{4,0},{1,5},{5,1},{2,6},{6,2},{3,7},{7,3},{8,12},{12,8},{9,1... | collective-permute-start | bytes 3145736 | tf_op jit(solution)/shard_map/ppermute | solution.py:322
  358.1 25.2 %collective-permute-start.38 = (bf16[1024,512]{1,0:T(8,128)(2,1)}, bf16[1024,512]{1,0:T(8,128)(2,1)}, u32[]{:S(2)}, u32[]{:S(2)}) collective-permute-start(bf16[1024,512]{1,0:T(8,128)(2,1)} %get-tuple-element.700), channel_id=1, source_target_pairs={{0,2},{2,0},{1,3},{3,1},{4,6},{6,4},{5,7},{7,5},{8,10},{10,8},{9,1... | collective-permute-start | bytes 3145736 | tf_op jit(solution)/shard_map/ppermute | solution.py:322
  383.4 20.7 %collective-permute-start.41 = (bf16[2048,512]{1,0:T(8,128)(2,1)}, bf16[2048,512]{1,0:T(8,128)(2,1)}, u32[]{:S(2)}, u32[]{:S(2)}) collective-permute-start(bf16[2048,512]{1,0:T(8,128)(2,1)} %get-tuple-element.719), channel_id=1, source_target_pairs={{0,1},{1,0},{2,3},{3,2},{4,5},{5,4},{6,7},{7,6},{8,9},{9,8},{10,11... | collective-permute-start | bytes 6291464 | tf_op jit(solution)/shard_map/ppermute | solution.py:322
  383.4 20.7 %collective-permute-start.42 = (bf16[2048,512]{1,0:T(8,128)(2,1)}, bf16[2048,512]{1,0:T(8,128)(2,1)}, u32[]{:S(2)}, u32[]{:S(2)}) collective-permute-start(bf16[2048,512]{1,0:T(8,128)(2,1)} %get-tuple-element.720), channel_id=1, source_target_pairs={{0,1},{1,0},{2,3},{3,2},{4,5},{5,4},{6,7},{7,6},{8,9},{9,8},{10,11... | collective-permute-start | bytes 6291464 | tf_op jit(solution)/shard_map/ppermute | solution.py:322
  386.8 14.1 %collective-permute-start.40 = (bf16[512,512]{1,0:T(8,128)(2,1)}, bf16[512,512]{1,0:T(8,128)(2,1)}, u32[]{:S(2)}, u32[]{:S(2)}) collective-permute-start(bf16[512,512]{1,0:T(8,128)(2,1)} %get-tuple-element.970), channel_id=1, source_target_pairs={{0,4},{4,0},{1,5},{5,1},{2,6},{6,2},{3,7},{7,3},{8,12},{12,8},{9,1... | collective-permute-start | bytes 1572872 | tf_op jit(solution)/shard_map/ppermute | solution.py:322
  390.0 14.1 %collective-permute-start.39 = (bf16[512,512]{1,0:T(8,128)(2,1)}, bf16[512,512]{1,0:T(8,128)(2,1)}, u32[]{:S(2)}, u32[]{:S(2)}) collective-permute-start(bf16[512,512]{1,0:T(8,128)(2,1)} %get-tuple-element.972), channel_id=1, source_target_pairs={{0,2},{2,0},{1,3},{3,1},{4,6},{6,4},{5,7},{7,5},{8,10},{10,8},{9,1... | collective-permute-start | bytes 1572872 | tf_op jit(solution)/shard_map/ppermute | solution.py:322
  392.4 155.6 %reduce-scatter.12.cloned.1.call-start = ((), (), s32[]{:S(2)}) async-start(), calls=%async_computation.11 | async-start | bytes 1310720 | tf_op jit(solution)/shard_map/reduce_scatter | solution.py:449
  422.4 24.5 %collective-permute-start.45 = (bf16[1024,512]{1,0:T(8,128)(2,1)S(1)}, bf16[1024,512]{1,0:T(8,128)(2,1)S(1)}, u32[]{:S(2)}, u32[]{:S(2)}) collective-permute-start(bf16[1024,512]{1,0:T(8,128)(2,1)S(1)} %get-tuple-element.767.refs_0_), channel_id=1, source_target_pairs={{0,2},{2,0},{1,3},{3,1},{4,6},{6,4},{5,7},{7,5},{8,10},{10,8},{9,1... | collective-permute-start | bytes 3145736 | tf_op jit(solution)/shard_map/ppermute | solution.py:322
  423.9 24.2 %collective-permute-start.46 = (bf16[1024,512]{1,0:T(8,128)(2,1)S(1)}, bf16[1024,512]{1,0:T(8,128)(2,1)S(1)}, u32[]{:S(2)}, u32[]{:S(2)}) collective-permute-start(bf16[1024,512]{1,0:T(8,128)(2,1)S(1)} %get-tuple-element.767.refs_0_), channel_id=1, source_target_pairs={{0,4},{4,0},{1,5},{5,1},{2,6},{6,2},{3,7},{7,3},{8,12},{12,8},{9,1... | collective-permute-start | bytes 3145736 | tf_op jit(solution)/shard_map/ppermute | solution.py:322
  425.3 22.8 %collective-permute-start.47 = (bf16[1024,512]{1,0:T(8,128)(2,1)S(1)}, bf16[1024,512]{1,0:T(8,128)(2,1)S(1)}, u32[]{:S(2)}, u32[]{:S(2)}) collective-permute-start(bf16[1024,512]{1,0:T(8,128)(2,1)S(1)} %get-tuple-element.767.refs_0_), channel_id=1, source_target_pairs={{0,1},{1,0},{2,3},{3,2},{4,5},{5,4},{6,7},{7,6},{8,9},{9,8},{10,11... | collective-permute-start | bytes 3145736 | tf_op jit(solution)/shard_map/ppermute | solution.py:322
  450.1 19.6 %collective-permute-start.48 = (bf16[1024,512]{1,0:T(8,128)(2,1)}, bf16[1024,512]{1,0:T(8,128)(2,1)}, u32[]{:S(2)}, u32[]{:S(2)}) collective-permute-start(bf16[1024,512]{1,0:T(8,128)(2,1)} %copy-done.17), channel_id=1, source_target_pairs={{0,1},{1,0},{2,3},{3,2},{4,5},{5,4},{6,7},{7,6},{8,9},{9,8},{10,11... | collective-permute-start | bytes 3145736 | tf_op jit(solution)/shard_map/ppermute | solution.py:322
  454.3 14.1 %collective-permute-start.49 = (bf16[512,512]{1,0:T(8,128)(2,1)}, bf16[512,512]{1,0:T(8,128)(2,1)}, u32[]{:S(2)}, u32[]{:S(2)}) collective-permute-start(bf16[512,512]{1,0:T(8,128)(2,1)} %slice.207), channel_id=1, source_target_pairs={{0,4},{4,0},{1,5},{5,1},{2,6},{6,2},{3,7},{7,3},{8,12},{12,8},{9,1... | collective-permute-start | bytes 1572872 | tf_op jit(solution)/shard_map/ppermute | solution.py:322
  455.8 13.9 %collective-permute-start.50 = (bf16[512,512]{1,0:T(8,128)(2,1)}, bf16[512,512]{1,0:T(8,128)(2,1)}, u32[]{:S(2)}, u32[]{:S(2)}) collective-permute-start(bf16[512,512]{1,0:T(8,128)(2,1)} %slice.208), channel_id=1, source_target_pairs={{0,2},{2,0},{1,3},{3,1},{4,6},{6,4},{5,7},{7,5},{8,10},{10,8},{9,1... | collective-permute-start | bytes 1572872 | tf_op jit(solution)/shard_map/ppermute | solution.py:322
  475.2 12.8 %collective-permute-start.52 = (bf16[256,768]{1,0:T(8,128)(2,1)}, bf16[256,768]{1,0:T(8,128)(2,1)}, u32[]{:S(2)}, u32[]{:S(2)}) collective-permute-start(bf16[256,768]{1,0:T(8,128)(2,1)} %constant_dynamic-slice_fusion.4), channel_id=1, source_target_pairs={{0,4},{4,0},{1,5},{5,1},{2,6},{6,2},{3,7},{7,3},{8,12},{12,8},{9,1... | collective-permute-start | bytes 1179656 | tf_op jit(solution)/shard_map/ppermute | solution.py:322
  488.0 27.1 %collective-permute-start.54 = (bf16[2,512,512]{2,1,0:T(8,128)(2,1)}, bf16[2,512,512]{2,1,0:T(8,128)(2,1)}, u32[]{:S(2)}, u32[]{:S(2)}) collective-permute-start(bf16[2,512,512]{2,1,0:T(8,128)(2,1)} %get-tuple-element.803), channel_id=1, source_target_pairs={{0,4},{4,0},{1,5},{5,1},{2,6},{6,2},{3,7},{7,3},{8,12},{12,8},{9,1... | collective-permute-start | bytes 3145736 | tf_op jit(solution)/shard_map/ppermute | solution.py:322
  488.9 26.2 %collective-permute-start.55 = (bf16[1024,512]{1,0:T(8,128)(2,1)}, bf16[1024,512]{1,0:T(8,128)(2,1)}, u32[]{:S(2)}, u32[]{:S(2)}) collective-permute-start(bf16[1024,512]{1,0:T(8,128)(2,1)} %get-tuple-element.805), channel_id=1, source_target_pairs={{0,2},{2,0},{1,3},{3,1},{4,6},{6,4},{5,7},{7,5},{8,10},{10,8},{9,1... | collective-permute-start | bytes 3145736 | tf_op jit(solution)/shard_map/ppermute | solution.py:322
  522.4 22.1 %collective-permute-start.56 = (bf16[2048,512]{1,0:T(8,128)(2,1)}, bf16[2048,512]{1,0:T(8,128)(2,1)S(1)}, u32[]{:S(2)}, u32[]{:S(2)}) collective-permute-start(bf16[2048,512]{1,0:T(8,128)(2,1)} %get-tuple-element.816), channel_id=1, source_target_pairs={{0,1},{1,0},{2,3},{3,2},{4,5},{5,4},{6,7},{7,6},{8,9},{9,8},{10,11... | collective-permute-start | bytes 6291464 | tf_op jit(solution)/shard_map/ppermute | solution.py:322
  522.4 22.1 %collective-permute-start.57 = (bf16[2048,512]{1,0:T(8,128)(2,1)}, bf16[2048,512]{1,0:T(8,128)(2,1)}, u32[]{:S(2)}, u32[]{:S(2)}) collective-permute-start(bf16[2048,512]{1,0:T(8,128)(2,1)} %get-tuple-element.817), channel_id=1, source_target_pairs={{0,1},{1,0},{2,3},{3,2},{4,5},{5,4},{6,7},{7,6},{8,9},{9,8},{10,11... | collective-permute-start | bytes 6291464 | tf_op jit(solution)/shard_map/ppermute | solution.py:322
  523.0 99.9 %reduce-scatter.14.cloned.1.call-start = ((), (), s32[]{:S(2)}) async-start(), calls=%async_computation.12 | async-start | bytes 3932160 | tf_op jit(solution)/shard_map/reduce_scatter | solution.py:449
  524.8 13.9 %collective-permute-start.58 = (bf16[256,768]{1,0:T(8,128)(2,1)}, bf16[256,768]{1,0:T(8,128)(2,1)}, u32[]{:S(2)}, u32[]{:S(2)}) collective-permute-start(bf16[256,768]{1,0:T(8,128)(2,1)} %constant_dynamic-slice_fusion.3), channel_id=1, source_target_pairs={{0,4},{4,0},{1,5},{5,1},{2,6},{6,2},{3,7},{7,3},{8,12},{12,8},{9,1... | collective-permute-start | bytes 1179656 | tf_op jit(solution)/shard_map/ppermute | solution.py:322
  526.8 17.7 %collective-permute-start.59 = (bf16[256,768]{1,0:T(8,128)(2,1)}, bf16[256,768]{1,0:T(8,128)(2,1)S(1)}, u32[]{:S(2)}, u32[]{:S(2)}) collective-permute-start(bf16[256,768]{1,0:T(8,128)(2,1)} %constant_dynamic-slice_fusion.2), channel_id=1, source_target_pairs={{0,4},{4,0},{1,5},{5,1},{2,6},{6,2},{3,7},{7,3},{8,12},{12,8},{9,1... | collective-permute-start | bytes 1179656 | tf_op jit(solution)/shard_map/ppermute | solution.py:322
  550.6 15.7 %collective-permute-start.62 = (bf16[512,512]{1,0:T(8,128)(2,1)}, bf16[512,512]{1,0:T(8,128)(2,1)S(1)}, u32[]{:S(2)}, u32[]{:S(2)}) collective-permute-start(bf16[512,512]{1,0:T(8,128)(2,1)} %get-tuple-element.965), channel_id=1, source_target_pairs={{0,4},{4,0},{1,5},{5,1},{2,6},{6,2},{3,7},{7,3},{8,12},{12,8},{9,1... | collective-permute-start | bytes 1572872 | tf_op jit(solution)/shard_map/ppermute | solution.py:322
  554.4 13.4 %collective-permute-start.61 = (bf16[512,512]{1,0:T(8,128)(2,1)}, bf16[512,512]{1,0:T(8,128)(2,1)S(1)}, u32[]{:S(2)}, u32[]{:S(2)}) collective-permute-start(bf16[512,512]{1,0:T(8,128)(2,1)} %get-tuple-element.967), channel_id=1, source_target_pairs={{0,2},{2,0},{1,3},{3,1},{4,6},{6,4},{5,7},{7,5},{8,10},{10,8},{9,1... | collective-permute-start | bytes 1572872 | tf_op jit(solution)/shard_map/ppermute | solution.py:322
  555.8 10.5 %collective-permute-start.60 = (f32[6,128]{1,0:T(8,128)S(1)}, f32[6,128]{1,0:T(8,128)S(1)}, u32[]{:S(2)}, u32[]{:S(2)}) collective-permute-start(f32[6,128]{1,0:T(8,128)S(1)} %pad_maximum_fusion.9), channel_id=1, source_target_pairs={{0,4},{4,0},{1,5},{5,1},{2,6},{6,2},{3,7},{7,3},{8,12},{12,8},{9,1... | collective-permute-start | bytes 9224 | tf_op jit(solution)/shard_map/ppermute | solution.py:322
  567.8 23.9 %collective-permute-start.64 = (bf16[2,512,512]{2,1,0:T(8,128)(2,1)}, bf16[2,512,512]{2,1,0:T(8,128)(2,1)S(1)}, u32[]{:S(2)}, u32[]{:S(2)}) collective-permute-start(bf16[2,512,512]{2,1,0:T(8,128)(2,1)} %get-tuple-element.868), channel_id=1, source_target_pairs={{0,4},{4,0},{1,5},{5,1},{2,6},{6,2},{3,7},{7,3},{8,12},{12,8},{9,1... | collective-permute-start | bytes 3145736 | tf_op jit(solution)/shard_map/ppermute | solution.py:322
  568.3 23.6 %collective-permute-start.65 = (bf16[1024,512]{1,0:T(8,128)(2,1)}, bf16[1024,512]{1,0:T(8,128)(2,1)S(1)}, u32[]{:S(2)}, u32[]{:S(2)}) collective-permute-start(bf16[1024,512]{1,0:T(8,128)(2,1)} %get-tuple-element.870), channel_id=1, source_target_pairs={{0,2},{2,0},{1,3},{3,1},{4,6},{6,4},{5,7},{7,5},{8,10},{10,8},{9,1... | collective-permute-start | bytes 3145736 | tf_op jit(solution)/shard_map/ppermute | solution.py:322
  592.2 11.5 %collective-permute-start.68 = (bf16[512,512]{1,0:T(8,128)(2,1)S(1)}, bf16[512,512]{1,0:T(8,128)(2,1)}, u32[]{:S(2)}, u32[]{:S(2)}) collective-permute-start(bf16[512,512]{1,0:T(8,128)(2,1)S(1)} %get-tuple-element.961), channel_id=1, source_target_pairs={{0,4},{4,0},{1,5},{5,1},{2,6},{6,2},{3,7},{7,3},{8,12},{12,8},{9,1... | collective-permute-start | bytes 1572872 | tf_op jit(solution)/shard_map/ppermute | solution.py:322
  594.1 11.2 %collective-permute-start.67 = (bf16[512,512]{1,0:T(8,128)(2,1)S(1)}, bf16[512,512]{1,0:T(8,128)(2,1)}, u32[]{:S(2)}, u32[]{:S(2)}) collective-permute-start(bf16[512,512]{1,0:T(8,128)(2,1)S(1)} %get-tuple-element.963), channel_id=1, source_target_pairs={{0,2},{2,0},{1,3},{3,1},{4,6},{6,4},{5,7},{7,5},{8,10},{10,8},{9,1... | collective-permute-start | bytes 1572872 | tf_op jit(solution)/shard_map/ppermute | solution.py:322
  (71 other events, 409.4 us)
Sparse Core Ops, SparseCore 0:
  27.2 82.0 all-gather.3
  110.9 62.0 all-gather.5
  175.1 113.9 all-gather.7
  320.4 58.4 reduce-scatter.5
  381.0 60.2 reduce-scatter.7
  443.5 60.2 reduce-scatter.9
  523.1 24.7 reduce-scatter.11
  550.3 59.0 reduce-scatter.13

commit v5 on v4

--- a/solution.py
+++ b/solution.py
@@ -395,13 +395,16 @@
     return (flip(own, "y"), flip(own, "x"), flip(own, "core"))
 
 
-def relay(own, via_y, via_x, own_core, place, gain, normed):
-    half = own.shape[0] // 2
+def relay_flips(via_y, via_x):
+    half = via_y.shape[0] // 2
     upper = flip(via_y[:half], "x")
     lower = flip(via_x[half:], "y")
-    x_core = flip(via_x, "core")
-    near = pack((own, own_core, via_y, flip(via_y, "core")), place, gain, normed, 0, None)
-    return (via_x, x_core, upper, lower, *near)
+    return (flip(via_y, "core"), via_x, flip(via_x, "core"), upper, lower)
+
+
+def relay(own, via_y, via_x, own_core, place, gain, normed):
+    y_core, *steps = relay_flips(via_y, via_x)
+    return (*steps, *pack((own, own_core, via_y, y_core), place, gain, normed, 0, None))
 
 
 def diagonal(via_x, x_core, upper, lower, target, place, gain, normed):
@@ -465,30 +468,33 @@
 vmem = pltpu.CompilerParams(vmem_limit_bytes=56 * 1024 * 1024)
 
 
-def fold_turn(near_ref, far_ref, near_turned, far_turned):
+def fold_turn(near_ref, far_ref, turned):
+    rows = near_ref.shape[0]
+
     @pl.when(pl.program_id(0) == 0)
     def turn():
-        near_turned[...] = near_ref[...].T
-        far_turned[...] = far_ref[...].T
-
-
-def fold_sent_kernel(
-    place_ref, operand_ref, near_ref, far_ref, near_out, far_out, near_turned, far_turned
-):
-    fold_turn(near_ref, far_ref, near_turned, far_turned)
-    for weight_ref, out_ref in ((near_turned, near_out), (far_turned, far_out)):
-        out_ref[...] = product_nn(operand_ref[...], weight_ref[...]).astype(out_ref.dtype)
+        turned[:, :rows] = near_ref[...].T
+        turned[:, rows:] = far_ref[...].T
+
+
+def fold_sent_kernel(place_ref, operand_ref, near_ref, far_ref, near_out, far_out, turned):
+    fold_turn(near_ref, far_ref, turned)
+    rows = near_out.shape[1]
+    both = product_nn(operand_ref[...], turned[...]).astype(near_out.dtype)
+    near_out[...] = both[:, :rows]
+    far_out[...] = both[:, rows:]
 
 
 def fold_held_kernel(
     place_ref, operand_ref, near_ref, far_ref, near_got, far_got,
-    upper_send, upper_keep, lower_send, lower_keep, near_turned, far_turned,
+    upper_send, upper_keep, lower_send, lower_keep, turned,
 ):
-    fold_turn(near_ref, far_ref, near_turned, far_turned)
+    fold_turn(near_ref, far_ref, turned)
     low = upper_send.dtype
-    near = product_nn(operand_ref[...], near_turned[...]) + near_got[...].astype(jnp.float32)
-    far = product_nn(operand_ref[...], far_turned[...]) + far_got[...].astype(jnp.float32)
-    near, far = near.astype(low), far.astype(low)
+    rows = near_got.shape[1]
+    both = product_nn(operand_ref[...], turned[...])
+    near = (both[:, :rows] + near_got[...].astype(jnp.float32)).astype(low)
+    far = (both[:, rows:] + far_got[...].astype(jnp.float32)).astype(low)
     step = pl.program_id(0)
 
     @pl.when(step == 0)
@@ -530,7 +536,7 @@
             grid=(4,),
             in_specs=fold_specs(tile, width, rows, column, 1, 3),
             out_specs=[out, out],
-            scratch_shapes=[pltpu.VMEM((width, rows), jnp.bfloat16)] * 2,
+            scratch_shapes=[pltpu.VMEM((width, 2 * rows), jnp.bfloat16)],
         ),
         out_shape=[jax.ShapeDtypeStruct((count, rows), jnp.bfloat16)] * 2,
         compiler_params=vmem,
@@ -557,7 +563,7 @@
             grid=(4,),
             in_specs=fold_specs(tile, width, rows, column, 0, 2) + [got, got],
             out_specs=[whole, whole, late, late],
-            scratch_shapes=[pltpu.VMEM((width, rows), jnp.bfloat16)] * 2,
+            scratch_shapes=[pltpu.VMEM((width, 2 * rows), jnp.bfloat16)],
         ),
         out_shape=[shape((2, tile, rows), jnp.bfloat16)] * 2
         + [shape((2 * tile, rows), jnp.bfloat16)] * 2,
@@ -570,17 +576,34 @@
     return (flip(upper_send, "x"), upper_keep, flip(lower_send, "y"), lower_keep)
 
 
+def fold_close_kernel(
+    upper_ref, upper_keep, own_ref, own_keep, other_ref, other_keep,
+    upper_near, upper_far, lower_own, lower_other,
+):
+    wide = lambda ref: ref[...].astype(jnp.float32)
+    total = wide(upper_ref) + wide(upper_keep)
+    upper_near[...] = total[0]
+    upper_far[...] = total[1].astype(upper_far.dtype)
+    lower_own[...] = wide(own_ref) + wide(own_keep)
+    lower_other[...] = (wide(other_ref) + wide(other_keep)).astype(lower_other.dtype)
+
+
 def fold_close(upper, upper_keep, lower, lower_keep):
-    low, wide = jnp.bfloat16, jnp.float32
-    half = lower.shape[0] // 2
-    upper_got = flip((upper_keep[1].astype(wide) + upper[1]).astype(low), "y")
-    lower_got = flip((lower_keep[half:].astype(wide) + lower[half:]).astype(low), "x")
-    return (
-        upper_keep[0].astype(wide) + upper[0],
-        upper_got,
-        lower_keep[:half].astype(wide) + lower[:half],
-        lower_got,
-    )
+    count, rows = upper.shape[1:]
+    tile = count // 2
+    pair = pl.BlockSpec((2, tile, rows), lambda i: (0, i, 0))
+    own = pl.BlockSpec((tile, rows), lambda i: (i, 0))
+    other = pl.BlockSpec((tile, rows), lambda i: (i + 2, 0))
+    shapes = [jax.ShapeDtypeStruct((count, rows), kind) for kind in (jnp.float32, jnp.bfloat16)]
+    upper_near, upper_far, lower_own, lower_other = pl.pallas_call(
+        fold_close_kernel,
+        grid=(2,),
+        in_specs=[pair, pair, own, own, other, other],
+        out_specs=[own] * 4,
+        out_shape=shapes * 2,
+        cost_estimate=light,
+    )(upper, upper_keep, lower, lower_keep, lower, lower_keep)
+    return (upper_near, flip(upper_far, "y"), lower_own, flip(lower_other, "x"))
 
 
 def fold_end(upper_near, upper_got, lower_own, lower_got):
@@ -994,20 +1017,22 @@
     hidden1, cosine, sine, first, *via_out = line.run(
         open_fourth, grad_out_low, segment_ids, segment_other, *steps, target
     )
-    steps = line.run(
-        lambda *v: relay(*v, place, gain_ffn, False), grad_out_low, *via_out
-    )
     out_column = joint_width // query_width
 
-    def attend(hidden1, first_weight, keep_pair, give_pair):
+    def attend(hidden1, first_weight, keep_pair, give_pair, via_y, via_x):
+        steps = relay_flips(via_y, via_x)
         got_pair = flip(give_pair, "x")
         joint = dot_in(hidden1, first_weight, joint_width)
         mixed, *kept = attend_fwd(
             joint, cosine, sine, first, gain_query, gain_key, heads, count
         )
-        return (rows_of(keep_pair, got_pair), joint, mixed, *kept)
-
-    pair_rows, joint, mixed, *kept = line.run(attend, hidden1, first_weight, keep_pair, give_pair)
+        return (rows_of(keep_pair, got_pair), joint, mixed, *kept, *steps)
+
+    out_y, out_x, out_core = via_out
+    pair_rows, joint, mixed, *rest = line.run(
+        attend, hidden1, first_weight, keep_pair, give_pair, out_y, out_x
+    )
+    kept, steps = rest[:4], rest[4:]
     pair_weight = weight_gather(pair_rows)
     near_got, far_got = line.run(
         lambda m, w: fold_swap(m, w, place, out_column), mixed, first_weight
@@ -1017,10 +1042,16 @@
         mixed, first_weight, near_got, far_got,
     )
 
-    def cross_out(*values):
-        return (*fold_cross(*values[:4]), diagonal(*values[4:], place, gain_ffn, False))
-
-    *sums, grad_out_full = line.run(cross_out, *sums, *steps)
+    def cross_out(grad_out_low, own_core, via_y, y_core, via_x, x_core, upper, lower, *sums):
+        crossing = fold_cross(*sums)
+        near = (grad_out_low, own_core, via_y, y_core)
+        target = pack(near, place, gain_ffn, False, 0, None)[0]
+        return (
+            *crossing,
+            diagonal(via_x, x_core, upper, lower, target, place, gain_ffn, False),
+        )
+
+    *sums, grad_out_full = line.run(cross_out, grad_out_low, out_core, out_y, *steps, *sums)
     ends = line.run(fold_close, *sums)
 
     def residual(values, *ends):
@@ -1039,32 +1070,30 @@
     hidden2 = line.run(lambda *v: diagonal(*v, place, gain_ffn, True), *steps, target)
     activated, grad_pair = line.run(ffn, hidden2, pair_weight, grad_act)
 
-    gate_grad = line.run(lambda h, g: dot_grad(h, g, hidden_width), hidden2, grad_pair)
-    gate_sum = grad_scatter(gate_grad)
 
     def sent_pair(hidden2, grad_pair, pair_weight):
         return (
             *fold_swap(grad_pair, pair_weight, place),
-            dot_grad(hidden2, grad_pair, hidden_width, 1),
-        )
-
-    near_got, far_got, up_grad = line.run(sent_pair, hidden2, grad_pair, pair_weight)
-    up_sum = grad_scatter(up_grad)
+            dot_grad(hidden2, grad_pair, hidden_width),
+        )
+
+    near_got, far_got, gate_grad = line.run(sent_pair, hidden2, grad_pair, pair_weight)
+    gate_sum = grad_scatter(gate_grad)
     sums = line.run(
         lambda *v: fold_held(v[0], v[1], place, *v[2:]), grad_pair, pair_weight, near_got, far_got
     )
 
-    def cross_pair(grad_out_full, activated, down_weight, *sums):
+    def cross_pair(hidden2, grad_pair, activated, down_weight, *sums):
         return (
             *fold_cross(*sums),
-            dot_grad(grad_out_full, activated),
+            dot_grad(hidden2, grad_pair, hidden_width, 1),
             *fold_sent(activated, down_weight, place),
         )
 
-    *sums, down_grad, near_ffn, far_ffn = line.run(
-        cross_pair, grad_out_full, activated, down_weight, *sums
-    )
-    down_sum = grad_scatter(down_grad)
+    *sums, up_grad, near_ffn, far_ffn = line.run(
+        cross_pair, hidden2, grad_pair, activated, down_weight, *sums
+    )
+    up_sum = grad_scatter(up_grad)
 
     def close_pair(near_ffn, far_ffn, *sums):
         return (*fold_close(*sums), flip(near_ffn, "core"), flip(far_ffn, "core"))
@@ -1101,56 +1130,54 @@
         norm_back, grad_hidden2, resid_low, inverse2, gain_ffn_own, dots, grad_out
     )
 
-    def start_branch(grad_branch, activated, down_weight, near_got, far_got):
+    def start_branch(grad_branch, grad_out_full, activated, down_weight, near_got, far_got):
         return (
             *direct(grad_branch),
+            dot_grad(grad_out_full, activated),
             *fold_held(activated, down_weight, place, near_got, far_got),
         )
 
-    via_y, via_x, own_core, *sums_ffn = line.run(
-        start_branch, grad_branch, activated, down_weight, near_got, far_got
-    )
+    via_y, via_x, own_core, down_grad, *sums_ffn = line.run(
+        start_branch, grad_branch, grad_out_full, activated, down_weight, near_got, far_got
+    )
+    down_sum = grad_scatter(down_grad)
     gate_sum, = line.enter(gate_sum)
     steps = line.run(
         lambda *v: relay(*v, place, gain_ffn, False), grad_branch, via_y, via_x, own_core
     )
 
     def mix_back(gate_sum, first_weight, *steps):
-        got = flip(give_rows(gate_sum, across), "x")
+        got_gate = flip(give_rows(gate_sum, across), "x")
         grad_branch_full = diagonal(*steps, place, gain_ffn, False)
-        grad_mixed = dot_in(grad_branch_full, first_weight, query_width, out_column)
-        return (got, grad_branch_full, grad_mixed)
+        return (
+            got_gate,
+            grad_branch_full,
+            dot_in(grad_branch_full, first_weight, query_width, out_column),
+        )
 
     got_gate, grad_branch_full, grad_mixed = line.run(mix_back, gate_sum, first_weight, *steps)
     up_sum, = line.enter(up_sum)
 
-    def attend_back(joint, grad_mixed, grad_branch_full, mixed, *sums):
+    def attend_back(joint, grad_mixed, *sums):
         grad_joint, head_gains = attend_bwd(
             joint, cosine, sine, first, gain_query, gain_key, kept, grad_mixed, count
         )
-        out_grad = dot_grad(grad_branch_full, mixed, None, 0, heavy)
-        return (grad_joint, head_gains, out_grad, *fold_cross(*sums))
-
-    grad_joint, head_gains, out_grad, *sums_ffn = line.run(
-        attend_back, joint, grad_mixed, grad_branch_full, mixed, *sums_ffn
-    )
-    out_sum = grad_scatter(out_grad)
-
-    down_sum, = line.enter(down_sum)
-
-    def sent_attn(hidden1, grad_joint, first_weight, up_sum, down_sum):
+        return (grad_joint, head_gains, *fold_cross(*sums))
+
+    grad_joint, head_gains, *sums_ffn = line.run(attend_back, joint, grad_mixed, *sums_ffn)
+
+    def sent_attn(hidden1, grad_joint, first_weight, up_sum):
         return (
             *fold_swap(grad_joint, first_weight, place),
+            dot_grad(hidden1, grad_joint),
             flip(give_rows(up_sum, across), "x"),
-            flip(give_rows(down_sum, across), "x"),
-            dot_grad(hidden1, grad_joint, None, 0, heavy),
-        )
-
-    near_got, far_got, got_up, got_down, attn_grads = line.run(
-        sent_attn, hidden1, grad_joint, first_weight, up_sum, down_sum
+        )
+
+    near_got, far_got, attn_grads, got_up = line.run(
+        sent_attn, hidden1, grad_joint, first_weight, up_sum
     )
     attn_sum = grad_scatter(attn_grads)
-    out_sum, = line.enter(out_sum)
+    down_sum, = line.enter(down_sum)
 
     def held_attn(grad_joint, first_weight, near_got, far_got, gain_ffn_grad, head_gains, *sums):
         early = jnp.concatenate([gain_ffn_grad, head_gains], axis=0)
@@ -1175,56 +1202,57 @@
     def join_all(rows, got):
         return join(rows, got, 0, rows.shape[1])
 
-    def cross_attn(early, resid, gate_sum, got_gate, *values):
+    def cross_attn(
+        grad_branch_full, mixed, early, resid, gate_sum, got_gate, *values
+    ):
         sums = fold_cross(*values[:4])
         output = (live * (resid + fold_end(*values[4:]))).astype(low)
-        return (early + z_flip(early, 1), output, join_all(gate_sum, got_gate), *sums)
-
-    early, output, ffgate_grad, *sums = line.run(
-        cross_attn, early, resid, gate_sum, got_gate, *sums, *ends_ffn
-    )
+        return (
+            early + z_flip(early, 1),
+            output,
+            join_all(gate_sum, got_gate),
+            dot_grad(grad_branch_full, mixed),
+            *sums,
+        )
+
+    early, output, ffgate_grad, out_grad, *sums = line.run(
+        cross_attn, grad_branch_full, mixed, early, resid, gate_sum, got_gate, *sums, *ends_ffn
+    )
+
+    out_sum = grad_scatter(out_grad)
 
     def close_attn(early, up_sum, got_up, *sums):
         return (early + z_flip(early, 2), join_all(up_sum, got_up), *fold_close(*sums))
 
     early, up_grad, *ends = line.run(close_attn, early, up_sum, got_up, *sums)
 
-    def last_dots(tokens, inverse1, out_sum, *ends):
+    attn_sum, = line.enter(attn_sum)
+
+    def last_dots(tokens, inverse1, attn_sum, down_sum, *ends):
+        got_down = flip(give_rows(down_sum, across), "x")
+        got_attn = flip(give_rows(attn_sum, across), "x")
         grad_own = fold_end(*ends)
         late = gain_part(grad_own, tokens, inverse1)
-        return (
-            flip(give_rows(out_sum, across), "x"),
-            grad_own,
-            partial_dots(grad_own, tokens, inverse1, gain_attn_own),
-            late,
-        )
-
-    got_out, grad_hidden1, dots, late = line.run(last_dots, tokens, inverse1, out_sum, *ends)
-
-    def last_norm(grad_hidden1, tokens, inverse1, dots, grad_resid, late):
-        grad_tokens, unused = norm_back(
-            grad_hidden1, tokens, inverse1, gain_attn_own, dots, grad_resid
-        )
-        return (grad_tokens, late + flip(late, "x"))
-
-    grad_tokens, late = line.run(
-        last_norm, grad_hidden1, tokens, inverse1, dots, grad_resid, late
-    )
-    attn_sum, = line.enter(attn_sum)
-
-    def last_out(late, attn_sum, out_sum, got_out, down_sum, got_down):
-        got_attn = flip(give_rows(attn_sum, across), "x")
         late = late + z_flip(late, 1)
         return (
             got_attn,
+            got_down,
+            grad_own,
+            partial_dots(grad_own, tokens, inverse1, gain_attn_own),
             late + z_flip(late, 2),
-            join_all(out_sum, got_out),
-            join_all(down_sum, got_down),
-        )
-
-    got_attn, late, out_part, down_part = line.run(
-        last_out, late, attn_sum, out_sum, got_out, down_sum, got_down
-    )
+        )
+
+    got_attn, got_down, grad_hidden1, dots, late = line.run(
+        last_dots, tokens, inverse1, attn_sum, down_sum, *ends
+    )
+    cuts = (
+        0,
+        query_width,
+        2 * query_width,
+        2 * query_width + key_width,
+        2 * query_width + 2 * key_width,
+    )
+
     blocks = local // 128
 
     def last_spot(late, early):
@@ -1236,21 +1264,28 @@
         spot = spot + flip(spot, "core")
         return spot + flip(spot, "y")
 
-    cuts = (
-        0,
-        query_width,
-        2 * query_width,
-        2 * query_width + key_width,
-        2 * query_width + 2 * key_width,
-    )
-
-    def last_parts(attn_sum, got_attn, late, early):
+    def last_norm(
+        grad_hidden1, tokens, inverse1, dots, grad_resid, late, early, attn_sum, got_attn, out_sum,
+        down_sum, got_down
+    ):
+        got_out = flip(give_rows(out_sum, across), "x")
+        spot = last_spot(late + flip(late, "x"), early)
+        grad_tokens, unused = norm_back(
+            grad_hidden1, tokens, inverse1, gain_attn_own, dots, grad_resid
+        )
         return (
-            last_spot(late, early),
+            got_out,
+            spot,
+            grad_tokens,
+            join_all(down_sum, got_down),
             *[join(attn_sum, got_attn, cuts[i], cuts[i + 1]) for i in range(4)],
         )
 
-    spot, *attn_parts = line.run(last_parts, attn_sum, got_attn, late, early)
+    got_out, spot, grad_tokens, down_part, *attn_parts = line.run(
+        last_norm, grad_hidden1, tokens, inverse1, dots, grad_resid, late, early, attn_sum,
+        got_attn, out_sum, down_sum, got_down
+    )
+    out_part = line.run(join_all, out_sum, got_out)
     lines = width // 128
     return (
         output,

time: 655 us -> 644 us (0.983)
  Pallas kernels: 245 us -> 261 us
  other arithmetic: 67.3 us -> 53.7 us
  waiting for transfers between devices: 209 us -> 198 us
    ppermute x74, waiting for transfers between devices: 189 us -> 163 us  [flip(): return lax.ppermute(values, axis, [(0, 1), (1, 0)])]
    pallas_call x0 -> x4, Pallas kernels: none -> 14.6 us  [fold_close(): pl.pallas_call(fold_close_kernel, grid=(2,), in_specs=[pair, pair, own, o...]
    convert_element_type x8 -> x0, other arithmetic: 14.4 us -> none  [the longest x4 7.7 us: fold_close(): (lower_keep[half:].astype(wide) + lower[half:]).astype(low)]
    all_gather x3, waiting for transfers between devices: 14 us -> 23.3 us  [weight_gather(): return lax.all_gather(rows, 'z', axis=0, tiled=True)]
    unnamed x104 -> x114, local copies, waits for them, and re-layouts: 22.5 us -> 20.6 us
  transfers between devices with their start and end apart: 86 -> 86, of which waited for: 48 -> 43; matrix products, arithmetic and copies ran while one was open for 15% -> 13% of each run, Pallas kernels for 32% -> 36%
where the time goes in v5:
time: 644 us; the launch traced here: 637 us
  Pallas kernels  261 us (41%)
  waiting for transfers between devices  198 us (31%)
  starting transfers between devices  60.7 us (9%)
  other arithmetic  53.7 us (8%)
  local copies, waits for them, and re-layouts  49.2 us (8%)
  between operations  15.1 us (2%)
    ppermute x74, waiting for transfers between devices, flip(): return lax.ppermute(values, axis, [(0, 1), (1, 0)])  163 us
    ppermute x74, starting transfers between devices, flip(): return lax.ppermute(values, axis, [(0, 1), (1, 0)])  57.8 us
    pallas_call x5, Pallas kernels, dot_grad(): pl.pallas_call(partial(matmul_kernel, product_tn), grid=(rows // tile,),...  50.3 us
    pallas_call x8, Pallas kernels, pack(): pl.pallas_call(partial(pack_kernel, normed), grid=(tiles,), in_specs=[pl....  42.4 us
    pallas_call x4, Pallas kernels, fold_held(): pl.pallas_call(fold_held_kernel, grid_spec=pltpu.PrefetchScalarGridSpec(n...  38.5 us
    pallas_call x4, Pallas kernels, fold_sent(): pl.pallas_call(fold_sent_kernel, grid_spec=pltpu.PrefetchScalarGridSpec(n...  31.1 us
    pallas_call x3, Pallas kernels, dot_in(): pl.pallas_call(partial(matmul_kernel, product_nn), grid=(count // tile,),...  29.8 us
    all_gather x3, waiting for transfers between devices, weight_gather(): return lax.all_gather(rows, 'z', axis=0, tiled=True)  23.3 us
  transfers between devices with their start and end apart: 86, of which 43 were waited for; matrix products, arithmetic and copies ran while one was open for 13% of the time, Pallas kernels for 36%

profile of v5, /device:TPU:0, one launch (start us, length us, event | category | flops | bytes accessed | tf_op | source)
XLA Modules:
  0.0 637.1 jit_solution(2611973185747321034)
XLA Ops:
  7.2 2.4 shard_map.254
  9.6 2.9 collective-permute-start
  15.2 9.5 %collective-permute-done = bf16[256,1024]{1,0:T(8,128)(2,1)S(1)} collective-permute-done((bf16[256,1024]{1,0:T(8,128)(2,1)}, bf16[256,1024]{1,0:T(8,128)(2,1)S(1)}, u32[]{:S(2)}, u32[]{:S(2)}) %collective-permute-start) | collective-permute-done | bytes 524320 | tf_op jit(solution)/shard_map/ppermute | solution.py:322
  31.3 2.1 shard_map.256
  33.4 2.7 shard_map.255
  36.0 7.7 %collective-permute-done.2 = bf16[512,512]{1,0:T(8,128)(2,1)} collective-permute-done((bf16[512,512]{1,0:T(8,128)(2,1)S(1)}, bf16[512,512]{1,0:T(8,128)(2,1)}, u32[]{:S(2)}, u32[]{:S(2)}) %collective-permute-start.2) | collective-permute-done | bytes 524320 | tf_op jit(solution)/shard_map/ppermute | solution.py:322
  45.0 6.8 %collective-permute-done.5 = s32[1024]{0:T(1024)S(1)} collective-permute-done((s32[1024]{0:T(1024)S(1)}, s32[1024]{0:T(1024)S(1)}, u32[]{:S(2)}, u32[]{:S(2)}) %collective-permute-start.5) | collective-permute-done | bytes 4128 | tf_op jit(solution)/shard_map/ppermute | solution.py:322
  57.5 7.1 %collective-permute-done.6 = bf16[256,768]{1,0:T(8,128)(2,1)} collective-permute-done((bf16[256,768]{1,0:T(8,128)(2,1)}, bf16[256,768]{1,0:T(8,128)(2,1)}, u32[]{:S(2)}, u32[]{:S(2)}) %collective-permute-start.6) | collective-permute-done | bytes 393248 | tf_op jit(solution)/shard_map/ppermute | solution.py:322
  67.7 5.7 shard_map.257
  85.7 3.7 fusion.10
  90.1 5.7 shard_map.258
  95.8 5.4 collective-permute-done.12.refs_2_
  102.4 6.9 %all-gather.4.cloned.1.call-done.weight_ref.near_ref.far_ref = bf16[2048,1024]{1,0:T(8,128)(2,1)} async-done(((bf16[512,1024]{1,0:T(8,128)(2,1)}), bf16[2048,1024]{1,0:T(8,128)(2,1)}) %all-gather.4.cloned.1.call-update) | async-done | bytes 4194320 | tf_op jit(solution)/shard_map/all_gather | solution.py:448
  117.1 11.6 %shard_map.259.joint_ref = f32[2048,768]{1,0:T(8,128)} custom-call(bf16[2048,2048]{1,0:T(8,128)(2,1)} %get-tuple-element.823.operand_ref, bf16[2048,1024]{1,0:T(8,128)(2,1)} %all-gather.4.cloned.1.call-done.weight_ref.near_ref.far_ref), custom_call_target="tpu_custom_call" | custom-call | tf_op jit(solution)/shard_map/pallas_call | solution.py:620
  128.7 2.8 copy-done
  131.5 10.4 %shard_map.260 = (bf16[2048,256]{1,0:T(8,128)(2,1)S(1)}, f32[2048,256]{1,0:T(8,128)S(1)}, bf16[2048,256]{1,0:T(8,128)(2,1)S(1)}, bf16[2048,128]{1,0:T(8,128)(2,1)S(1)}, f32[2,2,1024]{2,1,0:T(2,128)S(1)}) custom-call(f32[2048,768]{1,0:T(8,128)S(1)} %copy-done, f32[2048,128]{1,0:T(8,128)S(1)} %get-tuple-element.553.cos_ref, ...), custom_call_target="tpu_custom_call" | custom-call | tf_op jit(solution)/shard_map/pallas_call | solution.py:896
  146.5 5.0 shard_map.261
  152.0 3.9 collective-permute-done.20.near_got
  155.9 3.0 collective-permute-done.21.far_got
  160.2 6.6 %shard_map.262 = (bf16[2,512,512]{2,1,0:T(8,128)(2,1)}, bf16[2,512,512]{2,1,0:T(8,128)(2,1)}, bf16[1024,512]{1,0:T(8,128)(2,1)}, bf16[1024,512]{1,0:T(8,128)(2,1)}) custom-call(s32[1]{0:T(128)} %bitcast.place_ref.refs_4_, bf16[2048,256]{1,0:T(8,128)(2,1)} %copy-done.1, bf16[2048,1024]{1,0:T(8,128)(2,1)} %all-gather.4.cloned.1.call-done.weight_ref.near_ref.far_ref, ...), custom_call_target="tpu_custom_call" | custom-call | tf_op jit(solution)/shard_map/pallas_call | solution.py:559
  172.8 4.7 shard_map.263.refs_4_
  177.5 4.9 shard_map.264.operand_ref
  182.4 14.0 %collective-permute-done.22.upper_ref = bf16[2,512,512]{2,1,0:T(8,128)(2,1)} collective-permute-done((bf16[2,512,512]{2,1,0:T(8,128)(2,1)}, bf16[2,512,512]{2,1,0:T(8,128)(2,1)}, u32[]{:S(2)}, u32[]{:S(2)}) %collective-permute-start.22) | collective-permute-done | bytes 1048608 | tf_op jit(solution)/shard_map/ppermute | solution.py:322
  197.7 3.5 shard_map.265
  202.4 12.2 %collective-permute-done.25 = bf16[512,512]{1,0:T(8,128)(2,1)S(1)} collective-permute-done((bf16[512,512]{1,0:T(8,128)(2,1)}, bf16[512,512]{1,0:T(8,128)(2,1)S(1)}, u32[]{:S(2)}, u32[]{:S(2)}) %collective-permute-start.25) | collective-permute-done | bytes 524320 | tf_op jit(solution)/shard_map/ppermute | solution.py:322
  216.5 2.1 fusion.18
  220.6 11.3 %shard_map.266.grad_ref = f32[2048,768]{1,0:T(8,128)} custom-call(bf16[2048,2048]{1,0:T(8,128)(2,1)} %shard_map.264.operand_ref, bf16[2048,768]{1,0:T(8,128)(2,1)} %all-gather.6.cloned.1.call-done.weight_ref.near_ref.far_ref), custom_call_target="tpu_custom_call" | custom-call | tf_op jit(solution)/shard_map/pallas_call | solution.py:620
  232.0 10.0 %collective-permute-done.27.refs_2_ = bf16[1024,512]{1,0:T(8,128)(2,1)S(1)} collective-permute-done((bf16[1024,512]{1,0:T(8,128)(2,1)}, bf16[1024,512]{1,0:T(8,128)(2,1)S(1)}, u32[]{:S(2)}, u32[]{:S(2)}) %collective-permute-start.27) | collective-permute-done | bytes 1048608 | tf_op jit(solution)/shard_map/ppermute | solution.py:322
  247.8 5.7 shard_map.267
  253.5 7.2 %collective-permute-done.31 = bf16[512,512]{1,0:T(8,128)(2,1)} collective-permute-done((bf16[512,512]{1,0:T(8,128)(2,1)}, bf16[512,512]{1,0:T(8,128)(2,1)}, u32[]{:S(2)}, u32[]{:S(2)}) %collective-permute-start.31) | collective-permute-done | bytes 524320 | tf_op jit(solution)/shard_map/ppermute | solution.py:322
  264.2 2.8 collective-permute-done.34.refs_3_
  267.0 5.7 shard_map.268
  272.7 16.4 %all-gather.8.cloned.1.call-done.weight_ref.near_ref.far_ref = bf16[2048,1536]{1,0:T(8,128)(2,1)} async-done(((bf16[512,1536]{1,0:T(8,128)(2,1)}), bf16[2048,1536]{1,0:T(8,128)(2,1)}) %all-gather.8.cloned.1.call-update) | async-done | bytes 6291472 | tf_op jit(solution)/shard_map/all_gather | solution.py:448
  289.1 20.2 %shard_map.269 = (bf16[2048,768]{1,0:T(8,128)(2,1)}, bf16[2048,1536]{1,0:T(8,128)(2,1)}) custom-call(bf16[2048,2048]{1,0:T(8,128)(2,1)} %get-tuple-element.705.hidden_ref.operand_ref, bf16[2048,1536]{1,0:T(8,128)(2,1)} %all-gather.8.cloned.1.call-done.weight_ref.near_ref.far_ref, f32[2048,768]{1,0:T(8,128)} %shard_map.266.grad_ref), custom_call_target="tpu_custom_call" | custom-call | tf_op jit(solution)/shard_map/pallas_call | solution.py:673
  309.4 11.4 %shard_map.270 = (bf16[2048,512]{1,0:T(8,128)(2,1)}, bf16[2048,512]{1,0:T(8,128)(2,1)}) custom-call(s32[1]{0:T(128)} %bitcast.place_ref.refs_4_, bf16[2048,1536]{1,0:T(8,128)(2,1)} %get-tuple-element.706.operand_ref.weight_ref, bf16[2048,1536]{1,0:T(8,128)(2,1)} %all-gather.8.cloned.1.call-done.weight_ref.near_ref.far_ref, ...), custom_call_target="tpu_custom_call" | custom-call | tf_op jit(solution)/shard_map/pallas_call | solution.py:532
  321.3 10.9 %shard_map.271 = bf16[2048,768]{1,0:T(8,128)(2,1)} custom-call(bf16[2048,2048]{1,0:T(8,128)(2,1)} %get-tuple-element.705.hidden_ref.operand_ref, bf16[2048,1536]{1,0:T(8,128)(2,1)} %get-tuple-element.706.operand_ref.weight_ref), custom_call_target="tpu_custom_call" | custom-call | tf_op jit(solution)/shard_map/pallas_call | solution.py:638
  332.2 13.5 %shard_map.272 = (bf16[2,512,512]{2,1,0:T(8,128)(2,1)}, bf16[2,512,512]{2,1,0:T(8,128)(2,1)}, bf16[1024,512]{1,0:T(8,128)(2,1)}, bf16[1024,512]{1,0:T(8,128)(2,1)}) custom-call(s32[1]{0:T(128)} %bitcast.place_ref.refs_4_, bf16[2048,1536]{1,0:T(8,128)(2,1)} %get-tuple-element.706.operand_ref.weight_ref, ...), custom_call_target="tpu_custom_call" | custom-call | tf_op jit(solution)/shard_map/pallas_call | solution.py:559
  348.7 10.8 %shard_map.273 = bf16[2048,768]{1,0:T(8,128)(2,1)} custom-call(bf16[2048,2048]{1,0:T(8,128)(2,1)} %get-tuple-element.705.hidden_ref.operand_ref, bf16[2048,1536]{1,0:T(8,128)(2,1)} %get-tuple-element.706.operand_ref.weight_ref), custom_call_target="tpu_custom_call" | custom-call | tf_op jit(solution)/shard_map/pallas_call | solution.py:638
  359.6 7.3 %shard_map.274 = (bf16[2048,512]{1,0:T(8,128)(2,1)}, bf16[2048,512]{1,0:T(8,128)(2,1)}) custom-call(s32[1]{0:T(128)} %bitcast.place_ref.refs_4_, bf16[2048,768]{1,0:T(8,128)(2,1)} %get-tuple-element.759.operand_ref.weight_ref, bf16[2048,768]{1,0:T(8,128)(2,1)} %all-gather.6.cloned.1.call-done.weight_ref.near_ref.far_ref, ...), custom_call_target="tpu_custom_call" | custom-call | tf_op jit(solution)/shard_map/pallas_call | solution.py:532
  366.9 4.3 collective-permute-done.37.upper_ref
  373.0 3.4 shard_map.275
  379.2 11.4 %collective-permute-done.39 = bf16[512,512]{1,0:T(8,128)(2,1)} collective-permute-done((bf16[512,512]{1,0:T(8,128)(2,1)}, bf16[512,512]{1,0:T(8,128)(2,1)}, u32[]{:S(2)}, u32[]{:S(2)}) %collective-permute-start.39) | collective-permute-done | bytes 524320 | tf_op jit(solution)/shard_map/ppermute | solution.py:322
  396.1 2.0 fusion.3
  399.8 3.1 collective-permute-done.44
  404.2 4.8 fusion.17
  410.1 10.9 %shard_map.276 = bf16[2048,768]{1,0:T(8,128)(2,1)} custom-call(bf16[2048,2048]{1,0:T(8,128)(2,1)} %shard_map.264.operand_ref, bf16[2048,768]{1,0:T(8,128)(2,1)} %get-tuple-element.759.operand_ref.weight_ref), custom_call_target="tpu_custom_call" | custom-call | tf_op jit(solution)/shard_map/pallas_call | solution.py:638
  421.0 9.2 %shard_map.277 = (bf16[2,512,512]{2,1,0:T(8,128)(2,1)}, bf16[2,512,512]{2,1,0:T(8,128)(2,1)}, bf16[1024,512]{1,0:T(8,128)(2,1)}, bf16[1024,512]{1,0:T(8,128)(2,1)}) custom-call(s32[1]{0:T(128)} %bitcast.place_ref.refs_4_, bf16[2048,768]{1,0:T(8,128)(2,1)} %get-tuple-element.759.operand_ref.weight_ref, ...), custom_call_target="tpu_custom_call" | custom-call | tf_op jit(solution)/shard_map/pallas_call | solution.py:559
  430.2 3.6 collective-permute-done.45.refs_2_
  440.2 5.1 shard_map.278.refs_4_
  445.4 7.0 %collective-permute-done.49 = bf16[512,512]{1,0:T(8,128)(2,1)} collective-permute-done((bf16[512,512]{1,0:T(8,128)(2,1)}, bf16[512,512]{1,0:T(8,128)(2,1)}, u32[]{:S(2)}, u32[]{:S(2)}) %collective-permute-start.49) | collective-permute-done | bytes 524320 | tf_op jit(solution)/shard_map/ppermute | solution.py:322
  459.7 4.8 shard_map.279.operand_ref
  464.5 6.9 %shard_map.280.grad_mixed_ref = f32[2048,256]{1,0:T(8,128)} custom-call(bf16[2048,2048]{1,0:T(8,128)(2,1)} %shard_map.279.operand_ref, bf16[2048,1024]{1,0:T(8,128)(2,1)} %all-gather.4.cloned.1.call-done.weight_ref.near_ref.far_ref), custom_call_target="tpu_custom_call" | custom-call | tf_op jit(solution)/shard_map/pallas_call | solution.py:620
  477.0 16.0 %shard_map.281 = (bf16[2048,768]{1,0:T(8,128)(2,1)}, f32[2,128]{1,0:T(2,128)S(1)}) custom-call(f32[2048,768]{1,0:T(8,128)} %shard_map.259.joint_ref, f32[2048,128]{1,0:T(8,128)S(1)} %get-tuple-element.553.cos_ref, f32[2048,128]{1,0:T(8,128)S(1)} %get-tuple-element.554.sin_ref, s32[2,1,1024]{2,1,0:T(1,128)S(1)} %compare_select_fusion.first_ref, ...), custom_call_target="tpu_custom_call" | custom-call | tf_op jit(solution)/shard_map/pallas_call | solution.py:919
  493.0 4.0 collective-permute-done.54.upper_ref
  497.9 7.4 %shard_map.282 = (bf16[2048,512]{1,0:T(8,128)(2,1)}, bf16[2048,512]{1,0:T(8,128)(2,1)}) custom-call(s32[1]{0:T(128)} %bitcast.place_ref.refs_4_, bf16[2048,768]{1,0:T(8,128)(2,1)} %get-tuple-element.839.operand_ref.weight_ref, bf16[2048,1024]{1,0:T(8,128)(2,1)} %all-gather.4.cloned.1.call-done.weight_ref.near_ref.far_ref, ...), custom_call_target="tpu_custom_call" | custom-call | tf_op jit(solution)/shard_map/pallas_call | solution.py:532
  507.4 10.9 %shard_map.283 = bf16[2048,768]{1,0:T(8,128)(2,1)} custom-call(bf16[2048,2048]{1,0:T(8,128)(2,1)} %get-tuple-element.823.operand_ref, bf16[2048,768]{1,0:T(8,128)(2,1)} %get-tuple-element.839.operand_ref.weight_ref), custom_call_target="tpu_custom_call" | custom-call | tf_op jit(solution)/shard_map/pallas_call | solution.py:638
  518.4 4.2 shard_map.285
  527.2 9.2 %shard_map.284 = (bf16[2,512,512]{2,1,0:T(8,128)(2,1)}, bf16[2,512,512]{2,1,0:T(8,128)(2,1)}, bf16[1024,512]{1,0:T(8,128)(2,1)}, bf16[1024,512]{1,0:T(8,128)(2,1)}) custom-call(s32[1]{0:T(128)} %bitcast.place_ref.refs_4_, bf16[2048,768]{1,0:T(8,128)(2,1)} %get-tuple-element.839.operand_ref.weight_ref, ...), custom_call_target="tpu_custom_call" | custom-call | tf_op jit(solution)/shard_map/pallas_call | solution.py:559
  546.0 6.8 %shard_map.286 = bf16[2048,256]{1,0:T(8,128)(2,1)} custom-call(bf16[2048,2048]{1,0:T(8,128)(2,1)} %shard_map.279.operand_ref, bf16[2048,256]{1,0:T(8,128)(2,1)} %copy-done.1), custom_call_target="tpu_custom_call" | custom-call | tf_op jit(solution)/shard_map/pallas_call | solution.py:638
  552.8 10.0 %collective-permute-done.63.upper_ref = bf16[2,512,512]{2,1,0:T(8,128)(2,1)S(1)} collective-permute-done((bf16[2,512,512]{2,1,0:T(8,128)(2,1)}, bf16[2,512,512]{2,1,0:T(8,128)(2,1)S(1)}, u32[]{:S(2)}, u32[]{:S(2)}) %collective-permute-start.63) | collective-permute-done | bytes 1048608 | tf_op jit(solution)/shard_map/ppermute | solution.py:322
  564.7 3.5 shard_map.287
  571.1 8.7 %collective-permute-done.66 = bf16[512,512]{1,0:T(8,128)(2,1)S(1)} collective-permute-done((bf16[512,512]{1,0:T(8,128)(2,1)}, bf16[512,512]{1,0:T(8,128)(2,1)S(1)}, u32[]{:S(2)}, u32[]{:S(2)}) %collective-permute-start.66) | collective-permute-done | bytes 524320 | tf_op jit(solution)/shard_map/ppermute | solution.py:322
  594.4 5.4 collective-permute-done.69
  599.8 8.3 %reduce-scatter.14.cloned.1.call-done = bf16[512,256]{1,0:T(8,128)(2,1)} async-done(((bf16[2048,256]{1,0:T(8,128)(2,1)}), bf16[512,256]{1,0:T(8,128)(2,1)}) %reduce-scatter.14.cloned.1.call-update) | async-done | bytes 262160 | tf_op jit(solution)/shard_map/reduce_scatter | solution.py:452
  (360 shorter events, 164.4 us)
Async XLA Ops:
  7.2 102.1 %all-gather.4.cloned.1.call-start = ((), (), s32[]{:S(2)}) async-start(), calls=%async_computation.5 | async-start | bytes 5242880 | tf_op jit(solution)/shard_map/all_gather | solution.py:448
  9.6 15.1 %collective-permute-start = (bf16[256,1024]{1,0:T(8,128)(2,1)}, bf16[256,1024]{1,0:T(8,128)(2,1)S(1)}, u32[]{:S(2)}, u32[]{:S(2)}) collective-permute-start(bf16[256,1024]{1,0:T(8,128)(2,1)} %get-tuple-element.493), channel_id=1, source_target_pairs={{0,4},{4,0},{1,5},{5,1},{2,6},{6,2},{3,7},{7,3},{8,12},{12,8},{9,1... | collective-permute-start | bytes 1572872 | tf_op jit(solution)/shard_map/ppermute | solution.py:322
  13.6 13.4 %collective-permute-start.1 = (bf16[512,512]{1,0:T(8,128)(2,1)S(1)}, bf16[512,512]{1,0:T(8,128)(2,1)S(1)}, u32[]{:S(2)}, u32[]{:S(2)}) collective-permute-start(bf16[512,512]{1,0:T(8,128)(2,1)S(1)} %slice.84), channel_id=1, source_target_pairs={{0,2},{2,0},{1,3},{3,1},{4,6},{6,4},{5,7},{7,5},{8,10},{10,8},{9,1... | collective-permute-start | bytes 1572872 | tf_op jit(solution)/shard_map/ppermute | solution.py:322
  27.1 191.5 %all-gather.6.cloned.1.call-start = ((), (), s32[]{:S(2)}) async-start(), calls=%async_computation.6 | async-start | bytes 3932160 | tf_op jit(solution)/shard_map/all_gather | solution.py:448
  27.4 24.4 %collective-permute-start.3 = (bf16[1024,512]{1,0:T(8,128)(2,1)S(1)}, bf16[1024,512]{1,0:T(8,128)(2,1)S(1)}, u32[]{:S(2)}, u32[]{:S(2)}) collective-permute-start(bf16[1024,512]{1,0:T(8,128)(2,1)S(1)} %copy-done.8), channel_id=1, source_target_pairs={{0,4},{4,0},{1,5},{5,1},{2,6},{6,2},{3,7},{7,3},{8,12},{12,8},{9,1... | collective-permute-start | bytes 3145736 | tf_op jit(solution)/shard_map/ppermute | solution.py:322
  29.1 22.7 %collective-permute-start.4 = (bf16[1024,512]{1,0:T(8,128)(2,1)S(1)}, bf16[1024,512]{1,0:T(8,128)(2,1)}, u32[]{:S(2)}, u32[]{:S(2)}) collective-permute-start(bf16[1024,512]{1,0:T(8,128)(2,1)S(1)} %copy-done.8), channel_id=1, source_target_pairs={{0,1},{1,0},{2,3},{3,2},{4,5},{5,4},{6,7},{7,6},{8,9},{9,8},{10,11... | collective-permute-start | bytes 3145736 | tf_op jit(solution)/shard_map/ppermute | solution.py:322
  29.2 14.5 %collective-permute-start.2 = (bf16[512,512]{1,0:T(8,128)(2,1)S(1)}, bf16[512,512]{1,0:T(8,128)(2,1)}, u32[]{:S(2)}, u32[]{:S(2)}) collective-permute-start(bf16[512,512]{1,0:T(8,128)(2,1)S(1)} %slice.85), channel_id=1, source_target_pairs={{0,2},{2,0},{1,3},{3,1},{4,6},{6,4},{5,7},{7,5},{8,10},{10,8},{9,1... | collective-permute-start | bytes 1572872 | tf_op jit(solution)/shard_map/ppermute | solution.py:322
  30.8 21.1 %collective-permute-start.5 = (s32[1024]{0:T(1024)S(1)}, s32[1024]{0:T(1024)S(1)}, u32[]{:S(2)}, u32[]{:S(2)}) collective-permute-start(s32[1024]{0:T(1024)S(1)} %copy-done.52), channel_id=1, source_target_pairs={{0,4},{4,0},{1,5},{5,1},{2,6},{6,2},{3,7},{7,3},{8,12},{12,8},{9,1... | collective-permute-start | bytes 12296 | tf_op jit(solution)/shard_map/ppermute | solution.py:322
  51.8 14.9 %collective-permute-start.10 = (bf16[1024,512]{1,0:T(8,128)(2,1)S(1)}, bf16[1024,512]{1,0:T(8,128)(2,1)S(1)}, u32[]{:S(2)}, u32[]{:S(2)}) collective-permute-start(bf16[1024,512]{1,0:T(8,128)(2,1)S(1)} %pad_maximum_fusion.4.refs_2_), channel_id=1, source_target_pairs={{0,1},{1,0},{2,3},{3,2},{4,5},{5,4},{6,7},{7,6},{8,9},{9,8},{10,11... | collective-permute-start | bytes 3145736 | tf_op jit(solution)/shard_map/ppermute | solution.py:322
  51.9 23.2 %collective-permute-start.7 = (bf16[1024,512]{1,0:T(8,128)(2,1)S(1)}, bf16[1024,512]{1,0:T(8,128)(2,1)}, u32[]{:S(2)}, u32[]{:S(2)}) collective-permute-start(bf16[1024,512]{1,0:T(8,128)(2,1)S(1)} %collective-permute-done.3.refs_0_), channel_id=1, source_target_pairs={{0,1},{1,0},{2,3},{3,2},{4,5},{5,4},{6,7},{7,6},{8,9},{9,8},{10,11... | collective-permute-start | bytes 3145736 | tf_op jit(solution)/shard_map/ppermute | solution.py:322
  52.4 12.3 %collective-permute-start.6 = (bf16[256,768]{1,0:T(8,128)(2,1)}, bf16[256,768]{1,0:T(8,128)(2,1)}, u32[]{:S(2)}, u32[]{:S(2)}) collective-permute-start(bf16[256,768]{1,0:T(8,128)(2,1)} %get-tuple-element.517), channel_id=1, source_target_pairs={{0,4},{4,0},{1,5},{5,1},{2,6},{6,2},{3,7},{7,3},{8,12},{12,8},{9,1... | collective-permute-start | bytes 1179656 | tf_op jit(solution)/shard_map/ppermute | solution.py:322
  55.5 19.6 %collective-permute-start.8 = (bf16[512,512]{1,0:T(8,128)(2,1)}, bf16[512,512]{1,0:T(8,128)(2,1)}, u32[]{:S(2)}, u32[]{:S(2)}) collective-permute-start(bf16[512,512]{1,0:T(8,128)(2,1)} %slice.86), channel_id=1, source_target_pairs={{0,4},{4,0},{1,5},{5,1},{2,6},{6,2},{3,7},{7,3},{8,12},{12,8},{9,1... | collective-permute-start | bytes 1572872 | tf_op jit(solution)/shard_map/ppermute | solution.py:322
  56.1 19.0 %collective-permute-start.9 = (bf16[512,512]{1,0:T(8,128)(2,1)}, bf16[512,512]{1,0:T(8,128)(2,1)}, u32[]{:S(2)}, u32[]{:S(2)}) collective-permute-start(bf16[512,512]{1,0:T(8,128)(2,1)} %slice.87), channel_id=1, source_target_pairs={{0,2},{2,0},{1,3},{3,1},{4,6},{6,4},{5,7},{7,5},{8,10},{10,8},{9,1... | collective-permute-start | bytes 1572872 | tf_op jit(solution)/shard_map/ppermute | solution.py:322
  75.1 214.0 %all-gather.8.cloned.1.call-start = ((), (), s32[]{:S(2)}) async-start(), calls=%async_computation.7 | async-start | bytes 7864320 | tf_op jit(solution)/shard_map/all_gather | solution.py:448
  76.8 24.4 %collective-permute-start.12 = (bf16[1024,512]{1,0:T(8,128)(2,1)S(1)}, bf16[1024,512]{1,0:T(8,128)(2,1)}, u32[]{:S(2)}, u32[]{:S(2)}) collective-permute-start(bf16[1024,512]{1,0:T(8,128)(2,1)S(1)} %get-tuple-element.601.refs_0_), channel_id=1, source_target_pairs={{0,2},{2,0},{1,3},{3,1},{4,6},{6,4},{5,7},{7,5},{8,10},{10,8},{9,1... | collective-permute-start | bytes 3145736 | tf_op jit(solution)/shard_map/ppermute | solution.py:322
  78.3 24.1 %collective-permute-start.13 = (bf16[1024,512]{1,0:T(8,128)(2,1)S(1)}, bf16[1024,512]{1,0:T(8,128)(2,1)}, u32[]{:S(2)}, u32[]{:S(2)}) collective-permute-start(bf16[1024,512]{1,0:T(8,128)(2,1)S(1)} %get-tuple-element.601.refs_0_), channel_id=1, source_target_pairs={{0,4},{4,0},{1,5},{5,1},{2,6},{6,2},{3,7},{7,3},{8,12},{12,8},{9,1... | collective-permute-start | bytes 3145736 | tf_op jit(solution)/shard_map/ppermute | solution.py:322
  79.8 22.6 %collective-permute-start.14 = (bf16[1024,512]{1,0:T(8,128)(2,1)S(1)}, bf16[1024,512]{1,0:T(8,128)(2,1)}, u32[]{:S(2)}, u32[]{:S(2)}) collective-permute-start(bf16[1024,512]{1,0:T(8,128)(2,1)S(1)} %get-tuple-element.601.refs_0_), channel_id=1, source_target_pairs={{0,1},{1,0},{2,3},{3,2},{4,5},{5,4},{6,7},{7,6},{8,9},{9,8},{10,11... | collective-permute-start | bytes 3145736 | tf_op jit(solution)/shard_map/ppermute | solution.py:322
  109.3 35.7 %collective-permute-start.15 = (bf16[256,1536]{1,0:T(8,128)(2,1)}, bf16[256,1536]{1,0:T(8,128)(2,1)S(1)}, u32[]{:S(2)}, u32[]{:S(2)}) collective-permute-start(bf16[256,1536]{1,0:T(8,128)(2,1)} %get-tuple-element.550), channel_id=1, source_target_pairs={{0,4},{4,0},{1,5},{5,1},{2,6},{6,2},{3,7},{7,3},{8,12},{12,8},{9,1... | collective-permute-start | bytes 2359304 | tf_op jit(solution)/shard_map/ppermute | solution.py:322
  110.8 35.6 %collective-permute-start.16 = (bf16[1024,512]{1,0:T(8,128)(2,1)}, bf16[1024,512]{1,0:T(8,128)(2,1)}, u32[]{:S(2)}, u32[]{:S(2)}) collective-permute-start(bf16[1024,512]{1,0:T(8,128)(2,1)} %collective-permute-done.12.refs_2_), channel_id=1, source_target_pairs={{0,1},{1,0},{2,3},{3,2},{4,5},{5,4},{6,7},{7,6},{8,9},{9,8},{10,11... | collective-permute-start | bytes 3145736 | tf_op jit(solution)/shard_map/ppermute | solution.py:322
  110.8 35.6 %collective-permute-start.17 = (bf16[1024,512]{1,0:T(8,128)(2,1)}, bf16[1024,512]{1,0:T(8,128)(2,1)}, u32[]{:S(2)}, u32[]{:S(2)}) collective-permute-start(bf16[1024,512]{1,0:T(8,128)(2,1)} %collective-permute-done.13.refs_0_), channel_id=1, source_target_pairs={{0,1},{1,0},{2,3},{3,2},{4,5},{5,4},{6,7},{7,6},{8,9},{9,8},{10,11... | collective-permute-start | bytes 3145736 | tf_op jit(solution)/shard_map/ppermute | solution.py:322
  115.1 31.3 %collective-permute-start.18 = (bf16[512,512]{1,0:T(8,128)(2,1)}, bf16[512,512]{1,0:T(8,128)(2,1)}, u32[]{:S(2)}, u32[]{:S(2)}) collective-permute-start(bf16[512,512]{1,0:T(8,128)(2,1)} %slice.91), channel_id=1, source_target_pairs={{0,4},{4,0},{1,5},{5,1},{2,6},{6,2},{3,7},{7,3},{8,12},{12,8},{9,1... | collective-permute-start | bytes 1572872 | tf_op jit(solution)/shard_map/ppermute | solution.py:322
  115.6 30.8 %collective-permute-start.19 = (bf16[512,512]{1,0:T(8,128)(2,1)}, bf16[512,512]{1,0:T(8,128)(2,1)}, u32[]{:S(2)}, u32[]{:S(2)}) collective-permute-start(bf16[512,512]{1,0:T(8,128)(2,1)} %slice.92), channel_id=1, source_target_pairs={{0,2},{2,0},{1,3},{3,1},{4,6},{6,4},{5,7},{7,5},{8,10},{10,8},{9,1... | collective-permute-start | bytes 1572872 | tf_op jit(solution)/shard_map/ppermute | solution.py:322
  146.4 287.4 %reduce-scatter.6.cloned.1.call-start = ((), (), s32[]{:S(2)}) async-start(), calls=%async_computation.8 | async-start | bytes 3932160 | tf_op jit(solution)/shard_map/reduce_scatter | solution.py:452
  170.7 25.8 %collective-permute-start.22 = (bf16[2,512,512]{2,1,0:T(8,128)(2,1)}, bf16[2,512,512]{2,1,0:T(8,128)(2,1)}, u32[]{:S(2)}, u32[]{:S(2)}) collective-permute-start(bf16[2,512,512]{2,1,0:T(8,128)(2,1)} %get-tuple-element.593), channel_id=1, source_target_pairs={{0,4},{4,0},{1,5},{5,1},{2,6},{6,2},{3,7},{7,3},{8,12},{12,8},{9,1... | collective-permute-start | bytes 3145736 | tf_op jit(solution)/shard_map/ppermute | solution.py:322
  172.2 25.5 %collective-permute-start.23 = (bf16[1024,512]{1,0:T(8,128)(2,1)}, bf16[1024,512]{1,0:T(8,128)(2,1)}, u32[]{:S(2)}, u32[]{:S(2)}) collective-permute-start(bf16[1024,512]{1,0:T(8,128)(2,1)} %get-tuple-element.595), channel_id=1, source_target_pairs={{0,2},{2,0},{1,3},{3,1},{4,6},{6,4},{5,7},{7,5},{8,10},{10,8},{9,1... | collective-permute-start | bytes 3145736 | tf_op jit(solution)/shard_map/ppermute | solution.py:322
  201.2 13.4 %collective-permute-start.25 = (bf16[512,512]{1,0:T(8,128)(2,1)}, bf16[512,512]{1,0:T(8,128)(2,1)S(1)}, u32[]{:S(2)}, u32[]{:S(2)}) collective-permute-start(bf16[512,512]{1,0:T(8,128)(2,1)} %get-tuple-element.616), channel_id=1, source_target_pairs={{0,2},{2,0},{1,3},{3,1},{4,6},{6,4},{5,7},{7,5},{8,10},{10,8},{9,1... | collective-permute-start | bytes 1572872 | tf_op jit(solution)/shard_map/ppermute | solution.py:322
  201.8 13.0 %collective-permute-start.26 = (bf16[512,512]{1,0:T(8,128)(2,1)}, bf16[512,512]{1,0:T(8,128)(2,1)S(1)}, u32[]{:S(2)}, u32[]{:S(2)}) collective-permute-start(bf16[512,512]{1,0:T(8,128)(2,1)} %get-tuple-element.618), channel_id=1, source_target_pairs={{0,4},{4,0},{1,5},{5,1},{2,6},{6,2},{3,7},{7,3},{8,12},{12,8},{9,1... | collective-permute-start | bytes 1572872 | tf_op jit(solution)/shard_map/ppermute | solution.py:322
  218.6 23.4 %collective-permute-start.27 = (bf16[1024,512]{1,0:T(8,128)(2,1)}, bf16[1024,512]{1,0:T(8,128)(2,1)S(1)}, u32[]{:S(2)}, u32[]{:S(2)}) collective-permute-start(bf16[1024,512]{1,0:T(8,128)(2,1)} %get-tuple-element.749.refs_0_), channel_id=1, source_target_pairs={{0,2},{2,0},{1,3},{3,1},{4,6},{6,4},{5,7},{7,5},{8,10},{10,8},{9,1... | collective-permute-start | bytes 3145736 | tf_op jit(solution)/shard_map/ppermute | solution.py:322
  220.0 23.2 %collective-permute-start.28 = (bf16[1024,512]{1,0:T(8,128)(2,1)}, bf16[1024,512]{1,0:T(8,128)(2,1)}, u32[]{:S(2)}, u32[]{:S(2)}) collective-permute-start(bf16[1024,512]{1,0:T(8,128)(2,1)} %get-tuple-element.749.refs_0_), channel_id=1, source_target_pairs={{0,4},{4,0},{1,5},{5,1},{2,6},{6,2},{3,7},{7,3},{8,12},{12,8},{9,1... | collective-permute-start | bytes 3145736 | tf_op jit(solution)/shard_map/ppermute | solution.py:322
  220.6 22.6 %collective-permute-start.29 = (bf16[1024,512]{1,0:T(8,128)(2,1)}, bf16[1024,512]{1,0:T(8,128)(2,1)S(1)}, u32[]{:S(2)}, u32[]{:S(2)}) collective-permute-start(bf16[1024,512]{1,0:T(8,128)(2,1)} %get-tuple-element.749.refs_0_), channel_id=1, source_target_pairs={{0,1},{1,0},{2,3},{3,2},{4,5},{5,4},{6,7},{7,6},{8,9},{9,8},{10,11... | collective-permute-start | bytes 3145736 | tf_op jit(solution)/shard_map/ppermute | solution.py:322
  243.3 17.8 %collective-permute-start.30 = (bf16[1024,512]{1,0:T(8,128)(2,1)}, bf16[1024,512]{1,0:T(8,128)(2,1)}, u32[]{:S(2)}, u32[]{:S(2)}) collective-permute-start(bf16[1024,512]{1,0:T(8,128)(2,1)} %collective-permute-done.28.refs_0_), channel_id=1, source_target_pairs={{0,1},{1,0},{2,3},{3,2},{4,5},{5,4},{6,7},{7,6},{8,9},{9,8},{10,11... | collective-permute-start | bytes 3145736 | tf_op jit(solution)/shard_map/ppermute | solution.py:322
  246.5 14.2 %collective-permute-start.31 = (bf16[512,512]{1,0:T(8,128)(2,1)}, bf16[512,512]{1,0:T(8,128)(2,1)}, u32[]{:S(2)}, u32[]{:S(2)}) collective-permute-start(bf16[512,512]{1,0:T(8,128)(2,1)} %slice.93), channel_id=1, source_target_pairs={{0,4},{4,0},{1,5},{5,1},{2,6},{6,2},{3,7},{7,3},{8,12},{12,8},{9,1... | collective-permute-start | bytes 1572872 | tf_op jit(solution)/shard_map/ppermute | solution.py:322
  247.1 13.9 %collective-permute-start.32 = (bf16[512,512]{1,0:T(8,128)(2,1)}, bf16[512,512]{1,0:T(8,128)(2,1)}, u32[]{:S(2)}, u32[]{:S(2)}) collective-permute-start(bf16[512,512]{1,0:T(8,128)(2,1)} %slice.94), channel_id=1, source_target_pairs={{0,2},{2,0},{1,3},{3,1},{4,6},{6,4},{5,7},{7,5},{8,10},{10,8},{9,1... | collective-permute-start | bytes 1572872 | tf_op jit(solution)/shard_map/ppermute | solution.py:322
  332.2 139.2 %reduce-scatter.8.cloned.1.call-start = ((), (), s32[]{:S(2)}) async-start(), calls=%async_computation.9 | async-start | bytes 3932160 | tf_op jit(solution)/shard_map/reduce_scatter | solution.py:452
  345.7 25.4 %collective-permute-start.37 = (bf16[2,512,512]{2,1,0:T(8,128)(2,1)}, bf16[2,512,512]{2,1,0:T(8,128)(2,1)}, u32[]{:S(2)}, u32[]{:S(2)}) collective-permute-start(bf16[2,512,512]{2,1,0:T(8,128)(2,1)} %get-tuple-element.701), channel_id=1, source_target_pairs={{0,4},{4,0},{1,5},{5,1},{2,6},{6,2},{3,7},{7,3},{8,12},{12,8},{9,1... | collective-permute-start | bytes 3145736 | tf_op jit(solution)/shard_map/ppermute | solution.py:322
  347.2 25.2 %collective-permute-start.38 = (bf16[1024,512]{1,0:T(8,128)(2,1)}, bf16[1024,512]{1,0:T(8,128)(2,1)}, u32[]{:S(2)}, u32[]{:S(2)}) collective-permute-start(bf16[1024,512]{1,0:T(8,128)(2,1)} %get-tuple-element.703), channel_id=1, source_target_pairs={{0,2},{2,0},{1,3},{3,1},{4,6},{6,4},{5,7},{7,5},{8,10},{10,8},{9,1... | collective-permute-start | bytes 3145736 | tf_op jit(solution)/shard_map/ppermute | solution.py:322
  372.4 146.0 %reduce-scatter.10.cloned.1.call-start = ((), (), s32[]{:S(2)}) async-start(), calls=%async_computation.10 | async-start | bytes 3932160 | tf_op jit(solution)/shard_map/reduce_scatter | solution.py:452
  372.4 19.5 %collective-permute-start.41 = (bf16[2048,512]{1,0:T(8,128)(2,1)}, bf16[2048,512]{1,0:T(8,128)(2,1)}, u32[]{:S(2)}, u32[]{:S(2)}) collective-permute-start(bf16[2048,512]{1,0:T(8,128)(2,1)} %get-tuple-element.727), channel_id=1, source_target_pairs={{0,1},{1,0},{2,3},{3,2},{4,5},{5,4},{6,7},{7,6},{8,9},{9,8},{10,11... | collective-permute-start | bytes 6291464 | tf_op jit(solution)/shard_map/ppermute | solution.py:322
  372.5 19.4 %collective-permute-start.42 = (bf16[2048,512]{1,0:T(8,128)(2,1)}, bf16[2048,512]{1,0:T(8,128)(2,1)}, u32[]{:S(2)}, u32[]{:S(2)}) collective-permute-start(bf16[2048,512]{1,0:T(8,128)(2,1)} %get-tuple-element.728), channel_id=1, source_target_pairs={{0,1},{1,0},{2,3},{3,2},{4,5},{5,4},{6,7},{7,6},{8,9},{9,8},{10,11... | collective-permute-start | bytes 6291464 | tf_op jit(solution)/shard_map/ppermute | solution.py:322
  376.4 14.3 %collective-permute-start.39 = (bf16[512,512]{1,0:T(8,128)(2,1)}, bf16[512,512]{1,0:T(8,128)(2,1)}, u32[]{:S(2)}, u32[]{:S(2)}) collective-permute-start(bf16[512,512]{1,0:T(8,128)(2,1)} %get-tuple-element.724), channel_id=1, source_target_pairs={{0,2},{2,0},{1,3},{3,1},{4,6},{6,4},{5,7},{7,5},{8,10},{10,8},{9,1... | collective-permute-start | bytes 1572872 | tf_op jit(solution)/shard_map/ppermute | solution.py:322
  378.0 13.9 %collective-permute-start.40 = (bf16[512,512]{1,0:T(8,128)(2,1)}, bf16[512,512]{1,0:T(8,128)(2,1)}, u32[]{:S(2)}, u32[]{:S(2)}) collective-permute-start(bf16[512,512]{1,0:T(8,128)(2,1)} %get-tuple-element.726), channel_id=1, source_target_pairs={{0,4},{4,0},{1,5},{5,1},{2,6},{6,2},{3,7},{7,3},{8,12},{12,8},{9,1... | collective-permute-start | bytes 1572872 | tf_op jit(solution)/shard_map/ppermute | solution.py:322
  409.0 24.8 %collective-permute-start.45 = (bf16[1024,512]{1,0:T(8,128)(2,1)}, bf16[1024,512]{1,0:T(8,128)(2,1)}, u32[]{:S(2)}, u32[]{:S(2)}) collective-permute-start(bf16[1024,512]{1,0:T(8,128)(2,1)} %get-tuple-element.776.refs_0_), channel_id=1, source_target_pairs={{0,2},{2,0},{1,3},{3,1},{4,6},{6,4},{5,7},{7,5},{8,10},{10,8},{9,1... | collective-permute-start | bytes 3145736 | tf_op jit(solution)/shard_map/ppermute | solution.py:322
  409.5 24.3 %collective-permute-start.46 = (bf16[1024,512]{1,0:T(8,128)(2,1)}, bf16[1024,512]{1,0:T(8,128)(2,1)}, u32[]{:S(2)}, u32[]{:S(2)}) collective-permute-start(bf16[1024,512]{1,0:T(8,128)(2,1)} %get-tuple-element.776.refs_0_), channel_id=1, source_target_pairs={{0,4},{4,0},{1,5},{5,1},{2,6},{6,2},{3,7},{7,3},{8,12},{12,8},{9,1... | collective-permute-start | bytes 3145736 | tf_op jit(solution)/shard_map/ppermute | solution.py:322
  410.1 23.7 %collective-permute-start.47 = (bf16[1024,512]{1,0:T(8,128)(2,1)}, bf16[1024,512]{1,0:T(8,128)(2,1)}, u32[]{:S(2)}, u32[]{:S(2)}) collective-permute-start(bf16[1024,512]{1,0:T(8,128)(2,1)} %get-tuple-element.776.refs_0_), channel_id=1, source_target_pairs={{0,1},{1,0},{2,3},{3,2},{4,5},{5,4},{6,7},{7,6},{8,9},{9,8},{10,11... | collective-permute-start | bytes 3145736 | tf_op jit(solution)/shard_map/ppermute | solution.py:322
  433.8 146.4 %reduce-scatter.12.cloned.1.call-start = ((), (), s32[]{:S(2)}) async-start(), calls=%async_computation.11 | async-start | bytes 3932160 | tf_op jit(solution)/shard_map/reduce_scatter | solution.py:452
  433.9 18.6 %collective-permute-start.48 = (bf16[1024,512]{1,0:T(8,128)(2,1)}, bf16[1024,512]{1,0:T(8,128)(2,1)}, u32[]{:S(2)}, u32[]{:S(2)}) collective-permute-start(bf16[1024,512]{1,0:T(8,128)(2,1)} %collective-permute-done.46.refs_0_), channel_id=1, source_target_pairs={{0,1},{1,0},{2,3},{3,2},{4,5},{5,4},{6,7},{7,6},{8,9},{9,8},{10,11... | collective-permute-start | bytes 3145736 | tf_op jit(solution)/shard_map/ppermute | solution.py:322
  438.2 14.2 %collective-permute-start.49 = (bf16[512,512]{1,0:T(8,128)(2,1)}, bf16[512,512]{1,0:T(8,128)(2,1)}, u32[]{:S(2)}, u32[]{:S(2)}) collective-permute-start(bf16[512,512]{1,0:T(8,128)(2,1)} %slice.95), channel_id=1, source_target_pairs={{0,4},{4,0},{1,5},{5,1},{2,6},{6,2},{3,7},{7,3},{8,12},{12,8},{9,1... | collective-permute-start | bytes 1572872 | tf_op jit(solution)/shard_map/ppermute | solution.py:322
  438.6 13.9 %collective-permute-start.50 = (bf16[512,512]{1,0:T(8,128)(2,1)}, bf16[512,512]{1,0:T(8,128)(2,1)}, u32[]{:S(2)}, u32[]{:S(2)}) collective-permute-start(bf16[512,512]{1,0:T(8,128)(2,1)} %slice.96), channel_id=1, source_target_pairs={{0,2},{2,0},{1,3},{3,1},{4,6},{6,4},{5,7},{7,5},{8,10},{10,8},{9,1... | collective-permute-start | bytes 1572872 | tf_op jit(solution)/shard_map/ppermute | solution.py:322
  458.1 13.3 %collective-permute-start.52 = (bf16[256,768]{1,0:T(8,128)(2,1)}, bf16[256,768]{1,0:T(8,128)(2,1)}, u32[]{:S(2)}, u32[]{:S(2)}) collective-permute-start(bf16[256,768]{1,0:T(8,128)(2,1)} %constant_dynamic-slice_fusion.4), channel_id=1, source_target_pairs={{0,4},{4,0},{1,5},{5,1},{2,6},{6,2},{3,7},{7,3},{8,12},{12,8},{9,1... | collective-permute-start | bytes 1179656 | tf_op jit(solution)/shard_map/ppermute | solution.py:322
  471.4 25.6 %collective-permute-start.54 = (bf16[2,512,512]{2,1,0:T(8,128)(2,1)}, bf16[2,512,512]{2,1,0:T(8,128)(2,1)}, u32[]{:S(2)}, u32[]{:S(2)}) collective-permute-start(bf16[2,512,512]{2,1,0:T(8,128)(2,1)} %get-tuple-element.811), channel_id=1, source_target_pairs={{0,4},{4,0},{1,5},{5,1},{2,6},{6,2},{3,7},{7,3},{8,12},{12,8},{9,1... | collective-permute-start | bytes 3145736 | tf_op jit(solution)/shard_map/ppermute | solution.py:322
  472.6 25.3 %collective-permute-start.55 = (bf16[1024,512]{1,0:T(8,128)(2,1)}, bf16[1024,512]{1,0:T(8,128)(2,1)}, u32[]{:S(2)}, u32[]{:S(2)}) collective-permute-start(bf16[1024,512]{1,0:T(8,128)(2,1)} %get-tuple-element.813), channel_id=1, source_target_pairs={{0,2},{2,0},{1,3},{3,1},{4,6},{6,4},{5,7},{7,5},{8,10},{10,8},{9,1... | collective-permute-start | bytes 3145736 | tf_op jit(solution)/shard_map/ppermute | solution.py:322
  505.3 13.0 %collective-permute-start.56 = (bf16[2048,512]{1,0:T(8,128)(2,1)}, bf16[2048,512]{1,0:T(8,128)(2,1)S(1)}, u32[]{:S(2)}, u32[]{:S(2)}) collective-permute-start(bf16[2048,512]{1,0:T(8,128)(2,1)} %get-tuple-element.821), channel_id=1, source_target_pairs={{0,1},{1,0},{2,3},{3,2},{4,5},{5,4},{6,7},{7,6},{8,9},{9,8},{10,11... | collective-permute-start | bytes 6291464 | tf_op jit(solution)/shard_map/ppermute | solution.py:322
  505.3 13.0 %collective-permute-start.57 = (bf16[2048,512]{1,0:T(8,128)(2,1)}, bf16[2048,512]{1,0:T(8,128)(2,1)}, u32[]{:S(2)}, u32[]{:S(2)}) collective-permute-start(bf16[2048,512]{1,0:T(8,128)(2,1)} %get-tuple-element.822), channel_id=1, source_target_pairs={{0,1},{1,0},{2,3},{3,2},{4,5},{5,4},{6,7},{7,6},{8,9},{9,8},{10,11... | collective-permute-start | bytes 6291464 | tf_op jit(solution)/shard_map/ppermute | solution.py:322
  506.6 11.7 %collective-permute-start.58 = (bf16[256,768]{1,0:T(8,128)(2,1)}, bf16[256,768]{1,0:T(8,128)(2,1)S(1)}, u32[]{:S(2)}, u32[]{:S(2)}) collective-permute-start(bf16[256,768]{1,0:T(8,128)(2,1)} %constant_dynamic-slice_fusion.3), channel_id=1, source_target_pairs={{0,4},{4,0},{1,5},{5,1},{2,6},{6,2},{3,7},{7,3},{8,12},{12,8},{9,1... | collective-permute-start | bytes 1179656 | tf_op jit(solution)/shard_map/ppermute | solution.py:322
  518.3 89.8 %reduce-scatter.14.cloned.1.call-start = ((), (), s32[]{:S(2)}) async-start(), calls=%async_computation.12 | async-start | bytes 1310720 | tf_op jit(solution)/shard_map/reduce_scatter | solution.py:452
  522.6 15.4 %collective-permute-start.60 = (bf16[512,512]{1,0:T(8,128)(2,1)}, bf16[512,512]{1,0:T(8,128)(2,1)S(1)}, u32[]{:S(2)}, u32[]{:S(2)}) collective-permute-start(bf16[512,512]{1,0:T(8,128)(2,1)} %get-tuple-element.852), channel_id=1, source_target_pairs={{0,2},{2,0},{1,3},{3,1},{4,6},{6,4},{5,7},{7,5},{8,10},{10,8},{9,1... | collective-permute-start | bytes 1572872 | tf_op jit(solution)/shard_map/ppermute | solution.py:322
  524.4 13.6 %collective-permute-start.61 = (bf16[512,512]{1,0:T(8,128)(2,1)}, bf16[512,512]{1,0:T(8,128)(2,1)S(1)}, u32[]{:S(2)}, u32[]{:S(2)}) collective-permute-start(bf16[512,512]{1,0:T(8,128)(2,1)} %get-tuple-element.854), channel_id=1, source_target_pairs={{0,4},{4,0},{1,5},{5,1},{2,6},{6,2},{3,7},{7,3},{8,12},{12,8},{9,1... | collective-permute-start | bytes 1572872 | tf_op jit(solution)/shard_map/ppermute | solution.py:322
  525.6 12.4 %collective-permute-start.59 = (f32[6,128]{1,0:T(8,128)S(1)}, f32[6,128]{1,0:T(8,128)S(1)}, u32[]{:S(2)}, u32[]{:S(2)}) collective-permute-start(f32[6,128]{1,0:T(8,128)S(1)} %pad_maximum_fusion.9), channel_id=1, source_target_pairs={{0,4},{4,0},{1,5},{5,1},{2,6},{6,2},{3,7},{7,3},{8,12},{12,8},{9,1... | collective-permute-start | bytes 9224 | tf_op jit(solution)/shard_map/ppermute | solution.py:322
  538.0 14.7 %collective-permute-start.62 = (f32[6,128]{1,0:T(8,128)S(1)}, f32[6,128]{1,0:T(8,128)S(1)}, u32[]{:S(2)}, u32[]{:S(2)}) collective-permute-start(f32[6,128]{1,0:T(8,128)S(1)} %fusion.14), channel_id=1, source_target_pairs={{0,8},{8,0},{16,24},{24,16},{1,9},{9,1},{17,25},{25,17},{2,10},{10... | collective-permute-start | bytes 9224 | tf_op jit(solution)/shard_map/ppermute | solution.py:465
  539.0 23.9 %collective-permute-start.63 = (bf16[2,512,512]{2,1,0:T(8,128)(2,1)}, bf16[2,512,512]{2,1,0:T(8,128)(2,1)S(1)}, u32[]{:S(2)}, u32[]{:S(2)}) collective-permute-start(bf16[2,512,512]{2,1,0:T(8,128)(2,1)} %get-tuple-element.878), channel_id=1, source_target_pairs={{0,4},{4,0},{1,5},{5,1},{2,6},{6,2},{3,7},{7,3},{8,12},{12,8},{9,1... | collective-permute-start | bytes 3145736 | tf_op jit(solution)/shard_map/ppermute | solution.py:322
  540.1 23.6 %collective-permute-start.64 = (bf16[1024,512]{1,0:T(8,128)(2,1)}, bf16[1024,512]{1,0:T(8,128)(2,1)S(1)}, u32[]{:S(2)}, u32[]{:S(2)}) collective-permute-start(bf16[1024,512]{1,0:T(8,128)(2,1)} %get-tuple-element.880), channel_id=1, source_target_pairs={{0,2},{2,0},{1,3},{3,1},{4,6},{6,4},{5,7},{7,5},{8,10},{10,8},{9,1... | collective-permute-start | bytes 3145736 | tf_op jit(solution)/shard_map/ppermute | solution.py:322
  582.0 12.4 %collective-permute-start.68 = (bf16[256,768]{1,0:T(8,128)(2,1)}, bf16[256,768]{1,0:T(8,128)(2,1)S(1)}, u32[]{:S(2)}, u32[]{:S(2)}) collective-permute-start(bf16[256,768]{1,0:T(8,128)(2,1)} %constant_dynamic-slice_fusion.2), channel_id=1, source_target_pairs={{0,4},{4,0},{1,5},{5,1},{2,6},{6,2},{3,7},{7,3},{8,12},{12,8},{9,1... | collective-permute-start | bytes 1179656 | tf_op jit(solution)/shard_map/ppermute | solution.py:322
  586.1 13.6 %collective-permute-start.69 = (bf16[256,768]{1,0:T(8,128)(2,1)S(1)}, bf16[256,768]{1,0:T(8,128)(2,1)}, u32[]{:S(2)}, u32[]{:S(2)}) collective-permute-start(bf16[256,768]{1,0:T(8,128)(2,1)S(1)} %constant_dynamic-slice_fusion.1), channel_id=1, source_target_pairs={{0,4},{4,0},{1,5},{5,1},{2,6},{6,2},{3,7},{7,3},{8,12},{12,8},{9,1... | collective-permute-start | bytes 1179656 | tf_op jit(solution)/shard_map/ppermute | solution.py:322
  609.7 17.5 %collective-permute-start.74 = (bf16[256,256]{1,0:T(8,128)(2,1)}, bf16[256,256]{1,0:T(8,128)(2,1)}, u32[]{:S(2)}, u32[]{:S(2)}) collective-permute-start(bf16[256,256]{1,0:T(8,128)(2,1)} %constant_dynamic-slice_fusion), channel_id=1, source_target_pairs={{0,4},{4,0},{1,5},{5,1},{2,6},{6,2},{3,7},{7,3},{8,12},{12,8},{9,1... | collective-permute-start | bytes 393224 | tf_op jit(solution)/shard_map/ppermute | solution.py:322
  (76 other events, 466.6 us)
Sparse Core Ops, SparseCore 0:
  27.2 82.0 all-gather.3
  110.9 62.0 all-gather.5
  175.1 113.9 all-gather.7
  332.3 58.5 reduce-scatter.5
  393.0 60.2 reduce-scatter.7
  455.5 60.2 reduce-scatter.9
  518.4 60.0 reduce-scatter.11
  580.9 27.2 reduce-scatter.13

commit v6 on v5

--- a/solution.py
+++ b/solution.py
@@ -468,6 +468,32 @@
 vmem = pltpu.CompilerParams(vmem_limit_bytes=56 * 1024 * 1024)
 
 
+def join_kernel(widths, across_ref, sums_ref, got_ref, *out_refs):
+    across = across_ref[0]
+    rows = got_ref.shape[0]
+    keep = pl.ds(pl.multiple_of(across * rows, rows), rows)
+    at = 0
+    for width, out_ref in zip(widths, out_refs):
+        own = pl.ds(pl.multiple_of(across * width, width), width)
+        other = pl.ds(pl.multiple_of((1 - across) * width, width), width)
+        out_ref[:, own] = sums_ref[keep, at : at + width].astype(jnp.float32)
+        out_ref[:, other] = got_ref[:, at : at + width].astype(jnp.float32)
+        at += width
+
+
+def join_parts(sums, got, across, widths):
+    rows = got.shape[0]
+    whole = pl.BlockSpec(memory_space=pltpu.VMEM)
+    return pl.pallas_call(
+        partial(join_kernel, widths),
+        in_specs=[pl.BlockSpec(memory_space=pltpu.SMEM), whole, whole],
+        out_specs=[whole] * len(widths),
+        out_shape=[jax.ShapeDtypeStruct((rows, 2 * width), jnp.float32) for width in widths],
+        compiler_params=vmem,
+        cost_estimate=light,
+    )(across.reshape(1), sums, got)
+
+
 def fold_turn(near_ref, far_ref, turned):
     rows = near_ref.shape[0]
 
@@ -647,6 +673,31 @@
         compiler_params=vmem,
         cost_estimate=cost,
     )(first, second)
+
+
+def dot_grad_part(first, second, whole, column, target=None):
+    count, rows = first.shape
+    width = second.shape[1]
+    tile = 512
+    in_specs = [
+        pl.BlockSpec((count, tile), lambda i: (0, i)),
+        pl.BlockSpec((count, width), lambda i: (0, 0)),
+    ]
+    kernel, operands, aliases = partial(matmul_kernel, product_tn), (first, second), {}
+    if target is not None:
+        in_specs.append(pl.BlockSpec(memory_space=pl.ANY))
+        operands, aliases = (first, second, target), {2: 0}
+        kernel = lambda a, b, unused, out: matmul_kernel(product_tn, a, b, out)
+    return pl.pallas_call(
+        kernel,
+        grid=(rows // tile,),
+        in_specs=in_specs,
+        out_specs=pl.BlockSpec((tile, width), lambda i: (i, column)),
+        out_shape=jax.ShapeDtypeStruct((rows, whole), jnp.bfloat16),
+        input_output_aliases=aliases,
+        compiler_params=vmem,
+        cost_estimate=light,
+    )(*operands)
 
 
 def ffn_kernel(hidden_ref, weight_ref, grad_ref, activated_ref, pair_ref):
@@ -1158,25 +1209,30 @@
     got_gate, grad_branch_full, grad_mixed = line.run(mix_back, gate_sum, first_weight, *steps)
     up_sum, = line.enter(up_sum)
 
-    def attend_back(joint, grad_mixed, *sums):
+    def attend_back(joint, grad_mixed, grad_branch_full, mixed, *sums):
         grad_joint, head_gains = attend_bwd(
             joint, cosine, sine, first, gain_query, gain_key, kept, grad_mixed, count
         )
-        return (grad_joint, head_gains, *fold_cross(*sums))
-
-    grad_joint, head_gains, *sums_ffn = line.run(attend_back, joint, grad_mixed, *sums_ffn)
-
-    def sent_attn(hidden1, grad_joint, first_weight, up_sum):
+        last_grads = dot_grad_part(
+            grad_branch_full, mixed, joint_width + query_width, out_column
+        )
+        return (grad_joint, head_gains, last_grads, *fold_cross(*sums))
+
+    grad_joint, head_gains, last_grads, *sums_ffn = line.run(
+        attend_back, joint, grad_mixed, grad_branch_full, mixed, *sums_ffn
+    )
+
+    def sent_attn(hidden1, grad_joint, first_weight, last_grads, up_sum):
         return (
             *fold_swap(grad_joint, first_weight, place),
-            dot_grad(hidden1, grad_joint),
+            dot_grad_part(hidden1, grad_joint, last_grads.shape[1], 0, last_grads),
             flip(give_rows(up_sum, across), "x"),
         )
 
-    near_got, far_got, attn_grads, got_up = line.run(
-        sent_attn, hidden1, grad_joint, first_weight, up_sum
-    )
-    attn_sum = grad_scatter(attn_grads)
+    near_got, far_got, last_grads, got_up = line.run(
+        sent_attn, hidden1, grad_joint, first_weight, last_grads, up_sum
+    )
+    attn_sum = grad_scatter(last_grads)
     down_sum, = line.enter(down_sum)
 
     def held_attn(grad_joint, first_weight, near_got, far_got, gain_ffn_grad, head_gains, *sums):
@@ -1202,49 +1258,38 @@
     def join_all(rows, got):
         return join(rows, got, 0, rows.shape[1])
 
-    def cross_attn(
-        grad_branch_full, mixed, early, resid, gate_sum, got_gate, *values
-    ):
+    def cross_attn(early, resid, gate_sum, got_gate, *values):
         sums = fold_cross(*values[:4])
         output = (live * (resid + fold_end(*values[4:]))).astype(low)
         return (
             early + z_flip(early, 1),
             output,
             join_all(gate_sum, got_gate),
-            dot_grad(grad_branch_full, mixed),
             *sums,
         )
 
-    early, output, ffgate_grad, out_grad, *sums = line.run(
-        cross_attn, grad_branch_full, mixed, early, resid, gate_sum, got_gate, *sums, *ends_ffn
-    )
-
-    out_sum = grad_scatter(out_grad)
+    early, output, ffgate_grad, *sums = line.run(
+        cross_attn, early, resid, gate_sum, got_gate, *sums, *ends_ffn
+    )
 
     def close_attn(early, up_sum, got_up, *sums):
         return (early + z_flip(early, 2), join_all(up_sum, got_up), *fold_close(*sums))
 
     early, up_grad, *ends = line.run(close_attn, early, up_sum, got_up, *sums)
 
-    attn_sum, = line.enter(attn_sum)
-
-    def last_dots(tokens, inverse1, attn_sum, down_sum, *ends):
+    def last_dots(tokens, inverse1, down_sum, *ends):
         got_down = flip(give_rows(down_sum, across), "x")
-        got_attn = flip(give_rows(attn_sum, across), "x")
         grad_own = fold_end(*ends)
         late = gain_part(grad_own, tokens, inverse1)
         late = late + z_flip(late, 1)
         return (
-            got_attn,
             got_down,
             grad_own,
             partial_dots(grad_own, tokens, inverse1, gain_attn_own),
             late + z_flip(late, 2),
         )
 
-    got_attn, got_down, grad_hidden1, dots, late = line.run(
-        last_dots, tokens, inverse1, attn_sum, down_sum, *ends
-    )
+    got_down, grad_hidden1, dots, late = line.run(last_dots, tokens, inverse1, down_sum, *ends)
     cuts = (
         0,
         query_width,
@@ -1265,27 +1310,23 @@
         return spot + flip(spot, "y")
 
     def last_norm(
-        grad_hidden1, tokens, inverse1, dots, grad_resid, late, early, attn_sum, got_attn, out_sum,
-        down_sum, got_down
+        grad_hidden1, tokens, inverse1, dots, grad_resid, late, early, attn_sum, down_sum, got_down
     ):
-        got_out = flip(give_rows(out_sum, across), "x")
+        got_attn = flip(give_rows(attn_sum, across), "x")
         spot = last_spot(late + flip(late, "x"), early)
         grad_tokens, unused = norm_back(
             grad_hidden1, tokens, inverse1, gain_attn_own, dots, grad_resid
         )
-        return (
-            got_out,
-            spot,
-            grad_tokens,
-            join_all(down_sum, got_down),
-            *[join(attn_sum, got_attn, cuts[i], cuts[i + 1]) for i in range(4)],
-        )
-
-    got_out, spot, grad_tokens, down_part, *attn_parts = line.run(
+        return (got_attn, spot, grad_tokens, join_all(down_sum, got_down))
+
+    got_attn, spot, grad_tokens, down_part = line.run(
         last_norm, grad_hidden1, tokens, inverse1, dots, grad_resid, late, early, attn_sum,
-        got_attn, out_sum, down_sum, got_down
-    )
-    out_part = line.run(join_all, out_sum, got_out)
+        down_sum, got_down
+    )
+    widths = (query_width, query_width, key_width, key_width, query_width)
+    *attn_parts, out_part = line.run(
+        lambda sums, got: join_parts(sums, got, across, widths), attn_sum, got_attn
+    )
     lines = width // 128
     return (
         output,

time: 644 us -> 634 us (0.984)
    pallas_call x0 -> x3, Pallas kernels: none -> 20.5 us  [the longest x2 17.7 us: dot_grad_part(): pl.pallas_call(kernel, grid=(rows // tile,), in_specs=in_specs, out_specs...]
    pallas_call x5 -> x3, Pallas kernels: 50.3 us -> 32.6 us  [dot_grad(): pl.pallas_call(partial(matmul_kernel, product_tn), grid=(rows // tile,),...]
    reduce_scatter x5 -> x4, waiting for transfers between devices: 8.39 us -> 1 us  [grad_scatter(): return lax.psum_scatter(grads, 'z', scatter_dimension=0, tiled=True)]
    ppermute x74 -> x73, waiting for transfers between devices: 163 us -> 167 us  [flip(): return lax.ppermute(values, axis, [(0, 1), (1, 0)])]
    ppermute x74 -> x73, starting transfers between devices: 57.8 us -> 56.6 us  [flip(): return lax.ppermute(values, axis, [(0, 1), (1, 0)])]
    unnamed x114 -> x106, local copies, waits for them, and re-layouts: 20.6 us -> 19.8 us
  transfers between devices with their start and end apart: 86 -> 84, of which waited for: 43 -> 41; matrix products, arithmetic and copies ran while one was open for 13% -> 13% of each run, Pallas kernels for 36% -> 36%
where the time goes in v6:
time: 634 us; the launch traced here: 628 us
  Pallas kernels  263 us (41%)
  waiting for transfers between devices  195 us (31%)
  starting transfers between devices  59.6 us (9%)
  other arithmetic  48.5 us (8%)
  local copies, waits for them, and re-layouts  46.3 us (7%)
  between operations  15 us (2%)
    ppermute x73, waiting for transfers between devices, flip(): return lax.ppermute(values, axis, [(0, 1), (1, 0)])  167 us
    ppermute x73, starting transfers between devices, flip(): return lax.ppermute(values, axis, [(0, 1), (1, 0)])  56.6 us
    pallas_call x8, Pallas kernels, pack(): pl.pallas_call(partial(pack_kernel, normed), grid=(tiles,), in_specs=[pl....  42.4 us
    pallas_call x4, Pallas kernels, fold_held(): pl.pallas_call(fold_held_kernel, grid_spec=pltpu.PrefetchScalarGridSpec(n...  38.8 us
    pallas_call x3, Pallas kernels, dot_grad(): pl.pallas_call(partial(matmul_kernel, product_tn), grid=(rows // tile,),...  32.6 us
    pallas_call x4, Pallas kernels, fold_sent(): pl.pallas_call(fold_sent_kernel, grid_spec=pltpu.PrefetchScalarGridSpec(n...  31.5 us
    pallas_call x3, Pallas kernels, dot_in(): pl.pallas_call(partial(matmul_kernel, product_nn), grid=(count // tile,),...  29.8 us
    all_gather x3, waiting for transfers between devices, weight_gather(): return lax.all_gather(rows, 'z', axis=0, tiled=True)  23.2 us
  transfers between devices with their start and end apart: 84, of which 41 were waited for; matrix products, arithmetic and copies ran while one was open for 13% of the time, Pallas kernels for 36%

profile of v6, /device:TPU:0, one launch (start us, length us, event | category | flops | bytes accessed | tf_op | source)
XLA Modules:
  0.0 628.0 jit_solution(3374925647893313775)
XLA Ops:
  7.2 2.4 shard_map.254
  9.6 2.9 collective-permute-start
  15.2 9.5 %collective-permute-done = bf16[256,1024]{1,0:T(8,128)(2,1)S(1)} collective-permute-done((bf16[256,1024]{1,0:T(8,128)(2,1)}, bf16[256,1024]{1,0:T(8,128)(2,1)S(1)}, u32[]{:S(2)}, u32[]{:S(2)}) %collective-permute-start) | collective-permute-done | bytes 524320 | tf_op jit(solution)/shard_map/ppermute | solution.py:322
  31.3 2.1 shard_map.256
  33.4 2.6 shard_map.255
  36.0 7.7 %collective-permute-done.2 = bf16[512,512]{1,0:T(8,128)(2,1)} collective-permute-done((bf16[512,512]{1,0:T(8,128)(2,1)S(1)}, bf16[512,512]{1,0:T(8,128)(2,1)}, u32[]{:S(2)}, u32[]{:S(2)}) %collective-permute-start.2) | collective-permute-done | bytes 524320 | tf_op jit(solution)/shard_map/ppermute | solution.py:322
  45.0 6.8 %collective-permute-done.5 = s32[1024]{0:T(1024)S(1)} collective-permute-done((s32[1024]{0:T(1024)S(1)}, s32[1024]{0:T(1024)S(1)}, u32[]{:S(2)}, u32[]{:S(2)}) %collective-permute-start.5) | collective-permute-done | bytes 4128 | tf_op jit(solution)/shard_map/ppermute | solution.py:322
  57.5 7.1 %collective-permute-done.6 = bf16[256,768]{1,0:T(8,128)(2,1)} collective-permute-done((bf16[256,768]{1,0:T(8,128)(2,1)}, bf16[256,768]{1,0:T(8,128)(2,1)}, u32[]{:S(2)}, u32[]{:S(2)}) %collective-permute-start.6) | collective-permute-done | bytes 393248 | tf_op jit(solution)/shard_map/ppermute | solution.py:322
  67.7 5.7 shard_map.257
  85.7 3.7 fusion.10
  90.1 5.8 shard_map.258
  95.9 5.4 collective-permute-done.12.refs_2_
  102.4 6.9 %all-gather.4.cloned.1.call-done.weight_ref.near_ref.far_ref = bf16[2048,1024]{1,0:T(8,128)(2,1)} async-done(((bf16[512,1024]{1,0:T(8,128)(2,1)}), bf16[2048,1024]{1,0:T(8,128)(2,1)}) %all-gather.4.cloned.1.call-update) | async-done | bytes 4194320 | tf_op jit(solution)/shard_map/all_gather | solution.py:448
  117.1 11.6 %shard_map.259.joint_ref = f32[2048,768]{1,0:T(8,128)} custom-call(bf16[2048,2048]{1,0:T(8,128)(2,1)} %get-tuple-element.826.operand_ref.a, bf16[2048,1024]{1,0:T(8,128)(2,1)} %all-gather.4.cloned.1.call-done.weight_ref.near_ref.far_ref), custom_call_target="tpu_custom_call" | custom-call | tf_op jit(solution)/shard_map/pallas_call | solution.py:646
  128.7 2.8 copy-done
  131.5 10.4 %shard_map.260 = (bf16[2048,256]{1,0:T(8,128)(2,1)S(1)}, f32[2048,256]{1,0:T(8,128)S(1)}, bf16[2048,256]{1,0:T(8,128)(2,1)S(1)}, bf16[2048,128]{1,0:T(8,128)(2,1)S(1)}, f32[2,2,1024]{2,1,0:T(2,128)S(1)}) custom-call(f32[2048,768]{1,0:T(8,128)S(1)} %copy-done, f32[2048,128]{1,0:T(8,128)S(1)} %get-tuple-element.552.cos_ref, ...), custom_call_target="tpu_custom_call" | custom-call | tf_op jit(solution)/shard_map/pallas_call | solution.py:947
  146.5 5.1 shard_map.261
  152.1 3.9 collective-permute-done.20.near_got
  155.9 3.0 collective-permute-done.21.far_got
  160.2 6.6 %shard_map.262 = (bf16[2,512,512]{2,1,0:T(8,128)(2,1)}, bf16[2,512,512]{2,1,0:T(8,128)(2,1)}, bf16[1024,512]{1,0:T(8,128)(2,1)}, bf16[1024,512]{1,0:T(8,128)(2,1)}) custom-call(s32[1]{0:T(128)} %bitcast.place_ref.refs_4_, bf16[2048,256]{1,0:T(8,128)(2,1)} %copy-done.1, bf16[2048,1024]{1,0:T(8,128)(2,1)} %all-gather.4.cloned.1.call-done.weight_ref.near_ref.far_ref, ...), custom_call_target="tpu_custom_call" | custom-call | tf_op jit(solution)/shard_map/pallas_call | solution.py:585
  172.8 4.7 shard_map.263.refs_4_
  177.5 4.9 shard_map.264.operand_ref
  182.4 14.1 %collective-permute-done.22.upper_ref = bf16[2,512,512]{2,1,0:T(8,128)(2,1)} collective-permute-done((bf16[2,512,512]{2,1,0:T(8,128)(2,1)}, bf16[2,512,512]{2,1,0:T(8,128)(2,1)}, u32[]{:S(2)}, u32[]{:S(2)}) %collective-permute-start.22) | collective-permute-done | bytes 1048608 | tf_op jit(solution)/shard_map/ppermute | solution.py:322
  197.7 3.5 shard_map.265
  202.4 12.2 %collective-permute-done.25 = bf16[512,512]{1,0:T(8,128)(2,1)S(1)} collective-permute-done((bf16[512,512]{1,0:T(8,128)(2,1)}, bf16[512,512]{1,0:T(8,128)(2,1)S(1)}, u32[]{:S(2)}, u32[]{:S(2)}) %collective-permute-start.25) | collective-permute-done | bytes 524320 | tf_op jit(solution)/shard_map/ppermute | solution.py:322
  220.6 11.3 %shard_map.266.grad_ref = f32[2048,768]{1,0:T(8,128)} custom-call(bf16[2048,2048]{1,0:T(8,128)(2,1)} %shard_map.264.operand_ref, bf16[2048,768]{1,0:T(8,128)(2,1)} %all-gather.6.cloned.1.call-done.weight_ref.near_ref.far_ref), custom_call_target="tpu_custom_call" | custom-call | tf_op jit(solution)/shard_map/pallas_call | solution.py:646
  232.0 10.0 %collective-permute-done.27.refs_2_ = bf16[1024,512]{1,0:T(8,128)(2,1)S(1)} collective-permute-done((bf16[1024,512]{1,0:T(8,128)(2,1)}, bf16[1024,512]{1,0:T(8,128)(2,1)S(1)}, u32[]{:S(2)}, u32[]{:S(2)}) %collective-permute-start.27) | collective-permute-done | bytes 1048608 | tf_op jit(solution)/shard_map/ppermute | solution.py:322
  247.8 5.7 shard_map.267
  253.5 7.2 %collective-permute-done.31 = bf16[512,512]{1,0:T(8,128)(2,1)} collective-permute-done((bf16[512,512]{1,0:T(8,128)(2,1)}, bf16[512,512]{1,0:T(8,128)(2,1)}, u32[]{:S(2)}, u32[]{:S(2)}) %collective-permute-start.31) | collective-permute-done | bytes 524320 | tf_op jit(solution)/shard_map/ppermute | solution.py:322
  264.2 2.8 collective-permute-done.34.refs_3_
  267.0 5.7 shard_map.268
  272.8 16.4 %all-gather.8.cloned.1.call-done.weight_ref.near_ref.far_ref = bf16[2048,1536]{1,0:T(8,128)(2,1)} async-done(((bf16[512,1536]{1,0:T(8,128)(2,1)}), bf16[2048,1536]{1,0:T(8,128)(2,1)}) %all-gather.8.cloned.1.call-update) | async-done | bytes 6291472 | tf_op jit(solution)/shard_map/all_gather | solution.py:448
  289.1 20.3 %shard_map.269 = (bf16[2048,768]{1,0:T(8,128)(2,1)}, bf16[2048,1536]{1,0:T(8,128)(2,1)}) custom-call(bf16[2048,2048]{1,0:T(8,128)(2,1)} %get-tuple-element.706.hidden_ref.operand_ref, bf16[2048,1536]{1,0:T(8,128)(2,1)} %all-gather.8.cloned.1.call-done.weight_ref.near_ref.far_ref, f32[2048,768]{1,0:T(8,128)} %shard_map.266.grad_ref), custom_call_target="tpu_custom_call" | custom-call | tf_op jit(solution)/shard_map/pallas_call | solution.py:724
  309.4 11.4 %shard_map.270 = (bf16[2048,512]{1,0:T(8,128)(2,1)}, bf16[2048,512]{1,0:T(8,128)(2,1)}) custom-call(s32[1]{0:T(128)} %bitcast.place_ref.refs_4_, bf16[2048,1536]{1,0:T(8,128)(2,1)} %get-tuple-element.707.operand_ref.weight_ref, bf16[2048,1536]{1,0:T(8,128)(2,1)} %all-gather.8.cloned.1.call-done.weight_ref.near_ref.far_ref, ...), custom_call_target="tpu_custom_call" | custom-call | tf_op jit(solution)/shard_map/pallas_call | solution.py:558
  321.3 10.9 %shard_map.271 = bf16[2048,768]{1,0:T(8,128)(2,1)} custom-call(bf16[2048,2048]{1,0:T(8,128)(2,1)} %get-tuple-element.706.hidden_ref.operand_ref, bf16[2048,1536]{1,0:T(8,128)(2,1)} %get-tuple-element.707.operand_ref.weight_ref), custom_call_target="tpu_custom_call" | custom-call | tf_op jit(solution)/shard_map/pallas_call | solution.py:664
  332.3 13.5 %shard_map.272 = (bf16[2,512,512]{2,1,0:T(8,128)(2,1)}, bf16[2,512,512]{2,1,0:T(8,128)(2,1)}, bf16[1024,512]{1,0:T(8,128)(2,1)}, bf16[1024,512]{1,0:T(8,128)(2,1)}) custom-call(s32[1]{0:T(128)} %bitcast.place_ref.refs_4_, bf16[2048,1536]{1,0:T(8,128)(2,1)} %get-tuple-element.707.operand_ref.weight_ref, ...), custom_call_target="tpu_custom_call" | custom-call | tf_op jit(solution)/shard_map/pallas_call | solution.py:585
  348.8 10.8 %shard_map.273 = bf16[2048,768]{1,0:T(8,128)(2,1)} custom-call(bf16[2048,2048]{1,0:T(8,128)(2,1)} %get-tuple-element.706.hidden_ref.operand_ref, bf16[2048,1536]{1,0:T(8,128)(2,1)} %get-tuple-element.707.operand_ref.weight_ref), custom_call_target="tpu_custom_call" | custom-call | tf_op jit(solution)/shard_map/pallas_call | solution.py:664
  359.6 7.3 %shard_map.274 = (bf16[2048,512]{1,0:T(8,128)(2,1)}, bf16[2048,512]{1,0:T(8,128)(2,1)}) custom-call(s32[1]{0:T(128)} %bitcast.place_ref.refs_4_, bf16[2048,768]{1,0:T(8,128)(2,1)} %get-tuple-element.760.operand_ref.weight_ref, bf16[2048,768]{1,0:T(8,128)(2,1)} %all-gather.6.cloned.1.call-done.weight_ref.near_ref.far_ref, ...), custom_call_target="tpu_custom_call" | custom-call | tf_op jit(solution)/shard_map/pallas_call | solution.py:558
  366.9 4.3 collective-permute-done.37.upper_ref
  373.0 3.4 shard_map.275
  379.3 11.4 %collective-permute-done.39 = bf16[512,512]{1,0:T(8,128)(2,1)} collective-permute-done((bf16[512,512]{1,0:T(8,128)(2,1)}, bf16[512,512]{1,0:T(8,128)(2,1)}, u32[]{:S(2)}, u32[]{:S(2)}) %collective-permute-start.39) | collective-permute-done | bytes 524320 | tf_op jit(solution)/shard_map/ppermute | solution.py:322
  399.9 3.1 collective-permute-done.44
  404.3 4.8 fusion.17
  410.2 10.9 %shard_map.276 = bf16[2048,768]{1,0:T(8,128)(2,1)} custom-call(bf16[2048,2048]{1,0:T(8,128)(2,1)} %shard_map.264.operand_ref, bf16[2048,768]{1,0:T(8,128)(2,1)} %get-tuple-element.760.operand_ref.weight_ref), custom_call_target="tpu_custom_call" | custom-call | tf_op jit(solution)/shard_map/pallas_call | solution.py:664
  421.1 9.2 %shard_map.277 = (bf16[2,512,512]{2,1,0:T(8,128)(2,1)}, bf16[2,512,512]{2,1,0:T(8,128)(2,1)}, bf16[1024,512]{1,0:T(8,128)(2,1)}, bf16[1024,512]{1,0:T(8,128)(2,1)}) custom-call(s32[1]{0:T(128)} %bitcast.place_ref.refs_4_, bf16[2048,768]{1,0:T(8,128)(2,1)} %get-tuple-element.760.operand_ref.weight_ref, ...), custom_call_target="tpu_custom_call" | custom-call | tf_op jit(solution)/shard_map/pallas_call | solution.py:585
  430.3 3.6 collective-permute-done.45.refs_2_
  440.4 5.1 shard_map.278.refs_4_
  445.5 7.0 %collective-permute-done.49 = bf16[512,512]{1,0:T(8,128)(2,1)} collective-permute-done((bf16[512,512]{1,0:T(8,128)(2,1)}, bf16[512,512]{1,0:T(8,128)(2,1)}, u32[]{:S(2)}, u32[]{:S(2)}) %collective-permute-start.49) | collective-permute-done | bytes 524320 | tf_op jit(solution)/shard_map/ppermute | solution.py:322
  459.8 4.8 shard_map.279.operand_ref
  464.6 6.8 %shard_map.280.grad_mixed_ref = f32[2048,256]{1,0:T(8,128)} custom-call(bf16[2048,2048]{1,0:T(8,128)(2,1)} %shard_map.279.operand_ref, bf16[2048,1024]{1,0:T(8,128)(2,1)} %all-gather.4.cloned.1.call-done.weight_ref.near_ref.far_ref), custom_call_target="tpu_custom_call" | custom-call | tf_op jit(solution)/shard_map/pallas_call | solution.py:646
  474.5 6.8 %shard_map.282.unused = bf16[2048,1024]{1,0:T(8,128)(2,1)} custom-call(bf16[2048,2048]{1,0:T(8,128)(2,1)} %shard_map.279.operand_ref, bf16[2048,256]{1,0:T(8,128)(2,1)} %copy-done.1), custom_call_target="tpu_custom_call" | custom-call | tf_op jit(solution)/shard_map/pallas_call | solution.py:691
  481.3 16.0 %shard_map.281 = (bf16[2048,768]{1,0:T(8,128)(2,1)}, f32[2,128]{1,0:T(2,128)S(1)}) custom-call(f32[2048,768]{1,0:T(8,128)} %shard_map.259.joint_ref, f32[2048,128]{1,0:T(8,128)S(1)} %get-tuple-element.552.cos_ref, f32[2048,128]{1,0:T(8,128)S(1)} %get-tuple-element.553.sin_ref, s32[2,1,1024]{2,1,0:T(1,128)S(1)} %compare_select_fusion.first_ref, ...), custom_call_target="tpu_custom_call" | custom-call | tf_op jit(solution)/shard_map/pallas_call | solution.py:970
  498.0 7.7 %shard_map.283 = (bf16[2048,512]{1,0:T(8,128)(2,1)}, bf16[2048,512]{1,0:T(8,128)(2,1)}) custom-call(s32[1]{0:T(128)} %bitcast.place_ref.refs_4_, bf16[2048,768]{1,0:T(8,128)(2,1)} %get-tuple-element.843.operand_ref.b, bf16[2048,1024]{1,0:T(8,128)(2,1)} %all-gather.4.cloned.1.call-done.weight_ref.near_ref.far_ref, ...), custom_call_target="tpu_custom_call" | custom-call | tf_op jit(solution)/shard_map/pallas_call | solution.py:558
  507.9 10.9 %shard_map.284 = bf16[2048,1024]{1,0:T(8,128)(2,1)} custom-call(bf16[2048,2048]{1,0:T(8,128)(2,1)} %get-tuple-element.826.operand_ref.a, bf16[2048,768]{1,0:T(8,128)(2,1)} %get-tuple-element.843.operand_ref.b, bf16[2048,1024]{1,0:T(8,128)(2,1)} %shard_map.282.unused), custom_call_target="tpu_custom_call", output_to_operand_aliasing={{}: (2, {})} | custom-call | tf_op jit(solution)/shard_map/pallas_call | solution.py:691
  520.4 3.5 shard_map.286
  528.4 9.4 %shard_map.285 = (bf16[2,512,512]{2,1,0:T(8,128)(2,1)}, bf16[2,512,512]{2,1,0:T(8,128)(2,1)}, bf16[1024,512]{1,0:T(8,128)(2,1)}, bf16[1024,512]{1,0:T(8,128)(2,1)}) custom-call(s32[1]{0:T(128)} %bitcast.place_ref.refs_4_, bf16[2048,768]{1,0:T(8,128)(2,1)} %get-tuple-element.843.operand_ref.b, ...), custom_call_target="tpu_custom_call" | custom-call | tf_op jit(solution)/shard_map/pallas_call | solution.py:585
  547.2 17.0 %collective-permute-done.63.upper_ref = bf16[2,512,512]{2,1,0:T(8,128)(2,1)S(1)} collective-permute-done((bf16[2,512,512]{2,1,0:T(8,128)(2,1)}, bf16[2,512,512]{2,1,0:T(8,128)(2,1)S(1)}, u32[]{:S(2)}, u32[]{:S(2)}) %collective-permute-start.63) | collective-permute-done | bytes 1048608 | tf_op jit(solution)/shard_map/ppermute | solution.py:322
  566.1 3.4 shard_map.287
  572.5 8.8 %collective-permute-done.66 = bf16[512,512]{1,0:T(8,128)(2,1)S(1)} collective-permute-done((bf16[512,512]{1,0:T(8,128)(2,1)}, bf16[512,512]{1,0:T(8,128)(2,1)S(1)}, u32[]{:S(2)}, u32[]{:S(2)}) %collective-permute-start.66) | collective-permute-done | bytes 524320 | tf_op jit(solution)/shard_map/ppermute | solution.py:322
  586.4 2.2 collective-permute-done.71
  591.4 2.3 collective-permute-done.72
  600.4 3.4 multiply_add_fusion
  603.8 7.3 %collective-permute-done.74 = f32[4,128]{1,0:T(4,128)} collective-permute-done((f32[4,128]{1,0:T(4,128)}, f32[4,128]{1,0:T(4,128)}, u32[]{:S(2)}, u32[]{:S(2)}) %collective-permute-start.74) | collective-permute-done | bytes 2080 | tf_op jit(solution)/shard_map/ppermute | solution.py:322
  617.7 2.7 shard_map.288
  (339 shorter events, 152.2 us)
Async XLA Ops:
  7.2 102.1 %all-gather.4.cloned.1.call-start = ((), (), s32[]{:S(2)}) async-start(), calls=%async_computation.4 | async-start | bytes 5242880 | tf_op jit(solution)/shard_map/all_gather | solution.py:448
  9.6 15.1 %collective-permute-start = (bf16[256,1024]{1,0:T(8,128)(2,1)}, bf16[256,1024]{1,0:T(8,128)(2,1)S(1)}, u32[]{:S(2)}, u32[]{:S(2)}) collective-permute-start(bf16[256,1024]{1,0:T(8,128)(2,1)} %get-tuple-element.493), channel_id=1, source_target_pairs={{0,4},{4,0},{1,5},{5,1},{2,6},{6,2},{3,7},{7,3},{8,12},{12,8},{9,1... | collective-permute-start | bytes 1572872 | tf_op jit(solution)/shard_map/ppermute | solution.py:322
  13.6 13.4 %collective-permute-start.1 = (bf16[512,512]{1,0:T(8,128)(2,1)S(1)}, bf16[512,512]{1,0:T(8,128)(2,1)S(1)}, u32[]{:S(2)}, u32[]{:S(2)}) collective-permute-start(bf16[512,512]{1,0:T(8,128)(2,1)S(1)} %slice.60), channel_id=1, source_target_pairs={{0,2},{2,0},{1,3},{3,1},{4,6},{6,4},{5,7},{7,5},{8,10},{10,8},{9,1... | collective-permute-start | bytes 1572872 | tf_op jit(solution)/shard_map/ppermute | solution.py:322
  27.1 191.5 %all-gather.6.cloned.1.call-start = ((), (), s32[]{:S(2)}) async-start(), calls=%async_computation.5 | async-start | bytes 3932160 | tf_op jit(solution)/shard_map/all_gather | solution.py:448
  27.4 24.4 %collective-permute-start.3 = (bf16[1024,512]{1,0:T(8,128)(2,1)S(1)}, bf16[1024,512]{1,0:T(8,128)(2,1)S(1)}, u32[]{:S(2)}, u32[]{:S(2)}) collective-permute-start(bf16[1024,512]{1,0:T(8,128)(2,1)S(1)} %copy-done.8), channel_id=1, source_target_pairs={{0,4},{4,0},{1,5},{5,1},{2,6},{6,2},{3,7},{7,3},{8,12},{12,8},{9,1... | collective-permute-start | bytes 3145736 | tf_op jit(solution)/shard_map/ppermute | solution.py:322
  29.1 22.7 %collective-permute-start.4 = (bf16[1024,512]{1,0:T(8,128)(2,1)S(1)}, bf16[1024,512]{1,0:T(8,128)(2,1)}, u32[]{:S(2)}, u32[]{:S(2)}) collective-permute-start(bf16[1024,512]{1,0:T(8,128)(2,1)S(1)} %copy-done.8), channel_id=1, source_target_pairs={{0,1},{1,0},{2,3},{3,2},{4,5},{5,4},{6,7},{7,6},{8,9},{9,8},{10,11... | collective-permute-start | bytes 3145736 | tf_op jit(solution)/shard_map/ppermute | solution.py:322
  29.2 14.5 %collective-permute-start.2 = (bf16[512,512]{1,0:T(8,128)(2,1)S(1)}, bf16[512,512]{1,0:T(8,128)(2,1)}, u32[]{:S(2)}, u32[]{:S(2)}) collective-permute-start(bf16[512,512]{1,0:T(8,128)(2,1)S(1)} %slice.61), channel_id=1, source_target_pairs={{0,2},{2,0},{1,3},{3,1},{4,6},{6,4},{5,7},{7,5},{8,10},{10,8},{9,1... | collective-permute-start | bytes 1572872 | tf_op jit(solution)/shard_map/ppermute | solution.py:322
  30.8 21.1 %collective-permute-start.5 = (s32[1024]{0:T(1024)S(1)}, s32[1024]{0:T(1024)S(1)}, u32[]{:S(2)}, u32[]{:S(2)}) collective-permute-start(s32[1024]{0:T(1024)S(1)} %copy-done.49), channel_id=1, source_target_pairs={{0,4},{4,0},{1,5},{5,1},{2,6},{6,2},{3,7},{7,3},{8,12},{12,8},{9,1... | collective-permute-start | bytes 12296 | tf_op jit(solution)/shard_map/ppermute | solution.py:322
  51.8 14.9 %collective-permute-start.10 = (bf16[1024,512]{1,0:T(8,128)(2,1)S(1)}, bf16[1024,512]{1,0:T(8,128)(2,1)S(1)}, u32[]{:S(2)}, u32[]{:S(2)}) collective-permute-start(bf16[1024,512]{1,0:T(8,128)(2,1)S(1)} %pad_maximum_fusion.4.refs_2_), channel_id=1, source_target_pairs={{0,1},{1,0},{2,3},{3,2},{4,5},{5,4},{6,7},{7,6},{8,9},{9,8},{10,11... | collective-permute-start | bytes 3145736 | tf_op jit(solution)/shard_map/ppermute | solution.py:322
  51.9 23.2 %collective-permute-start.7 = (bf16[1024,512]{1,0:T(8,128)(2,1)S(1)}, bf16[1024,512]{1,0:T(8,128)(2,1)}, u32[]{:S(2)}, u32[]{:S(2)}) collective-permute-start(bf16[1024,512]{1,0:T(8,128)(2,1)S(1)} %collective-permute-done.3.refs_0_), channel_id=1, source_target_pairs={{0,1},{1,0},{2,3},{3,2},{4,5},{5,4},{6,7},{7,6},{8,9},{9,8},{10,11... | collective-permute-start | bytes 3145736 | tf_op jit(solution)/shard_map/ppermute | solution.py:322
  52.4 12.3 %collective-permute-start.6 = (bf16[256,768]{1,0:T(8,128)(2,1)}, bf16[256,768]{1,0:T(8,128)(2,1)}, u32[]{:S(2)}, u32[]{:S(2)}) collective-permute-start(bf16[256,768]{1,0:T(8,128)(2,1)} %get-tuple-element.517), channel_id=1, source_target_pairs={{0,4},{4,0},{1,5},{5,1},{2,6},{6,2},{3,7},{7,3},{8,12},{12,8},{9,1... | collective-permute-start | bytes 1179656 | tf_op jit(solution)/shard_map/ppermute | solution.py:322
  55.5 19.6 %collective-permute-start.8 = (bf16[512,512]{1,0:T(8,128)(2,1)}, bf16[512,512]{1,0:T(8,128)(2,1)}, u32[]{:S(2)}, u32[]{:S(2)}) collective-permute-start(bf16[512,512]{1,0:T(8,128)(2,1)} %slice.62), channel_id=1, source_target_pairs={{0,4},{4,0},{1,5},{5,1},{2,6},{6,2},{3,7},{7,3},{8,12},{12,8},{9,1... | collective-permute-start | bytes 1572872 | tf_op jit(solution)/shard_map/ppermute | solution.py:322
  56.1 19.0 %collective-permute-start.9 = (bf16[512,512]{1,0:T(8,128)(2,1)}, bf16[512,512]{1,0:T(8,128)(2,1)}, u32[]{:S(2)}, u32[]{:S(2)}) collective-permute-start(bf16[512,512]{1,0:T(8,128)(2,1)} %slice.63), channel_id=1, source_target_pairs={{0,2},{2,0},{1,3},{3,1},{4,6},{6,4},{5,7},{7,5},{8,10},{10,8},{9,1... | collective-permute-start | bytes 1572872 | tf_op jit(solution)/shard_map/ppermute | solution.py:322
  75.1 214.0 %all-gather.8.cloned.1.call-start = ((), (), s32[]{:S(2)}) async-start(), calls=%async_computation.6 | async-start | bytes 7864320 | tf_op jit(solution)/shard_map/all_gather | solution.py:448
  76.8 24.4 %collective-permute-start.12 = (bf16[1024,512]{1,0:T(8,128)(2,1)S(1)}, bf16[1024,512]{1,0:T(8,128)(2,1)}, u32[]{:S(2)}, u32[]{:S(2)}) collective-permute-start(bf16[1024,512]{1,0:T(8,128)(2,1)S(1)} %get-tuple-element.602.refs_0_), channel_id=1, source_target_pairs={{0,2},{2,0},{1,3},{3,1},{4,6},{6,4},{5,7},{7,5},{8,10},{10,8},{9,1... | collective-permute-start | bytes 3145736 | tf_op jit(solution)/shard_map/ppermute | solution.py:322
  78.3 24.1 %collective-permute-start.13 = (bf16[1024,512]{1,0:T(8,128)(2,1)S(1)}, bf16[1024,512]{1,0:T(8,128)(2,1)}, u32[]{:S(2)}, u32[]{:S(2)}) collective-permute-start(bf16[1024,512]{1,0:T(8,128)(2,1)S(1)} %get-tuple-element.602.refs_0_), channel_id=1, source_target_pairs={{0,4},{4,0},{1,5},{5,1},{2,6},{6,2},{3,7},{7,3},{8,12},{12,8},{9,1... | collective-permute-start | bytes 3145736 | tf_op jit(solution)/shard_map/ppermute | solution.py:322
  79.8 22.6 %collective-permute-start.14 = (bf16[1024,512]{1,0:T(8,128)(2,1)S(1)}, bf16[1024,512]{1,0:T(8,128)(2,1)}, u32[]{:S(2)}, u32[]{:S(2)}) collective-permute-start(bf16[1024,512]{1,0:T(8,128)(2,1)S(1)} %get-tuple-element.602.refs_0_), channel_id=1, source_target_pairs={{0,1},{1,0},{2,3},{3,2},{4,5},{5,4},{6,7},{7,6},{8,9},{9,8},{10,11... | collective-permute-start | bytes 3145736 | tf_op jit(solution)/shard_map/ppermute | solution.py:322
  109.3 35.7 %collective-permute-start.15 = (bf16[256,1536]{1,0:T(8,128)(2,1)}, bf16[256,1536]{1,0:T(8,128)(2,1)S(1)}, u32[]{:S(2)}, u32[]{:S(2)}) collective-permute-start(bf16[256,1536]{1,0:T(8,128)(2,1)} %get-tuple-element.549), channel_id=1, source_target_pairs={{0,4},{4,0},{1,5},{5,1},{2,6},{6,2},{3,7},{7,3},{8,12},{12,8},{9,1... | collective-permute-start | bytes 2359304 | tf_op jit(solution)/shard_map/ppermute | solution.py:322
  110.8 35.6 %collective-permute-start.16 = (bf16[1024,512]{1,0:T(8,128)(2,1)}, bf16[1024,512]{1,0:T(8,128)(2,1)}, u32[]{:S(2)}, u32[]{:S(2)}) collective-permute-start(bf16[1024,512]{1,0:T(8,128)(2,1)} %collective-permute-done.12.refs_2_), channel_id=1, source_target_pairs={{0,1},{1,0},{2,3},{3,2},{4,5},{5,4},{6,7},{7,6},{8,9},{9,8},{10,11... | collective-permute-start | bytes 3145736 | tf_op jit(solution)/shard_map/ppermute | solution.py:322
  110.8 35.6 %collective-permute-start.17 = (bf16[1024,512]{1,0:T(8,128)(2,1)}, bf16[1024,512]{1,0:T(8,128)(2,1)}, u32[]{:S(2)}, u32[]{:S(2)}) collective-permute-start(bf16[1024,512]{1,0:T(8,128)(2,1)} %collective-permute-done.13.refs_0_), channel_id=1, source_target_pairs={{0,1},{1,0},{2,3},{3,2},{4,5},{5,4},{6,7},{7,6},{8,9},{9,8},{10,11... | collective-permute-start | bytes 3145736 | tf_op jit(solution)/shard_map/ppermute | solution.py:322
  115.1 31.3 %collective-permute-start.18 = (bf16[512,512]{1,0:T(8,128)(2,1)}, bf16[512,512]{1,0:T(8,128)(2,1)}, u32[]{:S(2)}, u32[]{:S(2)}) collective-permute-start(bf16[512,512]{1,0:T(8,128)(2,1)} %slice.67), channel_id=1, source_target_pairs={{0,4},{4,0},{1,5},{5,1},{2,6},{6,2},{3,7},{7,3},{8,12},{12,8},{9,1... | collective-permute-start | bytes 1572872 | tf_op jit(solution)/shard_map/ppermute | solution.py:322
  115.6 30.8 %collective-permute-start.19 = (bf16[512,512]{1,0:T(8,128)(2,1)}, bf16[512,512]{1,0:T(8,128)(2,1)}, u32[]{:S(2)}, u32[]{:S(2)}) collective-permute-start(bf16[512,512]{1,0:T(8,128)(2,1)} %slice.68), channel_id=1, source_target_pairs={{0,2},{2,0},{1,3},{3,1},{4,6},{6,4},{5,7},{7,5},{8,10},{10,8},{9,1... | collective-permute-start | bytes 1572872 | tf_op jit(solution)/shard_map/ppermute | solution.py:322
  146.4 287.6 %reduce-scatter.5.cloned.1.call-start = ((), (), s32[]{:S(2)}) async-start(), calls=%async_computation.7 | async-start | bytes 3932160 | tf_op jit(solution)/shard_map/reduce_scatter | solution.py:452
  170.7 25.8 %collective-permute-start.22 = (bf16[2,512,512]{2,1,0:T(8,128)(2,1)}, bf16[2,512,512]{2,1,0:T(8,128)(2,1)}, u32[]{:S(2)}, u32[]{:S(2)}) collective-permute-start(bf16[2,512,512]{2,1,0:T(8,128)(2,1)} %get-tuple-element.594), channel_id=1, source_target_pairs={{0,4},{4,0},{1,5},{5,1},{2,6},{6,2},{3,7},{7,3},{8,12},{12,8},{9,1... | collective-permute-start | bytes 3145736 | tf_op jit(solution)/shard_map/ppermute | solution.py:322
  172.3 25.5 %collective-permute-start.23 = (bf16[1024,512]{1,0:T(8,128)(2,1)}, bf16[1024,512]{1,0:T(8,128)(2,1)}, u32[]{:S(2)}, u32[]{:S(2)}) collective-permute-start(bf16[1024,512]{1,0:T(8,128)(2,1)} %get-tuple-element.596), channel_id=1, source_target_pairs={{0,2},{2,0},{1,3},{3,1},{4,6},{6,4},{5,7},{7,5},{8,10},{10,8},{9,1... | collective-permute-start | bytes 3145736 | tf_op jit(solution)/shard_map/ppermute | solution.py:322
  201.2 13.4 %collective-permute-start.25 = (bf16[512,512]{1,0:T(8,128)(2,1)}, bf16[512,512]{1,0:T(8,128)(2,1)S(1)}, u32[]{:S(2)}, u32[]{:S(2)}) collective-permute-start(bf16[512,512]{1,0:T(8,128)(2,1)} %get-tuple-element.617), channel_id=1, source_target_pairs={{0,2},{2,0},{1,3},{3,1},{4,6},{6,4},{5,7},{7,5},{8,10},{10,8},{9,1... | collective-permute-start | bytes 1572872 | tf_op jit(solution)/shard_map/ppermute | solution.py:322
  201.9 13.0 %collective-permute-start.26 = (bf16[512,512]{1,0:T(8,128)(2,1)}, bf16[512,512]{1,0:T(8,128)(2,1)S(1)}, u32[]{:S(2)}, u32[]{:S(2)}) collective-permute-start(bf16[512,512]{1,0:T(8,128)(2,1)} %get-tuple-element.619), channel_id=1, source_target_pairs={{0,4},{4,0},{1,5},{5,1},{2,6},{6,2},{3,7},{7,3},{8,12},{12,8},{9,1... | collective-permute-start | bytes 1572872 | tf_op jit(solution)/shard_map/ppermute | solution.py:322
  218.6 23.4 %collective-permute-start.27 = (bf16[1024,512]{1,0:T(8,128)(2,1)}, bf16[1024,512]{1,0:T(8,128)(2,1)S(1)}, u32[]{:S(2)}, u32[]{:S(2)}) collective-permute-start(bf16[1024,512]{1,0:T(8,128)(2,1)} %get-tuple-element.750.refs_0_), channel_id=1, source_target_pairs={{0,2},{2,0},{1,3},{3,1},{4,6},{6,4},{5,7},{7,5},{8,10},{10,8},{9,1... | collective-permute-start | bytes 3145736 | tf_op jit(solution)/shard_map/ppermute | solution.py:322
  220.0 23.2 %collective-permute-start.28 = (bf16[1024,512]{1,0:T(8,128)(2,1)}, bf16[1024,512]{1,0:T(8,128)(2,1)}, u32[]{:S(2)}, u32[]{:S(2)}) collective-permute-start(bf16[1024,512]{1,0:T(8,128)(2,1)} %get-tuple-element.750.refs_0_), channel_id=1, source_target_pairs={{0,4},{4,0},{1,5},{5,1},{2,6},{6,2},{3,7},{7,3},{8,12},{12,8},{9,1... | collective-permute-start | bytes 3145736 | tf_op jit(solution)/shard_map/ppermute | solution.py:322
  220.6 22.6 %collective-permute-start.29 = (bf16[1024,512]{1,0:T(8,128)(2,1)}, bf16[1024,512]{1,0:T(8,128)(2,1)S(1)}, u32[]{:S(2)}, u32[]{:S(2)}) collective-permute-start(bf16[1024,512]{1,0:T(8,128)(2,1)} %get-tuple-element.750.refs_0_), channel_id=1, source_target_pairs={{0,1},{1,0},{2,3},{3,2},{4,5},{5,4},{6,7},{7,6},{8,9},{9,8},{10,11... | collective-permute-start | bytes 3145736 | tf_op jit(solution)/shard_map/ppermute | solution.py:322
  243.3 17.8 %collective-permute-start.30 = (bf16[1024,512]{1,0:T(8,128)(2,1)}, bf16[1024,512]{1,0:T(8,128)(2,1)}, u32[]{:S(2)}, u32[]{:S(2)}) collective-permute-start(bf16[1024,512]{1,0:T(8,128)(2,1)} %collective-permute-done.28.refs_0_), channel_id=1, source_target_pairs={{0,1},{1,0},{2,3},{3,2},{4,5},{5,4},{6,7},{7,6},{8,9},{9,8},{10,11... | collective-permute-start | bytes 3145736 | tf_op jit(solution)/shard_map/ppermute | solution.py:322
  246.5 14.2 %collective-permute-start.31 = (bf16[512,512]{1,0:T(8,128)(2,1)}, bf16[512,512]{1,0:T(8,128)(2,1)}, u32[]{:S(2)}, u32[]{:S(2)}) collective-permute-start(bf16[512,512]{1,0:T(8,128)(2,1)} %slice.69), channel_id=1, source_target_pairs={{0,4},{4,0},{1,5},{5,1},{2,6},{6,2},{3,7},{7,3},{8,12},{12,8},{9,1... | collective-permute-start | bytes 1572872 | tf_op jit(solution)/shard_map/ppermute | solution.py:322
  247.2 13.9 %collective-permute-start.32 = (bf16[512,512]{1,0:T(8,128)(2,1)}, bf16[512,512]{1,0:T(8,128)(2,1)}, u32[]{:S(2)}, u32[]{:S(2)}) collective-permute-start(bf16[512,512]{1,0:T(8,128)(2,1)} %slice.70), channel_id=1, source_target_pairs={{0,2},{2,0},{1,3},{3,1},{4,6},{6,4},{5,7},{7,5},{8,10},{10,8},{9,1... | collective-permute-start | bytes 1572872 | tf_op jit(solution)/shard_map/ppermute | solution.py:322
  320.8 11.4 %collective-permute-start.35 = (bf16[2048,512]{1,0:T(8,128)(2,1)}, bf16[2048,512]{1,0:T(8,128)(2,1)}, u32[]{:S(2)}, u32[]{:S(2)}) collective-permute-start(bf16[2048,512]{1,0:T(8,128)(2,1)} %get-tuple-element.678), channel_id=1, source_target_pairs={{0,1},{1,0},{2,3},{3,2},{4,5},{5,4},{6,7},{7,6},{8,9},{9,8},{10,11... | collective-permute-start | bytes 6291464 | tf_op jit(solution)/shard_map/ppermute | solution.py:322
  332.2 139.3 %reduce-scatter.7.cloned.1.call-start = ((), (), s32[]{:S(2)}) async-start(), calls=%async_computation.8 | async-start | bytes 3932160 | tf_op jit(solution)/shard_map/reduce_scatter | solution.py:452
  345.8 25.4 %collective-permute-start.37 = (bf16[2,512,512]{2,1,0:T(8,128)(2,1)}, bf16[2,512,512]{2,1,0:T(8,128)(2,1)}, u32[]{:S(2)}, u32[]{:S(2)}) collective-permute-start(bf16[2,512,512]{2,1,0:T(8,128)(2,1)} %get-tuple-element.702), channel_id=1, source_target_pairs={{0,4},{4,0},{1,5},{5,1},{2,6},{6,2},{3,7},{7,3},{8,12},{12,8},{9,1... | collective-permute-start | bytes 3145736 | tf_op jit(solution)/shard_map/ppermute | solution.py:322
  347.2 25.2 %collective-permute-start.38 = (bf16[1024,512]{1,0:T(8,128)(2,1)}, bf16[1024,512]{1,0:T(8,128)(2,1)}, u32[]{:S(2)}, u32[]{:S(2)}) collective-permute-start(bf16[1024,512]{1,0:T(8,128)(2,1)} %get-tuple-element.704), channel_id=1, source_target_pairs={{0,2},{2,0},{1,3},{3,1},{4,6},{6,4},{5,7},{7,5},{8,10},{10,8},{9,1... | collective-permute-start | bytes 3145736 | tf_op jit(solution)/shard_map/ppermute | solution.py:322
  372.4 148.0 %reduce-scatter.9.cloned.1.call-start = ((), (), s32[]{:S(2)}) async-start(), calls=%async_computation.9 | async-start | bytes 3932160 | tf_op jit(solution)/shard_map/reduce_scatter | solution.py:452
  372.5 19.5 %collective-permute-start.41 = (bf16[2048,512]{1,0:T(8,128)(2,1)}, bf16[2048,512]{1,0:T(8,128)(2,1)}, u32[]{:S(2)}, u32[]{:S(2)}) collective-permute-start(bf16[2048,512]{1,0:T(8,128)(2,1)} %get-tuple-element.728), channel_id=1, source_target_pairs={{0,1},{1,0},{2,3},{3,2},{4,5},{5,4},{6,7},{7,6},{8,9},{9,8},{10,11... | collective-permute-start | bytes 6291464 | tf_op jit(solution)/shard_map/ppermute | solution.py:322
  372.5 19.5 %collective-permute-start.42 = (bf16[2048,512]{1,0:T(8,128)(2,1)}, bf16[2048,512]{1,0:T(8,128)(2,1)}, u32[]{:S(2)}, u32[]{:S(2)}) collective-permute-start(bf16[2048,512]{1,0:T(8,128)(2,1)} %get-tuple-element.729), channel_id=1, source_target_pairs={{0,1},{1,0},{2,3},{3,2},{4,5},{5,4},{6,7},{7,6},{8,9},{9,8},{10,11... | collective-permute-start | bytes 6291464 | tf_op jit(solution)/shard_map/ppermute | solution.py:322
  376.5 14.3 %collective-permute-start.39 = (bf16[512,512]{1,0:T(8,128)(2,1)}, bf16[512,512]{1,0:T(8,128)(2,1)}, u32[]{:S(2)}, u32[]{:S(2)}) collective-permute-start(bf16[512,512]{1,0:T(8,128)(2,1)} %get-tuple-element.725), channel_id=1, source_target_pairs={{0,2},{2,0},{1,3},{3,1},{4,6},{6,4},{5,7},{7,5},{8,10},{10,8},{9,1... | collective-permute-start | bytes 1572872 | tf_op jit(solution)/shard_map/ppermute | solution.py:322
  378.0 13.9 %collective-permute-start.40 = (bf16[512,512]{1,0:T(8,128)(2,1)}, bf16[512,512]{1,0:T(8,128)(2,1)}, u32[]{:S(2)}, u32[]{:S(2)}) collective-permute-start(bf16[512,512]{1,0:T(8,128)(2,1)} %get-tuple-element.727), channel_id=1, source_target_pairs={{0,4},{4,0},{1,5},{5,1},{2,6},{6,2},{3,7},{7,3},{8,12},{12,8},{9,1... | collective-permute-start | bytes 1572872 | tf_op jit(solution)/shard_map/ppermute | solution.py:322
  409.1 24.8 %collective-permute-start.45 = (bf16[1024,512]{1,0:T(8,128)(2,1)}, bf16[1024,512]{1,0:T(8,128)(2,1)}, u32[]{:S(2)}, u32[]{:S(2)}) collective-permute-start(bf16[1024,512]{1,0:T(8,128)(2,1)} %get-tuple-element.777.refs_0_), channel_id=1, source_target_pairs={{0,2},{2,0},{1,3},{3,1},{4,6},{6,4},{5,7},{7,5},{8,10},{10,8},{9,1... | collective-permute-start | bytes 3145736 | tf_op jit(solution)/shard_map/ppermute | solution.py:322
  409.6 24.3 %collective-permute-start.46 = (bf16[1024,512]{1,0:T(8,128)(2,1)}, bf16[1024,512]{1,0:T(8,128)(2,1)}, u32[]{:S(2)}, u32[]{:S(2)}) collective-permute-start(bf16[1024,512]{1,0:T(8,128)(2,1)} %get-tuple-element.777.refs_0_), channel_id=1, source_target_pairs={{0,4},{4,0},{1,5},{5,1},{2,6},{6,2},{3,7},{7,3},{8,12},{12,8},{9,1... | collective-permute-start | bytes 3145736 | tf_op jit(solution)/shard_map/ppermute | solution.py:322
  410.2 23.7 %collective-permute-start.47 = (bf16[1024,512]{1,0:T(8,128)(2,1)}, bf16[1024,512]{1,0:T(8,128)(2,1)}, u32[]{:S(2)}, u32[]{:S(2)}) collective-permute-start(bf16[1024,512]{1,0:T(8,128)(2,1)} %get-tuple-element.777.refs_0_), channel_id=1, source_target_pairs={{0,1},{1,0},{2,3},{3,2},{4,5},{5,4},{6,7},{7,6},{8,9},{9,8},{10,11... | collective-permute-start | bytes 3145736 | tf_op jit(solution)/shard_map/ppermute | solution.py:322
  433.9 161.3 %reduce-scatter.11.cloned.1.call-start = ((), (), s32[]{:S(2)}) async-start(), calls=%async_computation.10 | async-start | bytes 5242880 | tf_op jit(solution)/shard_map/reduce_scatter | solution.py:452
  434.1 18.6 %collective-permute-start.48 = (bf16[1024,512]{1,0:T(8,128)(2,1)}, bf16[1024,512]{1,0:T(8,128)(2,1)}, u32[]{:S(2)}, u32[]{:S(2)}) collective-permute-start(bf16[1024,512]{1,0:T(8,128)(2,1)} %collective-permute-done.46.refs_0_), channel_id=1, source_target_pairs={{0,1},{1,0},{2,3},{3,2},{4,5},{5,4},{6,7},{7,6},{8,9},{9,8},{10,11... | collective-permute-start | bytes 3145736 | tf_op jit(solution)/shard_map/ppermute | solution.py:322
  438.3 14.2 %collective-permute-start.49 = (bf16[512,512]{1,0:T(8,128)(2,1)}, bf16[512,512]{1,0:T(8,128)(2,1)}, u32[]{:S(2)}, u32[]{:S(2)}) collective-permute-start(bf16[512,512]{1,0:T(8,128)(2,1)} %slice.71), channel_id=1, source_target_pairs={{0,4},{4,0},{1,5},{5,1},{2,6},{6,2},{3,7},{7,3},{8,12},{12,8},{9,1... | collective-permute-start | bytes 1572872 | tf_op jit(solution)/shard_map/ppermute | solution.py:322
  438.7 13.9 %collective-permute-start.50 = (bf16[512,512]{1,0:T(8,128)(2,1)}, bf16[512,512]{1,0:T(8,128)(2,1)}, u32[]{:S(2)}, u32[]{:S(2)}) collective-permute-start(bf16[512,512]{1,0:T(8,128)(2,1)} %slice.72), channel_id=1, source_target_pairs={{0,2},{2,0},{1,3},{3,1},{4,6},{6,4},{5,7},{7,5},{8,10},{10,8},{9,1... | collective-permute-start | bytes 1572872 | tf_op jit(solution)/shard_map/ppermute | solution.py:322
  458.2 13.2 %collective-permute-start.52 = (bf16[256,768]{1,0:T(8,128)(2,1)}, bf16[256,768]{1,0:T(8,128)(2,1)}, u32[]{:S(2)}, u32[]{:S(2)}) collective-permute-start(bf16[256,768]{1,0:T(8,128)(2,1)} %constant_dynamic-slice_fusion.3), channel_id=1, source_target_pairs={{0,4},{4,0},{1,5},{5,1},{2,6},{6,2},{3,7},{7,3},{8,12},{12,8},{9,1... | collective-permute-start | bytes 1179656 | tf_op jit(solution)/shard_map/ppermute | solution.py:322
  471.5 25.8 %collective-permute-start.54 = (bf16[2,512,512]{2,1,0:T(8,128)(2,1)}, bf16[2,512,512]{2,1,0:T(8,128)(2,1)S(1)}, u32[]{:S(2)}, u32[]{:S(2)}) collective-permute-start(bf16[2,512,512]{2,1,0:T(8,128)(2,1)} %get-tuple-element.813), channel_id=1, source_target_pairs={{0,4},{4,0},{1,5},{5,1},{2,6},{6,2},{3,7},{7,3},{8,12},{12,8},{9,1... | collective-permute-start | bytes 3145736 | tf_op jit(solution)/shard_map/ppermute | solution.py:322
  472.8 25.2 %collective-permute-start.55 = (bf16[1024,512]{1,0:T(8,128)(2,1)}, bf16[1024,512]{1,0:T(8,128)(2,1)S(1)}, u32[]{:S(2)}, u32[]{:S(2)}) collective-permute-start(bf16[1024,512]{1,0:T(8,128)(2,1)} %get-tuple-element.815), channel_id=1, source_target_pairs={{0,2},{2,0},{1,3},{3,1},{4,6},{6,4},{5,7},{7,5},{8,10},{10,8},{9,1... | collective-permute-start | bytes 3145736 | tf_op jit(solution)/shard_map/ppermute | solution.py:322
  505.7 13.2 %collective-permute-start.56 = (bf16[2048,512]{1,0:T(8,128)(2,1)}, bf16[2048,512]{1,0:T(8,128)(2,1)S(1)}, u32[]{:S(2)}, u32[]{:S(2)}) collective-permute-start(bf16[2048,512]{1,0:T(8,128)(2,1)} %get-tuple-element.824), channel_id=1, source_target_pairs={{0,1},{1,0},{2,3},{3,2},{4,5},{5,4},{6,7},{7,6},{8,9},{9,8},{10,11... | collective-permute-start | bytes 6291464 | tf_op jit(solution)/shard_map/ppermute | solution.py:322
  505.8 13.1 %collective-permute-start.57 = (bf16[2048,512]{1,0:T(8,128)(2,1)}, bf16[2048,512]{1,0:T(8,128)(2,1)}, u32[]{:S(2)}, u32[]{:S(2)}) collective-permute-start(bf16[2048,512]{1,0:T(8,128)(2,1)} %get-tuple-element.825), channel_id=1, source_target_pairs={{0,1},{1,0},{2,3},{3,2},{4,5},{5,4},{6,7},{7,6},{8,9},{9,8},{10,11... | collective-permute-start | bytes 6291464 | tf_op jit(solution)/shard_map/ppermute | solution.py:322
  507.1 11.8 %collective-permute-start.58 = (bf16[256,768]{1,0:T(8,128)(2,1)}, bf16[256,768]{1,0:T(8,128)(2,1)S(1)}, u32[]{:S(2)}, u32[]{:S(2)}) collective-permute-start(bf16[256,768]{1,0:T(8,128)(2,1)} %constant_dynamic-slice_fusion.2), channel_id=1, source_target_pairs={{0,4},{4,0},{1,5},{5,1},{2,6},{6,2},{3,7},{7,3},{8,12},{12,8},{9,1... | collective-permute-start | bytes 1179656 | tf_op jit(solution)/shard_map/ppermute | solution.py:322
  523.8 15.5 %collective-permute-start.60 = (bf16[512,512]{1,0:T(8,128)(2,1)}, bf16[512,512]{1,0:T(8,128)(2,1)S(1)}, u32[]{:S(2)}, u32[]{:S(2)}) collective-permute-start(bf16[512,512]{1,0:T(8,128)(2,1)} %get-tuple-element.856), channel_id=1, source_target_pairs={{0,2},{2,0},{1,3},{3,1},{4,6},{6,4},{5,7},{7,5},{8,10},{10,8},{9,1... | collective-permute-start | bytes 1572872 | tf_op jit(solution)/shard_map/ppermute | solution.py:322
  525.6 13.7 %collective-permute-start.61 = (bf16[512,512]{1,0:T(8,128)(2,1)}, bf16[512,512]{1,0:T(8,128)(2,1)S(1)}, u32[]{:S(2)}, u32[]{:S(2)}) collective-permute-start(bf16[512,512]{1,0:T(8,128)(2,1)} %get-tuple-element.858), channel_id=1, source_target_pairs={{0,4},{4,0},{1,5},{5,1},{2,6},{6,2},{3,7},{7,3},{8,12},{12,8},{9,1... | collective-permute-start | bytes 1572872 | tf_op jit(solution)/shard_map/ppermute | solution.py:322
  526.7 12.5 %collective-permute-start.59 = (f32[6,128]{1,0:T(8,128)S(1)}, f32[6,128]{1,0:T(8,128)S(1)}, u32[]{:S(2)}, u32[]{:S(2)}) collective-permute-start(f32[6,128]{1,0:T(8,128)S(1)} %pad_maximum_fusion.9), channel_id=1, source_target_pairs={{0,4},{4,0},{1,5},{5,1},{2,6},{6,2},{3,7},{7,3},{8,12},{12,8},{9,1... | collective-permute-start | bytes 9224 | tf_op jit(solution)/shard_map/ppermute | solution.py:322
  540.3 24.0 %collective-permute-start.63 = (bf16[2,512,512]{2,1,0:T(8,128)(2,1)}, bf16[2,512,512]{2,1,0:T(8,128)(2,1)S(1)}, u32[]{:S(2)}, u32[]{:S(2)}) collective-permute-start(bf16[2,512,512]{2,1,0:T(8,128)(2,1)} %get-tuple-element.880), channel_id=1, source_target_pairs={{0,4},{4,0},{1,5},{5,1},{2,6},{6,2},{3,7},{7,3},{8,12},{12,8},{9,1... | collective-permute-start | bytes 3145736 | tf_op jit(solution)/shard_map/ppermute | solution.py:322
  541.4 23.7 %collective-permute-start.64 = (bf16[1024,512]{1,0:T(8,128)(2,1)}, bf16[1024,512]{1,0:T(8,128)(2,1)S(1)}, u32[]{:S(2)}, u32[]{:S(2)}) collective-permute-start(bf16[1024,512]{1,0:T(8,128)(2,1)} %get-tuple-element.882), channel_id=1, source_target_pairs={{0,2},{2,0},{1,3},{3,1},{4,6},{6,4},{5,7},{7,5},{8,10},{10,8},{9,1... | collective-permute-start | bytes 3145736 | tf_op jit(solution)/shard_map/ppermute | solution.py:322
  569.5 11.8 %collective-permute-start.66 = (bf16[512,512]{1,0:T(8,128)(2,1)}, bf16[512,512]{1,0:T(8,128)(2,1)S(1)}, u32[]{:S(2)}, u32[]{:S(2)}) collective-permute-start(bf16[512,512]{1,0:T(8,128)(2,1)} %get-tuple-element.903), channel_id=1, source_target_pairs={{0,2},{2,0},{1,3},{3,1},{4,6},{6,4},{5,7},{7,5},{8,10},{10,8},{9,1... | collective-permute-start | bytes 1572872 | tf_op jit(solution)/shard_map/ppermute | solution.py:322
  570.1 11.6 %collective-permute-start.67 = (bf16[512,512]{1,0:T(8,128)(2,1)}, bf16[512,512]{1,0:T(8,128)(2,1)}, u32[]{:S(2)}, u32[]{:S(2)}) collective-permute-start(bf16[512,512]{1,0:T(8,128)(2,1)} %get-tuple-element.905), channel_id=1, source_target_pairs={{0,4},{4,0},{1,5},{5,1},{2,6},{6,2},{3,7},{7,3},{8,12},{12,8},{9,1... | collective-permute-start | bytes 1572872 | tf_op jit(solution)/shard_map/ppermute | solution.py:322
  597.1 20.0 %collective-permute-start.73 = (bf16[256,1024]{1,0:T(8,128)(2,1)}, bf16[256,1024]{1,0:T(8,128)(2,1)}, u32[]{:S(2)}, u32[]{:S(2)}) collective-permute-start(bf16[256,1024]{1,0:T(8,128)(2,1)} %constant_dynamic-slice_fusion), channel_id=1, source_target_pairs={{0,4},{4,0},{1,5},{5,1},{2,6},{6,2},{3,7},{7,3},{8,12},{12,8},{9,1... | collective-permute-start | bytes 1572872 | tf_op jit(solution)/shard_map/ppermute | solution.py:322
  598.6 12.6 %collective-permute-start.74 = (f32[4,128]{1,0:T(4,128)}, f32[4,128]{1,0:T(4,128)}, u32[]{:S(2)}, u32[]{:S(2)}) collective-permute-start(f32[4,128]{1,0:T(4,128)} %fusion.19), channel_id=1, source_target_pairs={{0,4},{4,0},{1,5},{5,1},{2,6},{6,2},{3,7},{7,3},{8,12},{12,8},{9,1... | collective-permute-start | bytes 6152 | tf_op jit(solution)/shard_map/ppermute | solution.py:322
  (70 other events, 450.2 us)
Sparse Core Ops, SparseCore 0:
  27.2 82.0 all-gather.3
  110.9 62.0 all-gather.5
  175.1 113.9 all-gather.7
  332.3 58.5 reduce-scatter.4
  393.1 60.2 reduce-scatter.6
  455.5 60.2 reduce-scatter.8
  519.0 76.1 reduce-scatter.10

commit v7 on v6

--- a/solution.py
+++ b/solution.py
@@ -395,10 +395,29 @@
     return (flip(own, "y"), flip(own, "x"), flip(own, "core"))
 
 
+def cut_kernel(first_ref, second_ref, upper_ref, lower_ref):
+    upper_ref[...] = first_ref[...]
+    lower_ref[...] = second_ref[...]
+
+
+def cut_halves(first, second):
+    half, width = first.shape[0] // 2, first.shape[1]
+    tile = half // 2
+    shape = jax.ShapeDtypeStruct((half, width), first.dtype)
+    out = pl.BlockSpec((tile, width), lambda i: (i, 0))
+    return pl.pallas_call(
+        cut_kernel,
+        grid=(2,),
+        in_specs=[out, pl.BlockSpec((tile, width), lambda i: (i + 2, 0))],
+        out_specs=[out, out],
+        out_shape=[shape, shape],
+        cost_estimate=light,
+    )(first, second)
+
+
 def relay_flips(via_y, via_x):
-    half = via_y.shape[0] // 2
-    upper = flip(via_y[:half], "x")
-    lower = flip(via_x[half:], "y")
+    upper, lower = cut_halves(via_y, via_x)
+    upper, lower = flip(upper, "x"), flip(lower, "y")
     return (flip(via_y, "core"), via_x, flip(via_x, "core"), upper, lower)
 
 
@@ -1317,7 +1336,7 @@
         grad_tokens, unused = norm_back(
             grad_hidden1, tokens, inverse1, gain_attn_own, dots, grad_resid
         )
-        return (got_attn, spot, grad_tokens, join_all(down_sum, got_down))
+        return (got_attn, spot, grad_tokens, *join_parts(down_sum, got_down, across, (hidden_width,)))
 
     got_attn, spot, grad_tokens, down_part = line.run(
         last_norm, grad_hidden1, tokens, inverse1, dots, grad_resid, late, early, attn_sum,

time: 634 us -> 631 us (level)
  local copies, waits for them, and re-layouts: 46.3 us -> 34.9 us
  Pallas kernels: 263 us -> 274 us
    slice x8 -> x0, local copies, waits for them, and re-layouts: 11.8 us -> none  [the longest x4 6.43 us: relay_flips(): lower = flip(via_x[half:], 'y')]
    pallas_call x0 -> x4, Pallas kernels: none -> 8.51 us  [cut_halves(): pl.pallas_call(cut_kernel, grid=(2,), in_specs=[out, pl.BlockSpec((tile,...]
    ppermute x73, waiting for transfers between devices: 167 us -> 159 us  [flip(): return lax.ppermute(values, axis, [(0, 1), (1, 0)])]
    unnamed x106 -> x104, local copies, waits for them, and re-layouts: 19.8 us -> 19 us
  transfers between devices with their start and end apart: 84 -> 84, of which waited for: 41 -> 39; matrix products, arithmetic and copies ran while one was open for 13% -> 12% of each run, Pallas kernels for 36% -> 38%
where the time goes in v7:
time: 631 us; the launch traced here: 625 us
  Pallas kernels  274 us (43%)
  waiting for transfers between devices  191 us (30%)
  starting transfers between devices  58.6 us (9%)
  other arithmetic  50.9 us (8%)
  local copies, waits for them, and re-layouts  34.9 us (6%)
  between operations  15 us (2%)
    ppermute x73, waiting for transfers between devices, flip(): return lax.ppermute(values, axis, [(0, 1), (1, 0)])  159 us
    ppermute x73, starting transfers between devices, flip(): return lax.ppermute(values, axis, [(0, 1), (1, 0)])  56 us
    pallas_call x8, Pallas kernels, pack(): pl.pallas_call(partial(pack_kernel, normed), grid=(tiles,), in_specs=[pl....  42.2 us
    pallas_call x4, Pallas kernels, fold_held(): pl.pallas_call(fold_held_kernel, grid_spec=pltpu.PrefetchScalarGridSpec(n...  38.8 us
    pallas_call x3, Pallas kernels, dot_grad(): pl.pallas_call(partial(matmul_kernel, product_tn), grid=(rows // tile,),...  32.6 us
    pallas_call x4, Pallas kernels, fold_sent(): pl.pallas_call(fold_sent_kernel, grid_spec=pltpu.PrefetchScalarGridSpec(n...  31.5 us
    pallas_call x3, Pallas kernels, dot_in(): pl.pallas_call(partial(matmul_kernel, product_nn), grid=(count // tile,),...  29.9 us
    all_gather x3, waiting for transfers between devices, weight_gather(): return lax.all_gather(rows, 'z', axis=0, tiled=True)  24.2 us
  transfers between devices with their start and end apart: 84, of which 39 were waited for; matrix products, arithmetic and copies ran while one was open for 12% of the time, Pallas kernels for 38%

profile of v7, /device:TPU:0, one launch (start us, length us, event | category | flops | bytes accessed | tf_op | source)
XLA Modules:
  0.0 624.5 jit_solution(2972349256867713116)
XLA Ops:
  9.6 2.9 collective-permute-start
  15.2 9.5 %collective-permute-done = bf16[256,1024]{1,0:T(8,128)(2,1)S(1)} collective-permute-done((bf16[256,1024]{1,0:T(8,128)(2,1)}, bf16[256,1024]{1,0:T(8,128)(2,1)S(1)}, u32[]{:S(2)}, u32[]{:S(2)}) %collective-permute-start) | collective-permute-done | bytes 524320 | tf_op jit(solution)/shard_map/ppermute | solution.py:322
  33.6 2.7 shard_map.255
  36.3 7.6 %collective-permute-done.2 = bf16[512,512]{1,0:T(8,128)(2,1)} collective-permute-done((bf16[512,512]{1,0:T(8,128)(2,1)S(1)}, bf16[512,512]{1,0:T(8,128)(2,1)}, u32[]{:S(2)}, u32[]{:S(2)}) %collective-permute-start.2) | collective-permute-done | bytes 524320 | tf_op jit(solution)/shard_map/ppermute | solution.py:322
  45.2 6.8 %collective-permute-done.5 = s32[1024]{0:T(1024)S(1)} collective-permute-done((s32[1024]{0:T(1024)S(1)}, s32[1024]{0:T(1024)S(1)}, u32[]{:S(2)}, u32[]{:S(2)}) %collective-permute-start.5) | collective-permute-done | bytes 4128 | tf_op jit(solution)/shard_map/ppermute | solution.py:322
  58.2 6.8 %collective-permute-done.6 = bf16[256,768]{1,0:T(8,128)(2,1)} collective-permute-done((bf16[256,768]{1,0:T(8,128)(2,1)}, bf16[256,768]{1,0:T(8,128)(2,1)}, u32[]{:S(2)}, u32[]{:S(2)}) %collective-permute-start.6) | collective-permute-done | bytes 393248 | tf_op jit(solution)/shard_map/ppermute | solution.py:322
  67.0 5.7 shard_map.258
  72.7 2.6 collective-permute-done.8
  86.0 3.7 fusion.10
  90.4 5.8 shard_map.259
  96.1 5.4 collective-permute-done.12.first_ref.refs_2_
  102.7 6.6 %all-gather.4.cloned.1.call-done.weight_ref.near_ref.far_ref = bf16[2048,1024]{1,0:T(8,128)(2,1)} async-done(((bf16[512,1024]{1,0:T(8,128)(2,1)}), bf16[2048,1024]{1,0:T(8,128)(2,1)}) %all-gather.4.cloned.1.call-update) | async-done | bytes 4194320 | tf_op jit(solution)/shard_map/all_gather | solution.py:467
  115.4 11.7 %shard_map.260.joint_ref = f32[2048,768]{1,0:T(8,128)} custom-call(bf16[2048,2048]{1,0:T(8,128)(2,1)} %get-tuple-element.842.operand_ref.a, bf16[2048,1024]{1,0:T(8,128)(2,1)} %all-gather.4.cloned.1.call-done.weight_ref.near_ref.far_ref), custom_call_target="tpu_custom_call" | custom-call | tf_op jit(solution)/shard_map/pallas_call | solution.py:665
  127.1 2.8 copy-done
  129.9 10.4 %shard_map.261 = (bf16[2048,256]{1,0:T(8,128)(2,1)S(1)}, f32[2048,256]{1,0:T(8,128)S(1)}, bf16[2048,256]{1,0:T(8,128)(2,1)S(1)}, bf16[2048,128]{1,0:T(8,128)(2,1)S(1)}, f32[2,2,1024]{2,1,0:T(2,128)S(1)}) custom-call(f32[2048,768]{1,0:T(8,128)S(1)} %copy-done, f32[2048,128]{1,0:T(8,128)S(1)} %get-tuple-element.562.cos_ref, ...), custom_call_target="tpu_custom_call" | custom-call | tf_op jit(solution)/shard_map/pallas_call | solution.py:966
  146.1 5.1 shard_map.263
  151.7 3.9 collective-permute-done.20.near_got
  155.5 3.0 collective-permute-done.21.far_got
  159.9 6.6 %shard_map.264 = (bf16[2,512,512]{2,1,0:T(8,128)(2,1)}, bf16[2,512,512]{2,1,0:T(8,128)(2,1)}, bf16[1024,512]{1,0:T(8,128)(2,1)}, bf16[1024,512]{1,0:T(8,128)(2,1)}) custom-call(s32[1]{0:T(128)} %bitcast.place_ref.refs_4_, bf16[2048,256]{1,0:T(8,128)(2,1)} %copy-done.1, bf16[2048,1024]{1,0:T(8,128)(2,1)} %all-gather.4.cloned.1.call-done.weight_ref.near_ref.far_ref, ...), custom_call_target="tpu_custom_call" | custom-call | tf_op jit(solution)/shard_map/pallas_call | solution.py:604
  172.2 4.7 shard_map.265.refs_4_
  176.9 4.9 shard_map.266.operand_ref
  181.8 14.3 %collective-permute-done.22.upper_ref = bf16[2,512,512]{2,1,0:T(8,128)(2,1)} collective-permute-done((bf16[2,512,512]{2,1,0:T(8,128)(2,1)}, bf16[2,512,512]{2,1,0:T(8,128)(2,1)}, u32[]{:S(2)}, u32[]{:S(2)}) %collective-permute-start.22) | collective-permute-done | bytes 1048608 | tf_op jit(solution)/shard_map/ppermute | solution.py:322
  197.3 3.5 shard_map.267
  201.7 12.5 %collective-permute-done.25 = bf16[512,512]{1,0:T(8,128)(2,1)S(1)} collective-permute-done((bf16[512,512]{1,0:T(8,128)(2,1)}, bf16[512,512]{1,0:T(8,128)(2,1)S(1)}, u32[]{:S(2)}, u32[]{:S(2)}) %collective-permute-start.25) | collective-permute-done | bytes 524320 | tf_op jit(solution)/shard_map/ppermute | solution.py:322
  220.2 11.3 %shard_map.268.grad_ref = f32[2048,768]{1,0:T(8,128)} custom-call(bf16[2048,2048]{1,0:T(8,128)(2,1)} %shard_map.266.operand_ref, bf16[2048,768]{1,0:T(8,128)(2,1)} %all-gather.6.cloned.1.call-done.weight_ref.near_ref.far_ref), custom_call_target="tpu_custom_call" | custom-call | tf_op jit(solution)/shard_map/pallas_call | solution.py:665
  231.6 10.1 %collective-permute-done.27.first_ref.refs_2_ = bf16[1024,512]{1,0:T(8,128)(2,1)} collective-permute-done((bf16[1024,512]{1,0:T(8,128)(2,1)}, bf16[1024,512]{1,0:T(8,128)(2,1)}, u32[]{:S(2)}, u32[]{:S(2)}) %collective-permute-start.27) | collective-permute-done | bytes 1048608 | tf_op jit(solution)/shard_map/ppermute | solution.py:322
  246.6 5.7 shard_map.270
  252.3 7.3 %collective-permute-done.31 = bf16[512,512]{1,0:T(8,128)(2,1)} collective-permute-done((bf16[512,512]{1,0:T(8,128)(2,1)}, bf16[512,512]{1,0:T(8,128)(2,1)}, u32[]{:S(2)}, u32[]{:S(2)}) %collective-permute-start.31) | collective-permute-done | bytes 524320 | tf_op jit(solution)/shard_map/ppermute | solution.py:322
  263.1 2.8 collective-permute-done.34.refs_3_
  265.8 5.7 shard_map.271
  271.5 17.6 %all-gather.8.cloned.1.call-done.weight_ref.near_ref.far_ref = bf16[2048,1536]{1,0:T(8,128)(2,1)} async-done(((bf16[512,1536]{1,0:T(8,128)(2,1)}), bf16[2048,1536]{1,0:T(8,128)(2,1)}) %all-gather.8.cloned.1.call-update) | async-done | bytes 6291472 | tf_op jit(solution)/shard_map/all_gather | solution.py:467
  289.1 20.3 %shard_map.272 = (bf16[2048,768]{1,0:T(8,128)(2,1)}, bf16[2048,1536]{1,0:T(8,128)(2,1)}) custom-call(bf16[2048,2048]{1,0:T(8,128)(2,1)} %get-tuple-element.720.hidden_ref.operand_ref, bf16[2048,1536]{1,0:T(8,128)(2,1)} %all-gather.8.cloned.1.call-done.weight_ref.near_ref.far_ref, f32[2048,768]{1,0:T(8,128)} %shard_map.268.grad_ref), custom_call_target="tpu_custom_call" | custom-call | tf_op jit(solution)/shard_map/pallas_call | solution.py:743
  309.4 11.4 %shard_map.273 = (bf16[2048,512]{1,0:T(8,128)(2,1)}, bf16[2048,512]{1,0:T(8,128)(2,1)}) custom-call(s32[1]{0:T(128)} %bitcast.place_ref.refs_4_, bf16[2048,1536]{1,0:T(8,128)(2,1)} %get-tuple-element.721.operand_ref.weight_ref, bf16[2048,1536]{1,0:T(8,128)(2,1)} %all-gather.8.cloned.1.call-done.weight_ref.near_ref.far_ref, ...), custom_call_target="tpu_custom_call" | custom-call | tf_op jit(solution)/shard_map/pallas_call | solution.py:577
  321.3 10.9 %shard_map.274 = bf16[2048,768]{1,0:T(8,128)(2,1)} custom-call(bf16[2048,2048]{1,0:T(8,128)(2,1)} %get-tuple-element.720.hidden_ref.operand_ref, bf16[2048,1536]{1,0:T(8,128)(2,1)} %get-tuple-element.721.operand_ref.weight_ref), custom_call_target="tpu_custom_call" | custom-call | tf_op jit(solution)/shard_map/pallas_call | solution.py:683
  332.2 13.5 %shard_map.275 = (bf16[2,512,512]{2,1,0:T(8,128)(2,1)}, bf16[2,512,512]{2,1,0:T(8,128)(2,1)}, bf16[1024,512]{1,0:T(8,128)(2,1)}, bf16[1024,512]{1,0:T(8,128)(2,1)}) custom-call(s32[1]{0:T(128)} %bitcast.place_ref.refs_4_, bf16[2048,1536]{1,0:T(8,128)(2,1)} %get-tuple-element.721.operand_ref.weight_ref, ...), custom_call_target="tpu_custom_call" | custom-call | tf_op jit(solution)/shard_map/pallas_call | solution.py:604
  348.7 10.8 %shard_map.276 = bf16[2048,768]{1,0:T(8,128)(2,1)} custom-call(bf16[2048,2048]{1,0:T(8,128)(2,1)} %get-tuple-element.720.hidden_ref.operand_ref, bf16[2048,1536]{1,0:T(8,128)(2,1)} %get-tuple-element.721.operand_ref.weight_ref), custom_call_target="tpu_custom_call" | custom-call | tf_op jit(solution)/shard_map/pallas_call | solution.py:683
  359.6 7.3 %shard_map.277 = (bf16[2048,512]{1,0:T(8,128)(2,1)}, bf16[2048,512]{1,0:T(8,128)(2,1)}) custom-call(s32[1]{0:T(128)} %bitcast.place_ref.refs_4_, bf16[2048,768]{1,0:T(8,128)(2,1)} %get-tuple-element.774.operand_ref.weight_ref, bf16[2048,768]{1,0:T(8,128)(2,1)} %all-gather.6.cloned.1.call-done.weight_ref.near_ref.far_ref, ...), custom_call_target="tpu_custom_call" | custom-call | tf_op jit(solution)/shard_map/pallas_call | solution.py:577
  366.9 4.3 collective-permute-done.37.upper_ref
  373.0 3.4 shard_map.278
  379.3 11.4 %collective-permute-done.39 = bf16[512,512]{1,0:T(8,128)(2,1)} collective-permute-done((bf16[512,512]{1,0:T(8,128)(2,1)}, bf16[512,512]{1,0:T(8,128)(2,1)}, u32[]{:S(2)}, u32[]{:S(2)}) %collective-permute-start.39) | collective-permute-done | bytes 524320 | tf_op jit(solution)/shard_map/ppermute | solution.py:322
  399.8 3.1 collective-permute-done.44
  404.2 4.8 fusion.17
  410.1 10.9 %shard_map.279 = bf16[2048,768]{1,0:T(8,128)(2,1)} custom-call(bf16[2048,2048]{1,0:T(8,128)(2,1)} %shard_map.266.operand_ref, bf16[2048,768]{1,0:T(8,128)(2,1)} %get-tuple-element.774.operand_ref.weight_ref), custom_call_target="tpu_custom_call" | custom-call | tf_op jit(solution)/shard_map/pallas_call | solution.py:683
  421.0 9.2 %shard_map.280 = (bf16[2,512,512]{2,1,0:T(8,128)(2,1)}, bf16[2,512,512]{2,1,0:T(8,128)(2,1)}, bf16[1024,512]{1,0:T(8,128)(2,1)}, bf16[1024,512]{1,0:T(8,128)(2,1)}) custom-call(s32[1]{0:T(128)} %bitcast.place_ref.refs_4_, bf16[2048,768]{1,0:T(8,128)(2,1)} %get-tuple-element.774.operand_ref.weight_ref, ...), custom_call_target="tpu_custom_call" | custom-call | tf_op jit(solution)/shard_map/pallas_call | solution.py:604
  430.3 3.6 collective-permute-done.45.first_ref.refs_2_
  434.5 2.4 shard_map.281
  439.0 4.7 shard_map.282.refs_4_
  443.7 7.4 %collective-permute-done.49 = bf16[512,512]{1,0:T(8,128)(2,1)} collective-permute-done((bf16[512,512]{1,0:T(8,128)(2,1)}, bf16[512,512]{1,0:T(8,128)(2,1)}, u32[]{:S(2)}, u32[]{:S(2)}) %collective-permute-start.49) | collective-permute-done | bytes 524320 | tf_op jit(solution)/shard_map/ppermute | solution.py:322
  458.5 5.0 shard_map.283.operand_ref
  463.5 6.8 %shard_map.284.grad_mixed_ref = f32[2048,256]{1,0:T(8,128)} custom-call(bf16[2048,2048]{1,0:T(8,128)(2,1)} %shard_map.283.operand_ref, bf16[2048,1024]{1,0:T(8,128)(2,1)} %all-gather.4.cloned.1.call-done.weight_ref.near_ref.far_ref), custom_call_target="tpu_custom_call" | custom-call | tf_op jit(solution)/shard_map/pallas_call | solution.py:665
  473.2 6.8 %shard_map.286.unused = bf16[2048,1024]{1,0:T(8,128)(2,1)} custom-call(bf16[2048,2048]{1,0:T(8,128)(2,1)} %shard_map.283.operand_ref, bf16[2048,256]{1,0:T(8,128)(2,1)} %copy-done.1), custom_call_target="tpu_custom_call" | custom-call | tf_op jit(solution)/shard_map/pallas_call | solution.py:710
  480.1 15.9 %shard_map.285 = (bf16[2048,768]{1,0:T(8,128)(2,1)}, f32[2,128]{1,0:T(2,128)S(1)}) custom-call(f32[2048,768]{1,0:T(8,128)} %shard_map.260.joint_ref, f32[2048,128]{1,0:T(8,128)S(1)} %get-tuple-element.562.cos_ref, f32[2048,128]{1,0:T(8,128)S(1)} %get-tuple-element.563.sin_ref, s32[2,1,1024]{2,1,0:T(1,128)S(1)} %compare_select_fusion.first_ref, ...), custom_call_target="tpu_custom_call" | custom-call | tf_op jit(solution)/shard_map/pallas_call | solution.py:989
  496.6 7.7 %shard_map.287 = (bf16[2048,512]{1,0:T(8,128)(2,1)}, bf16[2048,512]{1,0:T(8,128)(2,1)}) custom-call(s32[1]{0:T(128)} %bitcast.place_ref.refs_4_, bf16[2048,768]{1,0:T(8,128)(2,1)} %get-tuple-element.859.operand_ref.b, bf16[2048,1024]{1,0:T(8,128)(2,1)} %all-gather.4.cloned.1.call-done.weight_ref.near_ref.far_ref, ...), custom_call_target="tpu_custom_call" | custom-call | tf_op jit(solution)/shard_map/pallas_call | solution.py:577
  506.7 11.0 %shard_map.288 = bf16[2048,1024]{1,0:T(8,128)(2,1)} custom-call(bf16[2048,2048]{1,0:T(8,128)(2,1)} %get-tuple-element.842.operand_ref.a, bf16[2048,768]{1,0:T(8,128)(2,1)} %get-tuple-element.859.operand_ref.b, bf16[2048,1024]{1,0:T(8,128)(2,1)} %shard_map.286.unused), custom_call_target="tpu_custom_call", output_to_operand_aliasing={{}: (2, {})} | custom-call | tf_op jit(solution)/shard_map/pallas_call | solution.py:710
  519.2 3.5 shard_map.290
  527.2 9.5 %shard_map.289 = (bf16[2,512,512]{2,1,0:T(8,128)(2,1)}, bf16[2,512,512]{2,1,0:T(8,128)(2,1)}, bf16[1024,512]{1,0:T(8,128)(2,1)}, bf16[1024,512]{1,0:T(8,128)(2,1)}) custom-call(s32[1]{0:T(128)} %bitcast.place_ref.refs_4_, bf16[2048,768]{1,0:T(8,128)(2,1)} %get-tuple-element.859.operand_ref.b, ...), custom_call_target="tpu_custom_call" | custom-call | tf_op jit(solution)/shard_map/pallas_call | solution.py:604
  545.9 17.1 %collective-permute-done.63.upper_ref = bf16[2,512,512]{2,1,0:T(8,128)(2,1)S(1)} collective-permute-done((bf16[2,512,512]{2,1,0:T(8,128)(2,1)}, bf16[2,512,512]{2,1,0:T(8,128)(2,1)S(1)}, u32[]{:S(2)}, u32[]{:S(2)}) %collective-permute-start.63) | collective-permute-done | bytes 1048608 | tf_op jit(solution)/shard_map/ppermute | solution.py:322
  564.7 3.4 shard_map.291
  571.3 8.5 %collective-permute-done.66 = bf16[512,512]{1,0:T(8,128)(2,1)S(1)} collective-permute-done((bf16[512,512]{1,0:T(8,128)(2,1)}, bf16[512,512]{1,0:T(8,128)(2,1)S(1)}, u32[]{:S(2)}, u32[]{:S(2)}) %collective-permute-start.66) | collective-permute-done | bytes 524320 | tf_op jit(solution)/shard_map/ppermute | solution.py:322
  585.1 2.8 collective-permute-done.71
  589.9 3.8 collective-permute-done.72
  607.7 3.5 multiply_add_fusion
  611.1 2.5 shard_map.292
  614.2 2.7 shard_map.293
  (332 shorter events, 149.4 us)
Async XLA Ops:
  7.2 102.1 %all-gather.4.cloned.1.call-start = ((), (), s32[]{:S(2)}) async-start(), calls=%async_computation.4 | async-start | bytes 5242880 | tf_op jit(solution)/shard_map/all_gather | solution.py:467
  9.6 15.1 %collective-permute-start = (bf16[256,1024]{1,0:T(8,128)(2,1)}, bf16[256,1024]{1,0:T(8,128)(2,1)S(1)}, u32[]{:S(2)}, u32[]{:S(2)}) collective-permute-start(bf16[256,1024]{1,0:T(8,128)(2,1)} %get-tuple-element.501), channel_id=1, source_target_pairs={{0,4},{4,0},{1,5},{5,1},{2,6},{6,2},{3,7},{7,3},{8,12},{12,8},{9,1... | collective-permute-start | bytes 1572872 | tf_op jit(solution)/shard_map/ppermute | solution.py:322
  13.6 13.4 %collective-permute-start.1 = (bf16[512,512]{1,0:T(8,128)(2,1)S(1)}, bf16[512,512]{1,0:T(8,128)(2,1)S(1)}, u32[]{:S(2)}, u32[]{:S(2)}) collective-permute-start(bf16[512,512]{1,0:T(8,128)(2,1)S(1)} %slice.36), channel_id=1, source_target_pairs={{0,2},{2,0},{1,3},{3,1},{4,6},{6,4},{5,7},{7,5},{8,10},{10,8},{9,1... | collective-permute-start | bytes 1572872 | tf_op jit(solution)/shard_map/ppermute | solution.py:322
  27.9 190.1 %all-gather.6.cloned.1.call-start = ((), (), s32[]{:S(2)}) async-start(), calls=%async_computation.5 | async-start | bytes 3932160 | tf_op jit(solution)/shard_map/all_gather | solution.py:467
  27.9 24.2 %collective-permute-start.3 = (bf16[1024,512]{1,0:T(8,128)(2,1)S(1)}, bf16[1024,512]{1,0:T(8,128)(2,1)S(1)}, u32[]{:S(2)}, u32[]{:S(2)}) collective-permute-start(bf16[1024,512]{1,0:T(8,128)(2,1)S(1)} %copy-done.8), channel_id=1, source_target_pairs={{0,4},{4,0},{1,5},{5,1},{2,6},{6,2},{3,7},{7,3},{8,12},{12,8},{9,1... | collective-permute-start | bytes 3145736 | tf_op jit(solution)/shard_map/ppermute | solution.py:322
  29.4 22.7 %collective-permute-start.4 = (bf16[1024,512]{1,0:T(8,128)(2,1)S(1)}, bf16[1024,512]{1,0:T(8,128)(2,1)}, u32[]{:S(2)}, u32[]{:S(2)}) collective-permute-start(bf16[1024,512]{1,0:T(8,128)(2,1)S(1)} %copy-done.8), channel_id=1, source_target_pairs={{0,1},{1,0},{2,3},{3,2},{4,5},{5,4},{6,7},{7,6},{8,9},{9,8},{10,11... | collective-permute-start | bytes 3145736 | tf_op jit(solution)/shard_map/ppermute | solution.py:322
  29.4 14.5 %collective-permute-start.2 = (bf16[512,512]{1,0:T(8,128)(2,1)S(1)}, bf16[512,512]{1,0:T(8,128)(2,1)}, u32[]{:S(2)}, u32[]{:S(2)}) collective-permute-start(bf16[512,512]{1,0:T(8,128)(2,1)S(1)} %slice.37), channel_id=1, source_target_pairs={{0,2},{2,0},{1,3},{3,1},{4,6},{6,4},{5,7},{7,5},{8,10},{10,8},{9,1... | collective-permute-start | bytes 1572872 | tf_op jit(solution)/shard_map/ppermute | solution.py:322
  31.0 21.1 %collective-permute-start.5 = (s32[1024]{0:T(1024)S(1)}, s32[1024]{0:T(1024)S(1)}, u32[]{:S(2)}, u32[]{:S(2)}) collective-permute-start(s32[1024]{0:T(1024)S(1)} %copy-done.47), channel_id=1, source_target_pairs={{0,4},{4,0},{1,5},{5,1},{2,6},{6,2},{3,7},{7,3},{8,12},{12,8},{9,1... | collective-permute-start | bytes 12296 | tf_op jit(solution)/shard_map/ppermute | solution.py:322
  52.1 14.9 %collective-permute-start.10 = (bf16[1024,512]{1,0:T(8,128)(2,1)S(1)}, bf16[1024,512]{1,0:T(8,128)(2,1)}, u32[]{:S(2)}, u32[]{:S(2)}) collective-permute-start(bf16[1024,512]{1,0:T(8,128)(2,1)S(1)} %pad_maximum_fusion.4.first_ref.refs_2_), channel_id=1, source_target_pairs={{0,1},{1,0},{2,3},{3,2},{4,5},{5,4},{6,7},{7,6},{8,9},{9,8},{10,11... | collective-permute-start | bytes 3145736 | tf_op jit(solution)/shard_map/ppermute | solution.py:322
  52.2 23.2 %collective-permute-start.7 = (bf16[1024,512]{1,0:T(8,128)(2,1)S(1)}, bf16[1024,512]{1,0:T(8,128)(2,1)}, u32[]{:S(2)}, u32[]{:S(2)}) collective-permute-start(bf16[1024,512]{1,0:T(8,128)(2,1)S(1)} %collective-permute-done.3.second_ref.refs_0_), channel_id=1, source_target_pairs={{0,1},{1,0},{2,3},{3,2},{4,5},{5,4},{6,7},{7,6},{8,9},{9,8},{10,11... | collective-permute-start | bytes 3145736 | tf_op jit(solution)/shard_map/ppermute | solution.py:322
  52.7 12.3 %collective-permute-start.6 = (bf16[256,768]{1,0:T(8,128)(2,1)}, bf16[256,768]{1,0:T(8,128)(2,1)}, u32[]{:S(2)}, u32[]{:S(2)}) collective-permute-start(bf16[256,768]{1,0:T(8,128)(2,1)} %get-tuple-element.525), channel_id=1, source_target_pairs={{0,4},{4,0},{1,5},{5,1},{2,6},{6,2},{3,7},{7,3},{8,12},{12,8},{9,1... | collective-permute-start | bytes 1179656 | tf_op jit(solution)/shard_map/ppermute | solution.py:322
  56.1 19.2 %collective-permute-start.8 = (bf16[512,512]{1,0:T(8,128)(2,1)}, bf16[512,512]{1,0:T(8,128)(2,1)}, u32[]{:S(2)}, u32[]{:S(2)}) collective-permute-start(bf16[512,512]{1,0:T(8,128)(2,1)} %get-tuple-element.528), channel_id=1, source_target_pairs={{0,4},{4,0},{1,5},{5,1},{2,6},{6,2},{3,7},{7,3},{8,12},{12,8},{9,1... | collective-permute-start | bytes 1572872 | tf_op jit(solution)/shard_map/ppermute | solution.py:322
  56.7 18.6 %collective-permute-start.9 = (bf16[512,512]{1,0:T(8,128)(2,1)}, bf16[512,512]{1,0:T(8,128)(2,1)}, u32[]{:S(2)}, u32[]{:S(2)}) collective-permute-start(bf16[512,512]{1,0:T(8,128)(2,1)} %get-tuple-element.529), channel_id=1, source_target_pairs={{0,2},{2,0},{1,3},{3,1},{4,6},{6,4},{5,7},{7,5},{8,10},{10,8},{9,1... | collective-permute-start | bytes 1572872 | tf_op jit(solution)/shard_map/ppermute | solution.py:322
  75.3 213.8 %all-gather.8.cloned.1.call-start = ((), (), s32[]{:S(2)}) async-start(), calls=%async_computation.6 | async-start | bytes 7864320 | tf_op jit(solution)/shard_map/all_gather | solution.py:467
  77.1 24.4 %collective-permute-start.12 = (bf16[1024,512]{1,0:T(8,128)(2,1)S(1)}, bf16[1024,512]{1,0:T(8,128)(2,1)}, u32[]{:S(2)}, u32[]{:S(2)}) collective-permute-start(bf16[1024,512]{1,0:T(8,128)(2,1)S(1)} %get-tuple-element.614.refs_0_), channel_id=1, source_target_pairs={{0,2},{2,0},{1,3},{3,1},{4,6},{6,4},{5,7},{7,5},{8,10},{10,8},{9,1... | collective-permute-start | bytes 3145736 | tf_op jit(solution)/shard_map/ppermute | solution.py:322
  78.5 24.1 %collective-permute-start.13 = (bf16[1024,512]{1,0:T(8,128)(2,1)S(1)}, bf16[1024,512]{1,0:T(8,128)(2,1)}, u32[]{:S(2)}, u32[]{:S(2)}) collective-permute-start(bf16[1024,512]{1,0:T(8,128)(2,1)S(1)} %get-tuple-element.614.refs_0_), channel_id=1, source_target_pairs={{0,4},{4,0},{1,5},{5,1},{2,6},{6,2},{3,7},{7,3},{8,12},{12,8},{9,1... | collective-permute-start | bytes 3145736 | tf_op jit(solution)/shard_map/ppermute | solution.py:322
  80.0 22.6 %collective-permute-start.14 = (bf16[1024,512]{1,0:T(8,128)(2,1)S(1)}, bf16[1024,512]{1,0:T(8,128)(2,1)}, u32[]{:S(2)}, u32[]{:S(2)}) collective-permute-start(bf16[1024,512]{1,0:T(8,128)(2,1)S(1)} %get-tuple-element.614.refs_0_), channel_id=1, source_target_pairs={{0,1},{1,0},{2,3},{3,2},{4,5},{5,4},{6,7},{7,6},{8,9},{9,8},{10,11... | collective-permute-start | bytes 3145736 | tf_op jit(solution)/shard_map/ppermute | solution.py:322
  109.3 34.2 %collective-permute-start.15 = (bf16[256,1536]{1,0:T(8,128)(2,1)}, bf16[256,1536]{1,0:T(8,128)(2,1)}, u32[]{:S(2)}, u32[]{:S(2)}) collective-permute-start(bf16[256,1536]{1,0:T(8,128)(2,1)} %get-tuple-element.559), channel_id=1, source_target_pairs={{0,4},{4,0},{1,5},{5,1},{2,6},{6,2},{3,7},{7,3},{8,12},{12,8},{9,1... | collective-permute-start | bytes 2359304 | tf_op jit(solution)/shard_map/ppermute | solution.py:322
  110.8 35.2 %collective-permute-start.16 = (bf16[1024,512]{1,0:T(8,128)(2,1)}, bf16[1024,512]{1,0:T(8,128)(2,1)}, u32[]{:S(2)}, u32[]{:S(2)}) collective-permute-start(bf16[1024,512]{1,0:T(8,128)(2,1)} %collective-permute-done.12.first_ref.refs_2_), channel_id=1, source_target_pairs={{0,1},{1,0},{2,3},{3,2},{4,5},{5,4},{6,7},{7,6},{8,9},{9,8},{10,11... | collective-permute-start | bytes 3145736 | tf_op jit(solution)/shard_map/ppermute | solution.py:322
  110.8 35.2 %collective-permute-start.17 = (bf16[1024,512]{1,0:T(8,128)(2,1)}, bf16[1024,512]{1,0:T(8,128)(2,1)}, u32[]{:S(2)}, u32[]{:S(2)}) collective-permute-start(bf16[1024,512]{1,0:T(8,128)(2,1)} %collective-permute-done.13.second_ref.refs_0_), channel_id=1, source_target_pairs={{0,1},{1,0},{2,3},{3,2},{4,5},{5,4},{6,7},{7,6},{8,9},{9,8},{10,11... | collective-permute-start | bytes 3145736 | tf_op jit(solution)/shard_map/ppermute | solution.py:322
  113.3 32.7 %collective-permute-start.18 = (bf16[512,512]{1,0:T(8,128)(2,1)}, bf16[512,512]{1,0:T(8,128)(2,1)}, u32[]{:S(2)}, u32[]{:S(2)}) collective-permute-start(bf16[512,512]{1,0:T(8,128)(2,1)} %get-tuple-element.572), channel_id=1, source_target_pairs={{0,4},{4,0},{1,5},{5,1},{2,6},{6,2},{3,7},{7,3},{8,12},{12,8},{9,1... | collective-permute-start | bytes 1572872 | tf_op jit(solution)/shard_map/ppermute | solution.py:322
  113.9 32.1 %collective-permute-start.19 = (bf16[512,512]{1,0:T(8,128)(2,1)}, bf16[512,512]{1,0:T(8,128)(2,1)}, u32[]{:S(2)}, u32[]{:S(2)}) collective-permute-start(bf16[512,512]{1,0:T(8,128)(2,1)} %get-tuple-element.573), channel_id=1, source_target_pairs={{0,2},{2,0},{1,3},{3,1},{4,6},{6,4},{5,7},{7,5},{8,10},{10,8},{9,1... | collective-permute-start | bytes 1572872 | tf_op jit(solution)/shard_map/ppermute | solution.py:322
  146.0 287.9 %reduce-scatter.5.cloned.1.call-start = ((), (), s32[]{:S(2)}) async-start(), calls=%async_computation.7 | async-start | bytes 3932160 | tf_op jit(solution)/shard_map/reduce_scatter | solution.py:471
  170.4 25.8 %collective-permute-start.22 = (bf16[2,512,512]{2,1,0:T(8,128)(2,1)}, bf16[2,512,512]{2,1,0:T(8,128)(2,1)}, u32[]{:S(2)}, u32[]{:S(2)}) collective-permute-start(bf16[2,512,512]{2,1,0:T(8,128)(2,1)} %get-tuple-element.606), channel_id=1, source_target_pairs={{0,4},{4,0},{1,5},{5,1},{2,6},{6,2},{3,7},{7,3},{8,12},{12,8},{9,1... | collective-permute-start | bytes 3145736 | tf_op jit(solution)/shard_map/ppermute | solution.py:322
  171.9 25.5 %collective-permute-start.23 = (bf16[1024,512]{1,0:T(8,128)(2,1)}, bf16[1024,512]{1,0:T(8,128)(2,1)}, u32[]{:S(2)}, u32[]{:S(2)}) collective-permute-start(bf16[1024,512]{1,0:T(8,128)(2,1)} %get-tuple-element.608), channel_id=1, source_target_pairs={{0,2},{2,0},{1,3},{3,1},{4,6},{6,4},{5,7},{7,5},{8,10},{10,8},{9,1... | collective-permute-start | bytes 3145736 | tf_op jit(solution)/shard_map/ppermute | solution.py:322
  200.8 13.3 %collective-permute-start.25 = (bf16[512,512]{1,0:T(8,128)(2,1)}, bf16[512,512]{1,0:T(8,128)(2,1)S(1)}, u32[]{:S(2)}, u32[]{:S(2)}) collective-permute-start(bf16[512,512]{1,0:T(8,128)(2,1)} %get-tuple-element.629), channel_id=1, source_target_pairs={{0,2},{2,0},{1,3},{3,1},{4,6},{6,4},{5,7},{7,5},{8,10},{10,8},{9,1... | collective-permute-start | bytes 1572872 | tf_op jit(solution)/shard_map/ppermute | solution.py:322
  201.2 13.0 %collective-permute-start.26 = (bf16[512,512]{1,0:T(8,128)(2,1)}, bf16[512,512]{1,0:T(8,128)(2,1)S(1)}, u32[]{:S(2)}, u32[]{:S(2)}) collective-permute-start(bf16[512,512]{1,0:T(8,128)(2,1)} %get-tuple-element.631), channel_id=1, source_target_pairs={{0,4},{4,0},{1,5},{5,1},{2,6},{6,2},{3,7},{7,3},{8,12},{12,8},{9,1... | collective-permute-start | bytes 1572872 | tf_op jit(solution)/shard_map/ppermute | solution.py:322
  218.0 23.7 %collective-permute-start.27 = (bf16[1024,512]{1,0:T(8,128)(2,1)}, bf16[1024,512]{1,0:T(8,128)(2,1)}, u32[]{:S(2)}, u32[]{:S(2)}) collective-permute-start(bf16[1024,512]{1,0:T(8,128)(2,1)} %get-tuple-element.764.refs_0_), channel_id=1, source_target_pairs={{0,2},{2,0},{1,3},{3,1},{4,6},{6,4},{5,7},{7,5},{8,10},{10,8},{9,1... | collective-permute-start | bytes 3145736 | tf_op jit(solution)/shard_map/ppermute | solution.py:322
  219.6 23.2 %collective-permute-start.28 = (bf16[1024,512]{1,0:T(8,128)(2,1)}, bf16[1024,512]{1,0:T(8,128)(2,1)}, u32[]{:S(2)}, u32[]{:S(2)}) collective-permute-start(bf16[1024,512]{1,0:T(8,128)(2,1)} %get-tuple-element.764.refs_0_), channel_id=1, source_target_pairs={{0,4},{4,0},{1,5},{5,1},{2,6},{6,2},{3,7},{7,3},{8,12},{12,8},{9,1... | collective-permute-start | bytes 3145736 | tf_op jit(solution)/shard_map/ppermute | solution.py:322
  220.2 22.7 %collective-permute-start.29 = (bf16[1024,512]{1,0:T(8,128)(2,1)}, bf16[1024,512]{1,0:T(8,128)(2,1)}, u32[]{:S(2)}, u32[]{:S(2)}) collective-permute-start(bf16[1024,512]{1,0:T(8,128)(2,1)} %get-tuple-element.764.refs_0_), channel_id=1, source_target_pairs={{0,1},{1,0},{2,3},{3,2},{4,5},{5,4},{6,7},{7,6},{8,9},{9,8},{10,11... | collective-permute-start | bytes 3145736 | tf_op jit(solution)/shard_map/ppermute | solution.py:322
  242.9 17.0 %collective-permute-start.30 = (bf16[1024,512]{1,0:T(8,128)(2,1)}, bf16[1024,512]{1,0:T(8,128)(2,1)}, u32[]{:S(2)}, u32[]{:S(2)}) collective-permute-start(bf16[1024,512]{1,0:T(8,128)(2,1)} %collective-permute-done.28.second_ref.refs_0_), channel_id=1, source_target_pairs={{0,1},{1,0},{2,3},{3,2},{4,5},{5,4},{6,7},{7,6},{8,9},{9,8},{10,11... | collective-permute-start | bytes 3145736 | tf_op jit(solution)/shard_map/ppermute | solution.py:322
  245.4 14.1 %collective-permute-start.31 = (bf16[512,512]{1,0:T(8,128)(2,1)}, bf16[512,512]{1,0:T(8,128)(2,1)}, u32[]{:S(2)}, u32[]{:S(2)}) collective-permute-start(bf16[512,512]{1,0:T(8,128)(2,1)} %get-tuple-element.658), channel_id=1, source_target_pairs={{0,4},{4,0},{1,5},{5,1},{2,6},{6,2},{3,7},{7,3},{8,12},{12,8},{9,1... | collective-permute-start | bytes 1572872 | tf_op jit(solution)/shard_map/ppermute | solution.py:322
  246.1 13.9 %collective-permute-start.32 = (bf16[512,512]{1,0:T(8,128)(2,1)}, bf16[512,512]{1,0:T(8,128)(2,1)}, u32[]{:S(2)}, u32[]{:S(2)}) collective-permute-start(bf16[512,512]{1,0:T(8,128)(2,1)} %get-tuple-element.659), channel_id=1, source_target_pairs={{0,2},{2,0},{1,3},{3,1},{4,6},{6,4},{5,7},{7,5},{8,10},{10,8},{9,1... | collective-permute-start | bytes 1572872 | tf_op jit(solution)/shard_map/ppermute | solution.py:322
  320.8 11.4 %collective-permute-start.35 = (bf16[2048,512]{1,0:T(8,128)(2,1)}, bf16[2048,512]{1,0:T(8,128)(2,1)}, u32[]{:S(2)}, u32[]{:S(2)}) collective-permute-start(bf16[2048,512]{1,0:T(8,128)(2,1)} %get-tuple-element.692), channel_id=1, source_target_pairs={{0,1},{1,0},{2,3},{3,2},{4,5},{5,4},{6,7},{7,6},{8,9},{9,8},{10,11... | collective-permute-start | bytes 6291464 | tf_op jit(solution)/shard_map/ppermute | solution.py:322
  320.8 11.3 %collective-permute-start.36 = (bf16[2048,512]{1,0:T(8,128)(2,1)}, bf16[2048,512]{1,0:T(8,128)(2,1)}, u32[]{:S(2)}, u32[]{:S(2)}) collective-permute-start(bf16[2048,512]{1,0:T(8,128)(2,1)} %get-tuple-element.693), channel_id=1, source_target_pairs={{0,1},{1,0},{2,3},{3,2},{4,5},{5,4},{6,7},{7,6},{8,9},{9,8},{10,11... | collective-permute-start | bytes 6291464 | tf_op jit(solution)/shard_map/ppermute | solution.py:322
  332.2 138.1 %reduce-scatter.7.cloned.1.call-start = ((), (), s32[]{:S(2)}) async-start(), calls=%async_computation.8 | async-start | bytes 3932160 | tf_op jit(solution)/shard_map/reduce_scatter | solution.py:471
  345.7 25.4 %collective-permute-start.37 = (bf16[2,512,512]{2,1,0:T(8,128)(2,1)}, bf16[2,512,512]{2,1,0:T(8,128)(2,1)}, u32[]{:S(2)}, u32[]{:S(2)}) collective-permute-start(bf16[2,512,512]{2,1,0:T(8,128)(2,1)} %get-tuple-element.716), channel_id=1, source_target_pairs={{0,4},{4,0},{1,5},{5,1},{2,6},{6,2},{3,7},{7,3},{8,12},{12,8},{9,1... | collective-permute-start | bytes 3145736 | tf_op jit(solution)/shard_map/ppermute | solution.py:322
  347.2 25.2 %collective-permute-start.38 = (bf16[1024,512]{1,0:T(8,128)(2,1)}, bf16[1024,512]{1,0:T(8,128)(2,1)}, u32[]{:S(2)}, u32[]{:S(2)}) collective-permute-start(bf16[1024,512]{1,0:T(8,128)(2,1)} %get-tuple-element.718), channel_id=1, source_target_pairs={{0,2},{2,0},{1,3},{3,1},{4,6},{6,4},{5,7},{7,5},{8,10},{10,8},{9,1... | collective-permute-start | bytes 3145736 | tf_op jit(solution)/shard_map/ppermute | solution.py:322
  372.4 146.8 %reduce-scatter.9.cloned.1.call-start = ((), (), s32[]{:S(2)}) async-start(), calls=%async_computation.9 | async-start | bytes 3932160 | tf_op jit(solution)/shard_map/reduce_scatter | solution.py:471
  372.4 19.5 %collective-permute-start.41 = (bf16[2048,512]{1,0:T(8,128)(2,1)}, bf16[2048,512]{1,0:T(8,128)(2,1)}, u32[]{:S(2)}, u32[]{:S(2)}) collective-permute-start(bf16[2048,512]{1,0:T(8,128)(2,1)} %get-tuple-element.742), channel_id=1, source_target_pairs={{0,1},{1,0},{2,3},{3,2},{4,5},{5,4},{6,7},{7,6},{8,9},{9,8},{10,11... | collective-permute-start | bytes 6291464 | tf_op jit(solution)/shard_map/ppermute | solution.py:322
  372.5 19.5 %collective-permute-start.42 = (bf16[2048,512]{1,0:T(8,128)(2,1)}, bf16[2048,512]{1,0:T(8,128)(2,1)}, u32[]{:S(2)}, u32[]{:S(2)}) collective-permute-start(bf16[2048,512]{1,0:T(8,128)(2,1)} %get-tuple-element.743), channel_id=1, source_target_pairs={{0,1},{1,0},{2,3},{3,2},{4,5},{5,4},{6,7},{7,6},{8,9},{9,8},{10,11... | collective-permute-start | bytes 6291464 | tf_op jit(solution)/shard_map/ppermute | solution.py:322
  376.4 14.3 %collective-permute-start.39 = (bf16[512,512]{1,0:T(8,128)(2,1)}, bf16[512,512]{1,0:T(8,128)(2,1)}, u32[]{:S(2)}, u32[]{:S(2)}) collective-permute-start(bf16[512,512]{1,0:T(8,128)(2,1)} %get-tuple-element.739), channel_id=1, source_target_pairs={{0,2},{2,0},{1,3},{3,1},{4,6},{6,4},{5,7},{7,5},{8,10},{10,8},{9,1... | collective-permute-start | bytes 1572872 | tf_op jit(solution)/shard_map/ppermute | solution.py:322
  378.0 13.9 %collective-permute-start.40 = (bf16[512,512]{1,0:T(8,128)(2,1)}, bf16[512,512]{1,0:T(8,128)(2,1)}, u32[]{:S(2)}, u32[]{:S(2)}) collective-permute-start(bf16[512,512]{1,0:T(8,128)(2,1)} %get-tuple-element.741), channel_id=1, source_target_pairs={{0,4},{4,0},{1,5},{5,1},{2,6},{6,2},{3,7},{7,3},{8,12},{12,8},{9,1... | collective-permute-start | bytes 1572872 | tf_op jit(solution)/shard_map/ppermute | solution.py:322
  409.0 24.8 %collective-permute-start.45 = (bf16[1024,512]{1,0:T(8,128)(2,1)}, bf16[1024,512]{1,0:T(8,128)(2,1)}, u32[]{:S(2)}, u32[]{:S(2)}) collective-permute-start(bf16[1024,512]{1,0:T(8,128)(2,1)} %get-tuple-element.793.refs_0_), channel_id=1, source_target_pairs={{0,2},{2,0},{1,3},{3,1},{4,6},{6,4},{5,7},{7,5},{8,10},{10,8},{9,1... | collective-permute-start | bytes 3145736 | tf_op jit(solution)/shard_map/ppermute | solution.py:322
  409.5 24.3 %collective-permute-start.46 = (bf16[1024,512]{1,0:T(8,128)(2,1)}, bf16[1024,512]{1,0:T(8,128)(2,1)}, u32[]{:S(2)}, u32[]{:S(2)}) collective-permute-start(bf16[1024,512]{1,0:T(8,128)(2,1)} %get-tuple-element.793.refs_0_), channel_id=1, source_target_pairs={{0,4},{4,0},{1,5},{5,1},{2,6},{6,2},{3,7},{7,3},{8,12},{12,8},{9,1... | collective-permute-start | bytes 3145736 | tf_op jit(solution)/shard_map/ppermute | solution.py:322
  410.1 23.7 %collective-permute-start.47 = (bf16[1024,512]{1,0:T(8,128)(2,1)}, bf16[1024,512]{1,0:T(8,128)(2,1)}, u32[]{:S(2)}, u32[]{:S(2)}) collective-permute-start(bf16[1024,512]{1,0:T(8,128)(2,1)} %get-tuple-element.793.refs_0_), channel_id=1, source_target_pairs={{0,1},{1,0},{2,3},{3,2},{4,5},{5,4},{6,7},{7,6},{8,9},{9,8},{10,11... | collective-permute-start | bytes 3145736 | tf_op jit(solution)/shard_map/ppermute | solution.py:322
  433.9 161.3 %reduce-scatter.11.cloned.1.call-start = ((), (), s32[]{:S(2)}) async-start(), calls=%async_computation.10 | async-start | bytes 5242880 | tf_op jit(solution)/shard_map/reduce_scatter | solution.py:471
  434.0 17.3 %collective-permute-start.48 = (bf16[1024,512]{1,0:T(8,128)(2,1)}, bf16[1024,512]{1,0:T(8,128)(2,1)}, u32[]{:S(2)}, u32[]{:S(2)}) collective-permute-start(bf16[1024,512]{1,0:T(8,128)(2,1)} %collective-permute-done.46.second_ref.refs_0_), channel_id=1, source_target_pairs={{0,1},{1,0},{2,3},{3,2},{4,5},{5,4},{6,7},{7,6},{8,9},{9,8},{10,11... | collective-permute-start | bytes 3145736 | tf_op jit(solution)/shard_map/ppermute | solution.py:322
  436.9 14.2 %collective-permute-start.49 = (bf16[512,512]{1,0:T(8,128)(2,1)}, bf16[512,512]{1,0:T(8,128)(2,1)}, u32[]{:S(2)}, u32[]{:S(2)}) collective-permute-start(bf16[512,512]{1,0:T(8,128)(2,1)} %get-tuple-element.791), channel_id=1, source_target_pairs={{0,4},{4,0},{1,5},{5,1},{2,6},{6,2},{3,7},{7,3},{8,12},{12,8},{9,1... | collective-permute-start | bytes 1572872 | tf_op jit(solution)/shard_map/ppermute | solution.py:322
  437.4 13.9 %collective-permute-start.50 = (bf16[512,512]{1,0:T(8,128)(2,1)}, bf16[512,512]{1,0:T(8,128)(2,1)}, u32[]{:S(2)}, u32[]{:S(2)}) collective-permute-start(bf16[512,512]{1,0:T(8,128)(2,1)} %get-tuple-element.792), channel_id=1, source_target_pairs={{0,2},{2,0},{1,3},{3,1},{4,6},{6,4},{5,7},{7,5},{8,10},{10,8},{9,1... | collective-permute-start | bytes 1572872 | tf_op jit(solution)/shard_map/ppermute | solution.py:322
  456.9 13.4 %collective-permute-start.52 = (bf16[256,768]{1,0:T(8,128)(2,1)}, bf16[256,768]{1,0:T(8,128)(2,1)}, u32[]{:S(2)}, u32[]{:S(2)}) collective-permute-start(bf16[256,768]{1,0:T(8,128)(2,1)} %constant_dynamic-slice_fusion.3), channel_id=1, source_target_pairs={{0,4},{4,0},{1,5},{5,1},{2,6},{6,2},{3,7},{7,3},{8,12},{12,8},{9,1... | collective-permute-start | bytes 1179656 | tf_op jit(solution)/shard_map/ppermute | solution.py:322
  470.3 25.7 %collective-permute-start.54 = (bf16[2,512,512]{2,1,0:T(8,128)(2,1)}, bf16[2,512,512]{2,1,0:T(8,128)(2,1)S(1)}, u32[]{:S(2)}, u32[]{:S(2)}) collective-permute-start(bf16[2,512,512]{2,1,0:T(8,128)(2,1)} %get-tuple-element.829), channel_id=1, source_target_pairs={{0,4},{4,0},{1,5},{5,1},{2,6},{6,2},{3,7},{7,3},{8,12},{12,8},{9,1... | collective-permute-start | bytes 3145736 | tf_op jit(solution)/shard_map/ppermute | solution.py:322
  471.4 25.2 %collective-permute-start.55 = (bf16[1024,512]{1,0:T(8,128)(2,1)}, bf16[1024,512]{1,0:T(8,128)(2,1)S(1)}, u32[]{:S(2)}, u32[]{:S(2)}) collective-permute-start(bf16[1024,512]{1,0:T(8,128)(2,1)} %get-tuple-element.831), channel_id=1, source_target_pairs={{0,2},{2,0},{1,3},{3,1},{4,6},{6,4},{5,7},{7,5},{8,10},{10,8},{9,1... | collective-permute-start | bytes 3145736 | tf_op jit(solution)/shard_map/ppermute | solution.py:322
  504.3 13.4 %collective-permute-start.56 = (bf16[2048,512]{1,0:T(8,128)(2,1)}, bf16[2048,512]{1,0:T(8,128)(2,1)S(1)}, u32[]{:S(2)}, u32[]{:S(2)}) collective-permute-start(bf16[2048,512]{1,0:T(8,128)(2,1)} %get-tuple-element.840), channel_id=1, source_target_pairs={{0,1},{1,0},{2,3},{3,2},{4,5},{5,4},{6,7},{7,6},{8,9},{9,8},{10,11... | collective-permute-start | bytes 6291464 | tf_op jit(solution)/shard_map/ppermute | solution.py:322
  504.4 13.3 %collective-permute-start.57 = (bf16[2048,512]{1,0:T(8,128)(2,1)}, bf16[2048,512]{1,0:T(8,128)(2,1)}, u32[]{:S(2)}, u32[]{:S(2)}) collective-permute-start(bf16[2048,512]{1,0:T(8,128)(2,1)} %get-tuple-element.841), channel_id=1, source_target_pairs={{0,1},{1,0},{2,3},{3,2},{4,5},{5,4},{6,7},{7,6},{8,9},{9,8},{10,11... | collective-permute-start | bytes 6291464 | tf_op jit(solution)/shard_map/ppermute | solution.py:322
  505.7 12.0 %collective-permute-start.58 = (bf16[256,768]{1,0:T(8,128)(2,1)}, bf16[256,768]{1,0:T(8,128)(2,1)S(1)}, u32[]{:S(2)}, u32[]{:S(2)}) collective-permute-start(bf16[256,768]{1,0:T(8,128)(2,1)} %constant_dynamic-slice_fusion.2), channel_id=1, source_target_pairs={{0,4},{4,0},{1,5},{5,1},{2,6},{6,2},{3,7},{7,3},{8,12},{12,8},{9,1... | collective-permute-start | bytes 1179656 | tf_op jit(solution)/shard_map/ppermute | solution.py:322
  522.7 15.4 %collective-permute-start.60 = (bf16[512,512]{1,0:T(8,128)(2,1)}, bf16[512,512]{1,0:T(8,128)(2,1)S(1)}, u32[]{:S(2)}, u32[]{:S(2)}) collective-permute-start(bf16[512,512]{1,0:T(8,128)(2,1)} %get-tuple-element.872), channel_id=1, source_target_pairs={{0,2},{2,0},{1,3},{3,1},{4,6},{6,4},{5,7},{7,5},{8,10},{10,8},{9,1... | collective-permute-start | bytes 1572872 | tf_op jit(solution)/shard_map/ppermute | solution.py:322
  524.4 13.7 %collective-permute-start.61 = (bf16[512,512]{1,0:T(8,128)(2,1)}, bf16[512,512]{1,0:T(8,128)(2,1)S(1)}, u32[]{:S(2)}, u32[]{:S(2)}) collective-permute-start(bf16[512,512]{1,0:T(8,128)(2,1)} %get-tuple-element.874), channel_id=1, source_target_pairs={{0,4},{4,0},{1,5},{5,1},{2,6},{6,2},{3,7},{7,3},{8,12},{12,8},{9,1... | collective-permute-start | bytes 1572872 | tf_op jit(solution)/shard_map/ppermute | solution.py:322
  525.4 12.6 %collective-permute-start.59 = (f32[6,128]{1,0:T(8,128)S(1)}, f32[6,128]{1,0:T(8,128)S(1)}, u32[]{:S(2)}, u32[]{:S(2)}) collective-permute-start(f32[6,128]{1,0:T(8,128)S(1)} %pad_maximum_fusion.9), channel_id=1, source_target_pairs={{0,4},{4,0},{1,5},{5,1},{2,6},{6,2},{3,7},{7,3},{8,12},{12,8},{9,1... | collective-permute-start | bytes 9224 | tf_op jit(solution)/shard_map/ppermute | solution.py:322
  539.0 24.0 %collective-permute-start.63 = (bf16[2,512,512]{2,1,0:T(8,128)(2,1)}, bf16[2,512,512]{2,1,0:T(8,128)(2,1)S(1)}, u32[]{:S(2)}, u32[]{:S(2)}) collective-permute-start(bf16[2,512,512]{2,1,0:T(8,128)(2,1)} %get-tuple-element.896), channel_id=1, source_target_pairs={{0,4},{4,0},{1,5},{5,1},{2,6},{6,2},{3,7},{7,3},{8,12},{12,8},{9,1... | collective-permute-start | bytes 3145736 | tf_op jit(solution)/shard_map/ppermute | solution.py:322
  540.0 23.7 %collective-permute-start.64 = (bf16[1024,512]{1,0:T(8,128)(2,1)}, bf16[1024,512]{1,0:T(8,128)(2,1)S(1)}, u32[]{:S(2)}, u32[]{:S(2)}) collective-permute-start(bf16[1024,512]{1,0:T(8,128)(2,1)} %get-tuple-element.898), channel_id=1, source_target_pairs={{0,2},{2,0},{1,3},{3,1},{4,6},{6,4},{5,7},{7,5},{8,10},{10,8},{9,1... | collective-permute-start | bytes 3145736 | tf_op jit(solution)/shard_map/ppermute | solution.py:322
  568.1 11.7 %collective-permute-start.66 = (bf16[512,512]{1,0:T(8,128)(2,1)}, bf16[512,512]{1,0:T(8,128)(2,1)S(1)}, u32[]{:S(2)}, u32[]{:S(2)}) collective-permute-start(bf16[512,512]{1,0:T(8,128)(2,1)} %get-tuple-element.919), channel_id=1, source_target_pairs={{0,2},{2,0},{1,3},{3,1},{4,6},{6,4},{5,7},{7,5},{8,10},{10,8},{9,1... | collective-permute-start | bytes 1572872 | tf_op jit(solution)/shard_map/ppermute | solution.py:322
  568.8 11.5 %collective-permute-start.67 = (bf16[512,512]{1,0:T(8,128)(2,1)}, bf16[512,512]{1,0:T(8,128)(2,1)}, u32[]{:S(2)}, u32[]{:S(2)}) collective-permute-start(bf16[512,512]{1,0:T(8,128)(2,1)} %get-tuple-element.921), channel_id=1, source_target_pairs={{0,4},{4,0},{1,5},{5,1},{2,6},{6,2},{3,7},{7,3},{8,12},{12,8},{9,1... | collective-permute-start | bytes 1572872 | tf_op jit(solution)/shard_map/ppermute | solution.py:322
  599.1 14.5 %collective-permute-start.73 = (bf16[256,1024]{1,0:T(8,128)(2,1)}, bf16[256,1024]{1,0:T(8,128)(2,1)}, u32[]{:S(2)}, u32[]{:S(2)}) collective-permute-start(bf16[256,1024]{1,0:T(8,128)(2,1)} %constant_dynamic-slice_fusion), channel_id=1, source_target_pairs={{0,4},{4,0},{1,5},{5,1},{2,6},{6,2},{3,7},{7,3},{8,12},{12,8},{9,1... | collective-permute-start | bytes 1572872 | tf_op jit(solution)/shard_map/ppermute | solution.py:322
  (69 other events, 483.9 us)
Sparse Core Ops, SparseCore 0:
  27.2 82.0 all-gather.3
  110.9 62.0 all-gather.5
  175.1 113.9 all-gather.7
  332.3 58.5 reduce-scatter.4
  393.0 60.2 reduce-scatter.6
  455.5 60.2 reduce-scatter.8
  518.1 77.0 reduce-scatter.10
